TPU v7x, 256 devices: a whole 4x4x8 slice. The times are simulated.
256 devices in a mesh: dp: 8 (over y, core), mp: 32 (over x, z).
Axes of the slice: x: 4, y: 4, z: 8, core: 2. Of those that a mesh axis runs over, the one named last changes fastest.
Arguments:
- acts: bfloat16 [8192, 4096], P('dp', 'mp'), may hold values from -6 to 6
- grad_out: bfloat16 [8192, 14336], P('dp', 'mp'), may hold values from -0.29882812 to 0.29882812
- error_buffer: bfloat16 [32768, 14336], P('dp', 'mp'), may hold values from -6 to 6
- q_prev: float32 [32, 14336], P(None, 'mp'), may hold values from -0.046875 to 0.046875
- weight: float32 [4096, 14336], P('dp', 'mp'), may hold values from -0.12 to 0.12
- moment1: float32 [4096, 14336], P('dp', 'mp'), may hold values from -0.3 to 0.3
- moment2: float32 [4096, 14336], P('dp', 'mp'), may hold values from 1e-05 to 0.001
Outputs:
- new_weight: float32 [4096, 14336], P('dp', 'mp')
- new_moment1: float32 [4096, 14336], P('dp', 'mp')
- new_moment2: float32 [4096, 14336], P('dp', 'mp')
- new_error: bfloat16 [32768, 14336], P('dp', 'mp')
- q_new: float32 [32, 14336], P(None, 'mp')
All inputs are finite; a program needn't handle non-finite values.
Results may differ from a plain program's by a relative error of at most 0.001.
Values may be sent and summed in bfloat16 or wider, within the bound.
No kernel may reach another device: no remote copies, remote signals or barrier semaphores. Data moves between devices by JAX's collectives and lax.ppermute only.
A program may use at most 64 MiB of HBM per device.

v0:
```python
import jax
import jax.numpy as jnp
from jax import lax
from jax.sharding import PartitionSpec as P

ortho_eps = 1e-08
adam_eps = 1e-08
beta_one = 0.9
beta_two = 0.95
learn_rate = 0.01
corr_one = 1.0 - 0.9**10
corr_two = 1.0 - 0.95**10


def orthonormal_rows(panel):
    count = panel.shape[0]
    order = jnp.arange(count, dtype=jnp.int32)

    def visit(index, panel):
        row = lax.dynamic_slice_in_dim(panel, index, 1, 0)
        row = row / (jnp.sqrt(jnp.sum(row * row)) + ortho_eps)
        panel = lax.dynamic_update_slice_in_dim(panel, row, index, 0)
        inner = jnp.dot(panel, row[0], precision=lax.Precision.HIGHEST)
        later = (order > index).astype(panel.dtype)
        return panel - (inner * later)[:, None] * row

    return lax.fori_loop(0, count, visit, panel)


def shards(acts, grad_out, error_buffer, q_prev, weight, moment1, moment2):
    replicas = lax.axis_size("dp")
    grad = lax.dot_general(
        lax.all_gather(acts, "mp", axis=1, tiled=True),
        grad_out,
        (((0,), (0,)), ((), ())),
        preferred_element_type=jnp.float32,
    )
    field = grad + error_buffer.astype(jnp.float32)
    partial_panel = lax.dot_general(
        q_prev, field, (((1,), (1,)), ((), ())), precision=lax.Precision.HIGHEST
    )
    panel = lax.psum(partial_panel, ("dp", "mp")) / replicas
    basis = orthonormal_rows(panel)
    local_right = jnp.dot(basis, field, precision=lax.Precision.HIGHEST)
    q_new = lax.psum(local_right, "dp") / replicas
    approx = lax.dot_general(
        basis, q_new, (((0,), (0,)), ((), ())), precision=lax.Precision.HIGHEST
    )
    new_error = (field - approx).astype(jnp.bfloat16)
    block_rows = weight.shape[0]
    update = lax.dynamic_slice_in_dim(approx, lax.axis_index("dp") * block_rows, block_rows, 0)
    new_moment1 = beta_one * moment1 + (1.0 - beta_one) * update
    new_moment2 = beta_two * moment2 + (1.0 - beta_two) * update * update
    new_weight = weight - learn_rate * (new_moment1 / corr_one) / (
        jnp.sqrt(new_moment2 / corr_two) + adam_eps
    )
    return (new_weight, new_moment1, new_moment2, new_error, q_new)


def solution(mesh):
    placed = (
        P("dp", "mp"),
        P("dp", "mp"),
        P("dp", "mp"),
        P(None, "mp"),
        P("dp", "mp"),
        P("dp", "mp"),
        P("dp", "mp"),
    )
    return jax.shard_map(
        shards,
        mesh=mesh,
        in_specs=placed,
        out_specs=(P("dp", "mp"), P("dp", "mp"), P("dp", "mp"), P("dp", "mp"), P(None, "mp")),
        check_vma=False,
    )
```

profile of v0, /device:TPU:1, one launch (start us, length us, event | category | flops | bytes accessed | tf_op | source)
XLA Modules:
  0.0 513.0 jit_solution(14552253849673698170)
XLA Ops:
  7.2 0.7 all-gather.2.cloned.1.call-update
  8.0 107.5 %all-gather.2.cloned.1.call-done = bf16[1024,4096]{1,0:T(8,128)(2,1)} async-done(((bf16[1024,128]{1,0:T(8,128)(2,1)}), bf16[1024,4096]{1,0:T(8,128)(2,1)}) %all-gather.2.cloned.1.call-update) | async-done | bytes 8388624 | tf_op jit(solution)/shard_map/all_gather | solution.py:33
  115.5 8.4 %convert_add_fusion = f32[4096,448]{0,1:T(8,128)S(1)} fusion(bf16[4096,448]{0,1:T(8,128)(2,1)} %param.11, bf16[1024,448]{0,1:T(8,128)(2,1)S(1)} %copy-done, bf16[1024,4096]{1,0:T(8,128)(2,1)} %all-gather.2.cloned.1.call-done), kind=kOutput, calls=%fused_computation.8 | convolution fusion | flops 3761766400 | bytes 20316160 | tf_op jit(solution)/shard_map/dot_general | solution.py:32
  123.9 2.9 copy-done.1
  126.8 5.2 %convolution_bitcast_fusion.1 = f32[32,4096]{1,0:T(8,128)} fusion(f32[4096,448]{0,1:T(8,128)S(1)} %convert_add_fusion, f32[32,448]{1,0:T(8,128)S(1)} %copy-done.6), kind=kOutput, calls=%fused_computation.9 | convolution fusion | flops 704643072 | bytes 7921664 | tf_op jit(solution)/shard_map/dot_general | solution.py:39
  132.1 250.8 %all-reduce.2.cloned.1.call-done = f32[32,4096]{1,0:T(8,128)} async-done(((f32[32,4096]{1,0:T(8,128)}), f32[32,4096]{1,0:T(8,128)}) %all-reduce.2.cloned.1.call-update) | async-done | bytes 524304 | tf_op jit(solution)/shard_map/psum | solution.py:42
  382.9 1.1 broadcast_multiply_fusion
  384.0 78.5 %while.14 = (s32[]{:T(128)}, f32[32,4096]{1,0:T(8,128)S(1)}, s32[]{:T(128)}, f32[]{:T(128)}, s32[]{:T(128)}) while((s32[]{:T(128)}, f32[32,4096]{1,0:T(8,128)S(1)}, s32[]{:T(128)}, f32[]{:T(128)}, s32[]{:T(128)}) %tuple.38), condition=%wide.region_3.0_spmd.clone, body=%wide.region_1.0_spmd.clone.sunk | while | flops 1847362 | bytes 1687913 | solution.py:27
  391.4 0.6 multiply_reduce_fusion.2
  393.8 0.6 multiply_reduce_fusion.2
  396.3 0.6 multiply_reduce_fusion.2
  398.7 0.6 multiply_reduce_fusion.2
  401.2 0.6 multiply_reduce_fusion.2
  403.6 0.6 multiply_reduce_fusion.2
  406.1 0.6 multiply_reduce_fusion.2
  415.9 0.6 multiply_reduce_fusion.2
  418.4 0.6 multiply_reduce_fusion.2
  420.8 0.6 multiply_reduce_fusion.2
  423.3 0.6 multiply_reduce_fusion.2
  425.7 0.6 multiply_reduce_fusion.2
  462.5 8.6 %fusion.6 = f32[32,448]{1,0:T(8,128)S(1)} fusion(f32[32,4096]{1,0:T(8,128)S(1)} %get-tuple-element.69, f32[4096,448]{0,1:T(8,128)} %copy-done.1), kind=kOutput, calls=%fused_computation.16 | convolution fusion | flops 704643072 | bytes 7921664 | tf_op jit(solution)/shard_map/dot_general | solution.py:44
  471.1 23.1 %psum.15 = f32[32,448]{1,0:T(8,128)S(1)} all-reduce(f32[32,448]{1,0:T(8,128)S(1)} %fusion.6), channel_id=1, replica_groups=mesh['dp'=8,'mp'=32] {'dp'}, use_global_device_ids=true, to_apply=%region_4.0 | all-reduce | flops 14336 | bytes 114688 | tf_op jit(solution)/shard_map/psum | solution.py:45
  494.2 10.0 %subtract_convert_fusion = (bf16[4096,448]{0,1:T(8,128)(2,1)}, f32[4096,448]{0,1:T(8,128)S(1)}) fusion(f32[4096,448]{0,1:T(8,128)} %copy-done.1, f32[32,4096]{1,0:T(8,128)S(1)} %get-tuple-element.69, f32[32,448]{1,0:T(8,128)S(1)} %broadcast_multiply_fusion.1), kind=kOutput, calls=%fused_computation.7 | convolution fusion | flops 708313088 | bytes 18931712 | tf_op jit(solution)/shard_map/dot_general | solution.py:46
  504.2 2.0 divide_subtract_fusion
  (165 shorter events, 47.5 us)
Async XLA Ops:
  7.2 108.3 %copy-start = (bf16[1024,448]{0,1:T(8,128)(2,1)S(1)}, bf16[1024,448]{0,1:T(8,128)(2,1)}, u32[]{:S(2)}) copy-start(bf16[1024,448]{0,1:T(8,128)(2,1)} %param.10) | copy-start | bytes 2752516
  7.2 108.3 %all-gather.2.cloned.1.call-start = ((), (), s32[]{:S(2)}) async-start(), calls=%async_computation | async-start | bytes 8650752 | tf_op jit(solution)/shard_map/all_gather | solution.py:33
  7.9 118.9 %copy-start.6 = (f32[32,448]{1,0:T(8,128)S(1)}, f32[32,448]{1,0:T(8,128)}, u32[]{:S(2)}) copy-start(f32[32,448]{1,0:T(8,128)} %param.12) | copy-start | bytes 172036
  7.9 375.0 %all-reduce.2.cloned.1.call-start = ((), (), s32[]{:S(2)}) async-start(), calls=%async_computation.1 | async-start | bytes 1048576 | tf_op jit(solution)/shard_map/psum | solution.py:42
  123.9 2.9 copy-start.1
  494.2 10.0 %copy-start.5 = (f32[32,448]{1,0:T(8,128)}, f32[32,448]{1,0:T(8,128)S(1)}, u32[]{:S(2)}) copy-start(f32[32,448]{1,0:T(8,128)S(1)} %broadcast_multiply_fusion.1) | copy-start | bytes 172036
  494.2 10.0 %copy-start.2 = (f32[512,448]{0,1:T(8,128)S(1)}, f32[512,448]{0,1:T(8,128)}, u32[]{:S(2)}) copy-start(f32[512,448]{0,1:T(8,128)} %param.13) | copy-start | bytes 2752516
  494.2 10.0 %copy-start.3 = (f32[512,448]{0,1:T(8,128)S(1)}, f32[512,448]{0,1:T(8,128)}, u32[]{:S(2)}) copy-start(f32[512,448]{0,1:T(8,128)} %param.14) | copy-start | bytes 2752516
  494.2 10.0 %copy-start.4 = (f32[512,448]{0,1:T(8,128)S(1)}, f32[512,448]{0,1:T(8,128)}, u32[]{:S(2)}) copy-start(f32[512,448]{0,1:T(8,128)} %param.15) | copy-start | bytes 2752516
Sparse Core Ops, SparseCore 0:
  10.5 104.9 all-gather.1
  132.2 250.6 all-reduce.1
where the time goes:
time: 517 us; the launch traced here: 513 us
  waiting for transfers between devices  359 us (69%)
  matrix products  48.6 us (9%)
  other arithmetic  29.1 us (6%)
  loops' own time  23.4 us (5%)
  blocking collectives  23.1 us (4%)
  local copies, waits for them, and re-layouts  15.5 us (3%)
  between operations  14.2 us (3%)
    psum x1, waiting for transfers between devices, shards(): panel = lax.psum(partial_panel, ('dp', 'mp')) / replicas  251 us
    all_gather x1, waiting for transfers between devices, shards(): lax.all_gather(acts, 'mp', axis=1, tiled=True)  108 us
    another operation x1, loops' own time, orthonormal_rows(): return lax.fori_loop(0, count, visit, panel)  23.4 us
    psum x1, blocking collectives, shards(): q_new = lax.psum(local_right, 'dp') / replicas  23.1 us
    reduce_sum x32, other arithmetic, visit(): row = row / (jnp.sqrt(jnp.sum(row * row)) + ortho_eps)  20.5 us
    dot_general x32, matrix products, visit(): inner = jnp.dot(panel, row[0], precision=lax.Precision.HIGHEST)  16.4 us
    dynamic_update_slice x32, local copies, waits for them, and re-layouts, visit(): panel = lax.dynamic_update_slice_in_dim(panel, row, index, 0)  12.6 us
  transfers between devices with their start and end apart: 2, of which 2 were waited for; matrix products, arithmetic and copies ran while one was open for 0% of the time, Pallas kernels for 0%

commit v1 on v0

v1 whole, which is shorter than its diff:
```python
import functools

import jax
import jax.numpy as jnp
from jax import lax
from jax.experimental import pallas as pl
from jax.experimental.pallas import tpu as pltpu
from jax.sharding import PartitionSpec as P

ortho_eps = 1e-08
adam_eps = 1e-08
beta_one = 0.9
beta_two = 0.95
learn_rate = 0.01
corr_one = 1.0 - 0.9**10
corr_two = 1.0 - 0.95**10

NX, NZ, NDP = 4, 8, 8
NMP = NX * NZ
ROWS = 384
LANES = 128
F32, BF16 = jnp.float32, jnp.bfloat16
MIB = 1 << 20
SMEM = pl.BlockSpec(memory_space=pltpu.SMEM)
VMEM = pl.BlockSpec(memory_space=pltpu.VMEM)


def split3(value):
    hi = value.astype(BF16)
    rest = value - hi.astype(F32)
    mid = rest.astype(BF16)
    lo = (rest - mid.astype(F32)).astype(BF16)
    return jnp.concatenate([hi, mid, lo], axis=0)


def fold3(stacked):
    rows = stacked.shape[0] // 3
    return stacked[:rows] + (stacked[rows : 2 * rows] + stacked[2 * rows :])


def dot_nn(a, b):
    return lax.dot_general(a, b, (((1,), (0,)), ((), ())), preferred_element_type=F32)


def dot_nt(a, b):
    return lax.dot_general(a, b, (((1,), (1,)), ((), ())), preferred_element_type=F32)


def dot_tn(a, b):
    return lax.dot_general(a, b, (((0,), (0,)), ((), ())), preferred_element_type=F32)


def add_all(values):
    while len(values) > 1:
        values = [a + b for a, b in zip(values[::2], values[1::2])] + values[len(values) // 2 * 2 :]
    return values[0]


def lanes(array, block):
    return array[:, block * LANES : (block + 1) * LANES]


def wide(ref, count):
    return jnp.concatenate([ref[block] for block in range(count)], axis=1)


def token_kernel(q_ref, gt_ref, out):
    total = fold3(dot_nn(split3(q_ref[...]), gt_ref[...]))
    columns = total.shape[1] // LANES
    for row in range(total.shape[0] // 8):
        for column in range(columns):
            out[row * columns + column] = lanes(total[row * 8 : row * 8 + 8], column)


def error_kernel(q_ref, et_ref, tokens, out):
    tile = add_all([tokens[member] for member in range(NMP)])
    split = split3(q_ref[...])
    group = 4
    for start in range(0, NMP, group):
        part = fold3(dot_nn(split, et_ref[:, start * LANES : (start + group) * LANES]))
        for block in range(group):
            out[start + block, 0:8, :] = tile
            out[start + block, 8:, :] = lanes(part, block)


def piece_kernel(acts_ref, mixed, out):
    blocks = acts_ref.shape[0] // LANES
    terms = []
    for block in range(blocks):
        factor = jnp.concatenate([mixed[row * blocks + block, 0:8, :] for row in range(NMP // blocks)], axis=0)
        terms.append(dot_nn(split3(factor), acts_ref[block * LANES : (block + 1) * LANES, :]))
    piece = fold3(add_all(terms)) + add_all([mixed[member, 8:, :] for member in range(NMP)])
    for member in range(NDP):
        out[member] = piece


def mean_kernel(pieces, out):
    mean = add_all([pieces[member] for member in range(NDP)]) * (1.0 / NDP)
    for member in range(NMP):
        out[member] = mean


def ortho_kernel(panel_ref, split, panel):
    panel[...] = panel_ref[...]
    blocks, count = panel.shape[0], panel.shape[1]
    groups = count // 8

    def inner_of(index):
        first = index // 8
        sums = [None] * groups
        for block in range(blocks):
            row = panel[block, index : index + 1, :]
            for group in range(first, groups):
                term = panel[block, group * 8 : group * 8 + 8, :] * row
                sums[group] = term if sums[group] is None else sums[group] + term
        return [None if s is None else jnp.sum(s, axis=1, keepdims=True) for s in sums]

    order = lax.broadcasted_iota(jnp.int32, (8, 1), 0)
    for index in range(count):
        first, place = index // 8, index % 8
        inner = inner_of(index)
        scale = 1.0 / (jnp.sqrt(inner[first][place : place + 1, :]) + ortho_eps)
        weights = []
        for group in range(first, groups):
            weight = inner[group] * (scale * scale)
            if group == first:
                weight = jnp.where(order > place, weight, 0.0)
            weights.append(weight)
        for block in range(blocks):
            row = panel[block, index : index + 1, :]
            for group in range(first, groups):
                if group == first and place == 7:
                    continue
                rows = slice(group * 8, group * 8 + 8)
                panel[block, rows, :] = panel[block, rows, :] - weights[group - first] * row
            panel[block, index : index + 1, :] = row * scale
    for block in range(blocks):
        split[block] = split3(panel[block])


def field_kernel(x_ref, acts1, near0, near1, near3, far_a, far_b, basis_ref, et_ref, gt_ref, field, right, acts2, tokens1,
                 tokens2, errors):
    step = pl.program_id(0)

    @pl.when(step == 0)
    def _():
        tokens1[...] = jnp.zeros_like(tokens1)
        tokens2[...] = jnp.zeros_like(tokens2)
        errors[...] = jnp.zeros_like(errors)

    for place, ref in enumerate((near0, near0, near1, near1, near3, near3, far_a, far_b)):

        @pl.when(step == place)
        def _():
            acts2[...] = ref[...]

    count = acts2.shape[0]
    first = wide(acts1.at[:, 0], count)
    second = wide(acts2, count)
    error = et_ref[...]
    basis = wide(basis_ref, count)
    grad = dot_nn(gt_ref[:, :ROWS], first) + dot_nn(gt_ref[:, ROWS:], second)
    field[chunk_at(step, x_ref[0])] = grad + error.astype(F32)
    tokens1[...] += dot_nt(basis, first)
    tokens2[...] += dot_nt(basis, second)
    errors[...] += dot_nt(basis, error)

    @pl.when(step == pl.num_programs(0) - 1)
    def _():
        grads = dot_nt(split3(fold3(tokens1[...])), gt_ref[:, :ROWS])
        grads = grads + dot_nt(split3(fold3(tokens2[...])), gt_ref[:, ROWS:])
        total = fold3(grads) + fold3(errors[...])
        for member in range(NDP):
            right[member] = total


def shift_at(step):
    turn = step // 2
    return jnp.where(turn >= 2, 5 - turn, turn)


def chunk_at(step, x):
    return lax.rem(x - shift_at(step) + NX, NX) * 2 + lax.rem(step, 2)


def final_kernel(dp_ref, pieces, basis_ref, field, weight, moment1, moment2, new_weight, new_moment1, new_moment2,
                 new_error, q_new, updated, rounded, sems):
    mean = add_all([pieces[member] for member in range(NDP)]) * (1.0 / NDP)
    q_new[...] = mean
    stack = split3(mean)
    rows = mean.shape[0]
    hi, mid, lo = stack[:rows], stack[rows : 2 * rows], stack[2 * rows :]
    factor = jnp.concatenate([hi, hi, hi, mid, mid, lo], axis=0)
    chunks = field.shape[0]
    count = basis_ref.shape[0] // chunks

    def approx_of(chunk):
        basis = jnp.concatenate([basis_ref[chunk * count + block] for block in range(count)], axis=1)
        hi, mid, lo = basis[:rows], basis[rows : 2 * rows], basis[2 * rows :]
        return dot_tn(factor, jnp.concatenate([hi, mid, lo, hi, mid, hi], axis=0))

    update = approx_of(dp_ref[0])
    first = beta_one * moment1[...] + (1.0 - beta_one) * update
    second = beta_two * moment2[...] + (1.0 - beta_two) * update * update
    updated[0] = first
    updated[1] = second
    updated[2] = weight[...] - learn_rate * (first / corr_one) / (jnp.sqrt(second / corr_two) + adam_eps)
    copies = []

    def send(source, target):
        copy = pltpu.make_async_copy(source, target, sems.at[len(copies)])
        copy.start()
        copies.append(copy)

    send(updated.at[0], new_moment1)
    send(updated.at[1], new_moment2)
    send(updated.at[2], new_weight)
    width = field.shape[2]
    for chunk in range(chunks):
        rounded[chunk] = (field[chunk] - approx_of(chunk)).astype(BF16)
        send(rounded.at[chunk], new_error.at[:, chunk * width : (chunk + 1) * width])
    for copy in copies:
        copy.wait()


def call(kernel, outs, args, specs=None, out_specs=None, scratch=(), limit=16, flops=0, moved=0):
    return pl.pallas_call(
        kernel,
        out_shape=outs,
        in_specs=specs or [VMEM] * len(args),
        out_specs=out_specs or jax.tree.map(lambda _: VMEM, outs),
        scratch_shapes=scratch,
        compiler_params=pltpu.CompilerParams(vmem_limit_bytes=limit * MIB),
        cost_estimate=pl.CostEstimate(flops=flops, bytes_accessed=moved, transcendentals=0),
    )(*args)


def along_x(value, shift):
    return lax.ppermute(
        value, "mp", [(x * NZ + z, (x + shift) % NX * NZ + z) for x in range(NX) for z in range(NZ)]
    )


def gather_z(value):
    return lax.all_gather(value, "mp", axis=0, axis_index_groups=[[x * NZ + z for z in range(NZ)] for x in range(NX)])


def exchange(value, axis):
    return lax.all_to_all(value, axis, 0, 0)


def shards(acts, grad_out, error_buffer, q_prev, weight, moment1, moment2):
    x = (lax.axis_index("mp") // NZ).astype(jnp.int32).reshape(1)
    dp = lax.axis_index("dp").astype(jnp.int32).reshape(1)
    gt, et = grad_out.T, error_buffer.T
    rank, ff = q_prev.shape
    tokens, model = acts.shape[0], et.shape[1]
    array = jax.ShapeDtypeStruct

    near0 = gather_z(acts[ROWS:])
    head = acts[:ROWS]
    acts1 = gather_z(jnp.stack([head] + [along_x(head, shift) for shift in range(1, NX)]))
    near1, near3 = along_x(near0, 1), along_x(near0, 3)
    far_a, far_b = along_x(near1[: NZ // 2], 1), along_x(near3[NZ // 2 :], 3)

    factor = call(
        token_kernel, array((NMP, 8, LANES), F32), (q_prev, gt), flops=6 * rank * ff * tokens, moved=2 * ff * tokens
    )
    factor = exchange(factor, "mp")
    mixed = call(
        error_kernel, array((NMP, 8 + rank, LANES), F32), (q_prev, et, factor),
        flops=6 * rank * ff * model, moved=2 * ff * model,
    )
    mixed = exchange(mixed, "mp")
    panel = call(piece_kernel, array((NDP, rank, LANES), F32), (acts, mixed), moved=MIB)
    panel = exchange(panel, "dp")
    panel = call(mean_kernel, array((NMP, rank, LANES), F32), (panel,), moved=MIB)
    panel = exchange(panel, "mp")
    basis = call(
        ortho_kernel, array((NMP, 3 * rank, LANES), BF16), (panel,),
        scratch=[pltpu.VMEM((NMP, rank, LANES), F32)], flops=MIB, moved=4 * MIB,
    )

    chunks, count = 8, NZ // 2
    width = model // chunks
    half = lambda first: lambda i, x: (jnp.clip(i - first, 0, 1), 0, 0)
    whole = lambda i, x: (0, 0, 0)
    near = (count, tokens - ROWS, LANES)
    field, right = pl.pallas_call(
        field_kernel,
        grid_spec=pltpu.PrefetchScalarGridSpec(
            num_scalar_prefetch=1,
            grid=(chunks,),
            in_specs=[
                pl.BlockSpec((count, 1, ROWS, LANES), lambda i, x: (lax.rem(i, 2), shift_at(i), 0, 0)),
                pl.BlockSpec(near, half(0)),
                pl.BlockSpec(near, half(2)),
                pl.BlockSpec(near, half(4)),
                pl.BlockSpec(near, whole),
                pl.BlockSpec(near, whole),
                pl.BlockSpec((count, 3 * rank, LANES), lambda i, x: (chunk_at(i, x[0]), 0, 0)),
                pl.BlockSpec((ff, width), lambda i, x: (0, chunk_at(i, x[0]))),
                pl.BlockSpec((ff, tokens), lambda i, x: (0, 0)),
            ],
            out_specs=[VMEM, VMEM],
            scratch_shapes=[
                pltpu.VMEM(near, BF16),
                pltpu.VMEM((3 * rank, ROWS), F32),
                pltpu.VMEM((3 * rank, tokens - ROWS), F32),
                pltpu.VMEM((3 * rank, ff), F32),
            ],
        ),
        out_shape=[array((chunks, ff, width), F32), array((NDP, rank, ff), F32)],
        compiler_params=pltpu.CompilerParams(vmem_limit_bytes=36 * MIB),
        cost_estimate=pl.CostEstimate(flops=2 * model * ff * tokens, bytes_accessed=20 * MIB, transcendentals=0),
    )(x, acts1, near0, near1, near3, far_a, far_b, basis, et, gt)
    right = exchange(right, "dp")

    block = array((ff, width), F32)
    anywhere = pl.BlockSpec(memory_space=pl.ANY)
    outs = call(
        final_kernel,
        [block] * 3 + [array((ff, model), BF16), array((rank, ff), F32)],
        (dp, right, basis, field, weight.T, moment1.T, moment2.T),
        specs=[SMEM] + [VMEM] * 6,
        out_specs=[anywhere] * 4 + [VMEM],
        scratch=[
            pltpu.VMEM((3, ff, width), F32),
            pltpu.VMEM((chunks, ff, width), BF16),
            pltpu.SemaphoreType.DMA((3 + chunks,)),
        ],
        limit=32, flops=12 * rank * model * ff, moved=20 * MIB,
    )
    new_weight, new_moment1, new_moment2, new_error, q_new = outs
    return (new_weight.T, new_moment1.T, new_moment2.T, new_error.T, q_new)


def solution(mesh):
    placed = (
        P("dp", "mp"),
        P("dp", "mp"),
        P("dp", "mp"),
        P(None, "mp"),
        P("dp", "mp"),
        P("dp", "mp"),
        P("dp", "mp"),
    )
    return jax.shard_map(
        shards,
        mesh=mesh,
        in_specs=placed,
        out_specs=(P("dp", "mp"), P("dp", "mp"), P("dp", "mp"), P("dp", "mp"), P(None, "mp")),
        check_vma=False,
    )
```

time: 517 us -> 171 us (0.33)
  waiting for transfers between devices: 359 us -> 40.1 us
  matrix products: 48.6 us -> 0 us
  Pallas kernels: 0 us -> 28.6 us
  other arithmetic: 29.1 us -> 0.8 us
  starting transfers between devices: 0.08 us -> 28 us
  loops' own time: 23.4 us -> 0 us
  blocking collectives: 23.1 us -> 35.2 us
  local copies, waits for them, and re-layouts: 15.5 us -> 22.6 us
    psum x1 -> x0, waiting for transfers between devices: 251 us -> none  [shards(): panel = lax.psum(partial_panel, ('dp', 'mp')) / replicas]
    all_gather x1 -> x2, waiting for transfers between devices: 108 us -> 0.36 us  [gather_z(): lax.all_gather(value, 'mp', axis=0, axis_index_groups=[[x * NZ + z for z...]
    dot_general x36 -> x0, matrix products: 48.6 us -> none  [the longest x32 16.4 us: visit(): inner = jnp.dot(panel, row[0], precision=lax.Precision.HIGHEST)]
    all_to_all x0 -> x3, waiting for transfers between devices: none -> 35.9 us  [exchange(): return lax.all_to_all(value, axis, 0, 0)]
    all_to_all x0 -> x2, blocking collectives: none -> 35.2 us  [exchange(): return lax.all_to_all(value, axis, 0, 0)]
    pallas_call x0 -> x7, Pallas kernels: none -> 28.6 us  [the longest x1 15.5 us: shards(): pl.pallas_call(field_kernel, grid_spec=pltpu.PrefetchScalarGridSpec(num_s...]
    another operation x1 -> x0, loops' own time: 23.4 us -> none  [orthonormal_rows(): return lax.fori_loop(0, count, visit, panel)]
    psum x1 -> x0, blocking collectives: 23.1 us -> none  [shards(): q_new = lax.psum(local_right, 'dp') / replicas]
  transfers between devices with their start and end apart: 2 -> 12, of which waited for: 2 -> 5; matrix products, arithmetic and copies ran while one was open for 0% -> 2% of each run, Pallas kernels for 0% -> 5%
where the time goes in v1:
time: 171 us; the launch traced here: 170 us
  waiting for transfers between devices  40.1 us (23%)
  blocking collectives  35.2 us (21%)
  Pallas kernels  28.6 us (17%)
  starting transfers between devices  28 us (16%)
  local copies, waits for them, and re-layouts  22.6 us (13%)
  between operations  14.2 us (8%)
    all_to_all x3, waiting for transfers between devices, exchange(): return lax.all_to_all(value, axis, 0, 0)  35.9 us
    all_to_all x2, blocking collectives, exchange(): return lax.all_to_all(value, axis, 0, 0)  35.2 us
    unnamed x36, local copies, waits for them, and re-layouts  18.2 us
    all_to_all x3, starting transfers between devices, exchange(): return lax.all_to_all(value, axis, 0, 0)  16.5 us
    pallas_call x1, Pallas kernels, shards(): pl.pallas_call(field_kernel, grid_spec=pltpu.PrefetchScalarGridSpec(num_s...  15.5 us
    pallas_call x6, Pallas kernels, call(): pl.pallas_call(kernel, out_shape=outs, in_specs=specs or [VMEM] * len(arg...  13.2 us
    ppermute x7, starting transfers between devices, along_x(): lax.ppermute(value, 'mp', [(x * NZ + z, (x + shift) % NX * NZ + z) for x...  11.5 us
    ppermute x7, waiting for transfers between devices, along_x(): lax.ppermute(value, 'mp', [(x * NZ + z, (x + shift) % NX * NZ + z) for x...  3.84 us
  transfers between devices with their start and end apart: 12, of which 5 were waited for; matrix products, arithmetic and copies ran while one was open for 2% of the time, Pallas kernels for 5%

profile of v1, /device:TPU:1, one launch (start us, length us, event | category | flops | bytes accessed | tf_op | source)
XLA Modules:
  0.0 169.6 jit_solution(15918344281949897585)
XLA Ops:
  7.2 1.6 slice.13
  9.8 3.7 %collective-permute-start.1 = (bf16[384,128]{1,0:T(8,128)(2,1)S(1)}, bf16[384,128]{1,0:T(8,128)(2,1)S(1)}, u32[]{:S(2)}, u32[]{:S(2)}) collective-permute-start(bf16[384,128]{1,0:T(8,128)(2,1)S(1)} %get-tuple-element.20), channel_id=1, source_target_pairs={{0,16},{1,17},{2,18},{3,19},{4,20},{5,21},{6,22},{7,23},{8,24},{9,... | collective-permute-start | bytes 294920 | tf_op jit(solution)/shard_map/ppermute | solution.py:239
  13.8 2.4 %collective-permute-start.2 = (bf16[384,128]{1,0:T(8,128)(2,1)S(1)}, bf16[384,128]{1,0:T(8,128)(2,1)S(1)}, u32[]{:S(2)}, u32[]{:S(2)}) collective-permute-start(bf16[384,128]{1,0:T(8,128)(2,1)S(1)} %get-tuple-element.20), channel_id=1, source_target_pairs={{0,24},{1,25},{2,26},{3,27},{4,28},{5,29},{6,30},{7,31},{8,0},{9,1... | collective-permute-start | bytes 294920 | tf_op jit(solution)/shard_map/ppermute | solution.py:239
  16.2 3.8 %collective-permute-done = bf16[384,128]{1,0:T(8,128)(2,1)S(1)} collective-permute-done((bf16[384,128]{1,0:T(8,128)(2,1)S(1)}, bf16[384,128]{1,0:T(8,128)(2,1)S(1)}, u32[]{:S(2)}, u32[]{:S(2)}) %collective-permute-start) | collective-permute-done | bytes 98336 | tf_op jit(solution)/shard_map/ppermute | solution.py:239
  23.1 18.5 %all_to_all.25.tokens = f32[32,8,128]{2,1,0:T(8,128)S(1)} all-to-all(f32[32,8,128]{2,1,0:T(8,128)S(1)} %shard_map.110), channel_id=1, replica_groups=mesh['dp'=8,'mp'=32] {'mp'}, dimensions={0} | all-to-all | bytes 262144 | tf_op jit(solution)/shard_map/all_to_all | solution.py:249
  41.6 2.1 %copy-done.1 = bf16[4096,448]{0,1:T(8,128)(2,1)S(1)} copy-done((bf16[4096,448]{0,1:T(8,128)(2,1)S(1)}, bf16[4096,448]{0,1:T(8,128)(2,1)}, u32[]{:S(2)}) %copy-start.1) | copy-done | bytes 3670040
  43.7 1.6 shard_map.111
  45.2 4.7 %all-to-all-start.1 = ((f32[32,40,128]{2,1,0:T(8,128)}), f32[32,40,128]{2,1,0:T(8,128)S(1)}, u32[]{:S(2)}, u32[]{:S(2)}) async-start(f32[32,40,128]{2,1,0:T(8,128)} %shard_map.111), calls=%async_computation.1 | async-start | bytes 1310720 | tf_op jit(solution)/shard_map/all_to_all | solution.py:249
  50.3 2.5 %collective-permute-start.4 = (bf16[8,640,128]{2,1,0:T(8,128)(2,1)}, bf16[8,640,128]{2,1,0:T(8,128)(2,1)S(1)}, u32[]{:S(2)}, u32[]{:S(2)}) collective-permute-start(bf16[8,640,128]{2,1,0:T(8,128)(2,1)} %bitcast.26), channel_id=1, source_target_pairs={{0,24},{1,25},{2,26},{3,27},{4,28},{5,29},{6,30},{7,31},{8,0},{9,1... | collective-permute-start | bytes 3932168 | tf_op jit(solution)/shard_map/ppermute | solution.py:239
  52.8 11.1 %all-to-all-done.1.mixed = f32[32,40,128]{2,1,0:T(8,128)S(1)} async-done(((f32[32,40,128]{2,1,0:T(8,128)}), f32[32,40,128]{2,1,0:T(8,128)S(1)}, u32[]{:S(2)}, u32[]{:S(2)}) %all-to-all-start.1) | async-done | bytes 655392 | tf_op jit(solution)/shard_map/all_to_all | solution.py:249
  64.1 16.7 %all_to_all.26.pieces = f32[8,32,128]{2,1,0:T(8,128)S(1)} all-to-all(f32[8,32,128]{2,1,0:T(8,128)S(1)} %shard_map.112), channel_id=1, replica_groups=mesh['dp'=8,'mp'=32] {'dp'}, dimensions={0} | all-to-all | bytes 262144 | tf_op jit(solution)/shard_map/all_to_all | solution.py:249
  81.7 4.9 %all-to-all-start.3 = ((f32[32,32,128]{2,1,0:T(8,128)}), f32[32,32,128]{2,1,0:T(8,128)S(1)}, u32[]{:S(2)}, u32[]{:S(2)}) async-start(f32[32,32,128]{2,1,0:T(8,128)} %shard_map.113), calls=%async_computation.3 | async-start | bytes 1048576 | tf_op jit(solution)/shard_map/all_to_all | solution.py:249
  87.5 2.7 %collective-permute-start.6 = (bf16[4,640,128]{2,1,0:T(8,128)(2,1)}, bf16[4,640,128]{2,1,0:T(8,128)(2,1)}, u32[]{:S(2)}, u32[]{:S(2)}) collective-permute-start(bf16[4,640,128]{2,1,0:T(8,128)(2,1)} %slice.17), channel_id=1, source_target_pairs={{0,24},{1,25},{2,26},{3,27},{4,28},{5,29},{6,30},{7,31},{8,0},{9,1... | collective-permute-start | bytes 1966088 | tf_op jit(solution)/shard_map/ppermute | solution.py:239
  91.1 15.2 %all-to-all-done.3.panel_ref = f32[32,32,128]{2,1,0:T(8,128)S(1)} async-done(((f32[32,32,128]{2,1,0:T(8,128)}), f32[32,32,128]{2,1,0:T(8,128)S(1)}, u32[]{:S(2)}, u32[]{:S(2)}) %all-to-all-start.3) | async-done | bytes 524320 | tf_op jit(solution)/shard_map/all_to_all | solution.py:249
  106.4 5.8 %shard_map.114.basis_ref = bf16[32,96,128]{2,1,0:T(8,128)(2,1)S(1)} custom-call(f32[32,32,128]{2,1,0:T(8,128)S(1)} %all-to-all-done.3.panel_ref), custom_call_target="tpu_custom_call" | custom-call | flops 1048576 | bytes 4194304 | tf_op jit(solution)/shard_map/pallas_call | solution.py:227
  112.3 2.0 %copy-done.2 = bf16[4096,448]{0,1:T(8,128)(2,1)S(1)} copy-done((bf16[4096,448]{0,1:T(8,128)(2,1)S(1)}, bf16[4096,448]{0,1:T(8,128)(2,1)}, u32[]{:S(2)}) %copy-start.2) | copy-done | bytes 3670040
  116.8 1.3 copy-done.13
  118.1 1.9 %copy-done.16 = bf16[32,384,128]{2,1,0:T(8,128)(2,1)S(1)} copy-done((bf16[32,384,128]{2,1,0:T(8,128)(2,1)S(1)}, bf16[32,384,128]{2,1,0:T(8,128)(2,1)}, u32[]{:S(2)}) %copy-start.16) | copy-done | bytes 3145752
  120.0 1.3 copy-done.17
  121.4 15.5 %shard_map.115 = (f32[8,448,512]{2,1,0:T(8,128)}, f32[8,32,448]{2,1,0:T(8,128)S(1)}) custom-call(s32[1]{0:T(128)} %bitcast.1.x_ref, bf16[8,4,384,128]{3,2,1,0:T(8,128)(2,1)S(1)} %bitcast.25, bf16[8,640,128]{2,1,0:T(8,128)(2,1)S(1)} %bitcast.28, bf16[8,640,128]{2,1,0:T(8,128)(2,1)S(1)} %copy-done.13, bf16[8,640,128]{2,1,0:T(8,128)(2,1)S(1)} %copy-done.11, ...), custom_call_target="tpu_custom_call" | custom-call | flops 3758096384 | bytes 20971520 | tf_op jit(solution)/shard_map/pallas_call | solution.py:289
  137.6 6.9 %all-to-all-start.4 = ((f32[8,32,448]{2,1,0:T(8,128)}), f32[8,32,448]{2,1,0:T(8,128)S(1)}, u32[]{:S(2)}, u32[]{:S(2)}) async-start(f32[8,32,448]{2,1,0:T(8,128)} %copy-done.9), calls=%async_computation.4 | async-start | bytes 1048576 | tf_op jit(solution)/shard_map/all_to_all | solution.py:249
  144.5 9.5 %all-to-all-done.4.pieces = f32[8,32,448]{2,1,0:T(8,128)S(1)} async-done(((f32[8,32,448]{2,1,0:T(8,128)}), f32[8,32,448]{2,1,0:T(8,128)S(1)}, u32[]{:S(2)}, u32[]{:S(2)}) %all-to-all-start.4) | async-done | bytes 458784 | tf_op jit(solution)/shard_map/all_to_all | solution.py:249
  154.0 3.1 %copy-done = f32[8,448,512]{2,1,0:T(8,128)S(1)} copy-done((f32[8,448,512]{2,1,0:T(8,128)S(1)}, f32[8,448,512]{2,1,0:T(8,128)}, u32[]{:S(2)}) %copy-start) | copy-done | bytes 7340056
  158.3 4.4 %shard_map.116 = (f32[448,512]{1,0:T(8,128)}, f32[448,512]{1,0:T(8,128)}, f32[448,512]{1,0:T(8,128)}, bf16[448,4096]{1,0:T(8,128)(2,1)}, f32[32,448]{1,0:T(8,128)}) custom-call(s32[1]{0:T(128)} %bitcast.dp_ref, f32[8,32,448]{2,1,0:T(8,128)S(1)} %all-to-all-done.4.pieces, bf16[32,96,128]{2,1,0:T(8,128)(2,1)S(1)} %shard_map.114.basis_ref, ...), custom_call_target="tpu_custom_call" | custom-call | flops 704643072 | bytes 20971520 | tf_op jit(solution)/shard_map/pallas_call | solution.py:227
  (52 shorter events, 12.3 us)
Async XLA Ops:
  7.2 34.5 %copy-start.15 = (f32[32,448]{1,0:T(8,128)S(1)}, f32[32,448]{1,0:T(8,128)}, u32[]{:S(2)}) copy-start(f32[32,448]{1,0:T(8,128)} %q_ref.3) | copy-start | bytes 172036
  7.2 43.1 %all-gather.7.cloned.1.call-start = ((), (), s32[]{:S(2)}) async-start(), calls=%async_computation.6 | async-start | bytes 1474560 | tf_op jit(solution)/shard_map/all_gather | solution.py:245
  8.8 103.4 %all-gather.5.cloned.1.call-start = ((), (), s32[]{:S(2)}) async-start(), calls=%async_computation.5 | async-start | bytes 3538944 | tf_op jit(solution)/shard_map/all_gather | solution.py:245
  9.8 6.3 %collective-permute-start.1 = (bf16[384,128]{1,0:T(8,128)(2,1)S(1)}, bf16[384,128]{1,0:T(8,128)(2,1)S(1)}, u32[]{:S(2)}, u32[]{:S(2)}) collective-permute-start(bf16[384,128]{1,0:T(8,128)(2,1)S(1)} %get-tuple-element.20), channel_id=1, source_target_pairs={{0,16},{1,17},{2,18},{3,19},{4,20},{5,21},{6,22},{7,23},{8,24},{9,... | collective-permute-start | bytes 294920 | tf_op jit(solution)/shard_map/ppermute | solution.py:239
  13.5 6.5 %collective-permute-start = (bf16[384,128]{1,0:T(8,128)(2,1)S(1)}, bf16[384,128]{1,0:T(8,128)(2,1)S(1)}, u32[]{:S(2)}, u32[]{:S(2)}) collective-permute-start(bf16[384,128]{1,0:T(8,128)(2,1)S(1)} %get-tuple-element.20), channel_id=1, source_target_pairs={{0,8},{1,9},{2,10},{3,11},{4,12},{5,13},{6,14},{7,15},{8,16},{9,17... | collective-permute-start | bytes 294920 | tf_op jit(solution)/shard_map/ppermute | solution.py:239
  13.8 6.2 %collective-permute-start.2 = (bf16[384,128]{1,0:T(8,128)(2,1)S(1)}, bf16[384,128]{1,0:T(8,128)(2,1)S(1)}, u32[]{:S(2)}, u32[]{:S(2)}) collective-permute-start(bf16[384,128]{1,0:T(8,128)(2,1)S(1)} %get-tuple-element.20), channel_id=1, source_target_pairs={{0,24},{1,25},{2,26},{3,27},{4,28},{5,29},{6,30},{7,31},{8,0},{9,1... | collective-permute-start | bytes 294920 | tf_op jit(solution)/shard_map/ppermute | solution.py:239
  23.1 40.8 %copy-start.3 = (bf16[1024,128]{1,0:T(8,128)(2,1)S(1)}, bf16[1024,128]{1,0:T(8,128)(2,1)}, u32[]{:S(2)}) copy-start(bf16[1024,128]{1,0:T(8,128)(2,1)} %acts_ref.1) | copy-start | bytes 786436
  41.6 2.1 %copy-start.1 = (bf16[4096,448]{0,1:T(8,128)(2,1)S(1)}, bf16[4096,448]{0,1:T(8,128)(2,1)}, u32[]{:S(2)}) copy-start(bf16[4096,448]{0,1:T(8,128)(2,1)} %param.9) | copy-start | bytes 11010052
  45.2 18.6 %all-to-all-start.1 = ((f32[32,40,128]{2,1,0:T(8,128)}), f32[32,40,128]{2,1,0:T(8,128)S(1)}, u32[]{:S(2)}, u32[]{:S(2)}) async-start(f32[32,40,128]{2,1,0:T(8,128)} %shard_map.111), calls=%async_computation.1 | async-start | bytes 1310720 | tf_op jit(solution)/shard_map/all_to_all | solution.py:249
  50.3 36.3 %collective-permute-start.4 = (bf16[8,640,128]{2,1,0:T(8,128)(2,1)}, bf16[8,640,128]{2,1,0:T(8,128)(2,1)S(1)}, u32[]{:S(2)}, u32[]{:S(2)}) collective-permute-start(bf16[8,640,128]{2,1,0:T(8,128)(2,1)} %bitcast.26), channel_id=1, source_target_pairs={{0,24},{1,25},{2,26},{3,27},{4,28},{5,29},{6,30},{7,31},{8,0},{9,1... | collective-permute-start | bytes 3932168 | tf_op jit(solution)/shard_map/ppermute | solution.py:239
  52.7 37.4 %collective-permute-start.3 = (bf16[8,640,128]{2,1,0:T(8,128)(2,1)}, bf16[8,640,128]{2,1,0:T(8,128)(2,1)S(1)}, u32[]{:S(2)}, u32[]{:S(2)}) collective-permute-start(bf16[8,640,128]{2,1,0:T(8,128)(2,1)} %bitcast.27), channel_id=1, source_target_pairs={{0,8},{1,9},{2,10},{3,11},{4,12},{5,13},{6,14},{7,15},{8,16},{9,17... | collective-permute-start | bytes 3932168 | tf_op jit(solution)/shard_map/ppermute | solution.py:239
  81.7 24.7 %all-to-all-start.3 = ((f32[32,32,128]{2,1,0:T(8,128)}), f32[32,32,128]{2,1,0:T(8,128)S(1)}, u32[]{:S(2)}, u32[]{:S(2)}) async-start(f32[32,32,128]{2,1,0:T(8,128)} %shard_map.113), calls=%async_computation.3 | async-start | bytes 1048576 | tf_op jit(solution)/shard_map/all_to_all | solution.py:249
  86.6 4.6 %copy-start.10 = (bf16[8,640,128]{2,1,0:T(8,128)(2,1)}, bf16[8,640,128]{2,1,0:T(8,128)(2,1)S(1)}, u32[]{:S(2)}) copy-start(bf16[8,640,128]{2,1,0:T(8,128)(2,1)S(1)} %collective-permute-done.4.near3) | copy-start | bytes 3932164
  87.5 24.7 %collective-permute-start.6 = (bf16[4,640,128]{2,1,0:T(8,128)(2,1)}, bf16[4,640,128]{2,1,0:T(8,128)(2,1)}, u32[]{:S(2)}, u32[]{:S(2)}) collective-permute-start(bf16[4,640,128]{2,1,0:T(8,128)(2,1)} %slice.17), channel_id=1, source_target_pairs={{0,24},{1,25},{2,26},{3,27},{4,28},{5,29},{6,30},{7,31},{8,0},{9,1... | collective-permute-start | bytes 1966088 | tf_op jit(solution)/shard_map/ppermute | solution.py:239
  90.2 22.1 %copy-start.12 = (bf16[8,640,128]{2,1,0:T(8,128)(2,1)}, bf16[8,640,128]{2,1,0:T(8,128)(2,1)S(1)}, u32[]{:S(2)}) copy-start(bf16[8,640,128]{2,1,0:T(8,128)(2,1)S(1)} %collective-permute-done.3.near1) | copy-start | bytes 3932164
  91.1 21.1 %collective-permute-start.5 = (bf16[4,640,128]{2,1,0:T(8,128)(2,1)}, bf16[4,640,128]{2,1,0:T(8,128)(2,1)}, u32[]{:S(2)}, u32[]{:S(2)}) collective-permute-start(bf16[4,640,128]{2,1,0:T(8,128)(2,1)} %slice.16), channel_id=1, source_target_pairs={{0,8},{1,9},{2,10},{3,11},{4,12},{5,13},{6,14},{7,15},{8,16},{9,17... | collective-permute-start | bytes 1966088 | tf_op jit(solution)/shard_map/ppermute | solution.py:239
  112.3 2.0 %copy-start.2 = (bf16[4096,448]{0,1:T(8,128)(2,1)S(1)}, bf16[4096,448]{0,1:T(8,128)(2,1)}, u32[]{:S(2)}) copy-start(bf16[4096,448]{0,1:T(8,128)(2,1)} %param.9) | copy-start | bytes 11010052
  116.8 1.3 copy-start.13
  118.1 1.9 %copy-start.16 = (bf16[32,384,128]{2,1,0:T(8,128)(2,1)S(1)}, bf16[32,384,128]{2,1,0:T(8,128)(2,1)}, u32[]{:S(2)}) copy-start(bf16[32,384,128]{2,1,0:T(8,128)(2,1)} %all-gather.5.cloned.1.call-done) | copy-start | bytes 9437188
  120.0 1.3 copy-start.17
  121.4 32.7 %copy-start.4 = (f32[512,448]{0,1:T(8,128)S(1)}, f32[512,448]{0,1:T(8,128)}, u32[]{:S(2)}) copy-start(f32[512,448]{0,1:T(8,128)} %param.11) | copy-start | bytes 2752516
  121.4 32.7 %copy-start.5 = (f32[512,448]{0,1:T(8,128)S(1)}, f32[512,448]{0,1:T(8,128)}, u32[]{:S(2)}) copy-start(f32[512,448]{0,1:T(8,128)} %param.12) | copy-start | bytes 2752516
  137.6 16.4 %all-to-all-start.4 = ((f32[8,32,448]{2,1,0:T(8,128)}), f32[8,32,448]{2,1,0:T(8,128)S(1)}, u32[]{:S(2)}, u32[]{:S(2)}) async-start(f32[8,32,448]{2,1,0:T(8,128)} %copy-done.9), calls=%async_computation.4 | async-start | bytes 1048576 | tf_op jit(solution)/shard_map/all_to_all | solution.py:249
  154.0 3.1 %copy-start = (f32[8,448,512]{2,1,0:T(8,128)S(1)}, f32[8,448,512]{2,1,0:T(8,128)}, u32[]{:S(2)}) copy-start(f32[8,448,512]{2,1,0:T(8,128)} %get-tuple-element.13.field) | copy-start | bytes 22020100
  (6 other events, 6.5 us)
Sparse Core Ops, SparseCore 0:
  10.4 39.8 all-gather.6
  52.1 59.1 all-gather.4

commit v2 on v1

v2 whole, which is shorter than its diff:
```python
import jax
import jax.numpy as jnp
import numpy as np
from jax import lax
from jax.experimental import pallas as pl
from jax.experimental.pallas import tpu as pltpu
from jax.sharding import PartitionSpec as P

ortho_eps = 1e-08
adam_eps = 1e-08
beta_one = 0.9
beta_two = 0.95
learn_rate = 0.01
corr_one = 1.0 - 0.9**10
corr_two = 1.0 - 0.95**10

NX, NZ, NDP = 4, 8, 8
NMP = NX * NZ
ROWS = 512
LANES = 128
F32, BF16 = jnp.float32, jnp.bfloat16
MIB = 1 << 20
SMEM = pl.BlockSpec(memory_space=pltpu.SMEM)
VMEM = pl.BlockSpec(memory_space=pltpu.VMEM)
HBM = pl.BlockSpec(memory_space=pltpu.HBM)

RING4 = ([1, 0, 3, 2], [3, 2, 1, 0])
RING8 = ([1, 0, 3, 2, 5, 4, 7, 6], [7, 2, 1, 4, 3, 6, 5, 0], [3, 6, 5, 0, 7, 2, 1, 4])
ALONG_Z = [[x * NZ + to for x in range(NX) for to in level] for level in RING8]
ALONG_X = [[to * NZ + z for to in level for z in range(NZ)] for level in RING4]
ALONG_DP = [[1, 0, 3, 2, 5, 4, 7, 6]] + [[to * 2 + core for to in level for core in range(2)] for level in RING4]


def met(levels, members):
    held = [[member] for member in range(members)]
    for level in levels:
        held = [held[member] + held[level[member]] for member in range(members)]
    return np.array(held, np.int32)


def split3(value):
    hi = value.astype(BF16)
    rest = value - hi.astype(F32)
    mid = rest.astype(BF16)
    lo = (rest - mid.astype(F32)).astype(BF16)
    return jnp.concatenate([hi, mid, lo], axis=0)


def fold3(stacked):
    rows = stacked.shape[0] // 3
    return stacked[:rows] + (stacked[rows : 2 * rows] + stacked[2 * rows :])


def dot_nn(a, b):
    return lax.dot_general(a, b, (((1,), (0,)), ((), ())), preferred_element_type=F32)


def dot_nt(a, b):
    return lax.dot_general(a, b, (((1,), (1,)), ((), ())), preferred_element_type=F32)


def dot_tn(a, b):
    return lax.dot_general(a, b, (((0,), (0,)), ((), ())), preferred_element_type=F32)


def add_all(values):
    while len(values) > 1:
        values = [a + b for a, b in zip(values[::2], values[1::2])] + values[len(values) // 2 * 2 :]
    return values[0]


def lanes(array, block):
    return array[:, block * LANES : (block + 1) * LANES]


def wide(ref, count):
    return jnp.concatenate([ref[block] for block in range(count)], axis=1)


def lanes(array, block):
    return array[:, block * LANES : (block + 1) * LANES]


def add_all(values):
    while len(values) > 1:
        values = [a + b for a, b in zip(values[::2], values[1::2])]
    return values[0]


def token_kernel(q_hbm, gt_hbm, out, q_ref, gt_ref, sems):
    copies = [pltpu.make_async_copy(q_hbm, q_ref, sems.at[0]), pltpu.make_async_copy(gt_hbm, gt_ref, sems.at[1])]
    for copy in copies:
        copy.start()
    for copy in copies:
        copy.wait()
    out[...] = fold3(dot_nn(split3(q_ref[...]), gt_ref[...]))


def error_kernel(q_hbm, et_hbm, out, q_ref, et_ref, sems):
    count = et_ref.shape[0]
    width = et_ref.shape[2]
    copies = [
        pltpu.make_async_copy(et_hbm.at[:, chunk * width : (chunk + 1) * width], et_ref.at[chunk], sems.at[chunk])
        for chunk in range(count)
    ]
    first = pltpu.make_async_copy(q_hbm, q_ref, sems.at[count])
    first.start()
    for copy in copies:
        copy.start()
    first.wait()
    split = split3(q_ref[...])
    blocks = width // LANES
    for chunk in range(count):
        copies[chunk].wait()
        part = fold3(dot_nn(split, et_ref[chunk]))
        for block in range(blocks):
            out[chunk * blocks + block] = lanes(part, block)


def piece_kernel(factor, acts_ref, errors, out):
    piece = fold3(dot_nn(split3(factor[...]), acts_ref[...]))
    out[0] = piece + add_all([errors[member] for member in range(NMP)])


def ortho_kernel(place_ref, mine, theirs, split, panel):
    for block in range(NMP // 2):
        panel[place_ref[block]] = mine[block] * (1.0 / NDP)
        panel[place_ref[NMP // 2 + block]] = theirs[block] * (1.0 / NDP)
    blocks, count = panel.shape[0], panel.shape[1]
    groups = count // 8

    def inner_of(index):
        first = index // 8
        sums = [None] * groups
        for block in range(blocks):
            row = panel[block, index : index + 1, :]
            for group in range(first, groups):
                term = panel[block, group * 8 : group * 8 + 8, :] * row
                sums[group] = term if sums[group] is None else sums[group] + term
        return [None if s is None else jnp.sum(s, axis=1, keepdims=True) for s in sums]

    order = lax.broadcasted_iota(jnp.int32, (8, 1), 0)
    for index in range(count):
        first, place = index // 8, index % 8
        inner = inner_of(index)
        scale = 1.0 / (jnp.sqrt(inner[first][place : place + 1, :]) + ortho_eps)
        weights = []
        for group in range(first, groups):
            weight = inner[group] * (scale * scale)
            if group == first:
                weight = jnp.where(order > place, weight, 0.0)
            weights.append(weight)
        for block in range(blocks):
            row = panel[block, index : index + 1, :]
            for group in range(first, groups):
                if group == first and place == 7:
                    continue
                rows = slice(group * 8, group * 8 + 8)
                panel[block, rows, :] = panel[block, rows, :] - weights[group - first] * row
            panel[block, index : index + 1, :] = row * scale
    for block in range(blocks):
        split[block] = split3(panel[block])


def field_kernel(x_ref, place_ref, head, *refs):
    tails = refs[:8]
    basis_ref, et_hbm, gt_hbm, field, right, acts_v, error_v, gt_v, field_v, total = refs[8:18]
    tail_sems, head_sems, error_sems, field_sems = refs[18:]
    steps, count = acts_v.shape[0], acts_v.shape[1]
    below = pl.ds(ROWS, acts_v.shape[2] - ROWS)

    def block_at(step, k):
        turn = step // 2
        shift = jnp.where(turn >= 2, 5 - turn, turn)
        return lax.rem(x_ref[0] - shift + NX, NX) * NZ + place_ref[lax.rem(step, 2) * count + k]

    def fetch(step):
        for k in range(count):
            block = block_at(step, k)
            pltpu.make_async_copy(head.at[block], acts_v.at[step, k, pl.ds(0, ROWS)], head_sems.at[step]).start()
            columns = pl.ds(pl.multiple_of(block * LANES, LANES), LANES)
            pltpu.make_async_copy(et_hbm.at[:, columns], error_v.at[step, k], error_sems.at[step]).start()

    gt_copy = pltpu.make_async_copy(gt_hbm, gt_v, tail_sems.at[steps])
    gt_copy.start()
    fetch(0)
    for step in range(steps):
        pltpu.make_async_copy(tails[step], acts_v.at[step, :, below], tail_sems.at[step]).start()
        if step == 0:
            fetch(1)
    total[...] = jnp.zeros_like(total)
    gt_copy.wait()

    def body(step, carry):
        @pl.when(step + 2 < steps)
        def _():
            fetch(step + 2)

        top = acts_v.at[step, :, pl.ds(0, ROWS)]
        pltpu.make_async_copy(top, top, head_sems.at[step]).wait()
        bottom = acts_v.at[step, :, below]
        pltpu.make_async_copy(bottom, bottom, tail_sems.at[step]).wait()
        pltpu.make_async_copy(error_v.at[step], error_v.at[step], error_sems.at[step]).wait()
        blocks = [block_at(step, k) for k in range(count)]
        acts = jnp.concatenate([acts_v[step, k] for k in range(count)], axis=1)
        error = jnp.concatenate([error_v[step, k] for k in range(count)], axis=1)
        basis = jnp.concatenate([basis_ref[block] for block in blocks], axis=1)
        value = dot_nn(gt_v[...], acts) + error.astype(F32)
        for k in range(count):
            field_v[step, k] = lanes(value, k)
            pltpu.make_async_copy(field_v.at[step, k], field.at[blocks[k]], field_sems.at[step]).start()
        hi = value.astype(BF16)
        mid = (value - hi.astype(F32)).astype(BF16)
        total[...] += dot_nt(hi, basis) + dot_nt(mid, basis)
        return carry

    lax.fori_loop(0, steps, body, 0)
    right[...] = fold3(total[...].T)
    for step in range(steps):
        pltpu.make_async_copy(field_v.at[step], field_v.at[step], field_sems.at[step]).wait()


def final_kernel(dp_ref, sum_ref, basis_ref, field, weight, moment1, moment2, new_weight, new_moment1, new_moment2,
                 new_error, q_new, field_v, updated, rounded, field_sems, sems):
    chunks, width = rounded.shape[0], rounded.shape[2]
    count = width // LANES
    reads = []
    for chunk in range(chunks):
        blocks = pl.ds(chunk * count, count)
        reads.append(pltpu.make_async_copy(field.at[blocks], field_v.at[blocks], field_sems.at[chunk]))
        reads[-1].start()
    mean = sum_ref[...] * (1.0 / NDP)
    q_new[...] = mean
    rows, ff = mean.shape
    stack = split3(mean.T)
    hi, mid, lo = stack[:ff], stack[ff : 2 * ff], stack[2 * ff :]
    factor = jnp.concatenate([hi, hi, hi, mid, mid, lo], axis=1)

    def approx_of(chunk):
        basis = jnp.concatenate([basis_ref[chunk * count + block] for block in range(count)], axis=1)
        hi, mid, lo = basis[:rows], basis[rows : 2 * rows], basis[2 * rows :]
        return dot_nn(factor, jnp.concatenate([hi, mid, lo, hi, mid, hi], axis=0))

    copies = []

    def send(source, target):
        copy = pltpu.make_async_copy(source, target, sems.at[len(copies)])
        copy.start()
        copies.append(copy)

    update = approx_of(dp_ref[0])
    first = beta_one * moment1[...] + (1.0 - beta_one) * update
    second = beta_two * moment2[...] + (1.0 - beta_two) * update * update
    updated[0] = first
    updated[1] = second
    updated[2] = weight[...] - learn_rate * (first / corr_one) / (jnp.sqrt(second / corr_two) + adam_eps)
    send(updated.at[0], new_moment1)
    send(updated.at[1], new_moment2)
    send(updated.at[2], new_weight)
    for chunk in range(chunks):
        approx = approx_of(chunk)
        reads[chunk].wait()
        for block in range(count):
            columns = slice(block * LANES, (block + 1) * LANES)
            rounded[chunk, :, columns] = (field_v[chunk * count + block] - lanes(approx, block)).astype(BF16)
        send(rounded.at[chunk], new_error.at[:, chunk * width : (chunk + 1) * width])
    for copy in copies:
        copy.wait()


def call(kernel, outs, args, specs=None, out_specs=None, scratch=(), limit=16, flops=0, moved=0):
    return pl.pallas_call(
        kernel,
        out_shape=outs,
        in_specs=specs or [VMEM] * len(args),
        out_specs=out_specs or jax.tree.map(lambda _: VMEM, outs),
        scratch_shapes=scratch,
        compiler_params=pltpu.CompilerParams(vmem_limit_bytes=limit * MIB),
        cost_estimate=pl.CostEstimate(flops=flops, bytes_accessed=moved, transcendentals=0),
    )(*args)


def swap(value, axis, level):
    return lax.ppermute(value, axis, list(enumerate(level)))


def total(value, axis, levels):
    for level in levels:
        value = value + swap(value, axis, level)
    return value


def along_x(value, shift):
    return lax.ppermute(
        value, "mp", [(x * NZ + z, (x + shift) % NX * NZ + z) for x in range(NX) for z in range(NZ)]
    )


def shards(acts, grad_out, error_buffer, q_prev, weight, moment1, moment2):
    member = lax.axis_index("mp")
    x = (member // NZ).astype(jnp.int32).reshape(1)
    place = jnp.asarray(met(ALONG_Z + ALONG_X, NMP))[member]
    place_z = jnp.asarray(met(RING8, NZ))[member % NZ]
    dp = lax.axis_index("dp").astype(jnp.int32).reshape(1)
    gt, et = grad_out.T, error_buffer.T
    rank, ff = q_prev.shape
    tokens, model = acts.shape[0], et.shape[1]
    array = jax.ShapeDtypeStruct

    head = lax.all_gather(acts[:ROWS], "mp", axis=0)

    factor = call(
        token_kernel, array((rank, tokens), F32), (q_prev, gt), specs=[HBM] * 2,
        scratch=[pltpu.VMEM((rank, ff), F32), pltpu.VMEM((ff, tokens), BF16), pltpu.SemaphoreType.DMA((2,))],
        limit=60, flops=6 * rank * ff * tokens, moved=2 * ff * tokens,
    )
    errors = call(
        error_kernel, array((NMP, rank, LANES), F32), (q_prev, et), specs=[HBM] * 2,
        scratch=[
            pltpu.VMEM((rank, ff), F32), pltpu.VMEM((8, ff, model // 8), BF16), pltpu.SemaphoreType.DMA((9,)),
        ],
        limit=58, flops=6 * rank * ff * model, moved=2 * ff * model,
    )
    errors = lax.all_to_all(errors, "mp", 0, 0)
    factor = total(factor, "mp", ALONG_Z + ALONG_X)

    tail = acts[ROWS:][None]
    for level in ALONG_Z[:2]:
        tail = jnp.concatenate([tail, swap(tail, "mp", level)])
    near0 = (tail, swap(tail, "mp", ALONG_Z[2]))
    near1 = [along_x(part, 1) for part in near0]
    near3 = [along_x(part, 3) for part in near0]
    far = (along_x(near1[0], 1), along_x(near3[1], 3))

    panel = call(piece_kernel, array((1, rank, LANES), F32), (factor, acts, errors), moved=MIB)
    panel = total(panel, "dp", ALONG_DP)
    levels = ALONG_Z + ALONG_X
    for level in levels[:-1]:
        panel = jnp.concatenate([panel, swap(panel, "mp", level)])
    basis = call(
        ortho_kernel, array((NMP, 3 * rank, LANES), BF16), (place, panel, swap(panel, "mp", levels[-1])),
        specs=[SMEM, VMEM, VMEM], scratch=[pltpu.VMEM((NMP, rank, LANES), F32)], flops=MIB, moved=4 * MIB,
    )

    chunks, count = 8, NZ // 2
    width = model // chunks
    field, right = call(
        field_kernel,
        [array((NMP, ff, LANES), F32), array((rank, ff), F32)],
        (x, place_z, head, *near0, *near1, *near3, *far, basis, et, gt),
        specs=[SMEM, SMEM] + [HBM] * 9 + [VMEM, HBM, HBM],
        out_specs=[HBM, VMEM],
        scratch=[
            pltpu.VMEM((chunks, count, tokens, LANES), BF16),
            pltpu.VMEM((chunks, count, ff, LANES), BF16),
            pltpu.VMEM((ff, tokens), BF16),
            pltpu.VMEM((chunks, count, ff, LANES), F32),
            pltpu.VMEM((ff, 3 * rank), F32),
            pltpu.SemaphoreType.DMA((chunks + 1,)),
            pltpu.SemaphoreType.DMA((chunks,)),
            pltpu.SemaphoreType.DMA((chunks,)),
            pltpu.SemaphoreType.DMA((chunks,)),
        ],
        limit=49, flops=2 * model * ff * tokens, moved=13 * MIB,
    )
    right = total(right, "dp", ALONG_DP)

    block = array((ff, width), F32)
    outs = call(
        final_kernel,
        [block] * 3 + [array((ff, model), BF16), array((rank, ff), F32)],
        (dp, right, basis, field, weight.T, moment1.T, moment2.T),
        specs=[SMEM, VMEM, VMEM, HBM, VMEM, VMEM, VMEM],
        out_specs=[HBM] * 4 + [VMEM],
        scratch=[
            pltpu.VMEM((NMP, ff, LANES), F32),
            pltpu.VMEM((3, ff, width), F32),
            pltpu.VMEM((chunks, ff, width), BF16),
            pltpu.SemaphoreType.DMA((chunks,)),
            pltpu.SemaphoreType.DMA((3 + chunks,)),
        ],
        limit=57, flops=12 * rank * model * ff, moved=20 * MIB,
    )
    new_weight, new_moment1, new_moment2, new_error, q_new = outs
    return (new_weight.T, new_moment1.T, new_moment2.T, new_error.T, q_new)


def solution(mesh):
    placed = (
        P("dp", "mp"),
        P("dp", "mp"),
        P("dp", "mp"),
        P(None, "mp"),
        P("dp", "mp"),
        P("dp", "mp"),
        P("dp", "mp"),
    )
    return jax.shard_map(
        shards,
        mesh=mesh,
        in_specs=placed,
        out_specs=(P("dp", "mp"), P("dp", "mp"), P("dp", "mp"), P("dp", "mp"), P(None, "mp")),
        check_vma=False,
    )
```

time: 171 us -> 198 us (1.16)
  starting transfers between devices: 28 us -> 66.9 us
  waiting for transfers between devices: 40.1 us -> 76.9 us
  blocking collectives: 35.2 us -> 0 us
  local copies, waits for them, and re-layouts: 22.6 us -> 3.06 us
  Pallas kernels: 28.6 us -> 32.5 us
    ppermute x0 -> x19, waiting for transfers between devices: none -> 76.8 us  [swap(): return lax.ppermute(value, axis, list(enumerate(level)))]
    ppermute x0 -> x19, starting transfers between devices: none -> 50.8 us  [swap(): return lax.ppermute(value, axis, list(enumerate(level)))]
    all_to_all x3 -> x1, waiting for transfers between devices: 35.9 us -> 0.01 us  [shards(): errors = lax.all_to_all(errors, 'mp', 0, 0)]
    all_to_all x2 -> x0, blocking collectives: 35.2 us -> none  [exchange(): return lax.all_to_all(value, axis, 0, 0)]
    pallas_call x6, Pallas kernels: 13.2 us -> 32.5 us  [call(): pl.pallas_call(kernel, out_shape=outs, in_specs=specs or [VMEM] * len(arg...]
    unnamed x36 -> x7, local copies, waits for them, and re-layouts: 18.2 us -> 0.02 us
    pallas_call x1 -> x0, Pallas kernels: 15.5 us -> none  [shards(): pl.pallas_call(field_kernel, grid_spec=pltpu.PrefetchScalarGridSpec(num_s...]
    all_to_all x3 -> x1, starting transfers between devices: 16.5 us -> 10.1 us  [shards(): errors = lax.all_to_all(errors, 'mp', 0, 0)]
  transfers between devices with their start and end apart: 12 -> 27, of which waited for: 5 -> 16; matrix products, arithmetic and copies ran while one was open for 2% -> 1% of each run, Pallas kernels for 5% -> 6%
where the time goes in v2:
time: 198 us; the launch traced here: 195 us
  waiting for transfers between devices  76.9 us (39%)
  starting transfers between devices  66.9 us (34%)
  Pallas kernels  32.5 us (16%)
  between operations  14.3 us (7%)
  local copies, waits for them, and re-layouts  3.06 us (2%)
    ppermute x19, waiting for transfers between devices, swap(): return lax.ppermute(value, axis, list(enumerate(level)))  76.8 us
    ppermute x19, starting transfers between devices, swap(): return lax.ppermute(value, axis, list(enumerate(level)))  50.8 us
    pallas_call x6, Pallas kernels, call(): pl.pallas_call(kernel, out_shape=outs, in_specs=specs or [VMEM] * len(arg...  32.5 us
    all_to_all x1, starting transfers between devices, shards(): errors = lax.all_to_all(errors, 'mp', 0, 0)  10.1 us
    ppermute x6, starting transfers between devices, along_x(): lax.ppermute(value, 'mp', [(x * NZ + z, (x + shift) % NX * NZ + z) for x...  5.93 us
  transfers between devices with their start and end apart: 27, of which 16 were waited for; matrix products, arithmetic and copies ran while one was open for 1% of the time, Pallas kernels for 6%

profile of v2, /device:TPU:1, one launch (start us, length us, event | category | flops | bytes accessed | tf_op | source)
XLA Modules:
  0.0 195.3 jit_solution(17896661595126396845)
XLA Ops:
  8.9 2.6 %collective-permute-start = (bf16[1,512,128]{2,1,0:T(8,128)(2,1)S(1)}, bf16[1,512,128]{2,1,0:T(8,128)(2,1)S(1)}, u32[]{:S(2)}, u32[]{:S(2)}) collective-permute-start(bf16[1,512,128]{2,1,0:T(8,128)(2,1)S(1)} %get-tuple-element.21), channel_id=1, source_target_pairs={{0,1},{1,0},{2,3},{3,2},{4,5},{5,4},{6,7},{7,6},{8,9},{9,8},{10,11... | collective-permute-start | bytes 393224 | tf_op jit(solution)/shard_map/ppermute | solution.py:284
  11.4 3.7 %shard_map.129 = f32[32,32,128]{2,1,0:T(8,128)} custom-call(f32[32,448]{1,0:T(8,128)} %q_hbm.3, bf16[448,4096]{1,0:T(8,128)(2,1)} %bitcast.18), custom_call_target="tpu_custom_call" | custom-call | flops 352321536 | bytes 3670016 | tf_op jit(solution)/shard_map/pallas_call | solution.py:272
  15.1 10.1 %all-to-all-start = ((f32[32,32,128]{2,1,0:T(8,128)}), f32[32,32,128]{2,1,0:T(8,128)S(1)}, u32[]{:S(2)}, u32[]{:S(2)}) async-start(f32[32,32,128]{2,1,0:T(8,128)} %shard_map.129), calls=%async_computation | async-start | bytes 1048576 | tf_op jit(solution)/shard_map/all_to_all | solution.py:324
  25.3 2.5 %collective-permute-start.1 = (bf16[2,512,128]{2,1,0:T(8,128)(2,1)S(1)}, bf16[2,512,128]{2,1,0:T(8,128)(2,1)S(1)}, u32[]{:S(2)}, u32[]{:S(2)}) collective-permute-start(bf16[2,512,128]{2,1,0:T(8,128)(2,1)S(1)} %pad_maximum_fusion.1), channel_id=1, source_target_pairs={{0,7},{1,2},{2,1},{3,4},{4,3},{5,6},{6,5},{7,0},{8,15},{9,10},{10,... | collective-permute-start | bytes 786440 | tf_op jit(solution)/shard_map/ppermute | solution.py:284
  30.2 12.7 %collective-permute-done.9 = f32[32,1024]{1,0:T(8,128)S(1)} collective-permute-done((f32[32,1024]{1,0:T(8,128)}, f32[32,1024]{1,0:T(8,128)S(1)}, u32[]{:S(2)}, u32[]{:S(2)}) %collective-permute-start.9) | collective-permute-done | bytes 131104 | tf_op jit(solution)/shard_map/ppermute | solution.py:284
  47.7 3.6 %collective-permute-start.2 = (bf16[4,512,128]{2,1,0:T(8,128)(2,1)S(1)}, bf16[4,512,128]{2,1,0:T(8,128)(2,1)S(1)}, u32[]{:S(2)}, u32[]{:S(2)}) collective-permute-start(bf16[4,512,128]{2,1,0:T(8,128)(2,1)S(1)} %pad_maximum_fusion.refs_0_), channel_id=1, source_target_pairs={{0,3},{1,6},{2,5},{3,0},{4,7},{5,2},{6,1},{7,4},{8,11},{9,14},{10,... | collective-permute-start | bytes 1572872 | tf_op jit(solution)/shard_map/ppermute | solution.py:284
  51.6 5.8 %collective-permute-start.11 = (f32[32,1024]{1,0:T(8,128)S(1)}, f32[32,1024]{1,0:T(8,128)S(1)}, u32[]{:S(2)}, u32[]{:S(2)}) collective-permute-start(f32[32,1024]{1,0:T(8,128)S(1)} %add.48), channel_id=1, source_target_pairs={{0,3},{1,6},{2,5},{3,0},{4,7},{5,2},{6,1},{7,4},{8,11},{9,14},{10,... | collective-permute-start | bytes 393224 | tf_op jit(solution)/shard_map/ppermute | solution.py:284
  57.4 23.0 %collective-permute-done.11 = f32[32,1024]{1,0:T(8,128)S(1)} collective-permute-done((f32[32,1024]{1,0:T(8,128)S(1)}, f32[32,1024]{1,0:T(8,128)S(1)}, u32[]{:S(2)}, u32[]{:S(2)}) %collective-permute-start.11) | collective-permute-done | bytes 131104 | tf_op jit(solution)/shard_map/ppermute | solution.py:284
  80.5 4.4 %collective-permute-done.12 = f32[32,1024]{1,0:T(8,128)S(1)} collective-permute-done((f32[32,1024]{1,0:T(8,128)S(1)}, f32[32,1024]{1,0:T(8,128)S(1)}, u32[]{:S(2)}, u32[]{:S(2)}) %collective-permute-start.12) | collective-permute-done | bytes 131104 | tf_op jit(solution)/shard_map/ppermute | solution.py:284
  84.9 2.8 %collective-permute-start.13 = (f32[32,1024]{1,0:T(8,128)S(1)}, f32[32,1024]{1,0:T(8,128)S(1)}, u32[]{:S(2)}, u32[]{:S(2)}) collective-permute-start(f32[32,1024]{1,0:T(8,128)S(1)} %add.50), channel_id=1, source_target_pairs={{0,24},{1,25},{2,26},{3,27},{4,28},{5,29},{6,30},{7,31},{8,16},{9,... | collective-permute-start | bytes 393224 | tf_op jit(solution)/shard_map/ppermute | solution.py:284
  87.7 4.4 %collective-permute-done.13 = f32[32,1024]{1,0:T(8,128)S(1)} collective-permute-done((f32[32,1024]{1,0:T(8,128)S(1)}, f32[32,1024]{1,0:T(8,128)S(1)}, u32[]{:S(2)}, u32[]{:S(2)}) %collective-permute-start.13) | collective-permute-done | bytes 131104 | tf_op jit(solution)/shard_map/ppermute | solution.py:284
  92.4 11.8 %collective-permute-start.14 = (f32[1,32,128]{2,1,0:T(8,128)S(1)}, f32[1,32,128]{2,1,0:T(8,128)S(1)}, u32[]{:S(2)}, u32[]{:S(2)}) collective-permute-start(f32[1,32,128]{2,1,0:T(8,128)S(1)} %shard_map.130), channel_id=1, source_target_pairs={{0,32},{32,0},{64,96},{96,64},{128,160},{160,128},{192,224},{224,1... | collective-permute-start | bytes 49160 | tf_op jit(solution)/shard_map/ppermute | solution.py:284
  107.9 2.5 %collective-permute-start.16 = (f32[1,32,128]{2,1,0:T(8,128)S(1)}, f32[1,32,128]{2,1,0:T(8,128)S(1)}, u32[]{:S(2)}, u32[]{:S(2)}) collective-permute-start(f32[1,32,128]{2,1,0:T(8,128)S(1)} %add.53), channel_id=1, source_target_pairs={{0,192},{32,224},{64,128},{96,160},{128,64},{160,96},{192,0},{224,... | collective-permute-start | bytes 49160 | tf_op jit(solution)/shard_map/ppermute | solution.py:284
  111.9 2.3 %collective-permute-start.17 = (f32[1,32,128]{2,1,0:T(8,128)S(1)}, f32[1,32,128]{2,1,0:T(8,128)S(1)}, u32[]{:S(2)}, u32[]{:S(2)}) collective-permute-start(f32[1,32,128]{2,1,0:T(8,128)S(1)} %get-tuple-element.20), channel_id=1, source_target_pairs={{0,1},{1,0},{2,3},{3,2},{4,5},{5,4},{6,7},{7,6},{8,9},{9,8},{10,11... | collective-permute-start | bytes 49160 | tf_op jit(solution)/shard_map/ppermute | solution.py:284
  119.7 3.0 %collective-permute-start.19 = (f32[4,32,128]{2,1,0:T(8,128)S(1)}, f32[4,32,128]{2,1,0:T(8,128)S(1)}, u32[]{:S(2)}, u32[]{:S(2)}) collective-permute-start(f32[4,32,128]{2,1,0:T(8,128)S(1)} %pad_maximum_fusion.3), channel_id=1, source_target_pairs={{0,3},{1,6},{2,5},{3,0},{4,7},{5,2},{6,1},{7,4},{8,11},{9,14},{10,... | collective-permute-start | bytes 196616 | tf_op jit(solution)/shard_map/ppermute | solution.py:284
  124.8 2.5 %collective-permute-start.8 = (bf16[4,512,128]{2,1,0:T(8,128)(2,1)S(1)}, bf16[4,512,128]{2,1,0:T(8,128)(2,1)}, u32[]{:S(2)}, u32[]{:S(2)}) collective-permute-start(bf16[4,512,128]{2,1,0:T(8,128)(2,1)S(1)} %collective-permute-done.6.refs_5_), channel_id=1, source_target_pairs={{0,24},{1,25},{2,26},{3,27},{4,28},{5,29},{6,30},{7,31},{8,0},{9,1... | collective-permute-start | bytes 1572872 | tf_op jit(solution)/shard_map/ppermute | solution.py:294
  127.4 13.4 %collective-permute-done.20 = f32[8,32,128]{2,1,0:T(8,128)S(1)} collective-permute-done((f32[8,32,128]{2,1,0:T(8,128)S(1)}, f32[8,32,128]{2,1,0:T(8,128)S(1)}, u32[]{:S(2)}, u32[]{:S(2)}) %collective-permute-start.20) | collective-permute-done | bytes 131104 | tf_op jit(solution)/shard_map/ppermute | solution.py:284
  144.4 5.1 %collective-permute-done.21.theirs = f32[16,32,128]{2,1,0:T(8,128)S(1)} collective-permute-done((f32[16,32,128]{2,1,0:T(8,128)S(1)}, f32[16,32,128]{2,1,0:T(8,128)S(1)}, u32[]{:S(2)}, u32[]{:S(2)}) %collective-permute-start.21) | collective-permute-done | bytes 262176 | tf_op jit(solution)/shard_map/ppermute | solution.py:284
  149.5 6.4 %shard_map.131.refs_8_.basis_ref = bf16[32,96,128]{2,1,0:T(8,128)(2,1)S(1)} custom-call(s32[32]{0:T(128)S(1)} %dynamic-slice_bitcast_fusion.place_ref, f32[16,32,128]{2,1,0:T(8,128)S(1)} %constant_dynamic-update-slice_fusion.mine, f32[16,32,128]{2,1,0:T(8,128)S(1)} %collective-permute-done.21.theirs), custom_call_target="tpu_custom_call" | custom-call | flops 1048576 | bytes 4194304 | tf_op jit(solution)/shard_map/pallas_call | solution.py:272
  156.0 11.0 %shard_map.132 = (f32[32,448,128]{2,1,0:T(8,128)}, f32[32,448]{1,0:T(8,128)S(1)}) custom-call(s32[1]{0:T(128)} %bitcast.1.x_ref, s32[8]{0:T(128)S(1)} %dynamic-slice_bitcast_fusion.1.place_ref, bf16[32,512,128]{2,1,0:T(8,128)(2,1)} %bitcast.25, bf16[4,512,128]{2,1,0:T(8,128)(2,1)S(1)} %pad_maximum_fusion.refs_0_, ...), custom_call_target="tpu_custom_call" | custom-call | flops 3758096384 | bytes 13631488 | tf_op jit(solution)/shard_map/pallas_call | solution.py:272
  167.0 3.3 %collective-permute-start.22 = (f32[32,448]{1,0:T(8,128)S(1)}, f32[32,448]{1,0:T(8,128)S(1)}, u32[]{:S(2)}, u32[]{:S(2)}) collective-permute-start(f32[32,448]{1,0:T(8,128)S(1)} %get-tuple-element.12), channel_id=1, source_target_pairs={{0,32},{32,0},{64,96},{96,64},{128,160},{160,128},{192,224},{224,1... | collective-permute-start | bytes 172040 | tf_op jit(solution)/shard_map/ppermute | solution.py:284
  171.4 3.1 %collective-permute-done.23 = f32[32,448]{1,0:T(8,128)S(1)} collective-permute-done((f32[32,448]{1,0:T(8,128)S(1)}, f32[32,448]{1,0:T(8,128)S(1)}, u32[]{:S(2)}, u32[]{:S(2)}) %collective-permute-start.23) | collective-permute-done | bytes 57376 | tf_op jit(solution)/shard_map/ppermute | solution.py:284
  174.5 2.8 %collective-permute-start.24 = (f32[32,448]{1,0:T(8,128)S(1)}, f32[32,448]{1,0:T(8,128)S(1)}, u32[]{:S(2)}, u32[]{:S(2)}) collective-permute-start(f32[32,448]{1,0:T(8,128)S(1)} %add.56), channel_id=1, source_target_pairs={{0,192},{32,224},{64,128},{96,160},{128,64},{160,96},{192,0},{224,... | collective-permute-start | bytes 172040 | tf_op jit(solution)/shard_map/ppermute | solution.py:284
  179.5 9.0 %shard_map.133 = (f32[448,512]{1,0:T(8,128)}, f32[448,512]{1,0:T(8,128)}, f32[448,512]{1,0:T(8,128)}, bf16[448,4096]{1,0:T(8,128)(2,1)}, f32[32,448]{1,0:T(8,128)}) custom-call(s32[1]{0:T(128)} %bitcast.dp_ref, f32[32,448]{1,0:T(8,128)} %add.57.sum_ref, bf16[32,96,128]{2,1,0:T(8,128)(2,1)} %copy-done, f32[32,448,128]{2,1,0:T(8,128)} %get-tuple-element.13.field, ...), custom_call_target="tpu_custom_call" | custom-call | flops 704643072 | bytes 20971520 | tf_op jit(solution)/shard_map/pallas_call | solution.py:272
  (64 shorter events, 29.2 us)
Async XLA Ops:
  7.2 148.8 %all-gather.3.cloned.1.call-start = ((), (), s32[]{:S(2)}) async-start(), calls=%async_computation.1 | async-start | bytes 4325376 | tf_op jit(solution)/shard_map/all_gather | solution.py:310
  8.9 16.4 %collective-permute-start = (bf16[1,512,128]{2,1,0:T(8,128)(2,1)S(1)}, bf16[1,512,128]{2,1,0:T(8,128)(2,1)S(1)}, u32[]{:S(2)}, u32[]{:S(2)}) collective-permute-start(bf16[1,512,128]{2,1,0:T(8,128)(2,1)S(1)} %get-tuple-element.21), channel_id=1, source_target_pairs={{0,1},{1,0},{2,3},{3,2},{4,5},{5,4},{6,7},{7,6},{8,9},{9,8},{10,11... | collective-permute-start | bytes 393224 | tf_op jit(solution)/shard_map/ppermute | solution.py:284
  15.1 77.1 %all-to-all-start = ((f32[32,32,128]{2,1,0:T(8,128)}), f32[32,32,128]{2,1,0:T(8,128)S(1)}, u32[]{:S(2)}, u32[]{:S(2)}) async-start(f32[32,32,128]{2,1,0:T(8,128)} %shard_map.129), calls=%async_computation | async-start | bytes 1048576 | tf_op jit(solution)/shard_map/all_to_all | solution.py:324
  25.3 22.3 %collective-permute-start.1 = (bf16[2,512,128]{2,1,0:T(8,128)(2,1)S(1)}, bf16[2,512,128]{2,1,0:T(8,128)(2,1)S(1)}, u32[]{:S(2)}, u32[]{:S(2)}) collective-permute-start(bf16[2,512,128]{2,1,0:T(8,128)(2,1)S(1)} %pad_maximum_fusion.1), channel_id=1, source_target_pairs={{0,7},{1,2},{2,1},{3,4},{4,3},{5,6},{6,5},{7,0},{8,15},{9,10},{10,... | collective-permute-start | bytes 786440 | tf_op jit(solution)/shard_map/ppermute | solution.py:284
  30.1 12.8 %collective-permute-start.9 = (f32[32,1024]{1,0:T(8,128)}, f32[32,1024]{1,0:T(8,128)S(1)}, u32[]{:S(2)}, u32[]{:S(2)}) collective-permute-start(f32[32,1024]{1,0:T(8,128)} %shard_map.128), channel_id=1, source_target_pairs={{0,1},{1,0},{2,3},{3,2},{4,5},{5,4},{6,7},{7,6},{8,9},{9,8},{10,11... | collective-permute-start | bytes 393224 | tf_op jit(solution)/shard_map/ppermute | solution.py:284
  43.9 7.7 %collective-permute-start.10 = (f32[32,1024]{1,0:T(8,128)S(1)}, f32[32,1024]{1,0:T(8,128)S(1)}, u32[]{:S(2)}, u32[]{:S(2)}) collective-permute-start(f32[32,1024]{1,0:T(8,128)S(1)} %add.47), channel_id=1, source_target_pairs={{0,7},{1,2},{2,1},{3,4},{4,3},{5,6},{6,5},{7,0},{8,15},{9,10},{10,... | collective-permute-start | bytes 393224 | tf_op jit(solution)/shard_map/ppermute | solution.py:284
  47.7 62.7 %collective-permute-start.2 = (bf16[4,512,128]{2,1,0:T(8,128)(2,1)S(1)}, bf16[4,512,128]{2,1,0:T(8,128)(2,1)S(1)}, u32[]{:S(2)}, u32[]{:S(2)}) collective-permute-start(bf16[4,512,128]{2,1,0:T(8,128)(2,1)S(1)} %pad_maximum_fusion.refs_0_), channel_id=1, source_target_pairs={{0,3},{1,6},{2,5},{3,0},{4,7},{5,2},{6,1},{7,4},{8,11},{9,14},{10,... | collective-permute-start | bytes 1572872 | tf_op jit(solution)/shard_map/ppermute | solution.py:284
  51.6 28.8 %collective-permute-start.11 = (f32[32,1024]{1,0:T(8,128)S(1)}, f32[32,1024]{1,0:T(8,128)S(1)}, u32[]{:S(2)}, u32[]{:S(2)}) collective-permute-start(f32[32,1024]{1,0:T(8,128)S(1)} %add.48), channel_id=1, source_target_pairs={{0,3},{1,6},{2,5},{3,0},{4,7},{5,2},{6,1},{7,4},{8,11},{9,14},{10,... | collective-permute-start | bytes 393224 | tf_op jit(solution)/shard_map/ppermute | solution.py:284
  80.4 4.5 %collective-permute-start.12 = (f32[32,1024]{1,0:T(8,128)S(1)}, f32[32,1024]{1,0:T(8,128)S(1)}, u32[]{:S(2)}, u32[]{:S(2)}) collective-permute-start(f32[32,1024]{1,0:T(8,128)S(1)} %add.49), channel_id=1, source_target_pairs={{0,8},{1,9},{2,10},{3,11},{4,12},{5,13},{6,14},{7,15},{8,0},{9,1},... | collective-permute-start | bytes 393224 | tf_op jit(solution)/shard_map/ppermute | solution.py:284
  84.9 7.3 %collective-permute-start.13 = (f32[32,1024]{1,0:T(8,128)S(1)}, f32[32,1024]{1,0:T(8,128)S(1)}, u32[]{:S(2)}, u32[]{:S(2)}) collective-permute-start(f32[32,1024]{1,0:T(8,128)S(1)} %add.50), channel_id=1, source_target_pairs={{0,24},{1,25},{2,26},{3,27},{4,28},{5,29},{6,30},{7,31},{8,16},{9,... | collective-permute-start | bytes 393224 | tf_op jit(solution)/shard_map/ppermute | solution.py:284
  87.7 31.2 %collective-permute-start.3 = (bf16[4,512,128]{2,1,0:T(8,128)(2,1)S(1)}, bf16[4,512,128]{2,1,0:T(8,128)(2,1)S(1)}, u32[]{:S(2)}, u32[]{:S(2)}) collective-permute-start(bf16[4,512,128]{2,1,0:T(8,128)(2,1)S(1)} %pad_maximum_fusion.refs_0_), channel_id=1, source_target_pairs={{0,8},{1,9},{2,10},{3,11},{4,12},{5,13},{6,14},{7,15},{8,16},{9,17... | collective-permute-start | bytes 1572872 | tf_op jit(solution)/shard_map/ppermute | solution.py:294
  92.4 12.6 %collective-permute-start.14 = (f32[1,32,128]{2,1,0:T(8,128)S(1)}, f32[1,32,128]{2,1,0:T(8,128)S(1)}, u32[]{:S(2)}, u32[]{:S(2)}) collective-permute-start(f32[1,32,128]{2,1,0:T(8,128)S(1)} %shard_map.130), channel_id=1, source_target_pairs={{0,32},{32,0},{64,96},{96,64},{128,160},{160,128},{192,224},{224,1... | collective-permute-start | bytes 49160 | tf_op jit(solution)/shard_map/ppermute | solution.py:284
  107.9 3.9 %collective-permute-start.16 = (f32[1,32,128]{2,1,0:T(8,128)S(1)}, f32[1,32,128]{2,1,0:T(8,128)S(1)}, u32[]{:S(2)}, u32[]{:S(2)}) collective-permute-start(f32[1,32,128]{2,1,0:T(8,128)S(1)} %add.53), channel_id=1, source_target_pairs={{0,192},{32,224},{64,128},{96,160},{128,64},{160,96},{192,0},{224,... | collective-permute-start | bytes 49160 | tf_op jit(solution)/shard_map/ppermute | solution.py:284
  110.4 14.4 %collective-permute-start.6 = (bf16[4,512,128]{2,1,0:T(8,128)(2,1)S(1)}, bf16[4,512,128]{2,1,0:T(8,128)(2,1)S(1)}, u32[]{:S(2)}, u32[]{:S(2)}) collective-permute-start(bf16[4,512,128]{2,1,0:T(8,128)(2,1)S(1)} %collective-permute-done.2.refs_1_), channel_id=1, source_target_pairs={{0,24},{1,25},{2,26},{3,27},{4,28},{5,29},{6,30},{7,31},{8,0},{9,1... | collective-permute-start | bytes 1572872 | tf_op jit(solution)/shard_map/ppermute | solution.py:294
  115.7 4.0 %collective-permute-start.18 = (f32[2,32,128]{2,1,0:T(8,128)S(1)}, f32[2,32,128]{2,1,0:T(8,128)S(1)}, u32[]{:S(2)}, u32[]{:S(2)}) collective-permute-start(f32[2,32,128]{2,1,0:T(8,128)S(1)} %pad_maximum_fusion.4), channel_id=1, source_target_pairs={{0,7},{1,2},{2,1},{3,4},{4,3},{5,6},{6,5},{7,0},{8,15},{9,10},{10,... | collective-permute-start | bytes 98312 | tf_op jit(solution)/shard_map/ppermute | solution.py:284
  117.4 38.5 %collective-permute-start.5 = (bf16[4,512,128]{2,1,0:T(8,128)(2,1)S(1)}, bf16[4,512,128]{2,1,0:T(8,128)(2,1)}, u32[]{:S(2)}, u32[]{:S(2)}) collective-permute-start(bf16[4,512,128]{2,1,0:T(8,128)(2,1)S(1)} %pad_maximum_fusion.refs_0_), channel_id=1, source_target_pairs={{0,24},{1,25},{2,26},{3,27},{4,28},{5,29},{6,30},{7,31},{8,0},{9,1... | collective-permute-start | bytes 1572872 | tf_op jit(solution)/shard_map/ppermute | solution.py:294
  118.1 37.8 %collective-permute-start.4 = (bf16[4,512,128]{2,1,0:T(8,128)(2,1)S(1)}, bf16[4,512,128]{2,1,0:T(8,128)(2,1)}, u32[]{:S(2)}, u32[]{:S(2)}) collective-permute-start(bf16[4,512,128]{2,1,0:T(8,128)(2,1)S(1)} %collective-permute-done.2.refs_1_), channel_id=1, source_target_pairs={{0,8},{1,9},{2,10},{3,11},{4,12},{5,13},{6,14},{7,15},{8,16},{9,17... | collective-permute-start | bytes 1572872 | tf_op jit(solution)/shard_map/ppermute | solution.py:294
  118.9 37.0 %collective-permute-start.7 = (bf16[4,512,128]{2,1,0:T(8,128)(2,1)S(1)}, bf16[4,512,128]{2,1,0:T(8,128)(2,1)}, u32[]{:S(2)}, u32[]{:S(2)}) collective-permute-start(bf16[4,512,128]{2,1,0:T(8,128)(2,1)S(1)} %collective-permute-done.3.refs_2_), channel_id=1, source_target_pairs={{0,8},{1,9},{2,10},{3,11},{4,12},{5,13},{6,14},{7,15},{8,16},{9,17... | collective-permute-start | bytes 1572872 | tf_op jit(solution)/shard_map/ppermute | solution.py:294
  119.7 5.0 %collective-permute-start.19 = (f32[4,32,128]{2,1,0:T(8,128)S(1)}, f32[4,32,128]{2,1,0:T(8,128)S(1)}, u32[]{:S(2)}, u32[]{:S(2)}) collective-permute-start(f32[4,32,128]{2,1,0:T(8,128)S(1)} %pad_maximum_fusion.3), channel_id=1, source_target_pairs={{0,3},{1,6},{2,5},{3,0},{4,7},{5,2},{6,1},{7,4},{8,11},{9,14},{10,... | collective-permute-start | bytes 196616 | tf_op jit(solution)/shard_map/ppermute | solution.py:284
  124.7 16.1 %collective-permute-start.20 = (f32[8,32,128]{2,1,0:T(8,128)S(1)}, f32[8,32,128]{2,1,0:T(8,128)S(1)}, u32[]{:S(2)}, u32[]{:S(2)}) collective-permute-start(f32[8,32,128]{2,1,0:T(8,128)S(1)} %pad_maximum_fusion.2), channel_id=1, source_target_pairs={{0,8},{1,9},{2,10},{3,11},{4,12},{5,13},{6,14},{7,15},{8,0},{9,1},... | collective-permute-start | bytes 393224 | tf_op jit(solution)/shard_map/ppermute | solution.py:284
  124.8 31.1 %collective-permute-start.8 = (bf16[4,512,128]{2,1,0:T(8,128)(2,1)S(1)}, bf16[4,512,128]{2,1,0:T(8,128)(2,1)}, u32[]{:S(2)}, u32[]{:S(2)}) collective-permute-start(bf16[4,512,128]{2,1,0:T(8,128)(2,1)S(1)} %collective-permute-done.6.refs_5_), channel_id=1, source_target_pairs={{0,24},{1,25},{2,26},{3,27},{4,28},{5,29},{6,30},{7,31},{8,0},{9,1... | collective-permute-start | bytes 1572872 | tf_op jit(solution)/shard_map/ppermute | solution.py:294
  140.8 8.8 %collective-permute-start.21 = (f32[16,32,128]{2,1,0:T(8,128)S(1)}, f32[16,32,128]{2,1,0:T(8,128)S(1)}, u32[]{:S(2)}, u32[]{:S(2)}) collective-permute-start(f32[16,32,128]{2,1,0:T(8,128)S(1)} %constant_dynamic-update-slice_fusion.mine), channel_id=1, source_target_pairs={{0,24},{1,25},{2,26},{3,27},{4,28},{5,29},{6,30},{7,31},{8,16},{9,... | collective-permute-start | bytes 786440 | tf_op jit(solution)/shard_map/ppermute | solution.py:284
  167.0 4.2 %collective-permute-start.22 = (f32[32,448]{1,0:T(8,128)S(1)}, f32[32,448]{1,0:T(8,128)S(1)}, u32[]{:S(2)}, u32[]{:S(2)}) collective-permute-start(f32[32,448]{1,0:T(8,128)S(1)} %get-tuple-element.12), channel_id=1, source_target_pairs={{0,32},{32,0},{64,96},{96,64},{128,160},{160,128},{192,224},{224,1... | collective-permute-start | bytes 172040 | tf_op jit(solution)/shard_map/ppermute | solution.py:284
  174.5 4.4 %collective-permute-start.24 = (f32[32,448]{1,0:T(8,128)S(1)}, f32[32,448]{1,0:T(8,128)S(1)}, u32[]{:S(2)}, u32[]{:S(2)}) collective-permute-start(f32[32,448]{1,0:T(8,128)S(1)} %add.56), channel_id=1, source_target_pairs={{0,192},{32,224},{64,128},{96,160},{128,64},{160,96},{192,0},{224,... | collective-permute-start | bytes 172040 | tf_op jit(solution)/shard_map/ppermute | solution.py:284
  (5 other events, 101.7 us)
Sparse Core Ops, SparseCore 0:
  11.2 94.4 all-gather.2

commit v3 on v2

v3 whole, which is shorter than its diff:
```python
import jax
import jax.numpy as jnp
import numpy as np
from jax import lax
from jax.experimental import pallas as pl
from jax.experimental.pallas import tpu as pltpu
from jax.sharding import PartitionSpec as P

ortho_eps = 1e-08
adam_eps = 1e-08
beta_one = 0.9
beta_two = 0.95
learn_rate = 0.01
corr_one = 1.0 - 0.9**10
corr_two = 1.0 - 0.95**10

NX, NZ, NDP = 4, 8, 8
NMP = NX * NZ
LANES = 128
F32, BF16 = jnp.float32, jnp.bfloat16
MIB = 1 << 20
SMEM = pl.BlockSpec(memory_space=pltpu.SMEM)
VMEM = pl.BlockSpec(memory_space=pltpu.VMEM)
HBM = pl.BlockSpec(memory_space=pltpu.HBM)

RING4 = ([1, 0, 3, 2], [3, 2, 1, 0])
RING8 = ([1, 0, 3, 2, 5, 4, 7, 6], [7, 2, 1, 4, 3, 6, 5, 0], [3, 6, 5, 0, 7, 2, 1, 4])
ALONG_Z = [[x * NZ + to for x in range(NX) for to in level] for level in RING8]
ALONG_X = [[to * NZ + z for to in level for z in range(NZ)] for level in RING4]
ALONG_DP = [[1, 0, 3, 2, 5, 4, 7, 6]] + [[to * 2 + core for to in level for core in range(2)] for level in RING4]


def met(levels, members):
    held = [[member] for member in range(members)]
    for level in levels:
        held = [held[member] + held[level[member]] for member in range(members)]
    return np.array(held, np.int32)


def split3(value):
    hi = value.astype(BF16)
    rest = value - hi.astype(F32)
    mid = rest.astype(BF16)
    lo = (rest - mid.astype(F32)).astype(BF16)
    return jnp.concatenate([hi, mid, lo], axis=0)


def fold3(stacked):
    rows = stacked.shape[0] // 3
    return stacked[:rows] + (stacked[rows : 2 * rows] + stacked[2 * rows :])


def dot_nn(a, b):
    return lax.dot_general(a, b, (((1,), (0,)), ((), ())), preferred_element_type=F32)


def dot_nt(a, b):
    return lax.dot_general(a, b, (((1,), (1,)), ((), ())), preferred_element_type=F32)


def dot_tn(a, b):
    return lax.dot_general(a, b, (((0,), (0,)), ((), ())), preferred_element_type=F32)


def add_all(values):
    while len(values) > 1:
        values = [a + b for a, b in zip(values[::2], values[1::2])] + values[len(values) // 2 * 2 :]
    return values[0]


def lanes(array, block):
    return array[:, block * LANES : (block + 1) * LANES]


def wide(ref, count):
    return jnp.concatenate([ref[block] for block in range(count)], axis=1)


def lanes(array, block):
    return array[:, block * LANES : (block + 1) * LANES]


def add_all(values):
    while len(values) > 1:
        values = [a + b for a, b in zip(values[::2], values[1::2])]
    return values[0]


def token_kernel(q_hbm, gt_hbm, out, q_ref, gt_ref, sems):
    copies = [pltpu.make_async_copy(q_hbm, q_ref, sems.at[0]), pltpu.make_async_copy(gt_hbm, gt_ref, sems.at[1])]
    for copy in copies:
        copy.start()
    for copy in copies:
        copy.wait()
    out[...] = fold3(dot_nn(split3(q_ref[...]), gt_ref[...]))


def error_kernel(q_hbm, et_hbm, out, q_ref, et_ref, sems):
    count = et_ref.shape[0]
    width = et_ref.shape[2]
    copies = [
        pltpu.make_async_copy(et_hbm.at[:, chunk * width : (chunk + 1) * width], et_ref.at[chunk], sems.at[chunk])
        for chunk in range(count)
    ]
    first = pltpu.make_async_copy(q_hbm, q_ref, sems.at[count])
    first.start()
    for copy in copies:
        copy.start()
    first.wait()
    split = split3(q_ref[...])
    blocks = width // LANES
    for chunk in range(count):
        copies[chunk].wait()
        part = fold3(dot_nn(split, et_ref[chunk]))
        for block in range(blocks):
            out[chunk * blocks + block] = lanes(part, block)


def piece_kernel(factor, acts_ref, errors, out):
    piece = fold3(dot_nn(split3(factor[...]), acts_ref[...]))
    out[0] = piece + add_all([errors[member] for member in range(NMP)])


def ortho_kernel(member_ref, place_ref, mine, theirs, acts_ref, split, tokens, panel):
    member = member_ref[0]
    for block in range(NMP // 2):
        panel[place_ref[member, block]] = mine[block] * (1.0 / NDP)
        panel[place_ref[member, NMP // 2 + block]] = theirs[block] * (1.0 / NDP)
    blocks, count = panel.shape[0], panel.shape[1]
    groups = count // 8

    def inner_of(index):
        first = index // 8
        sums = [None] * groups
        for block in range(blocks):
            row = panel[block, index : index + 1, :]
            for group in range(first, groups):
                term = panel[block, group * 8 : group * 8 + 8, :] * row
                sums[group] = term if sums[group] is None else sums[group] + term
        return [None if s is None else jnp.sum(s, axis=1, keepdims=True) for s in sums]

    order = lax.broadcasted_iota(jnp.int32, (8, 1), 0)
    for index in range(count):
        first, place = index // 8, index % 8
        inner = inner_of(index)
        scale = 1.0 / (jnp.sqrt(inner[first][place : place + 1, :]) + ortho_eps)
        weights = []
        for group in range(first, groups):
            weight = inner[group] * (scale * scale)
            if group == first:
                weight = jnp.where(order > place, weight, 0.0)
            weights.append(weight)
        for block in range(blocks):
            row = panel[block, index : index + 1, :]
            for group in range(first, groups):
                if group == first and place == 7:
                    continue
                rows = slice(group * 8, group * 8 + 8)
                panel[block, rows, :] = panel[block, rows, :] - weights[group - first] * row
            panel[block, index : index + 1, :] = row * scale
    for block in range(blocks):
        split[block] = split3(panel[block])
    tokens[...] = fold3(dot_nt(split[member], acts_ref[...]))


def errors_kernel(basis_ref, et_hbm, out, et_ref, sems):
    chunks, width = et_ref.shape[0], et_ref.shape[2]
    copies = [
        pltpu.make_async_copy(et_hbm.at[:, chunk * width : (chunk + 1) * width], et_ref.at[chunk], sems.at[chunk])
        for chunk in range(chunks)
    ]
    for copy in copies:
        copy.start()
    total = None
    for chunk in range(chunks):
        copies[chunk].wait()
        part = dot_nt(et_ref[chunk], wide(basis_ref, chunk, width))
        total = part if total is None else total + part
    out[...] = fold3(total.T)


def right_kernel(tokens, gt_ref, errors, out):
    out[...] = fold3(dot_nt(split3(tokens[...]), gt_ref[...])) + errors[...]


def wide(ref, chunk, width):
    count = width // LANES
    return jnp.concatenate([ref[chunk * count + block] for block in range(count)], axis=1)


def final_kernel(dp_ref, sum_ref, basis_ref, acts_hbm, et_hbm, gt_hbm, weight, moment1, moment2, new_weight, new_moment1,
                 new_moment2, new_error, q_new, acts_v, error_v, gt_v, updated, rounded, acts_sems, error_sems, sems):
    chunks, width = rounded.shape[0], rounded.shape[2]
    count = width // LANES
    gt_copy = pltpu.make_async_copy(gt_hbm, gt_v, sems.at[3])
    gt_copy.start()
    reads = []
    for chunk in range(chunks):
        blocks = pl.ds(chunk * count, count)
        columns = pl.ds(chunk * width, width)
        reads.append(pltpu.make_async_copy(acts_hbm.at[blocks], acts_v.at[blocks], acts_sems.at[chunk]))
        reads.append(pltpu.make_async_copy(et_hbm.at[:, columns], error_v.at[chunk], error_sems.at[chunk]))
    for copy in reads:
        copy.start()
    mean = sum_ref[...] * (1.0 / NDP)
    q_new[...] = mean
    rows, ff = mean.shape
    stack = split3(mean.T)
    hi, mid, lo = stack[:ff], stack[ff : 2 * ff], stack[2 * ff :]
    factor = jnp.concatenate([hi, hi, hi, mid, mid, lo], axis=1)

    def approx_of(chunk):
        basis = wide(basis_ref, chunk, width)
        hi, mid, lo = basis[:rows], basis[rows : 2 * rows], basis[2 * rows :]
        return dot_nn(factor, jnp.concatenate([hi, mid, lo, hi, mid, hi], axis=0))

    update = approx_of(dp_ref[0])
    first = beta_one * moment1[...] + (1.0 - beta_one) * update
    second = beta_two * moment2[...] + (1.0 - beta_two) * update * update
    updated[0] = first
    updated[1] = second
    updated[2] = weight[...] - learn_rate * (first / corr_one) / (jnp.sqrt(second / corr_two) + adam_eps)
    writes = [
        pltpu.make_async_copy(updated.at[0], new_moment1, sems.at[0]),
        pltpu.make_async_copy(updated.at[1], new_moment2, sems.at[1]),
        pltpu.make_async_copy(updated.at[2], new_weight, sems.at[2]),
    ]
    for copy in writes:
        copy.start()
    gt_copy.wait()

    def body(chunk, carry):
        blocks = pl.ds(chunk * count, count)
        pltpu.make_async_copy(acts_v.at[blocks], acts_v.at[blocks], acts_sems.at[chunk]).wait()
        pltpu.make_async_copy(error_v.at[chunk], error_v.at[chunk], error_sems.at[chunk]).wait()
        field = dot_nn(gt_v[...], wide(acts_v, chunk, width)) + error_v[chunk].astype(F32)
        rounded[chunk] = (field - approx_of(chunk)).astype(BF16)
        columns = pl.ds(pl.multiple_of(chunk * width, width), width)
        pltpu.make_async_copy(rounded.at[chunk], new_error.at[:, columns], error_sems.at[chunk]).start()
        return carry

    lax.fori_loop(0, chunks, body, 0)
    for copy in writes:
        copy.wait()
    for chunk in range(chunks):
        pltpu.make_async_copy(rounded.at[chunk], rounded.at[chunk], error_sems.at[chunk]).wait()


def call(kernel, outs, args, specs=None, out_specs=None, scratch=(), limit=16, flops=0, moved=0):
    return pl.pallas_call(
        kernel,
        out_shape=outs,
        in_specs=specs or [VMEM] * len(args),
        out_specs=out_specs or jax.tree.map(lambda _: VMEM, outs),
        scratch_shapes=scratch,
        compiler_params=pltpu.CompilerParams(vmem_limit_bytes=limit * MIB),
        cost_estimate=pl.CostEstimate(flops=flops, bytes_accessed=moved, transcendentals=0),
    )(*args)


def swap(value, axis, level):
    return lax.ppermute(value, axis, list(enumerate(level)))


def total(value, axis, levels):
    for level in levels:
        value = value + swap(value, axis, level)
    return value


def shards(acts, grad_out, error_buffer, q_prev, weight, moment1, moment2):
    member = lax.axis_index("mp").astype(jnp.int32).reshape(1)
    dp = lax.axis_index("dp").astype(jnp.int32).reshape(1)
    gt, et = grad_out.T, error_buffer.T
    rank, ff = q_prev.shape
    tokens, model = acts.shape[0], et.shape[1]
    chunks, width = 8, model // 8
    array = jax.ShapeDtypeStruct
    along = ALONG_Z + ALONG_X

    gathered = lax.all_gather(acts, "mp", axis=0)

    factor = call(
        token_kernel, array((rank, tokens), F32), (q_prev, gt), specs=[HBM] * 2,
        scratch=[pltpu.VMEM((rank, ff), F32), pltpu.VMEM((ff, tokens), BF16), pltpu.SemaphoreType.DMA((2,))],
        limit=60, flops=6 * rank * ff * tokens, moved=2 * ff * tokens,
    )
    factor, late = lax.optimization_barrier((factor, q_prev))
    errors = call(
        error_kernel, array((NMP, rank, LANES), F32), (late, et), specs=[HBM] * 2,
        scratch=[
            pltpu.VMEM((rank, ff), F32), pltpu.VMEM((chunks, ff, width), BF16), pltpu.SemaphoreType.DMA((9,)),
        ],
        limit=58, flops=6 * rank * ff * model, moved=2 * ff * model,
    )
    factor, errors = lax.optimization_barrier((total(factor, "mp", along[:1]), errors))
    errors = lax.all_to_all(errors, "mp", 0, 0)
    factor = total(factor, "mp", along[1:])

    panel = call(piece_kernel, array((1, rank, LANES), F32), (factor, acts, errors), moved=MIB)
    panel = total(panel, "dp", ALONG_DP)
    for level in along[:-1]:
        panel = jnp.concatenate([panel, swap(panel, "mp", level)])
    basis, factor = call(
        ortho_kernel, [array((NMP, 3 * rank, LANES), BF16), array((rank, tokens), F32)],
        (member, jnp.asarray(met(along, NMP)), panel, swap(panel, "mp", along[-1]), acts),
        specs=[SMEM, SMEM, VMEM, VMEM, VMEM],
        scratch=[pltpu.VMEM((NMP, rank, LANES), F32)], flops=MIB, moved=4 * MIB,
    )

    errors = call(
        errors_kernel, array((rank, ff), F32), (basis, et), specs=[VMEM, HBM],
        scratch=[pltpu.VMEM((chunks, ff, width), BF16), pltpu.SemaphoreType.DMA((chunks,))],
        limit=16, flops=6 * rank * ff * model, moved=2 * ff * model,
    )
    factor = total(factor, "mp", along)
    right = call(
        right_kernel, array((rank, ff), F32), (factor, gt, errors), flops=6 * rank * ff * tokens, moved=2 * ff * tokens
    )
    right = total(right, "dp", ALONG_DP)

    block = array((ff, width), F32)
    outs = call(
        final_kernel,
        [block] * 3 + [array((ff, model), BF16), array((rank, ff), F32)],
        (dp, right, basis, gathered, et, gt, weight.T, moment1.T, moment2.T),
        specs=[SMEM, VMEM, VMEM, HBM, HBM, HBM, VMEM, VMEM, VMEM],
        out_specs=[HBM] * 4 + [VMEM],
        scratch=[
            pltpu.VMEM((NMP, tokens, LANES), BF16),
            pltpu.VMEM((chunks, ff, width), BF16),
            pltpu.VMEM((ff, tokens), BF16),
            pltpu.VMEM((3, ff, width), F32),
            pltpu.VMEM((chunks, ff, width), BF16),
            pltpu.SemaphoreType.DMA((chunks,)),
            pltpu.SemaphoreType.DMA((chunks,)),
            pltpu.SemaphoreType.DMA((4,)),
        ],
        limit=56, flops=2 * model * ff * (tokens + 6 * rank), moved=22 * MIB,
    )
    new_weight, new_moment1, new_moment2, new_error, q_new = outs
    return (new_weight.T, new_moment1.T, new_moment2.T, new_error.T, q_new)


def solution(mesh):
    placed = (
        P("dp", "mp"),
        P("dp", "mp"),
        P("dp", "mp"),
        P(None, "mp"),
        P("dp", "mp"),
        P("dp", "mp"),
        P("dp", "mp"),
    )
    return jax.shard_map(
        shards,
        mesh=mesh,
        in_specs=placed,
        out_specs=(P("dp", "mp"), P("dp", "mp"), P("dp", "mp"), P("dp", "mp"), P(None, "mp")),
        check_vma=False,
    )
```

time: 198 us -> 189 us (0.955)
  starting transfers between devices: 66.9 us -> 56.4 us
  waiting for transfers between devices: 76.9 us -> 84.1 us
  Pallas kernels: 32.5 us -> 30.2 us
    ppermute x19 -> x21, waiting for transfers between devices: 76.8 us -> 83.4 us  [swap(): return lax.ppermute(value, axis, list(enumerate(level)))]
    ppermute x6 -> x0, starting transfers between devices: 5.93 us -> none  [along_x(): lax.ppermute(value, 'mp', [(x * NZ + z, (x + shift) % NX * NZ + z) for x...]
    ppermute x19 -> x21, starting transfers between devices: 50.8 us -> 46.1 us  [swap(): return lax.ppermute(value, axis, list(enumerate(level)))]
    pallas_call x6 -> x7, Pallas kernels: 32.5 us -> 30.2 us  [call(): pl.pallas_call(kernel, out_shape=outs, in_specs=specs or [VMEM] * len(arg...]
    unnamed x7 -> x15, local copies, waits for them, and re-layouts: 0.02 us -> 2.11 us
  transfers between devices with their start and end apart: 27 -> 23, of which waited for: 16 -> 19; matrix products, arithmetic and copies ran while one was open for 1% -> 0% of each run, Pallas kernels for 6% -> 9%
where the time goes in v3:
time: 189 us; the launch traced here: 188 us
  waiting for transfers between devices  84.1 us (44%)
  starting transfers between devices  56.4 us (30%)
  Pallas kernels  30.2 us (16%)
  between operations  14.3 us (8%)
  local copies, waits for them, and re-layouts  2.12 us (1%)
    ppermute x21, waiting for transfers between devices, swap(): return lax.ppermute(value, axis, list(enumerate(level)))  83.4 us
    ppermute x21, starting transfers between devices, swap(): return lax.ppermute(value, axis, list(enumerate(level)))  46.1 us
    pallas_call x7, Pallas kernels, call(): pl.pallas_call(kernel, out_shape=outs, in_specs=specs or [VMEM] * len(arg...  30.2 us
    all_to_all x1, starting transfers between devices, shards(): errors = lax.all_to_all(errors, 'mp', 0, 0)  10.3 us
  transfers between devices with their start and end apart: 23, of which 19 were waited for; matrix products, arithmetic and copies ran while one was open for 0% of the time, Pallas kernels for 9%

profile of v3, /device:TPU:1, one launch (start us, length us, event | category | flops | bytes accessed | tf_op | source)
XLA Modules:
  0.0 188.0 jit_solution(17261504567849890738)
XLA Ops:
  12.7 3.7 %shard_map.120 = f32[32,32,128]{2,1,0:T(8,128)} custom-call(f32[32,448]{1,0:T(8,128)} %q_hbm.2, bf16[448,4096]{1,0:T(8,128)(2,1)} %bitcast.12), custom_call_target="tpu_custom_call" | custom-call | flops 352321536 | bytes 3670016 | tf_op jit(solution)/shard_map/pallas_call | solution.py:250
  16.4 10.3 %all-to-all-start = ((f32[32,32,128]{2,1,0:T(8,128)}), f32[32,32,128]{2,1,0:T(8,128)S(1)}, u32[]{:S(2)}, u32[]{:S(2)}) async-start(f32[32,32,128]{2,1,0:T(8,128)} %shard_map.120), calls=%async_computation | async-start | bytes 1048576 | tf_op jit(solution)/shard_map/all_to_all | solution.py:297
  29.2 19.0 %collective-permute-done.1 = f32[32,1024]{1,0:T(8,128)S(1)} collective-permute-done((f32[32,1024]{1,0:T(8,128)S(1)}, f32[32,1024]{1,0:T(8,128)S(1)}, u32[]{:S(2)}, u32[]{:S(2)}) %collective-permute-start.1) | collective-permute-done | bytes 131104 | tf_op jit(solution)/shard_map/ppermute | solution.py:262
  48.3 3.4 %collective-permute-start.2 = (f32[32,1024]{1,0:T(8,128)S(1)}, f32[32,1024]{1,0:T(8,128)S(1)}, u32[]{:S(2)}, u32[]{:S(2)}) collective-permute-start(f32[32,1024]{1,0:T(8,128)S(1)} %add.49), channel_id=1, source_target_pairs={{0,3},{1,6},{2,5},{3,0},{4,7},{5,2},{6,1},{7,4},{8,11},{9,14},{10,... | collective-permute-start | bytes 393224 | tf_op jit(solution)/shard_map/ppermute | solution.py:262
  51.7 5.8 %collective-permute-done.2 = f32[32,1024]{1,0:T(8,128)S(1)} collective-permute-done((f32[32,1024]{1,0:T(8,128)S(1)}, f32[32,1024]{1,0:T(8,128)S(1)}, u32[]{:S(2)}, u32[]{:S(2)}) %collective-permute-start.2) | collective-permute-done | bytes 131104 | tf_op jit(solution)/shard_map/ppermute | solution.py:262
  58.3 3.5 %collective-permute-done.3 = f32[32,1024]{1,0:T(8,128)S(1)} collective-permute-done((f32[32,1024]{1,0:T(8,128)S(1)}, f32[32,1024]{1,0:T(8,128)S(1)}, u32[]{:S(2)}, u32[]{:S(2)}) %collective-permute-start.3) | collective-permute-done | bytes 131104 | tf_op jit(solution)/shard_map/ppermute | solution.py:262
  61.8 2.9 %collective-permute-start.4 = (f32[32,1024]{1,0:T(8,128)S(1)}, f32[32,1024]{1,0:T(8,128)S(1)}, u32[]{:S(2)}, u32[]{:S(2)}) collective-permute-start(f32[32,1024]{1,0:T(8,128)S(1)} %add.51), channel_id=1, source_target_pairs={{0,24},{1,25},{2,26},{3,27},{4,28},{5,29},{6,30},{7,31},{8,16},{9,... | collective-permute-start | bytes 393224 | tf_op jit(solution)/shard_map/ppermute | solution.py:262
  67.3 6.0 %collective-permute-start.5 = (f32[1,32,128]{2,1,0:T(8,128)S(1)}, f32[1,32,128]{2,1,0:T(8,128)S(1)}, u32[]{:S(2)}, u32[]{:S(2)}) collective-permute-start(f32[1,32,128]{2,1,0:T(8,128)S(1)} %shard_map.121), channel_id=1, source_target_pairs={{0,32},{32,0},{64,96},{96,64},{128,160},{160,128},{192,224},{224,1... | collective-permute-start | bytes 49160 | tf_op jit(solution)/shard_map/ppermute | solution.py:262
  77.6 5.3 %collective-permute-start.7 = (f32[1,32,128]{2,1,0:T(8,128)S(1)}, f32[1,32,128]{2,1,0:T(8,128)S(1)}, u32[]{:S(2)}, u32[]{:S(2)}) collective-permute-start(f32[1,32,128]{2,1,0:T(8,128)S(1)} %add.54), channel_id=1, source_target_pairs={{0,192},{32,224},{64,128},{96,160},{128,64},{160,96},{192,0},{224,... | collective-permute-start | bytes 49160 | tf_op jit(solution)/shard_map/ppermute | solution.py:262
  87.4 5.0 %collective-permute-done.9 = f32[2,32,128]{2,1,0:T(8,128)S(1)} collective-permute-done((f32[2,32,128]{2,1,0:T(8,128)S(1)}, f32[2,32,128]{2,1,0:T(8,128)S(1)}, u32[]{:S(2)}, u32[]{:S(2)}) %collective-permute-start.9) | collective-permute-done | bytes 32800 | tf_op jit(solution)/shard_map/ppermute | solution.py:262
  92.4 6.6 %collective-permute-done.10 = f32[4,32,128]{2,1,0:T(8,128)S(1)} collective-permute-done((f32[4,32,128]{2,1,0:T(8,128)S(1)}, f32[4,32,128]{2,1,0:T(8,128)S(1)}, u32[]{:S(2)}, u32[]{:S(2)}) %collective-permute-start.10) | collective-permute-done | bytes 65568 | tf_op jit(solution)/shard_map/ppermute | solution.py:262
  99.1 7.0 %collective-permute-done.11 = f32[8,32,128]{2,1,0:T(8,128)S(1)} collective-permute-done((f32[8,32,128]{2,1,0:T(8,128)S(1)}, f32[8,32,128]{2,1,0:T(8,128)S(1)}, u32[]{:S(2)}, u32[]{:S(2)}) %collective-permute-start.11) | collective-permute-done | bytes 131104 | tf_op jit(solution)/shard_map/ppermute | solution.py:262
  106.1 4.0 %collective-permute-start.12 = (f32[16,32,128]{2,1,0:T(8,128)S(1)}, f32[16,32,128]{2,1,0:T(8,128)S(1)}, u32[]{:S(2)}, u32[]{:S(2)}) collective-permute-start(f32[16,32,128]{2,1,0:T(8,128)S(1)} %constant_dynamic-update-slice_fusion.mine), channel_id=1, source_target_pairs={{0,24},{1,25},{2,26},{3,27},{4,28},{5,29},{6,30},{7,31},{8,16},{9,... | collective-permute-start | bytes 786440 | tf_op jit(solution)/shard_map/ppermute | solution.py:262
  110.1 4.2 %collective-permute-done.12.theirs = f32[16,32,128]{2,1,0:T(8,128)S(1)} collective-permute-done((f32[16,32,128]{2,1,0:T(8,128)S(1)}, f32[16,32,128]{2,1,0:T(8,128)S(1)}, u32[]{:S(2)}, u32[]{:S(2)}) %collective-permute-start.12) | collective-permute-done | bytes 262176 | tf_op jit(solution)/shard_map/ppermute | solution.py:262
  114.3 6.8 %shard_map.122 = (bf16[32,96,128]{2,1,0:T(8,128)(2,1)S(1)}, f32[32,1024]{1,0:T(8,128)S(1)}) custom-call(s32[1]{0:T(128)} %bitcast.1.member_ref, s32[32,32]{1,0:T(8,128)S(1)} %copy-done.4, f32[16,32,128]{2,1,0:T(8,128)S(1)} %constant_dynamic-update-slice_fusion.mine, f32[16,32,128]{2,1,0:T(8,128)S(1)} %collective-permute-done.12.theirs, ...), custom_call_target="tpu_custom_call" | custom-call | flops 1048576 | bytes 4194304 | tf_op jit(solution)/shard_map/pallas_call | solution.py:250
  121.2 3.8 %collective-permute-done.13 = f32[32,1024]{1,0:T(8,128)S(1)} collective-permute-done((f32[32,1024]{1,0:T(8,128)S(1)}, f32[32,1024]{1,0:T(8,128)S(1)}, u32[]{:S(2)}, u32[]{:S(2)}) %collective-permute-start.13) | collective-permute-done | bytes 131104 | tf_op jit(solution)/shard_map/ppermute | solution.py:262
  125.2 5.0 %collective-permute-done.14 = f32[32,1024]{1,0:T(8,128)S(1)} collective-permute-done((f32[32,1024]{1,0:T(8,128)S(1)}, f32[32,1024]{1,0:T(8,128)S(1)}, u32[]{:S(2)}, u32[]{:S(2)}) %collective-permute-start.14) | collective-permute-done | bytes 131104 | tf_op jit(solution)/shard_map/ppermute | solution.py:262
  131.5 5.4 %collective-permute-done.15 = f32[32,1024]{1,0:T(8,128)S(1)} collective-permute-done((f32[32,1024]{1,0:T(8,128)S(1)}, f32[32,1024]{1,0:T(8,128)S(1)}, u32[]{:S(2)}, u32[]{:S(2)}) %collective-permute-start.15) | collective-permute-done | bytes 131104 | tf_op jit(solution)/shard_map/ppermute | solution.py:262
  137.0 3.8 %collective-permute-done.16 = f32[32,1024]{1,0:T(8,128)S(1)} collective-permute-done((f32[32,1024]{1,0:T(8,128)S(1)}, f32[32,1024]{1,0:T(8,128)S(1)}, u32[]{:S(2)}, u32[]{:S(2)}) %collective-permute-start.16) | collective-permute-done | bytes 131104 | tf_op jit(solution)/shard_map/ppermute | solution.py:262
  145.4 2.8 %shard_map.123.errors = f32[32,448]{1,0:T(8,128)S(1)} custom-call(bf16[32,96,128]{2,1,0:T(8,128)(2,1)S(1)} %get-tuple-element.21.basis_ref, bf16[448,4096]{1,0:T(8,128)(2,1)S(1)} %bitcast.14), custom_call_target="tpu_custom_call" | custom-call | flops 352321536 | bytes 3670016 | tf_op jit(solution)/shard_map/pallas_call | solution.py:250
  148.7 8.7 %collective-permute-start.18 = (f32[32,448]{1,0:T(8,128)S(1)}, f32[32,448]{1,0:T(8,128)S(1)}, u32[]{:S(2)}, u32[]{:S(2)}) collective-permute-start(f32[32,448]{1,0:T(8,128)S(1)} %shard_map.124), channel_id=1, source_target_pairs={{0,32},{32,0},{64,96},{96,64},{128,160},{160,128},{192,224},{224,1... | collective-permute-start | bytes 172040 | tf_op jit(solution)/shard_map/ppermute | solution.py:262
  158.5 3.0 %collective-permute-done.19 = f32[32,448]{1,0:T(8,128)S(1)} collective-permute-done((f32[32,448]{1,0:T(8,128)S(1)}, f32[32,448]{1,0:T(8,128)S(1)}, u32[]{:S(2)}, u32[]{:S(2)}) %collective-permute-start.19) | collective-permute-done | bytes 57376 | tf_op jit(solution)/shard_map/ppermute | solution.py:262
  161.5 3.1 %collective-permute-start.20 = (f32[32,448]{1,0:T(8,128)S(1)}, f32[32,448]{1,0:T(8,128)S(1)}, u32[]{:S(2)}, u32[]{:S(2)}) collective-permute-start(f32[32,448]{1,0:T(8,128)S(1)} %add.62), channel_id=1, source_target_pairs={{0,192},{32,224},{64,128},{96,160},{128,64},{160,96},{192,0},{224,... | collective-permute-start | bytes 172040 | tf_op jit(solution)/shard_map/ppermute | solution.py:262
  167.0 14.2 %shard_map.125 = (f32[448,512]{1,0:T(8,128)}, f32[448,512]{1,0:T(8,128)}, f32[448,512]{1,0:T(8,128)}, bf16[448,4096]{1,0:T(8,128)(2,1)}, f32[32,448]{1,0:T(8,128)}) custom-call(s32[1]{0:T(128)} %bitcast.dp_ref, f32[32,448]{1,0:T(8,128)} %add.63.sum_ref, bf16[32,96,128]{2,1,0:T(8,128)(2,1)} %copy-done.2, bf16[32,1024,128]{2,1,0:T(8,128)(2,1)} %bitcast.18, ...), custom_call_target="tpu_custom_call" | custom-call | flops 4462739456 | bytes 23068672 | tf_op jit(solution)/shard_map/pallas_call | solution.py:250
  (65 shorter events, 30.6 us)
Async XLA Ops:
  7.2 159.8 %all-gather.3.cloned.1.call-start = ((), (), s32[]{:S(2)}) async-start(), calls=%async_computation.1 | async-start | bytes 8650752 | tf_op jit(solution)/shard_map/all_gather | solution.py:281
  10.1 6.2 %collective-permute-start = (f32[32,1024]{1,0:T(8,128)}, f32[32,1024]{1,0:T(8,128)S(1)}, u32[]{:S(2)}, u32[]{:S(2)}) collective-permute-start(f32[32,1024]{1,0:T(8,128)} %shard_map.119), channel_id=1, source_target_pairs={{0,1},{1,0},{2,3},{3,2},{4,5},{5,4},{6,7},{7,6},{8,9},{9,8},{10,11... | collective-permute-start | bytes 393224 | tf_op jit(solution)/shard_map/ppermute | solution.py:262
  12.7 101.6 %copy-start.4 = (s32[32,32]{1,0:T(8,128)S(1)}, s32[32,32]{1,0:T(8,128)}, u32[]{:S(2)}) copy-start(s32[32,32]{1,0:T(8,128)} %constant.11.clone.place_ref) | copy-start | bytes 12292
  16.4 50.6 %all-to-all-start = ((f32[32,32,128]{2,1,0:T(8,128)}), f32[32,32,128]{2,1,0:T(8,128)S(1)}, u32[]{:S(2)}, u32[]{:S(2)}) async-start(f32[32,32,128]{2,1,0:T(8,128)} %shard_map.120), calls=%async_computation | async-start | bytes 1048576 | tf_op jit(solution)/shard_map/all_to_all | solution.py:297
  26.7 21.6 %collective-permute-start.1 = (f32[32,1024]{1,0:T(8,128)S(1)}, f32[32,1024]{1,0:T(8,128)S(1)}, u32[]{:S(2)}, u32[]{:S(2)}) collective-permute-start(f32[32,1024]{1,0:T(8,128)S(1)} %add.48), channel_id=1, source_target_pairs={{0,7},{1,2},{2,1},{3,4},{4,3},{5,6},{6,5},{7,0},{8,15},{9,10},{10,... | collective-permute-start | bytes 393224 | tf_op jit(solution)/shard_map/ppermute | solution.py:262
  48.3 9.1 %collective-permute-start.2 = (f32[32,1024]{1,0:T(8,128)S(1)}, f32[32,1024]{1,0:T(8,128)S(1)}, u32[]{:S(2)}, u32[]{:S(2)}) collective-permute-start(f32[32,1024]{1,0:T(8,128)S(1)} %add.49), channel_id=1, source_target_pairs={{0,3},{1,6},{2,5},{3,0},{4,7},{5,2},{6,1},{7,4},{8,11},{9,14},{10,... | collective-permute-start | bytes 393224 | tf_op jit(solution)/shard_map/ppermute | solution.py:262
  57.4 4.3 %collective-permute-start.3 = (f32[32,1024]{1,0:T(8,128)S(1)}, f32[32,1024]{1,0:T(8,128)S(1)}, u32[]{:S(2)}, u32[]{:S(2)}) collective-permute-start(f32[32,1024]{1,0:T(8,128)S(1)} %add.50), channel_id=1, source_target_pairs={{0,8},{1,9},{2,10},{3,11},{4,12},{5,13},{6,14},{7,15},{8,0},{9,1},... | collective-permute-start | bytes 393224 | tf_op jit(solution)/shard_map/ppermute | solution.py:262
  61.8 5.2 %collective-permute-start.4 = (f32[32,1024]{1,0:T(8,128)S(1)}, f32[32,1024]{1,0:T(8,128)S(1)}, u32[]{:S(2)}, u32[]{:S(2)}) collective-permute-start(f32[32,1024]{1,0:T(8,128)S(1)} %add.51), channel_id=1, source_target_pairs={{0,24},{1,25},{2,26},{3,27},{4,28},{5,29},{6,30},{7,31},{8,16},{9,... | collective-permute-start | bytes 393224 | tf_op jit(solution)/shard_map/ppermute | solution.py:262
  67.3 6.9 %collective-permute-start.5 = (f32[1,32,128]{2,1,0:T(8,128)S(1)}, f32[1,32,128]{2,1,0:T(8,128)S(1)}, u32[]{:S(2)}, u32[]{:S(2)}) collective-permute-start(f32[1,32,128]{2,1,0:T(8,128)S(1)} %shard_map.121), channel_id=1, source_target_pairs={{0,32},{32,0},{64,96},{96,64},{128,160},{160,128},{192,224},{224,1... | collective-permute-start | bytes 49160 | tf_op jit(solution)/shard_map/ppermute | solution.py:262
  74.1 3.4 %collective-permute-start.6 = (f32[1,32,128]{2,1,0:T(8,128)S(1)}, f32[1,32,128]{2,1,0:T(8,128)S(1)}, u32[]{:S(2)}, u32[]{:S(2)}) collective-permute-start(f32[1,32,128]{2,1,0:T(8,128)S(1)} %add.53), channel_id=1, source_target_pairs={{0,64},{32,96},{64,0},{96,32},{128,192},{160,224},{192,128},{224,1... | collective-permute-start | bytes 49160 | tf_op jit(solution)/shard_map/ppermute | solution.py:262
  77.6 6.8 %collective-permute-start.7 = (f32[1,32,128]{2,1,0:T(8,128)S(1)}, f32[1,32,128]{2,1,0:T(8,128)S(1)}, u32[]{:S(2)}, u32[]{:S(2)}) collective-permute-start(f32[1,32,128]{2,1,0:T(8,128)S(1)} %add.54), channel_id=1, source_target_pairs={{0,192},{32,224},{64,128},{96,160},{128,64},{160,96},{192,0},{224,... | collective-permute-start | bytes 49160 | tf_op jit(solution)/shard_map/ppermute | solution.py:262
  84.4 3.0 %collective-permute-start.8 = (f32[1,32,128]{2,1,0:T(8,128)S(1)}, f32[1,32,128]{2,1,0:T(8,128)S(1)}, u32[]{:S(2)}, u32[]{:S(2)}) collective-permute-start(f32[1,32,128]{2,1,0:T(8,128)S(1)} %get-tuple-element.28), channel_id=1, source_target_pairs={{0,1},{1,0},{2,3},{3,2},{4,5},{5,4},{6,7},{7,6},{8,9},{9,8},{10,11... | collective-permute-start | bytes 49160 | tf_op jit(solution)/shard_map/ppermute | solution.py:262
  87.4 5.0 %collective-permute-start.9 = (f32[2,32,128]{2,1,0:T(8,128)S(1)}, f32[2,32,128]{2,1,0:T(8,128)S(1)}, u32[]{:S(2)}, u32[]{:S(2)}) collective-permute-start(f32[2,32,128]{2,1,0:T(8,128)S(1)} %pad_maximum_fusion.2), channel_id=1, source_target_pairs={{0,7},{1,2},{2,1},{3,4},{4,3},{5,6},{6,5},{7,0},{8,15},{9,10},{10,... | collective-permute-start | bytes 98312 | tf_op jit(solution)/shard_map/ppermute | solution.py:262
  92.4 6.6 %collective-permute-start.10 = (f32[4,32,128]{2,1,0:T(8,128)S(1)}, f32[4,32,128]{2,1,0:T(8,128)S(1)}, u32[]{:S(2)}, u32[]{:S(2)}) collective-permute-start(f32[4,32,128]{2,1,0:T(8,128)S(1)} %pad_maximum_fusion.1), channel_id=1, source_target_pairs={{0,3},{1,6},{2,5},{3,0},{4,7},{5,2},{6,1},{7,4},{8,11},{9,14},{10,... | collective-permute-start | bytes 196616 | tf_op jit(solution)/shard_map/ppermute | solution.py:262
  99.0 7.1 %collective-permute-start.11 = (f32[8,32,128]{2,1,0:T(8,128)S(1)}, f32[8,32,128]{2,1,0:T(8,128)S(1)}, u32[]{:S(2)}, u32[]{:S(2)}) collective-permute-start(f32[8,32,128]{2,1,0:T(8,128)S(1)} %pad_maximum_fusion), channel_id=1, source_target_pairs={{0,8},{1,9},{2,10},{3,11},{4,12},{5,13},{6,14},{7,15},{8,0},{9,1},... | collective-permute-start | bytes 393224 | tf_op jit(solution)/shard_map/ppermute | solution.py:262
  106.1 8.2 %collective-permute-start.12 = (f32[16,32,128]{2,1,0:T(8,128)S(1)}, f32[16,32,128]{2,1,0:T(8,128)S(1)}, u32[]{:S(2)}, u32[]{:S(2)}) collective-permute-start(f32[16,32,128]{2,1,0:T(8,128)S(1)} %constant_dynamic-update-slice_fusion.mine), channel_id=1, source_target_pairs={{0,24},{1,25},{2,26},{3,27},{4,28},{5,29},{6,30},{7,31},{8,16},{9,... | collective-permute-start | bytes 786440 | tf_op jit(solution)/shard_map/ppermute | solution.py:262
  121.1 3.9 %collective-permute-start.13 = (f32[32,1024]{1,0:T(8,128)S(1)}, f32[32,1024]{1,0:T(8,128)S(1)}, u32[]{:S(2)}, u32[]{:S(2)}) collective-permute-start(f32[32,1024]{1,0:T(8,128)S(1)} %get-tuple-element.20), channel_id=1, source_target_pairs={{0,1},{1,0},{2,3},{3,2},{4,5},{5,4},{6,7},{7,6},{8,9},{9,8},{10,11... | collective-permute-start | bytes 393224 | tf_op jit(solution)/shard_map/ppermute | solution.py:262
  125.0 5.1 %collective-permute-start.14 = (f32[32,1024]{1,0:T(8,128)S(1)}, f32[32,1024]{1,0:T(8,128)S(1)}, u32[]{:S(2)}, u32[]{:S(2)}) collective-permute-start(f32[32,1024]{1,0:T(8,128)S(1)} %add.56), channel_id=1, source_target_pairs={{0,7},{1,2},{2,1},{3,4},{4,3},{5,6},{6,5},{7,0},{8,15},{9,10},{10,... | collective-permute-start | bytes 393224 | tf_op jit(solution)/shard_map/ppermute | solution.py:262
  130.2 6.7 %collective-permute-start.15 = (f32[32,1024]{1,0:T(8,128)S(1)}, f32[32,1024]{1,0:T(8,128)S(1)}, u32[]{:S(2)}, u32[]{:S(2)}) collective-permute-start(f32[32,1024]{1,0:T(8,128)S(1)} %add.57), channel_id=1, source_target_pairs={{0,3},{1,6},{2,5},{3,0},{4,7},{5,2},{6,1},{7,4},{8,11},{9,14},{10,... | collective-permute-start | bytes 393224 | tf_op jit(solution)/shard_map/ppermute | solution.py:262
  136.9 3.9 %collective-permute-start.16 = (f32[32,1024]{1,0:T(8,128)S(1)}, f32[32,1024]{1,0:T(8,128)S(1)}, u32[]{:S(2)}, u32[]{:S(2)}) collective-permute-start(f32[32,1024]{1,0:T(8,128)S(1)} %add.58), channel_id=1, source_target_pairs={{0,8},{1,9},{2,10},{3,11},{4,12},{5,13},{6,14},{7,15},{8,0},{9,1},... | collective-permute-start | bytes 393224 | tf_op jit(solution)/shard_map/ppermute | solution.py:262
  140.8 7.4 %collective-permute-start.17 = (f32[32,1024]{1,0:T(8,128)S(1)}, f32[32,1024]{1,0:T(8,128)S(1)}, u32[]{:S(2)}, u32[]{:S(2)}) collective-permute-start(f32[32,1024]{1,0:T(8,128)S(1)} %add.59), channel_id=1, source_target_pairs={{0,24},{1,25},{2,26},{3,27},{4,28},{5,29},{6,30},{7,31},{8,16},{9,... | collective-permute-start | bytes 393224 | tf_op jit(solution)/shard_map/ppermute | solution.py:262
  148.7 9.6 %collective-permute-start.18 = (f32[32,448]{1,0:T(8,128)S(1)}, f32[32,448]{1,0:T(8,128)S(1)}, u32[]{:S(2)}, u32[]{:S(2)}) collective-permute-start(f32[32,448]{1,0:T(8,128)S(1)} %shard_map.124), channel_id=1, source_target_pairs={{0,32},{32,0},{64,96},{96,64},{128,160},{160,128},{192,224},{224,1... | collective-permute-start | bytes 172040 | tf_op jit(solution)/shard_map/ppermute | solution.py:262
  158.3 3.2 %collective-permute-start.19 = (f32[32,448]{1,0:T(8,128)S(1)}, f32[32,448]{1,0:T(8,128)S(1)}, u32[]{:S(2)}, u32[]{:S(2)}) collective-permute-start(f32[32,448]{1,0:T(8,128)S(1)} %add.61), channel_id=1, source_target_pairs={{0,64},{32,96},{64,0},{96,32},{128,192},{160,224},{192,128},{224,1... | collective-permute-start | bytes 172040 | tf_op jit(solution)/shard_map/ppermute | solution.py:262
  161.5 4.8 %collective-permute-start.20 = (f32[32,448]{1,0:T(8,128)S(1)}, f32[32,448]{1,0:T(8,128)S(1)}, u32[]{:S(2)}, u32[]{:S(2)}) collective-permute-start(f32[32,448]{1,0:T(8,128)S(1)} %add.62), channel_id=1, source_target_pairs={{0,192},{32,224},{64,128},{96,160},{128,64},{160,96},{192,0},{224,... | collective-permute-start | bytes 172040 | tf_op jit(solution)/shard_map/ppermute | solution.py:262
  (5 other events, 134.9 us)
Sparse Core Ops, SparseCore 0:
  10.6 110.1 all-gather.2

commit v4 on v3

--- a/solution.py
+++ b/solution.py
@@ -16,6 +16,7 @@
 
 NX, NZ, NDP = 4, 8, 8
 NMP = NX * NZ
+FACTOR = 32
 LANES = 128
 F32, BF16 = jnp.float32, jnp.bfloat16
 MIB = 1 << 20
@@ -86,18 +87,19 @@
     return values[0]
 
 
-def token_kernel(q_hbm, gt_hbm, out, q_ref, gt_ref, sems):
-    copies = [pltpu.make_async_copy(q_hbm, q_ref, sems.at[0]), pltpu.make_async_copy(gt_hbm, gt_ref, sems.at[1])]
-    for copy in copies:
-        copy.start()
-    for copy in copies:
-        copy.wait()
-    out[...] = fold3(dot_nn(split3(q_ref[...]), gt_ref[...]))
-
-
-def error_kernel(q_hbm, et_hbm, out, q_ref, et_ref, sems):
-    count = et_ref.shape[0]
-    width = et_ref.shape[2]
+def tiles_of(value, out):
+    columns = value.shape[1] // LANES
+    for row in range(value.shape[0] // 8):
+        for column in range(columns):
+            out[row * columns + column] = lanes(value[row * 8 : row * 8 + 8], column)
+
+
+def rows_of(tiles, column, columns, rows):
+    return jnp.concatenate([tiles[row * columns + column] for row in range(rows // 8)], axis=0)
+
+
+def error_kernel(member_ref, core_ref, place_ref, q_hbm, et_hbm, keep, send, q_ref, et_ref, parts, sems):
+    count, width = et_ref.shape[0], et_ref.shape[2]
     copies = [
         pltpu.make_async_copy(et_hbm.at[:, chunk * width : (chunk + 1) * width], et_ref.at[chunk], sems.at[chunk])
         for chunk in range(count)
@@ -109,24 +111,114 @@
     first.wait()
     split = split3(q_ref[...])
     blocks = width // LANES
+    half = parts.shape[1] // 2
     for chunk in range(count):
         copies[chunk].wait()
         part = fold3(dot_nn(split, et_ref[chunk]))
         for block in range(blocks):
-            out[chunk * blocks + block] = lanes(part, block)
-
-
-def piece_kernel(factor, acts_ref, errors, out):
-    piece = fold3(dot_nn(split3(factor[...]), acts_ref[...]))
-    out[0] = piece + add_all([errors[member] for member in range(NMP)])
-
-
-def ortho_kernel(member_ref, place_ref, mine, theirs, acts_ref, split, tokens, panel):
+            parts[chunk * blocks + block] = lanes(part, block)
+    lower = core_ref[0] == 0
+    for place in range(NMP):
+        block = parts[place_ref[member_ref[0], place]]
+        keep[place] = jnp.where(lower, block[:half], block[half:])
+        send[place] = jnp.where(lower, block[half:], block[:half])
+
+
+def token_kernel(q_hbm, gt_hbm, out, q_ref, gt_ref, sems):
+    copies = [pltpu.make_async_copy(q_hbm, q_ref, sems.at[0]), pltpu.make_async_copy(gt_hbm, gt_ref, sems.at[1])]
+    for copy in copies:
+        copy.start()
+    for copy in copies:
+        copy.wait()
+    tiles_of(fold3(dot_nn(split3(q_ref[...]), gt_ref[...])), out)
+
+
+def store_blocks(value, out, start):
+    for block in range(value.shape[0]):
+        out[start + 2 * block] = value[block, :8]
+        out[start + 2 * block + 1] = value[block, 8:]
+
+
+def load_blocks(ref, start, count):
+    return jnp.stack(
+        [jnp.concatenate([ref[start + 2 * block], ref[start + 2 * block + 1]], axis=0) for block in range(count)]
+    )
+
+
+def open_kernel(tokens, mine, theirs, message, keep):
+    message[:FACTOR] = tokens[...]
+    both = mine[...] + theirs[...]
+    half = both.shape[0] // 2
+    keep[...] = both[:half]
+    store_blocks(both[half:], message, FACTOR)
+
+
+def halve_kernel(sent, kept, came, message, keep):
+    message[:FACTOR] = sent[:FACTOR] + came[:FACTOR]
+    count = kept.shape[0]
+    both = kept[...] + load_blocks(came, FACTOR, count)
+    keep[...] = both[: count // 2]
+    store_blocks(both[count // 2 :], message, FACTOR)
+
+
+def piece_kernel(core_ref, acts_ref, sent, kept, came, keep, send):
+    blocks = acts_ref.shape[0] // LANES
+    terms = []
+    for block in range(blocks):
+        factor = rows_of(sent, block, blocks, FACTOR) + rows_of(came, block, blocks, FACTOR)
+        terms.append(dot_nn(split3(factor), acts_ref[block * LANES : (block + 1) * LANES, :]))
+    while len(terms) > 1:
+        terms = [a + b for a, b in zip(terms[::2], terms[1::2])]
+    piece = fold3(terms[0])
+    half = piece.shape[0] // 2
+    lower = core_ref[0] == 0
+    keep[...] = jnp.where(lower, piece[:half], piece[half:]) + (kept[...] + load_blocks(came, FACTOR, 1))[0]
+    send[...] = jnp.where(lower, piece[half:], piece[:half])
+
+
+def start_kernel(core_ref, mine, theirs, acts_ref, message):
+    lower = core_ref[0] == 0
+    first, second = mine[...] * (1.0 / NDP), theirs[...] * (1.0 / NDP)
+    panel = jnp.concatenate([jnp.where(lower, first, second), jnp.where(lower, second, first)], axis=0)
+    tiles_of(fold3(dot_nt(split3(panel), acts_ref[...])), message)
+    store_blocks(first[None], message, FACTOR)
+
+
+def double_kernel(sent, came, message):
+    count = sent.shape[0] - FACTOR
+    message[:FACTOR] = sent[:FACTOR] + came[:FACTOR]
+    message[FACTOR : FACTOR + count] = sent[FACTOR:]
+    message[FACTOR + count :] = came[FACTOR:]
+
+
+def last_kernel(sent, came, factor, rows):
+    count = sent.shape[0] - FACTOR
+    factor[...] = sent[:FACTOR] + came[:FACTOR]
+    rows[:count] = sent[FACTOR:]
+    rows[count:] = came[FACTOR:]
+
+
+def ortho_kernel(member_ref, core_ref, place_ref, mine, theirs, tokens, gt_ref, et_hbm, split, right, panel, et_ref, sems):
+    chunks, width = et_ref.shape[0], et_ref.shape[2]
+    copies = [
+        pltpu.make_async_copy(et_hbm.at[:, chunk * width : (chunk + 1) * width], et_ref.at[chunk], sems.at[chunk])
+        for chunk in range(chunks)
+    ]
+    for copy in copies:
+        copy.start()
     member = member_ref[0]
-    for block in range(NMP // 2):
-        panel[place_ref[member, block]] = mine[block] * (1.0 / NDP)
-        panel[place_ref[member, NMP // 2 + block]] = theirs[block] * (1.0 / NDP)
-    blocks, count = panel.shape[0], panel.shape[1]
+    lower = core_ref[0] == 0
+    half = panel.shape[1] // 2
+    for place in range(NMP):
+        first = jnp.concatenate([mine[2 * place], mine[2 * place + 1]], axis=0)
+        second = jnp.concatenate([theirs[2 * place], theirs[2 * place + 1]], axis=0)
+        block = place_ref[member, place]
+        panel[block, :half] = jnp.where(lower, first, second)
+        panel[block, half:] = jnp.where(lower, second, first)
+    square = panel.shape[1:]
+    same = lax.broadcasted_iota(jnp.int32, square, 0) == lax.broadcasted_iota(jnp.int32, square, 1)
+    panel[NMP] = jnp.where(same, 1.0, 0.0)
+    blocks, count = NMP, panel.shape[1]
     groups = count // 8
 
     def inner_of(index):
@@ -150,7 +242,7 @@
             if group == first:
                 weight = jnp.where(order > place, weight, 0.0)
             weights.append(weight)
-        for block in range(blocks):
+        for block in range(blocks + 1):
             row = panel[block, index : index + 1, :]
             for group in range(first, groups):
                 if group == first and place == 7:
@@ -160,7 +252,213 @@
             panel[block, index : index + 1, :] = row * scale
     for block in range(blocks):
         split[block] = split3(panel[block])
-    tokens[...] = fold3(dot_nt(split[member], acts_ref[...]))
+    columns = gt_ref.shape[1] // LANES
+    factor = jnp.concatenate([rows_of(tokens, column, columns, FACTOR) for column in range(columns)], axis=1)
+    grads = fold3(dot_nt(split3(factor), gt_ref[...]))
+    total = None
+    for chunk in range(chunks):
+        copies[chunk].wait()
+        part = dot_nt(et_ref[chunk], wide(split, chunk, width))
+        total = part if total is None else total + part
+    turned = lax.dot_general(
+        panel[NMP][:, :count], grads, (((1,), (0,)), ((), ())), precision=lax.Precision.HIGHEST,
+        preferred_element_type=F32,
+    )
+    right[...] = turned + fold3(total.T)
+
+
+def wide(ref, count):
+    return jnp.concatenate([ref[block] for block in range(count)], axis=1)
+
+
+def lanes(array, block):
+    return array[:, block * LANES : (block + 1) * LANES]
+
+
+def add_all(values):
+    while len(values) > 1:
+        values = [a + b for a, b in zip(values[::2], values[1::2])]
+    return values[0]
+
+
+def tiles_of(value, out):
+    columns = value.shape[1] // LANES
+    for row in range(value.shape[0] // 8):
+        for column in range(columns):
+            out[row * columns + column] = lanes(value[row * 8 : row * 8 + 8], column)
+
+
+def rows_of(tiles, column, columns, rows):
+    return jnp.concatenate([tiles[row * columns + column] for row in range(rows // 8)], axis=0)
+
+
+def error_kernel(member_ref, core_ref, place_ref, q_hbm, et_hbm, keep, send, q_ref, et_ref, parts, sems):
+    count, width = et_ref.shape[0], et_ref.shape[2]
+    copies = [
+        pltpu.make_async_copy(et_hbm.at[:, chunk * width : (chunk + 1) * width], et_ref.at[chunk], sems.at[chunk])
+        for chunk in range(count)
+    ]
+    first = pltpu.make_async_copy(q_hbm, q_ref, sems.at[count])
+    first.start()
+    for copy in copies:
+        copy.start()
+    first.wait()
+    split = split3(q_ref[...])
+    blocks = width // LANES
+    half = parts.shape[1] // 2
+    for chunk in range(count):
+        copies[chunk].wait()
+        part = fold3(dot_nn(split, et_ref[chunk]))
+        for block in range(blocks):
+            parts[chunk * blocks + block] = lanes(part, block)
+    lower = core_ref[0] == 0
+    for place in range(NMP):
+        block = parts[place_ref[member_ref[0], place]]
+        keep[place] = jnp.where(lower, block[:half], block[half:])
+        send[place] = jnp.where(lower, block[half:], block[:half])
+
+
+def token_kernel(q_hbm, gt_hbm, out, q_ref, gt_ref, sems):
+    copies = [pltpu.make_async_copy(q_hbm, q_ref, sems.at[0]), pltpu.make_async_copy(gt_hbm, gt_ref, sems.at[1])]
+    for copy in copies:
+        copy.start()
+    for copy in copies:
+        copy.wait()
+    tiles_of(fold3(dot_nn(split3(q_ref[...]), gt_ref[...])), out)
+
+
+def store_blocks(value, out, start):
+    for block in range(value.shape[0]):
+        out[start + 2 * block] = value[block, :8]
+        out[start + 2 * block + 1] = value[block, 8:]
+
+
+def load_blocks(ref, start, count):
+    return jnp.stack(
+        [jnp.concatenate([ref[start + 2 * block], ref[start + 2 * block + 1]], axis=0) for block in range(count)]
+    )
+
+
+def open_kernel(tokens, mine, theirs, message, keep):
+    message[:FACTOR] = tokens[...]
+    both = mine[...] + theirs[...]
+    half = both.shape[0] // 2
+    keep[...] = both[:half]
+    store_blocks(both[half:], message, FACTOR)
+
+
+def halve_kernel(sent, kept, came, message, keep):
+    message[:FACTOR] = sent[:FACTOR] + came[:FACTOR]
+    count = kept.shape[0]
+    both = kept[...] + load_blocks(came, FACTOR, count)
+    keep[...] = both[: count // 2]
+    store_blocks(both[count // 2 :], message, FACTOR)
+
+
+def piece_kernel(core_ref, acts_ref, sent, kept, came, keep, send):
+    blocks = acts_ref.shape[0] // LANES
+    terms = []
+    for block in range(blocks):
+        factor = rows_of(sent, block, blocks, FACTOR) + rows_of(came, block, blocks, FACTOR)
+        terms.append(dot_nn(split3(factor), acts_ref[block * LANES : (block + 1) * LANES, :]))
+    while len(terms) > 1:
+        terms = [a + b for a, b in zip(terms[::2], terms[1::2])]
+    piece = fold3(terms[0])
+    half = piece.shape[0] // 2
+    lower = core_ref[0] == 0
+    keep[...] = jnp.where(lower, piece[:half], piece[half:]) + (kept[...] + load_blocks(came, FACTOR, 1))[0]
+    send[...] = jnp.where(lower, piece[half:], piece[:half])
+
+
+def start_kernel(core_ref, mine, theirs, acts_ref, message):
+    lower = core_ref[0] == 0
+    first, second = mine[...] * (1.0 / NDP), theirs[...] * (1.0 / NDP)
+    panel = jnp.concatenate([jnp.where(lower, first, second), jnp.where(lower, second, first)], axis=0)
+    tiles_of(fold3(dot_nt(split3(panel), acts_ref[...])), message)
+    store_blocks(first[None], message, FACTOR)
+
+
+def double_kernel(sent, came, message):
+    count = sent.shape[0] - FACTOR
+    message[:FACTOR] = sent[:FACTOR] + came[:FACTOR]
+    message[FACTOR : FACTOR + count] = sent[FACTOR:]
+    message[FACTOR + count :] = came[FACTOR:]
+
+
+def last_kernel(sent, came, factor, rows):
+    count = sent.shape[0] - FACTOR
+    factor[...] = sent[:FACTOR] + came[:FACTOR]
+    rows[:count] = sent[FACTOR:]
+    rows[count:] = came[FACTOR:]
+
+
+def ortho_kernel(member_ref, core_ref, place_ref, mine, theirs, tokens, gt_ref, et_hbm, split, right, panel, et_ref, sems):
+    chunks, width = et_ref.shape[0], et_ref.shape[2]
+    copies = [
+        pltpu.make_async_copy(et_hbm.at[:, chunk * width : (chunk + 1) * width], et_ref.at[chunk], sems.at[chunk])
+        for chunk in range(chunks)
+    ]
+    for copy in copies:
+        copy.start()
+    member = member_ref[0]
+    lower = core_ref[0] == 0
+    half = panel.shape[1] // 2
+    for place in range(NMP):
+        first = jnp.concatenate([mine[2 * place], mine[2 * place + 1]], axis=0)
+        second = jnp.concatenate([theirs[2 * place], theirs[2 * place + 1]], axis=0)
+        block = place_ref[member, place]
+        panel[block, :half] = jnp.where(lower, first, second)
+        panel[block, half:] = jnp.where(lower, second, first)
+    square = panel.shape[1:]
+    same = lax.broadcasted_iota(jnp.int32, square, 0) == lax.broadcasted_iota(jnp.int32, square, 1)
+    panel[NMP] = jnp.where(same, 1.0, 0.0)
+    blocks, count = NMP, panel.shape[1]
+    groups = count // 8
+
+    def inner_of(index):
+        first = index // 8
+        sums = [None] * groups
+        for block in range(blocks):
+            row = panel[block, index : index + 1, :]
+            for group in range(first, groups):
+                term = panel[block, group * 8 : group * 8 + 8, :] * row
+                sums[group] = term if sums[group] is None else sums[group] + term
+        return [None if s is None else jnp.sum(s, axis=1, keepdims=True) for s in sums]
+
+    order = lax.broadcasted_iota(jnp.int32, (8, 1), 0)
+    for index in range(count):
+        first, place = index // 8, index % 8
+        inner = inner_of(index)
+        scale = 1.0 / (jnp.sqrt(inner[first][place : place + 1, :]) + ortho_eps)
+        weights = []
+        for group in range(first, groups):
+            weight = inner[group] * (scale * scale)
+            if group == first:
+                weight = jnp.where(order > place, weight, 0.0)
+            weights.append(weight)
+        for block in range(blocks + 1):
+            row = panel[block, index : index + 1, :]
+            for group in range(first, groups):
+                if group == first and place == 7:
+                    continue
+                rows = slice(group * 8, group * 8 + 8)
+                panel[block, rows, :] = panel[block, rows, :] - weights[group - first] * row
+            panel[block, index : index + 1, :] = row * scale
+    for block in range(blocks):
+        split[block] = split3(panel[block])
+    columns = gt_ref.shape[1] // LANES
+    factor = jnp.concatenate([rows_of(tokens, column, columns, FACTOR) for column in range(columns)], axis=1)
+    grads = fold3(dot_nt(split3(factor), gt_ref[...]))
+    total = None
+    for chunk in range(chunks):
+        copies[chunk].wait()
+        part = dot_nt(et_ref[chunk], wide(split, chunk, width))
+        total = part if total is None else total + part
+    turned = lax.dot_general(
+        panel[NMP][:, :count], grads, (((1,), (0,)), ((), ())), precision=lax.Precision.HIGHEST,
+        preferred_element_type=F32,
+    )
+    right[...] = turned + fold3(total.T)
 
 
 def errors_kernel(basis_ref, et_hbm, out, et_ref, sems):
@@ -271,6 +569,7 @@
 def shards(acts, grad_out, error_buffer, q_prev, weight, moment1, moment2):
     member = lax.axis_index("mp").astype(jnp.int32).reshape(1)
     dp = lax.axis_index("dp").astype(jnp.int32).reshape(1)
+    core = dp % 2
     gt, et = grad_out.T, error_buffer.T
     rank, ff = q_prev.shape
     tokens, model = acts.shape[0], et.shape[1]
@@ -280,42 +579,57 @@
 
     gathered = lax.all_gather(acts, "mp", axis=0)
 
+    half = rank // 2
+    table = jnp.asarray(met(along, NMP))
+    blocks = array((NMP, half, LANES), F32)
+    mine, send = call(
+        error_kernel, [blocks, blocks], (member, core, table, q_prev, et), specs=[SMEM] * 3 + [HBM] * 2,
+        scratch=[
+            pltpu.VMEM((rank, ff), F32), pltpu.VMEM((chunks, ff, width), BF16), pltpu.VMEM((NMP, rank, LANES), F32),
+            pltpu.SemaphoreType.DMA((chunks + 1,)),
+        ],
+        limit=60, flops=6 * rank * ff * model, moved=2 * ff * model,
+    )
+    theirs = swap(send, "dp", ALONG_DP[0])
     factor = call(
-        token_kernel, array((rank, tokens), F32), (q_prev, gt), specs=[HBM] * 2,
+        token_kernel, array((FACTOR, 8, LANES), F32), (q_prev, gt), specs=[HBM] * 2,
         scratch=[pltpu.VMEM((rank, ff), F32), pltpu.VMEM((ff, tokens), BF16), pltpu.SemaphoreType.DMA((2,))],
-        limit=60, flops=6 * rank * ff * tokens, moved=2 * ff * tokens,
-    )
-    factor, late = lax.optimization_barrier((factor, q_prev))
-    errors = call(
-        error_kernel, array((NMP, rank, LANES), F32), (late, et), specs=[HBM] * 2,
+        limit=58, flops=6 * rank * ff * tokens, moved=2 * ff * tokens,
+    )
+    count = NMP // 2
+    message = lambda tiles: array((FACTOR + tiles, 8, LANES), F32)
+    kept = lambda count: array((count, half, LANES), F32)
+    sent, keep = call(open_kernel, [message(2 * count), kept(count)], (factor, mine, theirs), moved=MIB)
+    for level in along[:0:-1]:
+        came = swap(sent, "mp", level)
+        count //= 2
+        sent, keep = call(halve_kernel, [message(2 * count), kept(count)], (sent, keep, came), moved=MIB)
+    came = swap(sent, "mp", along[0])
+
+    piece = array((half, LANES), F32)
+    keep, send = call(
+        piece_kernel, [piece, piece], (core, acts, sent, keep, came), specs=[SMEM] + [VMEM] * 4, moved=MIB
+    )
+    keep = total(keep + swap(send, "dp", ALONG_DP[0]), "dp", ALONG_DP[1:])
+    sent = call(
+        start_kernel, message(2), (core, keep, swap(keep, "dp", ALONG_DP[0]), acts), specs=[SMEM] + [VMEM] * 3, moved=MIB
+    )
+    for place, level in enumerate(along[:-1]):
+        sent = call(double_kernel, message(4 << place), (sent, swap(sent, "mp", level)), moved=MIB)
+    factor, mine = call(
+        last_kernel, [array((FACTOR, 8, LANES), F32), array((2 * NMP, 8, LANES), F32)],
+        (sent, swap(sent, "mp", along[-1])), moved=MIB,
+    )
+    basis, right = call(
+        ortho_kernel, [array((NMP, 3 * rank, LANES), BF16), array((rank, ff), F32)],
+        (member, core, table, mine, swap(mine, "dp", ALONG_DP[0]), factor, gt, et),
+        specs=[SMEM] * 3 + [VMEM] * 4 + [HBM],
         scratch=[
-            pltpu.VMEM((rank, ff), F32), pltpu.VMEM((chunks, ff, width), BF16), pltpu.SemaphoreType.DMA((9,)),
+            pltpu.VMEM((NMP + 1, rank, LANES), F32),
+            pltpu.VMEM((chunks, ff, width), BF16),
+            pltpu.SemaphoreType.DMA((chunks,)),
         ],
-        limit=58, flops=6 * rank * ff * model, moved=2 * ff * model,
-    )
-    factor, errors = lax.optimization_barrier((total(factor, "mp", along[:1]), errors))
-    errors = lax.all_to_all(errors, "mp", 0, 0)
-    factor = total(factor, "mp", along[1:])
-
-    panel = call(piece_kernel, array((1, rank, LANES), F32), (factor, acts, errors), moved=MIB)
-    panel = total(panel, "dp", ALONG_DP)
-    for level in along[:-1]:
-        panel = jnp.concatenate([panel, swap(panel, "mp", level)])
-    basis, factor = call(
-        ortho_kernel, [array((NMP, 3 * rank, LANES), BF16), array((rank, tokens), F32)],
-        (member, jnp.asarray(met(along, NMP)), panel, swap(panel, "mp", along[-1]), acts),
-        specs=[SMEM, SMEM, VMEM, VMEM, VMEM],
-        scratch=[pltpu.VMEM((NMP, rank, LANES), F32)], flops=MIB, moved=4 * MIB,
-    )
-
-    errors = call(
-        errors_kernel, array((rank, ff), F32), (basis, et), specs=[VMEM, HBM],
-        scratch=[pltpu.VMEM((chunks, ff, width), BF16), pltpu.SemaphoreType.DMA((chunks,))],
-        limit=16, flops=6 * rank * ff * model, moved=2 * ff * model,
-    )
-    factor = total(factor, "mp", along)
-    right = call(
-        right_kernel, array((rank, ff), F32), (factor, gt, errors), flops=6 * rank * ff * tokens, moved=2 * ff * tokens
+        limit=24, flops=8 * rank * ff * model, moved=2 * ff * model,
     )
     right = total(right, "dp", ALONG_DP)
 

time: 189 us -> 168 us (0.89)
  starting transfers between devices: 56.4 us -> 39.2 us
  waiting for transfers between devices: 84.1 us -> 78.6 us
    all_to_all x1 -> x0, starting transfers between devices: 10.3 us -> none  [shards(): errors = lax.all_to_all(errors, 'mp', 0, 0)]
    ppermute x21 -> x19, starting transfers between devices: 46.1 us -> 39.2 us  [swap(): return lax.ppermute(value, axis, list(enumerate(level)))]
    ppermute x21 -> x19, waiting for transfers between devices: 83.4 us -> 77.9 us  [swap(): return lax.ppermute(value, axis, list(enumerate(level)))]
    pallas_call x7 -> x16, Pallas kernels: 30.2 us -> 31.1 us  [call(): pl.pallas_call(kernel, out_shape=outs, in_specs=specs or [VMEM] * len(arg...]
  transfers between devices with their start and end apart: 23 -> 20, of which waited for: 19 -> 18; matrix products, arithmetic and copies ran while one was open for 0% -> 0% of each run, Pallas kernels for 9% -> 10%
where the time goes in v4:
time: 168 us; the launch traced here: 167 us
  waiting for transfers between devices  78.6 us (47%)
  starting transfers between devices  39.2 us (23%)
  Pallas kernels  31.1 us (19%)
  between operations  14.2 us (8%)
  local copies, waits for them, and re-layouts  2.79 us (2%)
    ppermute x19, waiting for transfers between devices, swap(): return lax.ppermute(value, axis, list(enumerate(level)))  77.9 us
    ppermute x19, starting transfers between devices, swap(): return lax.ppermute(value, axis, list(enumerate(level)))  39.2 us
    pallas_call x16, Pallas kernels, call(): pl.pallas_call(kernel, out_shape=outs, in_specs=specs or [VMEM] * len(arg...  31.1 us
  transfers between devices with their start and end apart: 20, of which 18 were waited for; matrix products, arithmetic and copies ran while one was open for 0% of the time, Pallas kernels for 10%

profile of v4, /device:TPU:1, one launch (start us, length us, event | category | flops | bytes accessed | tf_op | source)
XLA Modules:
  0.0 166.6 jit_solution(12808211335646808611)
XLA Ops:
  7.9 4.7 %shard_map.120 = (f32[32,16,128]{2,1,0:T(8,128)}, f32[32,16,128]{2,1,0:T(8,128)}) custom-call(s32[1]{0:T(128)} %bitcast.1.member_ref, s32[1]{0:T(128)S(6)} %select_n.7.core_ref, s32[32,32]{1,0:T(8,128)} %constant.30.clone.place_ref, f32[32,448]{1,0:T(8,128)} %q_hbm.3, bf16[448,4096]{1,0:T(8,128)(2,1)} %bitcast.12), custom_call_target="tpu_custom_call" | custom-call | flops 352321536 | bytes 3670016 | tf_op jit(solution)/shard_map/pallas_call | solution.py:548
  12.7 3.3 %collective-permute-start = (f32[32,16,128]{2,1,0:T(8,128)}, f32[32,16,128]{2,1,0:T(8,128)S(1)}, u32[]{:S(2)}, u32[]{:S(2)}) collective-permute-start(f32[32,16,128]{2,1,0:T(8,128)} %get-tuple-element.29), channel_id=1, source_target_pairs={{0,32},{32,0},{64,96},{96,64},{128,160},{160,128},{192,224},{224,1... | collective-permute-start | bytes 786440 | tf_op jit(solution)/shard_map/ppermute | solution.py:560
  16.0 2.2 %shard_map.119.tokens = f32[32,8,128]{2,1,0:T(8,128)} custom-call(f32[32,448]{1,0:T(8,128)} %q_hbm.3, bf16[448,1024]{1,0:T(8,128)(2,1)} %bitcast.15), custom_call_target="tpu_custom_call" | custom-call | flops 88080384 | bytes 917504 | tf_op jit(solution)/shard_map/pallas_call | solution.py:548
  21.3 7.8 %collective-permute-done.1.came = f32[64,8,128]{2,1,0:T(8,128)S(1)} collective-permute-done((f32[64,8,128]{2,1,0:T(8,128)S(1)}, f32[64,8,128]{2,1,0:T(8,128)S(1)}, u32[]{:S(2)}, u32[]{:S(2)}) %collective-permute-start.1) | collective-permute-done | bytes 262176 | tf_op jit(solution)/shard_map/ppermute | solution.py:560
  29.3 6.3 %collective-permute-done.2.came = f32[48,8,128]{2,1,0:T(8,128)S(1)} collective-permute-done((f32[48,8,128]{2,1,0:T(8,128)S(1)}, f32[48,8,128]{2,1,0:T(8,128)S(1)}, u32[]{:S(2)}, u32[]{:S(2)}) %collective-permute-start.2) | collective-permute-done | bytes 196640 | tf_op jit(solution)/shard_map/ppermute | solution.py:560
  35.7 4.7 %collective-permute-start.3 = (f32[40,8,128]{2,1,0:T(8,128)S(1)}, f32[40,8,128]{2,1,0:T(8,128)S(1)}, u32[]{:S(2)}, u32[]{:S(2)}) collective-permute-start(f32[40,8,128]{2,1,0:T(8,128)S(1)} %get-tuple-element.34.sent), channel_id=1, source_target_pairs={{0,3},{1,6},{2,5},{3,0},{4,7},{5,2},{6,1},{7,4},{8,11},{9,14},{10,... | collective-permute-start | bytes 491528 | tf_op jit(solution)/shard_map/ppermute | solution.py:560
  40.3 9.5 %collective-permute-done.3.came = f32[40,8,128]{2,1,0:T(8,128)S(1)} collective-permute-done((f32[40,8,128]{2,1,0:T(8,128)S(1)}, f32[40,8,128]{2,1,0:T(8,128)S(1)}, u32[]{:S(2)}, u32[]{:S(2)}) %collective-permute-start.3) | collective-permute-done | bytes 163872 | tf_op jit(solution)/shard_map/ppermute | solution.py:560
  49.8 4.1 %collective-permute-start.4 = (f32[36,8,128]{2,1,0:T(8,128)S(1)}, f32[36,8,128]{2,1,0:T(8,128)S(1)}, u32[]{:S(2)}, u32[]{:S(2)}) collective-permute-start(f32[36,8,128]{2,1,0:T(8,128)S(1)} %get-tuple-element.36.sent), channel_id=1, source_target_pairs={{0,7},{1,2},{2,1},{3,4},{4,3},{5,6},{6,5},{7,0},{8,15},{9,10},{10,... | collective-permute-start | bytes 442376 | tf_op jit(solution)/shard_map/ppermute | solution.py:560
  53.9 2.9 %collective-permute-done.4.came = f32[36,8,128]{2,1,0:T(8,128)S(1)} collective-permute-done((f32[36,8,128]{2,1,0:T(8,128)S(1)}, f32[36,8,128]{2,1,0:T(8,128)S(1)}, u32[]{:S(2)}, u32[]{:S(2)}) %collective-permute-start.4) | collective-permute-done | bytes 147488 | tf_op jit(solution)/shard_map/ppermute | solution.py:560
  57.0 3.8 %collective-permute-done.5.came = f32[34,8,128]{2,1,0:T(8,128)S(1)} collective-permute-done((f32[34,8,128]{2,1,0:T(8,128)S(1)}, f32[34,8,128]{2,1,0:T(8,128)S(1)}, u32[]{:S(2)}, u32[]{:S(2)}) %collective-permute-start.5) | collective-permute-done | bytes 139296 | tf_op jit(solution)/shard_map/ppermute | solution.py:560
  61.1 5.1 %collective-permute-start.6 = (f32[16,128]{1,0:T(8,128)S(1)}, f32[16,128]{1,0:T(8,128)S(1)}, u32[]{:S(2)}, u32[]{:S(2)}) collective-permute-start(f32[16,128]{1,0:T(8,128)S(1)} %get-tuple-element.41), channel_id=1, source_target_pairs={{0,32},{32,0},{64,96},{96,64},{128,160},{160,128},{192,224},{224,1... | collective-permute-start | bytes 24584 | tf_op jit(solution)/shard_map/ppermute | solution.py:560
  71.7 2.3 %collective-permute-done.8 = f32[16,128]{1,0:T(8,128)S(1)} collective-permute-done((f32[16,128]{1,0:T(8,128)S(1)}, f32[16,128]{1,0:T(8,128)S(1)}, u32[]{:S(2)}, u32[]{:S(2)}) %collective-permute-start.8) | collective-permute-done | bytes 8224 | tf_op jit(solution)/shard_map/ppermute | solution.py:560
  77.9 6.5 %collective-permute-done.10.came = f32[34,8,128]{2,1,0:T(8,128)S(1)} collective-permute-done((f32[34,8,128]{2,1,0:T(8,128)S(1)}, f32[34,8,128]{2,1,0:T(8,128)S(1)}, u32[]{:S(2)}, u32[]{:S(2)}) %collective-permute-start.10) | collective-permute-done | bytes 139296 | tf_op jit(solution)/shard_map/ppermute | solution.py:560
  84.5 2.8 %collective-permute-start.11 = (f32[36,8,128]{2,1,0:T(8,128)S(1)}, f32[36,8,128]{2,1,0:T(8,128)S(1)}, u32[]{:S(2)}, u32[]{:S(2)}) collective-permute-start(f32[36,8,128]{2,1,0:T(8,128)S(1)} %shard_map.128.sent), channel_id=1, source_target_pairs={{0,7},{1,2},{2,1},{3,4},{4,3},{5,6},{6,5},{7,0},{8,15},{9,10},{10,... | collective-permute-start | bytes 442376 | tf_op jit(solution)/shard_map/ppermute | solution.py:560
  87.2 7.1 %collective-permute-done.11.came = f32[36,8,128]{2,1,0:T(8,128)S(1)} collective-permute-done((f32[36,8,128]{2,1,0:T(8,128)S(1)}, f32[36,8,128]{2,1,0:T(8,128)S(1)}, u32[]{:S(2)}, u32[]{:S(2)}) %collective-permute-start.11) | collective-permute-done | bytes 147488 | tf_op jit(solution)/shard_map/ppermute | solution.py:560
  96.2 12.5 %collective-permute-done.12.came = f32[40,8,128]{2,1,0:T(8,128)S(1)} collective-permute-done((f32[40,8,128]{2,1,0:T(8,128)S(1)}, f32[40,8,128]{2,1,0:T(8,128)S(1)}, u32[]{:S(2)}, u32[]{:S(2)}) %collective-permute-start.12) | collective-permute-done | bytes 163872 | tf_op jit(solution)/shard_map/ppermute | solution.py:560
  109.5 4.2 %collective-permute-done.13.came = f32[48,8,128]{2,1,0:T(8,128)S(1)} collective-permute-done((f32[48,8,128]{2,1,0:T(8,128)S(1)}, f32[48,8,128]{2,1,0:T(8,128)S(1)}, u32[]{:S(2)}, u32[]{:S(2)}) %collective-permute-start.13) | collective-permute-done | bytes 196640 | tf_op jit(solution)/shard_map/ppermute | solution.py:560
  113.8 2.0 %collective-permute-start.14 = (f32[64,8,128]{2,1,0:T(8,128)S(1)}, f32[64,8,128]{2,1,0:T(8,128)S(1)}, u32[]{:S(2)}, u32[]{:S(2)}) collective-permute-start(f32[64,8,128]{2,1,0:T(8,128)S(1)} %shard_map.131.sent), channel_id=1, source_target_pairs={{0,24},{1,25},{2,26},{3,27},{4,28},{5,29},{6,30},{7,31},{8,16},{9,... | collective-permute-start | bytes 786440 | tf_op jit(solution)/shard_map/ppermute | solution.py:560
  115.8 4.5 %collective-permute-done.14.came = f32[64,8,128]{2,1,0:T(8,128)S(1)} collective-permute-done((f32[64,8,128]{2,1,0:T(8,128)S(1)}, f32[64,8,128]{2,1,0:T(8,128)S(1)}, u32[]{:S(2)}, u32[]{:S(2)}) %collective-permute-start.14) | collective-permute-done | bytes 262176 | tf_op jit(solution)/shard_map/ppermute | solution.py:560
  120.3 4.1 %collective-permute-start.15 = (f32[64,8,128]{2,1,0:T(8,128)S(1)}, f32[64,8,128]{2,1,0:T(8,128)S(1)}, u32[]{:S(2)}, u32[]{:S(2)}) collective-permute-start(f32[64,8,128]{2,1,0:T(8,128)S(1)} %get-tuple-element.42.mine), channel_id=1, source_target_pairs={{0,32},{32,0},{64,96},{96,64},{128,160},{160,128},{192,224},{224,1... | collective-permute-start | bytes 786440 | tf_op jit(solution)/shard_map/ppermute | solution.py:560
  125.6 9.4 %shard_map.133 = (bf16[32,96,128]{2,1,0:T(8,128)(2,1)S(1)}, f32[32,448]{1,0:T(8,128)S(1)}) custom-call(s32[1]{0:T(128)} %bitcast.1.member_ref, s32[1]{0:T(128)S(6)} %select_n.7.core_ref, s32[32,32]{1,0:T(8,128)S(1)} %copy-done.6, f32[64,8,128]{2,1,0:T(8,128)S(1)} %get-tuple-element.42.mine, f32[64,8,128]{2,1,0:T(8,128)S(1)} %collective-permute-done.15.theirs, ...), custom_call_target="tpu_custom_call" | custom-call | flops 469762048 | bytes 3670016 | tf_op jit(solution)/shard_map/pallas_call | solution.py:548
  137.5 2.9 %collective-permute-done.17 = f32[32,448]{1,0:T(8,128)S(1)} collective-permute-done((f32[32,448]{1,0:T(8,128)S(1)}, f32[32,448]{1,0:T(8,128)S(1)}, u32[]{:S(2)}, u32[]{:S(2)}) %collective-permute-start.17) | collective-permute-done | bytes 57376 | tf_op jit(solution)/shard_map/ppermute | solution.py:560
  140.4 2.8 %collective-permute-start.18 = (f32[32,448]{1,0:T(8,128)S(1)}, f32[32,448]{1,0:T(8,128)S(1)}, u32[]{:S(2)}, u32[]{:S(2)}) collective-permute-start(f32[32,448]{1,0:T(8,128)S(1)} %add.29), channel_id=1, source_target_pairs={{0,192},{32,224},{64,128},{96,160},{128,64},{160,96},{192,0},{224,... | collective-permute-start | bytes 172040 | tf_op jit(solution)/shard_map/ppermute | solution.py:560
  145.6 14.2 %shard_map.134 = (f32[448,512]{1,0:T(8,128)}, f32[448,512]{1,0:T(8,128)}, f32[448,512]{1,0:T(8,128)}, bf16[448,4096]{1,0:T(8,128)(2,1)}, f32[32,448]{1,0:T(8,128)}) custom-call(s32[1]{0:T(128)} %bitcast.dp_ref, f32[32,448]{1,0:T(8,128)} %add.30.sum_ref, bf16[32,96,128]{2,1,0:T(8,128)(2,1)} %copy-done.3, bf16[32,1024,128]{2,1,0:T(8,128)(2,1)} %bitcast.18, ...), custom_call_target="tpu_custom_call" | custom-call | flops 4462739456 | bytes 23068672 | tf_op jit(solution)/shard_map/pallas_call | solution.py:548
  (53 shorter events, 22.6 us)
Async XLA Ops:
  7.2 138.4 %all-gather.3.cloned.1.call-start = ((), (), s32[]{:S(2)}) async-start(), calls=%async_computation | async-start | bytes 8650752 | tf_op jit(solution)/shard_map/all_gather | solution.py:580
  7.9 52.9 %copy-start.2 = (bf16[1024,128]{1,0:T(8,128)(2,1)S(1)}, bf16[1024,128]{1,0:T(8,128)(2,1)}, u32[]{:S(2)}) copy-start(bf16[1024,128]{1,0:T(8,128)(2,1)} %acts_ref.3) | copy-start | bytes 786436
  7.9 117.6 %copy-start.6 = (s32[32,32]{1,0:T(8,128)S(1)}, s32[32,32]{1,0:T(8,128)}, u32[]{:S(2)}) copy-start(s32[32,32]{1,0:T(8,128)} %constant.30.clone.place_ref) | copy-start | bytes 12292
  12.7 112.9 %copy-start = (bf16[4096,448]{0,1:T(8,128)(2,1)S(1)}, bf16[4096,448]{0,1:T(8,128)(2,1)}, u32[]{:S(2)}) copy-start(bf16[4096,448]{0,1:T(8,128)(2,1)} %param.10) | copy-start | bytes 11010052
  12.7 112.9 %copy-start.1 = (bf16[1024,448]{0,1:T(8,128)(2,1)S(1)}, bf16[1024,448]{0,1:T(8,128)(2,1)}, u32[]{:S(2)}) copy-start(bf16[1024,448]{0,1:T(8,128)(2,1)} %param.9) | copy-start | bytes 2752516
  12.7 5.5 %collective-permute-start = (f32[32,16,128]{2,1,0:T(8,128)}, f32[32,16,128]{2,1,0:T(8,128)S(1)}, u32[]{:S(2)}, u32[]{:S(2)}) collective-permute-start(f32[32,16,128]{2,1,0:T(8,128)} %get-tuple-element.29), channel_id=1, source_target_pairs={{0,32},{32,0},{64,96},{96,64},{128,160},{160,128},{192,224},{224,1... | collective-permute-start | bytes 786440 | tf_op jit(solution)/shard_map/ppermute | solution.py:560
  20.1 9.1 %collective-permute-start.1 = (f32[64,8,128]{2,1,0:T(8,128)S(1)}, f32[64,8,128]{2,1,0:T(8,128)S(1)}, u32[]{:S(2)}, u32[]{:S(2)}) collective-permute-start(f32[64,8,128]{2,1,0:T(8,128)S(1)} %get-tuple-element.30.sent), channel_id=1, source_target_pairs={{0,24},{1,25},{2,26},{3,27},{4,28},{5,29},{6,30},{7,31},{8,16},{9,... | collective-permute-start | bytes 786440 | tf_op jit(solution)/shard_map/ppermute | solution.py:560
  29.2 6.4 %collective-permute-start.2 = (f32[48,8,128]{2,1,0:T(8,128)S(1)}, f32[48,8,128]{2,1,0:T(8,128)S(1)}, u32[]{:S(2)}, u32[]{:S(2)}) collective-permute-start(f32[48,8,128]{2,1,0:T(8,128)S(1)} %get-tuple-element.32.sent), channel_id=1, source_target_pairs={{0,8},{1,9},{2,10},{3,11},{4,12},{5,13},{6,14},{7,15},{8,0},{9,1},... | collective-permute-start | bytes 589832 | tf_op jit(solution)/shard_map/ppermute | solution.py:560
  35.7 14.2 %collective-permute-start.3 = (f32[40,8,128]{2,1,0:T(8,128)S(1)}, f32[40,8,128]{2,1,0:T(8,128)S(1)}, u32[]{:S(2)}, u32[]{:S(2)}) collective-permute-start(f32[40,8,128]{2,1,0:T(8,128)S(1)} %get-tuple-element.34.sent), channel_id=1, source_target_pairs={{0,3},{1,6},{2,5},{3,0},{4,7},{5,2},{6,1},{7,4},{8,11},{9,14},{10,... | collective-permute-start | bytes 491528 | tf_op jit(solution)/shard_map/ppermute | solution.py:560
  49.8 7.0 %collective-permute-start.4 = (f32[36,8,128]{2,1,0:T(8,128)S(1)}, f32[36,8,128]{2,1,0:T(8,128)S(1)}, u32[]{:S(2)}, u32[]{:S(2)}) collective-permute-start(f32[36,8,128]{2,1,0:T(8,128)S(1)} %get-tuple-element.36.sent), channel_id=1, source_target_pairs={{0,7},{1,2},{2,1},{3,4},{4,3},{5,6},{6,5},{7,0},{8,15},{9,10},{10,... | collective-permute-start | bytes 442376 | tf_op jit(solution)/shard_map/ppermute | solution.py:560
  56.9 4.0 %collective-permute-start.5 = (f32[34,8,128]{2,1,0:T(8,128)S(1)}, f32[34,8,128]{2,1,0:T(8,128)S(1)}, u32[]{:S(2)}, u32[]{:S(2)}) collective-permute-start(f32[34,8,128]{2,1,0:T(8,128)S(1)} %get-tuple-element.38.sent), channel_id=1, source_target_pairs={{0,1},{1,0},{2,3},{3,2},{4,5},{5,4},{6,7},{7,6},{8,9},{9,8},{10,11... | collective-permute-start | bytes 417800 | tf_op jit(solution)/shard_map/ppermute | solution.py:560
  61.1 5.9 %collective-permute-start.6 = (f32[16,128]{1,0:T(8,128)S(1)}, f32[16,128]{1,0:T(8,128)S(1)}, u32[]{:S(2)}, u32[]{:S(2)}) collective-permute-start(f32[16,128]{1,0:T(8,128)S(1)} %get-tuple-element.41), channel_id=1, source_target_pairs={{0,32},{32,0},{64,96},{96,64},{128,160},{160,128},{192,224},{224,1... | collective-permute-start | bytes 24584 | tf_op jit(solution)/shard_map/ppermute | solution.py:560
  67.0 2.9 %collective-permute-start.7 = (f32[16,128]{1,0:T(8,128)S(1)}, f32[16,128]{1,0:T(8,128)S(1)}, u32[]{:S(2)}, u32[]{:S(2)}) collective-permute-start(f32[16,128]{1,0:T(8,128)S(1)} %add.25), channel_id=1, source_target_pairs={{0,64},{32,96},{64,0},{96,32},{128,192},{160,224},{192,128},{224,1... | collective-permute-start | bytes 24584 | tf_op jit(solution)/shard_map/ppermute | solution.py:560
  69.9 4.1 %collective-permute-start.8 = (f32[16,128]{1,0:T(8,128)S(1)}, f32[16,128]{1,0:T(8,128)S(1)}, u32[]{:S(2)}, u32[]{:S(2)}) collective-permute-start(f32[16,128]{1,0:T(8,128)S(1)} %add.26), channel_id=1, source_target_pairs={{0,192},{32,224},{64,128},{96,160},{128,64},{160,96},{192,0},{224,... | collective-permute-start | bytes 24584 | tf_op jit(solution)/shard_map/ppermute | solution.py:560
  74.0 2.7 %collective-permute-start.9 = (f32[16,128]{1,0:T(8,128)S(1)}, f32[16,128]{1,0:T(8,128)S(1)}, u32[]{:S(2)}, u32[]{:S(2)}) collective-permute-start(f32[16,128]{1,0:T(8,128)S(1)} %add.27.mine), channel_id=1, source_target_pairs={{0,32},{32,0},{64,96},{96,64},{128,160},{160,128},{192,224},{224,1... | collective-permute-start | bytes 24584 | tf_op jit(solution)/shard_map/ppermute | solution.py:560
  76.9 7.6 %collective-permute-start.10 = (f32[34,8,128]{2,1,0:T(8,128)S(1)}, f32[34,8,128]{2,1,0:T(8,128)S(1)}, u32[]{:S(2)}, u32[]{:S(2)}) collective-permute-start(f32[34,8,128]{2,1,0:T(8,128)S(1)} %shard_map.127.sent), channel_id=1, source_target_pairs={{0,1},{1,0},{2,3},{3,2},{4,5},{5,4},{6,7},{7,6},{8,9},{9,8},{10,11... | collective-permute-start | bytes 417800 | tf_op jit(solution)/shard_map/ppermute | solution.py:560
  84.5 9.9 %collective-permute-start.11 = (f32[36,8,128]{2,1,0:T(8,128)S(1)}, f32[36,8,128]{2,1,0:T(8,128)S(1)}, u32[]{:S(2)}, u32[]{:S(2)}) collective-permute-start(f32[36,8,128]{2,1,0:T(8,128)S(1)} %shard_map.128.sent), channel_id=1, source_target_pairs={{0,7},{1,2},{2,1},{3,4},{4,3},{5,6},{6,5},{7,0},{8,15},{9,10},{10,... | collective-permute-start | bytes 442376 | tf_op jit(solution)/shard_map/ppermute | solution.py:560
  94.4 14.3 %collective-permute-start.12 = (f32[40,8,128]{2,1,0:T(8,128)S(1)}, f32[40,8,128]{2,1,0:T(8,128)S(1)}, u32[]{:S(2)}, u32[]{:S(2)}) collective-permute-start(f32[40,8,128]{2,1,0:T(8,128)S(1)} %shard_map.129.sent), channel_id=1, source_target_pairs={{0,3},{1,6},{2,5},{3,0},{4,7},{5,2},{6,1},{7,4},{8,11},{9,14},{10,... | collective-permute-start | bytes 491528 | tf_op jit(solution)/shard_map/ppermute | solution.py:560
  108.7 5.0 %collective-permute-start.13 = (f32[48,8,128]{2,1,0:T(8,128)S(1)}, f32[48,8,128]{2,1,0:T(8,128)S(1)}, u32[]{:S(2)}, u32[]{:S(2)}) collective-permute-start(f32[48,8,128]{2,1,0:T(8,128)S(1)} %shard_map.130.sent), channel_id=1, source_target_pairs={{0,8},{1,9},{2,10},{3,11},{4,12},{5,13},{6,14},{7,15},{8,0},{9,1},... | collective-permute-start | bytes 589832 | tf_op jit(solution)/shard_map/ppermute | solution.py:560
  113.8 6.5 %collective-permute-start.14 = (f32[64,8,128]{2,1,0:T(8,128)S(1)}, f32[64,8,128]{2,1,0:T(8,128)S(1)}, u32[]{:S(2)}, u32[]{:S(2)}) collective-permute-start(f32[64,8,128]{2,1,0:T(8,128)S(1)} %shard_map.131.sent), channel_id=1, source_target_pairs={{0,24},{1,25},{2,26},{3,27},{4,28},{5,29},{6,30},{7,31},{8,16},{9,... | collective-permute-start | bytes 786440 | tf_op jit(solution)/shard_map/ppermute | solution.py:560
  120.3 5.2 %collective-permute-start.15 = (f32[64,8,128]{2,1,0:T(8,128)S(1)}, f32[64,8,128]{2,1,0:T(8,128)S(1)}, u32[]{:S(2)}, u32[]{:S(2)}) collective-permute-start(f32[64,8,128]{2,1,0:T(8,128)S(1)} %get-tuple-element.42.mine), channel_id=1, source_target_pairs={{0,32},{32,0},{64,96},{96,64},{128,160},{160,128},{192,224},{224,1... | collective-permute-start | bytes 786440 | tf_op jit(solution)/shard_map/ppermute | solution.py:560
  135.9 1.3 collective-permute-start.16
  137.2 3.2 %collective-permute-start.17 = (f32[32,448]{1,0:T(8,128)S(1)}, f32[32,448]{1,0:T(8,128)S(1)}, u32[]{:S(2)}, u32[]{:S(2)}) collective-permute-start(f32[32,448]{1,0:T(8,128)S(1)} %add.28), channel_id=1, source_target_pairs={{0,64},{32,96},{64,0},{96,32},{128,192},{160,224},{192,128},{224,1... | collective-permute-start | bytes 172040 | tf_op jit(solution)/shard_map/ppermute | solution.py:560
  140.4 4.5 %collective-permute-start.18 = (f32[32,448]{1,0:T(8,128)S(1)}, f32[32,448]{1,0:T(8,128)S(1)}, u32[]{:S(2)}, u32[]{:S(2)}) collective-permute-start(f32[32,448]{1,0:T(8,128)S(1)} %add.29), channel_id=1, source_target_pairs={{0,192},{32,224},{64,128},{96,160},{128,64},{160,96},{192,0},{224,... | collective-permute-start | bytes 172040 | tf_op jit(solution)/shard_map/ppermute | solution.py:560
  (3 other events, 2.8 us)
Sparse Core Ops, SparseCore 0:
  10.6 110.1 all-gather.2

commit v5 on v3

v5 whole, which is shorter than its diff:
```python
import functools

import jax
import jax.numpy as jnp
import numpy as np
from jax import lax
from jax.experimental import pallas as pl
from jax.experimental.pallas import tpu as pltpu
from jax.sharding import PartitionSpec as P

ortho_eps = 1e-08
adam_eps = 1e-08
beta_one = 0.9
beta_two = 0.95
learn_rate = 0.01
corr_one = 1.0 - 0.9**10
corr_two = 1.0 - 0.95**10

NX, NZ, NDP = 4, 8, 8
NMP = NX * NZ
FACTOR = 32
LANES = 128
F32, BF16 = jnp.float32, jnp.bfloat16
MIB = 1 << 20
SMEM = pl.BlockSpec(memory_space=pltpu.SMEM)
VMEM = pl.BlockSpec(memory_space=pltpu.VMEM)
HBM = pl.BlockSpec(memory_space=pltpu.HBM)

RING4 = ([1, 0, 3, 2], [3, 2, 1, 0])
RING8 = ([3, 6, 5, 0, 7, 2, 1, 4], [7, 2, 1, 4, 3, 6, 5, 0], [1, 0, 3, 2, 5, 4, 7, 6])
ALONG_Z = [[x * NZ + to for x in range(NX) for to in level] for level in RING8]
ALONG_X = [[to * NZ + z for to in level for z in range(NZ)] for level in RING4]
ALONG_DP = [[1, 0, 3, 2, 5, 4, 7, 6]] + [[to * 2 + core for to in level for core in range(2)] for level in RING4]


def met(levels, members):
    held = [[member] for member in range(members)]
    for level in levels:
        held = [held[member] + held[level[member]] for member in range(members)]
    return np.array(held, np.int32)


def split3(value):
    hi = value.astype(BF16)
    rest = value - hi.astype(F32)
    mid = rest.astype(BF16)
    lo = (rest - mid.astype(F32)).astype(BF16)
    return jnp.concatenate([hi, mid, lo], axis=0)


def fold3(stacked):
    rows = stacked.shape[0] // 3
    return stacked[:rows] + (stacked[rows : 2 * rows] + stacked[2 * rows :])


def dot_nn(a, b):
    return lax.dot_general(a, b, (((1,), (0,)), ((), ())), preferred_element_type=F32)


def dot_nt(a, b):
    return lax.dot_general(a, b, (((1,), (1,)), ((), ())), preferred_element_type=F32)


def dot_tn(a, b):
    return lax.dot_general(a, b, (((0,), (0,)), ((), ())), preferred_element_type=F32)


def add_all(values):
    while len(values) > 1:
        values = [a + b for a, b in zip(values[::2], values[1::2])] + values[len(values) // 2 * 2 :]
    return values[0]


def lanes(array, block):
    return array[:, block * LANES : (block + 1) * LANES]


def tiles_of(value, out):
    columns = value.shape[1] // LANES
    for row in range(value.shape[0] // 8):
        for column in range(columns):
            out[row * columns + column] = lanes(value[row * 8 : row * 8 + 8], column)


def rows_of(tiles, column, columns, rows):
    return jnp.concatenate([tiles[row * columns + column] for row in range(rows // 8)], axis=0)


def error_kernel(member_ref, core_ref, place_ref, q_hbm, et_hbm, keep, send, q_ref, et_ref, parts, sems):
    count, width = et_ref.shape[0], et_ref.shape[2]
    copies = [
        pltpu.make_async_copy(et_hbm.at[:, chunk * width : (chunk + 1) * width], et_ref.at[chunk], sems.at[chunk])
        for chunk in range(count)
    ]
    first = pltpu.make_async_copy(q_hbm, q_ref, sems.at[count])
    first.start()
    for copy in copies:
        copy.start()
    first.wait()
    split = split3(q_ref[...])
    blocks = width // LANES
    half = parts.shape[1] // 2
    for chunk in range(count):
        copies[chunk].wait()
        part = fold3(dot_nn(split, et_ref[chunk]))
        for block in range(blocks):
            parts[chunk * blocks + block] = lanes(part, block)
    lower = core_ref[0] == 0
    for place in range(NMP):
        block = parts[place_ref[member_ref[0], place]]
        keep[place] = jnp.where(lower, block[:half], block[half:])
        send[place] = jnp.where(lower, block[half:], block[:half])


def token_kernel(q_hbm, gt_hbm, out, q_ref, gt_ref, sems):
    copies = [pltpu.make_async_copy(q_hbm, q_ref, sems.at[0]), pltpu.make_async_copy(gt_hbm, gt_ref, sems.at[1])]
    for copy in copies:
        copy.start()
    for copy in copies:
        copy.wait()
    tiles_of(fold3(dot_nn(split3(q_ref[...]), gt_ref[...])), out)


def store_blocks(value, out, start):
    for block in range(value.shape[0]):
        out[start + 2 * block] = value[block, :8]
        out[start + 2 * block + 1] = value[block, 8:]


def load_blocks(ref, start, count):
    return jnp.stack(
        [jnp.concatenate([ref[start + 2 * block], ref[start + 2 * block + 1]], axis=0) for block in range(count)]
    )


def open_kernel(tokens, mine, theirs, message, keep):
    message[:FACTOR] = tokens[...]
    both = mine[...] + theirs[...]
    half = both.shape[0] // 2
    keep[...] = both[:half]
    store_blocks(both[half:], message, FACTOR)


def halve_kernel(sent, kept, came, message, keep):
    message[:FACTOR] = sent[:FACTOR] + came[:FACTOR]
    count = kept.shape[0]
    both = kept[...] + load_blocks(came, FACTOR, count)
    keep[...] = both[: count // 2]
    store_blocks(both[count // 2 :], message, FACTOR)


def piece_kernel(core_ref, sent, kept, came, *refs):
    acts_refs, keep, send = refs[:NX], refs[NX], refs[NX + 1]
    blocks = acts_refs[0].shape[0] // LANES
    half = keep.shape[1]
    lower = core_ref[0] == 0
    errors = kept[...] + load_blocks(came, FACTOR, NX)
    factors = []
    for block in range(blocks):
        factors.append(split3(rows_of(sent, block, blocks, FACTOR) + rows_of(came, block, blocks, FACTOR)))
    factor = jnp.concatenate(factors, axis=1)
    for place in range(NX):
        piece = fold3(dot_nn(factor, acts_refs[place][...]))
        keep[place] = jnp.where(lower, piece[:half], piece[half:]) + errors[place]
        send[place] = jnp.where(lower, piece[half:], piece[:half])


def start_kernel(core_ref, mine, theirs, *refs):
    acts_refs, message = refs[:NX], refs[NX]
    lower = core_ref[0] == 0
    total = None
    for place in range(NX):
        first, second = mine[place] * (1.0 / NDP), theirs[place] * (1.0 / NDP)
        panel = jnp.concatenate([jnp.where(lower, first, second), jnp.where(lower, second, first)], axis=0)
        part = dot_nt(split3(panel), acts_refs[place][...])
        total = part if total is None else total + part
    tiles_of(fold3(total), message)
    store_blocks(mine[...] * (1.0 / NDP), message, FACTOR)


def double_kernel(sent, came, message):
    count = sent.shape[0] - FACTOR
    message[:FACTOR] = sent[:FACTOR] + came[:FACTOR]
    message[FACTOR : FACTOR + count] = sent[FACTOR:]
    message[FACTOR + count :] = came[FACTOR:]


def last_kernel(sent, came, factor, rows):
    count = sent.shape[0] - FACTOR
    factor[...] = sent[:FACTOR] + came[:FACTOR]
    rows[:count] = sent[FACTOR:]
    rows[count:] = came[FACTOR:]


def ortho_kernel(member_ref, core_ref, place_ref, mine, theirs, tokens, gt_ref, et_hbm, split, right, panel, et_ref, sems):
    chunks, width = et_ref.shape[0], et_ref.shape[2]
    copies = [
        pltpu.make_async_copy(et_hbm.at[:, chunk * width : (chunk + 1) * width], et_ref.at[chunk], sems.at[chunk])
        for chunk in range(chunks)
    ]
    for copy in copies:
        copy.start()
    member = member_ref[0]
    lower = core_ref[0] == 0
    half = panel.shape[1] // 2
    for place in range(NMP):
        first = jnp.concatenate([mine[2 * place], mine[2 * place + 1]], axis=0)
        second = jnp.concatenate([theirs[2 * place], theirs[2 * place + 1]], axis=0)
        block = place_ref[member, place]
        panel[block, :half] = jnp.where(lower, first, second)
        panel[block, half:] = jnp.where(lower, second, first)
    square = panel.shape[1:]
    same = lax.broadcasted_iota(jnp.int32, square, 0) == lax.broadcasted_iota(jnp.int32, square, 1)
    panel[NMP] = jnp.where(same, 1.0, 0.0)
    blocks, count = NMP, panel.shape[1]
    groups = count // 8

    def inner_of(index):
        first = index // 8
        sums = [None] * groups
        for block in range(blocks):
            row = panel[block, index : index + 1, :]
            for group in range(first, groups):
                term = panel[block, group * 8 : group * 8 + 8, :] * row
                sums[group] = term if sums[group] is None else sums[group] + term
        return [None if s is None else jnp.sum(s, axis=1, keepdims=True) for s in sums]

    order = lax.broadcasted_iota(jnp.int32, (8, 1), 0)
    for index in range(count):
        first, place = index // 8, index % 8
        inner = inner_of(index)
        scale = 1.0 / (jnp.sqrt(inner[first][place : place + 1, :]) + ortho_eps)
        weights = []
        for group in range(first, groups):
            weight = inner[group] * (scale * scale)
            if group == first:
                weight = jnp.where(order > place, weight, 0.0)
            weights.append(weight)
        for block in range(blocks + 1):
            row = panel[block, index : index + 1, :]
            for group in range(first, groups):
                if group == first and place == 7:
                    continue
                rows = slice(group * 8, group * 8 + 8)
                panel[block, rows, :] = panel[block, rows, :] - weights[group - first] * row
            panel[block, index : index + 1, :] = row * scale
    for block in range(blocks):
        split[block] = split3(panel[block])
    columns = gt_ref.shape[1] // LANES
    factor = jnp.concatenate([rows_of(tokens, column, columns, FACTOR) for column in range(columns)], axis=1)
    grads = fold3(dot_nt(split3(factor), gt_ref[...]))
    total = None
    for chunk in range(chunks):
        copies[chunk].wait()
        part = dot_nt(et_ref[chunk], wide(split, chunk, width))
        total = part if total is None else total + part
    turned = lax.dot_general(
        panel[NMP][:, :count], grads, (((1,), (0,)), ((), ())), precision=lax.Precision.HIGHEST,
        preferred_element_type=F32,
    )
    right[...] = turned + fold3(total.T)


def wide(ref, chunk, width):
    count = width // LANES
    return jnp.concatenate([ref[chunk * count + block] for block in range(count)], axis=1)


def field_kernel(start, acts_hbm, et_hbm, gt_hbm, field, acts_v, error_v, gt_v, acts_sems, error_sems, gt_sem):
    chunks, width = error_v.shape[0], error_v.shape[2]
    count = width // LANES
    gt_copy = pltpu.make_async_copy(gt_hbm, gt_v, gt_sem)
    gt_copy.start()
    for chunk in range(chunks):
        blocks = pl.ds(start + chunk * count, count)
        columns = pl.ds(start * LANES + chunk * width, width)
        place = pl.ds(chunk * count, count)
        pltpu.make_async_copy(acts_hbm.at[blocks], acts_v.at[place], acts_sems.at[chunk]).start()
        pltpu.make_async_copy(et_hbm.at[:, columns], error_v.at[chunk], error_sems.at[chunk]).start()
    gt_copy.wait()

    def body(chunk, carry):
        place = pl.ds(chunk * count, count)
        pltpu.make_async_copy(acts_v.at[place], acts_v.at[place], acts_sems.at[chunk]).wait()
        pltpu.make_async_copy(error_v.at[chunk], error_v.at[chunk], error_sems.at[chunk]).wait()
        value = dot_nn(gt_v[...], wide(acts_v, chunk, width)) + error_v[chunk].astype(F32)
        for block in range(count):
            field[chunk * count + block] = lanes(value, block)
        return carry

    lax.fori_loop(0, chunks, body, 0)


def final_kernel(dp_ref, sum_ref, basis_ref, lower, upper, weight, moment1, moment2, new_weight, new_moment1,
                 new_moment2, new_error, q_new, updated, rounded, sems):
    mean = sum_ref[...] * (1.0 / NDP)
    q_new[...] = mean
    rows, ff = mean.shape
    stack = split3(mean.T)
    hi, mid, lo = stack[:ff], stack[ff : 2 * ff], stack[2 * ff :]
    factor = jnp.concatenate([hi, hi, hi, mid, mid, lo], axis=1)
    chunks, width = rounded.shape[0], rounded.shape[2]
    count = width // LANES

    def approx_of(chunk):
        basis = wide(basis_ref, chunk, width)
        hi, mid, lo = basis[:rows], basis[rows : 2 * rows], basis[2 * rows :]
        return dot_nn(factor, jnp.concatenate([hi, mid, lo, hi, mid, hi], axis=0))

    copies = []

    def send(source, target):
        copy = pltpu.make_async_copy(source, target, sems.at[len(copies)])
        copy.start()
        copies.append(copy)

    update = approx_of(dp_ref[0])
    first = beta_one * moment1[...] + (1.0 - beta_one) * update
    second = beta_two * moment2[...] + (1.0 - beta_two) * update * update
    updated[0] = first
    updated[1] = second
    updated[2] = weight[...] - learn_rate * (first / corr_one) / (jnp.sqrt(second / corr_two) + adam_eps)
    send(updated.at[0], new_moment1)
    send(updated.at[1], new_moment2)
    send(updated.at[2], new_weight)
    for chunk in range(chunks):
        approx = approx_of(chunk)
        field = lower if chunk < chunks // 2 else upper
        first = chunk % (chunks // 2) * count
        for block in range(count):
            columns = slice(block * LANES, (block + 1) * LANES)
            rounded[chunk, :, columns] = (field[first + block] - lanes(approx, block)).astype(BF16)
        send(rounded.at[chunk], new_error.at[:, chunk * width : (chunk + 1) * width])
    for copy in copies:
        copy.wait()


def call(kernel, outs, args, specs=None, out_specs=None, scratch=(), limit=16, flops=0, moved=0):
    return pl.pallas_call(
        kernel,
        out_shape=outs,
        in_specs=specs or [VMEM] * len(args),
        out_specs=out_specs or jax.tree.map(lambda _: VMEM, outs),
        scratch_shapes=scratch,
        compiler_params=pltpu.CompilerParams(vmem_limit_bytes=limit * MIB),
        cost_estimate=pl.CostEstimate(flops=flops, bytes_accessed=moved, transcendentals=0),
    )(*args)


def swap(value, axis, level):
    return lax.ppermute(value, axis, list(enumerate(level)))


def total(value, axis, levels):
    for level in levels:
        value = value + swap(value, axis, level)
    return value


def shards(acts, grad_out, error_buffer, q_prev, weight, moment1, moment2):
    member = lax.axis_index("mp").astype(jnp.int32).reshape(1)
    dp = lax.axis_index("dp").astype(jnp.int32).reshape(1)
    core = dp % 2
    gt, et = grad_out.T, error_buffer.T
    rank, ff = q_prev.shape
    tokens, model = acts.shape[0], et.shape[1]
    chunks, width = 8, model // 8
    array = jax.ShapeDtypeStruct

    gathered = lax.all_gather(acts, "mp", axis=0)

    half = rank // 2
    table = jnp.asarray(met(ALONG_X + ALONG_Z, NMP))
    blocks = array((NMP, half, LANES), F32)
    mine, send = call(
        error_kernel, [blocks, blocks], (member, core, table, q_prev, et), specs=[SMEM] * 3 + [HBM] * 2,
        scratch=[
            pltpu.VMEM((rank, ff), F32), pltpu.VMEM((chunks, ff, width), BF16), pltpu.VMEM((NMP, rank, LANES), F32),
            pltpu.SemaphoreType.DMA((chunks + 1,)),
        ],
        limit=60, flops=6 * rank * ff * model, moved=2 * ff * model,
    )
    theirs = swap(send, "dp", ALONG_DP[0])
    factor = call(
        token_kernel, array((FACTOR, 8, LANES), F32), (q_prev, gt), specs=[HBM] * 2,
        scratch=[pltpu.VMEM((rank, ff), F32), pltpu.VMEM((ff, tokens), BF16), pltpu.SemaphoreType.DMA((2,))],
        limit=58, flops=6 * rank * ff * tokens, moved=2 * ff * tokens,
    )
    count = NMP // 2
    message = lambda tiles: array((FACTOR + tiles, 8, LANES), F32)
    kept = lambda count: array((count, half, LANES), F32)
    sent, keep = call(open_kernel, [message(2 * count), kept(count)], (factor, mine, theirs), moved=MIB)
    ring = [acts] + [swap(acts, "mp", level) for level in ALONG_X]
    ring.append(swap(acts, "mp", [(x + 2) % NX * NZ + z for x in range(NX) for z in range(NZ)]))
    for level in ALONG_Z[:0:-1]:
        came = swap(sent, "mp", level)
        count //= 2
        sent, keep = call(halve_kernel, [message(2 * count), kept(count)], (sent, keep, came), moved=MIB)
    came = swap(sent, "mp", ALONG_Z[0])

    keep, send = call(
        piece_kernel, [kept(NX), kept(NX)], (core, sent, keep, came, *ring), specs=[SMEM] + [VMEM] * 7, moved=MIB
    )
    keep = keep + swap(send, "dp", ALONG_DP[0])
    keep = keep[:2] + swap(keep[2:], "mp", ALONG_X[1])
    keep = keep[:1] + swap(keep[1:], "mp", ALONG_X[0])
    keep = total(keep, "dp", ALONG_DP[1:])
    for level in ALONG_X:
        keep = jnp.concatenate([keep, swap(keep, "mp", level)])
    sent = call(
        start_kernel, message(2 * NX), (core, keep, swap(keep, "dp", ALONG_DP[0]), *ring),
        specs=[SMEM] + [VMEM] * 6, moved=MIB,
    )
    for place, level in enumerate(ALONG_Z[:-1]):
        sent = call(double_kernel, message(4 * NX << place), (sent, swap(sent, "mp", level)), moved=MIB)
    factor, mine = call(
        last_kernel, [array((FACTOR, 8, LANES), F32), array((2 * NMP, 8, LANES), F32)],
        (sent, swap(sent, "mp", ALONG_Z[-1])), moved=MIB,
    )
    basis, right = call(
        ortho_kernel, [array((NMP, 3 * rank, LANES), BF16), array((rank, ff), F32)],
        (member, core, table, mine, swap(mine, "dp", ALONG_DP[0]), factor, gt, et),
        specs=[SMEM] * 3 + [VMEM] * 4 + [HBM],
        scratch=[
            pltpu.VMEM((NMP + 1, rank, LANES), F32),
            pltpu.VMEM((chunks, ff, width), BF16),
            pltpu.SemaphoreType.DMA((chunks,)),
        ],
        limit=24, flops=8 * rank * ff * model, moved=2 * ff * model,
    )
    right, gathered = lax.optimization_barrier((right, gathered))
    halves = []
    for part, level in enumerate(ALONG_DP[1:]):
        half = call(
            functools.partial(field_kernel, part * NMP // 2), array((NMP // 2, ff, LANES), F32), (gathered, et, gt),
            specs=[HBM] * 3,
            scratch=[
                pltpu.VMEM((NMP // 2, tokens, LANES), BF16),
                pltpu.VMEM((chunks // 2, ff, width), BF16),
                pltpu.VMEM((ff, tokens), BF16),
                pltpu.SemaphoreType.DMA((chunks // 2,)),
                pltpu.SemaphoreType.DMA((chunks // 2,)),
                pltpu.SemaphoreType.DMA,
            ],
            limit=48, flops=model * ff * tokens, moved=10 * MIB,
        )
        right, half = lax.optimization_barrier((total(right, "dp", [level]), half))
        halves.append(half)
    right = total(right, "dp", ALONG_DP[:1])

    block = array((ff, width), F32)
    outs = call(
        final_kernel,
        [block] * 3 + [array((ff, model), BF16), array((rank, ff), F32)],
        (dp, right, basis, *halves, weight.T, moment1.T, moment2.T),
        specs=[SMEM] + [VMEM] * 7,
        out_specs=[HBM] * 4 + [VMEM],
        scratch=[
            pltpu.VMEM((3, ff, width), F32),
            pltpu.VMEM((chunks, ff, width), BF16),
            pltpu.SemaphoreType.DMA((3 + chunks,)),
        ],
        limit=24, flops=12 * rank * model * ff, moved=20 * MIB,
    )
    new_weight, new_moment1, new_moment2, new_error, q_new = outs
    return (new_weight.T, new_moment1.T, new_moment2.T, new_error.T, q_new)


def solution(mesh):
    placed = (
        P("dp", "mp"),
        P("dp", "mp"),
        P("dp", "mp"),
        P(None, "mp"),
        P("dp", "mp"),
        P("dp", "mp"),
        P("dp", "mp"),
    )
    return jax.shard_map(
        shards,
        mesh=mesh,
        in_specs=placed,
        out_specs=(P("dp", "mp"), P("dp", "mp"), P("dp", "mp"), P("dp", "mp"), P(None, "mp")),
        check_vma=False,
    )
```

time: 189 us -> 160 us (0.85)
  waiting for transfers between devices: 84.1 us -> 69.2 us
  starting transfers between devices: 56.4 us -> 43.9 us
    ppermute x21 -> x22, waiting for transfers between devices: 83.4 us -> 68.5 us  [swap(): return lax.ppermute(value, axis, list(enumerate(level)))]
    all_to_all x1 -> x0, starting transfers between devices: 10.3 us -> none  [shards(): errors = lax.all_to_all(errors, 'mp', 0, 0)]
    ppermute x21 -> x22, starting transfers between devices: 46.1 us -> 43.8 us  [swap(): return lax.ppermute(value, axis, list(enumerate(level)))]
    pallas_call x7 -> x14, Pallas kernels: 30.2 us -> 30.3 us  [call(): pl.pallas_call(kernel, out_shape=outs, in_specs=specs or [VMEM] * len(arg...]
  transfers between devices with their start and end apart: 23 -> 23, of which waited for: 19 -> 18; matrix products, arithmetic and copies ran while one was open for 0% -> 0% of each run, Pallas kernels for 9% -> 16%
where the time goes in v5:
time: 160 us
  waiting for transfers between devices  69.2 us (43%)
  starting transfers between devices  43.9 us (27%)
  Pallas kernels  30.3 us (19%)
  between operations  14.3 us (9%)
  local copies, waits for them, and re-layouts  1.89 us (1%)
    ppermute x22, waiting for transfers between devices, swap(): return lax.ppermute(value, axis, list(enumerate(level)))  68.5 us
    ppermute x22, starting transfers between devices, swap(): return lax.ppermute(value, axis, list(enumerate(level)))  43.8 us
    pallas_call x14, Pallas kernels, call(): pl.pallas_call(kernel, out_shape=outs, in_specs=specs or [VMEM] * len(arg...  30.3 us
  transfers between devices with their start and end apart: 23, of which 18 were waited for; matrix products, arithmetic and copies ran while one was open for 0% of the time, Pallas kernels for 16%

profile of v5, /device:TPU:1, one launch (start us, length us, event | category | flops | bytes accessed | tf_op | source)
XLA Modules:
  0.0 159.6 jit_solution(16250198210061677637)
XLA Ops:
  7.9 4.6 %shard_map.120 = (f32[32,16,128]{2,1,0:T(8,128)}, f32[32,16,128]{2,1,0:T(8,128)}) custom-call(s32[1]{0:T(128)} %bitcast.1.member_ref, s32[1]{0:T(128)S(6)} %select_n.7.core_ref, s32[32,32]{1,0:T(8,128)} %constant.30.clone.place_ref, f32[32,448]{1,0:T(8,128)} %q_hbm.3, bf16[448,4096]{1,0:T(8,128)(2,1)} %bitcast.12), custom_call_target="tpu_custom_call" | custom-call | flops 352321536 | bytes 3670016 | tf_op jit(solution)/shard_map/pallas_call | solution.py:339
  12.5 3.3 %collective-permute-start = (f32[32,16,128]{2,1,0:T(8,128)}, f32[32,16,128]{2,1,0:T(8,128)S(1)}, u32[]{:S(2)}, u32[]{:S(2)}) collective-permute-start(f32[32,16,128]{2,1,0:T(8,128)} %get-tuple-element.31), channel_id=1, source_target_pairs={{0,32},{32,0},{64,96},{96,64},{128,160},{160,128},{192,224},{224,1... | collective-permute-start | bytes 786440 | tf_op jit(solution)/shard_map/ppermute | solution.py:351
  15.9 2.3 %shard_map.119.tokens = f32[32,8,128]{2,1,0:T(8,128)} custom-call(f32[32,448]{1,0:T(8,128)} %q_hbm.3, bf16[448,1024]{1,0:T(8,128)(2,1)} %bitcast.16), custom_call_target="tpu_custom_call" | custom-call | flops 88080384 | bytes 917504 | tf_op jit(solution)/shard_map/pallas_call | solution.py:339
  20.2 7.9 %collective-permute-done.1.came = f32[64,8,128]{2,1,0:T(8,128)S(1)} collective-permute-done((f32[64,8,128]{2,1,0:T(8,128)S(1)}, f32[64,8,128]{2,1,0:T(8,128)S(1)}, u32[]{:S(2)}, u32[]{:S(2)}) %collective-permute-start.1) | collective-permute-done | bytes 262176 | tf_op jit(solution)/shard_map/ppermute | solution.py:351
  28.1 4.0 %collective-permute-start.2 = (f32[48,8,128]{2,1,0:T(8,128)S(1)}, f32[48,8,128]{2,1,0:T(8,128)S(1)}, u32[]{:S(2)}, u32[]{:S(2)}) collective-permute-start(f32[48,8,128]{2,1,0:T(8,128)S(1)} %get-tuple-element.34.sent), channel_id=1, source_target_pairs={{0,7},{1,2},{2,1},{3,4},{4,3},{5,6},{6,5},{7,0},{8,15},{9,10},{10,... | collective-permute-start | bytes 589832 | tf_op jit(solution)/shard_map/ppermute | solution.py:351
  32.2 2.7 %collective-permute-start.6 = (bf16[1024,128]{1,0:T(8,128)(2,1)S(1)}, bf16[1024,128]{1,0:T(8,128)(2,1)S(1)}, u32[]{:S(2)}, u32[]{:S(2)}) collective-permute-start(bf16[1024,128]{1,0:T(8,128)(2,1)S(1)} %copy-done.2), channel_id=1, source_target_pairs={{0,16},{1,17},{2,18},{3,19},{4,20},{5,21},{6,22},{7,23},{8,24},{9,... | collective-permute-start | bytes 786440 | tf_op jit(solution)/shard_map/ppermute | solution.py:351
  38.0 3.0 %collective-permute-start.3 = (f32[40,8,128]{2,1,0:T(8,128)S(1)}, f32[40,8,128]{2,1,0:T(8,128)S(1)}, u32[]{:S(2)}, u32[]{:S(2)}) collective-permute-start(f32[40,8,128]{2,1,0:T(8,128)S(1)} %get-tuple-element.36.sent), channel_id=1, source_target_pairs={{0,3},{1,6},{2,5},{3,0},{4,7},{5,2},{6,1},{7,4},{8,11},{9,14},{10,... | collective-permute-start | bytes 491528 | tf_op jit(solution)/shard_map/ppermute | solution.py:351
  41.9 7.8 %collective-permute-done.5.refs_2_ = bf16[1024,128]{1,0:T(8,128)(2,1)S(1)} collective-permute-done((bf16[1024,128]{1,0:T(8,128)(2,1)S(1)}, bf16[1024,128]{1,0:T(8,128)(2,1)S(1)}, u32[]{:S(2)}, u32[]{:S(2)}) %collective-permute-start.5) | collective-permute-done | bytes 262176 | tf_op jit(solution)/shard_map/ppermute | solution.py:351
  55.1 3.0 %collective-permute-start.8 = (f32[2,16,128]{2,1,0:T(8,128)S(1)}, f32[2,16,128]{2,1,0:T(8,128)S(1)}, u32[]{:S(2)}, u32[]{:S(2)}) collective-permute-start(f32[2,16,128]{2,1,0:T(8,128)S(1)} %slice.17), channel_id=1, source_target_pairs={{0,24},{1,25},{2,26},{3,27},{4,28},{5,29},{6,30},{7,31},{8,16},{9,... | collective-permute-start | bytes 49160 | tf_op jit(solution)/shard_map/ppermute | solution.py:351
  59.3 2.4 %collective-permute-done.9 = f32[1,16,128]{2,1,0:T(8,128)S(1)} collective-permute-done((f32[1,16,128]{2,1,0:T(8,128)S(1)}, f32[1,16,128]{2,1,0:T(8,128)S(1)}, u32[]{:S(2)}, u32[]{:S(2)}) %collective-permute-start.9) | collective-permute-done | bytes 8224 | tf_op jit(solution)/shard_map/ppermute | solution.py:351
  64.3 3.1 %collective-permute-start.11 = (f32[1,16,128]{2,1,0:T(8,128)S(1)}, f32[1,16,128]{2,1,0:T(8,128)S(1)}, u32[]{:S(2)}, u32[]{:S(2)}) collective-permute-start(f32[1,16,128]{2,1,0:T(8,128)S(1)} %add.34), channel_id=1, source_target_pairs={{0,192},{32,224},{64,128},{96,160},{128,64},{160,96},{192,0},{224,... | collective-permute-start | bytes 24584 | tf_op jit(solution)/shard_map/ppermute | solution.py:351
  68.4 2.9 %collective-permute-done.12 = f32[1,16,128]{2,1,0:T(8,128)S(1)} collective-permute-done((f32[1,16,128]{2,1,0:T(8,128)S(1)}, f32[1,16,128]{2,1,0:T(8,128)S(1)}, u32[]{:S(2)}, u32[]{:S(2)}) %collective-permute-start.12) | collective-permute-done | bytes 8224 | tf_op jit(solution)/shard_map/ppermute | solution.py:351
  71.3 2.4 %collective-permute-start.13 = (f32[2,16,128]{2,1,0:T(8,128)S(1)}, f32[2,16,128]{2,1,0:T(8,128)S(1)}, u32[]{:S(2)}, u32[]{:S(2)}) collective-permute-start(f32[2,16,128]{2,1,0:T(8,128)S(1)} %pad_maximum_fusion.1), channel_id=1, source_target_pairs={{0,24},{1,25},{2,26},{3,27},{4,28},{5,29},{6,30},{7,31},{8,16},{9,... | collective-permute-start | bytes 49160 | tf_op jit(solution)/shard_map/ppermute | solution.py:351
  75.9 5.9 %collective-permute-start.14 = (f32[4,16,128]{2,1,0:T(8,128)S(1)}, f32[4,16,128]{2,1,0:T(8,128)S(1)}, u32[]{:S(2)}, u32[]{:S(2)}) collective-permute-start(f32[4,16,128]{2,1,0:T(8,128)S(1)} %pad_maximum_fusion.mine), channel_id=1, source_target_pairs={{0,32},{32,0},{64,96},{96,64},{128,160},{160,128},{192,224},{224,1... | collective-permute-start | bytes 98312 | tf_op jit(solution)/shard_map/ppermute | solution.py:351
  83.1 2.5 %collective-permute-start.15 = (f32[40,8,128]{2,1,0:T(8,128)S(1)}, f32[40,8,128]{2,1,0:T(8,128)S(1)}, u32[]{:S(2)}, u32[]{:S(2)}) collective-permute-start(f32[40,8,128]{2,1,0:T(8,128)S(1)} %shard_map.125.sent), channel_id=1, source_target_pairs={{0,3},{1,6},{2,5},{3,0},{4,7},{5,2},{6,1},{7,4},{8,11},{9,14},{10,... | collective-permute-start | bytes 491528 | tf_op jit(solution)/shard_map/ppermute | solution.py:351
  85.6 10.7 %collective-permute-done.15.came = f32[40,8,128]{2,1,0:T(8,128)S(1)} collective-permute-done((f32[40,8,128]{2,1,0:T(8,128)S(1)}, f32[40,8,128]{2,1,0:T(8,128)S(1)}, u32[]{:S(2)}, u32[]{:S(2)}) %collective-permute-start.15) | collective-permute-done | bytes 163872 | tf_op jit(solution)/shard_map/ppermute | solution.py:351
  96.3 3.5 %collective-permute-start.16 = (f32[48,8,128]{2,1,0:T(8,128)S(1)}, f32[48,8,128]{2,1,0:T(8,128)S(1)}, u32[]{:S(2)}, u32[]{:S(2)}) collective-permute-start(f32[48,8,128]{2,1,0:T(8,128)S(1)} %shard_map.126.sent), channel_id=1, source_target_pairs={{0,7},{1,2},{2,1},{3,4},{4,3},{5,6},{6,5},{7,0},{8,15},{9,10},{10,... | collective-permute-start | bytes 589832 | tf_op jit(solution)/shard_map/ppermute | solution.py:351
  99.8 8.8 %collective-permute-done.16.came = f32[48,8,128]{2,1,0:T(8,128)S(1)} collective-permute-done((f32[48,8,128]{2,1,0:T(8,128)S(1)}, f32[48,8,128]{2,1,0:T(8,128)S(1)}, u32[]{:S(2)}, u32[]{:S(2)}) %collective-permute-start.16) | collective-permute-done | bytes 196640 | tf_op jit(solution)/shard_map/ppermute | solution.py:351
  108.7 13.4 %collective-permute-done.17.came = f32[64,8,128]{2,1,0:T(8,128)S(1)} collective-permute-done((f32[64,8,128]{2,1,0:T(8,128)S(1)}, f32[64,8,128]{2,1,0:T(8,128)S(1)}, u32[]{:S(2)}, u32[]{:S(2)}) %collective-permute-start.17) | collective-permute-done | bytes 262176 | tf_op jit(solution)/shard_map/ppermute | solution.py:351
  125.4 9.4 %shard_map.129 = (bf16[32,96,128]{2,1,0:T(8,128)(2,1)S(1)}, f32[32,448]{1,0:T(8,128)S(1)}) custom-call(s32[1]{0:T(128)} %bitcast.1.member_ref, s32[1]{0:T(128)S(6)} %select_n.7.core_ref, s32[32,32]{1,0:T(8,128)S(1)} %copy-done.8, f32[64,8,128]{2,1,0:T(8,128)S(1)} %get-tuple-element.40.mine, f32[64,8,128]{2,1,0:T(8,128)S(1)} %collective-permute-done.18.theirs, ...), custom_call_target="tpu_custom_call" | custom-call | flops 469762048 | bytes 3670016 | tf_op jit(solution)/shard_map/pallas_call | solution.py:339
  135.0 4.2 %shard_map.130.lower = f32[16,448,128]{2,1,0:T(8,128)S(1)} custom-call(bf16[32,1024,128]{2,1,0:T(8,128)(2,1)} %bitcast.23, bf16[448,4096]{1,0:T(8,128)(2,1)} %bitcast.13, bf16[448,1024]{1,0:T(8,128)(2,1)S(1)} %bitcast.18), custom_call_target="tpu_custom_call" | custom-call | flops 1879048192 | bytes 10485760 | tf_op jit(solution)/shard_map/pallas_call | solution.py:339
  139.3 3.0 %collective-permute-start.20 = (f32[32,448]{1,0:T(8,128)S(1)}, f32[32,448]{1,0:T(8,128)S(1)}, u32[]{:S(2)}, u32[]{:S(2)}) collective-permute-start(f32[32,448]{1,0:T(8,128)S(1)} %add.36), channel_id=1, source_target_pairs={{0,192},{32,224},{64,128},{96,160},{128,64},{160,96},{192,0},{224,... | collective-permute-start | bytes 172040 | tf_op jit(solution)/shard_map/ppermute | solution.py:351
  142.3 4.2 %shard_map.131.upper = f32[16,448,128]{2,1,0:T(8,128)S(1)} custom-call(bf16[32,1024,128]{2,1,0:T(8,128)(2,1)} %bitcast.24, bf16[448,4096]{1,0:T(8,128)(2,1)} %bitcast.14, bf16[448,1024]{1,0:T(8,128)(2,1)S(1)} %bitcast.19), custom_call_target="tpu_custom_call" | custom-call | flops 1879048192 | bytes 10485760 | tf_op jit(solution)/shard_map/pallas_call | solution.py:339
  148.2 4.5 %shard_map.132 = (f32[448,512]{1,0:T(8,128)}, f32[448,512]{1,0:T(8,128)}, f32[448,512]{1,0:T(8,128)}, bf16[448,4096]{1,0:T(8,128)(2,1)}, f32[32,448]{1,0:T(8,128)}) custom-call(s32[1]{0:T(128)} %bitcast.dp_ref, f32[32,448]{1,0:T(8,128)S(1)} %add.38.sum_ref, bf16[32,96,128]{2,1,0:T(8,128)(2,1)S(1)} %get-tuple-element.47.basis_ref, ...), custom_call_target="tpu_custom_call" | custom-call | flops 704643072 | bytes 20971520 | tf_op jit(solution)/shard_map/pallas_call | solution.py:339
  (67 shorter events, 25.5 us)
Async XLA Ops:
  7.2 127.7 %all-gather.3.cloned.1.call-start = ((), (), s32[]{:S(2)}) async-start(), calls=%async_computation | async-start | bytes 8650752 | tf_op jit(solution)/shard_map/all_gather | solution.py:370
  12.5 5.7 %collective-permute-start = (f32[32,16,128]{2,1,0:T(8,128)}, f32[32,16,128]{2,1,0:T(8,128)S(1)}, u32[]{:S(2)}, u32[]{:S(2)}) collective-permute-start(f32[32,16,128]{2,1,0:T(8,128)} %get-tuple-element.31), channel_id=1, source_target_pairs={{0,32},{32,0},{64,96},{96,64},{128,160},{160,128},{192,224},{224,1... | collective-permute-start | bytes 786440 | tf_op jit(solution)/shard_map/ppermute | solution.py:351
  15.9 109.6 %copy-start.1 = (bf16[1024,448]{0,1:T(8,128)(2,1)S(1)}, bf16[1024,448]{0,1:T(8,128)(2,1)}, u32[]{:S(2)}) copy-start(bf16[1024,448]{0,1:T(8,128)(2,1)} %param.9) | copy-start | bytes 2752516
  20.1 8.0 %collective-permute-start.1 = (f32[64,8,128]{2,1,0:T(8,128)S(1)}, f32[64,8,128]{2,1,0:T(8,128)S(1)}, u32[]{:S(2)}, u32[]{:S(2)}) collective-permute-start(f32[64,8,128]{2,1,0:T(8,128)S(1)} %get-tuple-element.32.sent), channel_id=1, source_target_pairs={{0,1},{1,0},{2,3},{3,2},{4,5},{5,4},{6,7},{7,6},{8,9},{9,8},{10,11... | collective-permute-start | bytes 786440 | tf_op jit(solution)/shard_map/ppermute | solution.py:351
  28.1 9.9 %collective-permute-start.2 = (f32[48,8,128]{2,1,0:T(8,128)S(1)}, f32[48,8,128]{2,1,0:T(8,128)S(1)}, u32[]{:S(2)}, u32[]{:S(2)}) collective-permute-start(f32[48,8,128]{2,1,0:T(8,128)S(1)} %get-tuple-element.34.sent), channel_id=1, source_target_pairs={{0,7},{1,2},{2,1},{3,4},{4,3},{5,6},{6,5},{7,0},{8,15},{9,10},{10,... | collective-permute-start | bytes 589832 | tf_op jit(solution)/shard_map/ppermute | solution.py:351
  32.2 9.7 %collective-permute-start.6 = (bf16[1024,128]{1,0:T(8,128)(2,1)S(1)}, bf16[1024,128]{1,0:T(8,128)(2,1)S(1)}, u32[]{:S(2)}, u32[]{:S(2)}) collective-permute-start(bf16[1024,128]{1,0:T(8,128)(2,1)S(1)} %copy-done.2), channel_id=1, source_target_pairs={{0,16},{1,17},{2,18},{3,19},{4,20},{5,21},{6,22},{7,23},{8,24},{9,... | collective-permute-start | bytes 786440 | tf_op jit(solution)/shard_map/ppermute | solution.py:351
  34.9 14.8 %collective-permute-start.5 = (bf16[1024,128]{1,0:T(8,128)(2,1)S(1)}, bf16[1024,128]{1,0:T(8,128)(2,1)S(1)}, u32[]{:S(2)}, u32[]{:S(2)}) collective-permute-start(bf16[1024,128]{1,0:T(8,128)(2,1)S(1)} %copy-done.2), channel_id=1, source_target_pairs={{0,24},{1,25},{2,26},{3,27},{4,28},{5,29},{6,30},{7,31},{8,16},{9,... | collective-permute-start | bytes 786440 | tf_op jit(solution)/shard_map/ppermute | solution.py:351
  35.8 14.0 %collective-permute-start.4 = (bf16[1024,128]{1,0:T(8,128)(2,1)S(1)}, bf16[1024,128]{1,0:T(8,128)(2,1)S(1)}, u32[]{:S(2)}, u32[]{:S(2)}) collective-permute-start(bf16[1024,128]{1,0:T(8,128)(2,1)S(1)} %copy-done.2), channel_id=1, source_target_pairs={{0,8},{1,9},{2,10},{3,11},{4,12},{5,13},{6,14},{7,15},{8,0},{9,1},... | collective-permute-start | bytes 786440 | tf_op jit(solution)/shard_map/ppermute | solution.py:351
  38.0 14.0 %collective-permute-start.3 = (f32[40,8,128]{2,1,0:T(8,128)S(1)}, f32[40,8,128]{2,1,0:T(8,128)S(1)}, u32[]{:S(2)}, u32[]{:S(2)}) collective-permute-start(f32[40,8,128]{2,1,0:T(8,128)S(1)} %get-tuple-element.36.sent), channel_id=1, source_target_pairs={{0,3},{1,6},{2,5},{3,0},{4,7},{5,2},{6,1},{7,4},{8,11},{9,14},{10,... | collective-permute-start | bytes 491528 | tf_op jit(solution)/shard_map/ppermute | solution.py:351
  52.4 2.6 %collective-permute-start.7 = (f32[4,16,128]{2,1,0:T(8,128)S(1)}, f32[4,16,128]{2,1,0:T(8,128)S(1)}, u32[]{:S(2)}, u32[]{:S(2)}) collective-permute-start(f32[4,16,128]{2,1,0:T(8,128)S(1)} %get-tuple-element.39), channel_id=1, source_target_pairs={{0,32},{32,0},{64,96},{96,64},{128,160},{160,128},{192,224},{224,1... | collective-permute-start | bytes 98312 | tf_op jit(solution)/shard_map/ppermute | solution.py:351
  55.1 4.2 %collective-permute-start.8 = (f32[2,16,128]{2,1,0:T(8,128)S(1)}, f32[2,16,128]{2,1,0:T(8,128)S(1)}, u32[]{:S(2)}, u32[]{:S(2)}) collective-permute-start(f32[2,16,128]{2,1,0:T(8,128)S(1)} %slice.17), channel_id=1, source_target_pairs={{0,24},{1,25},{2,26},{3,27},{4,28},{5,29},{6,30},{7,31},{8,16},{9,... | collective-permute-start | bytes 49160 | tf_op jit(solution)/shard_map/ppermute | solution.py:351
  59.3 2.5 %collective-permute-start.9 = (f32[1,16,128]{2,1,0:T(8,128)S(1)}, f32[1,16,128]{2,1,0:T(8,128)S(1)}, u32[]{:S(2)}, u32[]{:S(2)}) collective-permute-start(f32[1,16,128]{2,1,0:T(8,128)S(1)} %slice.19), channel_id=1, source_target_pairs={{0,8},{1,9},{2,10},{3,11},{4,12},{5,13},{6,14},{7,15},{8,0},{9,1},... | collective-permute-start | bytes 24584 | tf_op jit(solution)/shard_map/ppermute | solution.py:351
  61.8 2.5 %collective-permute-start.10 = (f32[1,16,128]{2,1,0:T(8,128)S(1)}, f32[1,16,128]{2,1,0:T(8,128)S(1)}, u32[]{:S(2)}, u32[]{:S(2)}) collective-permute-start(f32[1,16,128]{2,1,0:T(8,128)S(1)} %slice_add_fusion.1), channel_id=1, source_target_pairs={{0,64},{32,96},{64,0},{96,32},{128,192},{160,224},{192,128},{224,1... | collective-permute-start | bytes 24584 | tf_op jit(solution)/shard_map/ppermute | solution.py:351
  64.3 4.2 %collective-permute-start.11 = (f32[1,16,128]{2,1,0:T(8,128)S(1)}, f32[1,16,128]{2,1,0:T(8,128)S(1)}, u32[]{:S(2)}, u32[]{:S(2)}) collective-permute-start(f32[1,16,128]{2,1,0:T(8,128)S(1)} %add.34), channel_id=1, source_target_pairs={{0,192},{32,224},{64,128},{96,160},{128,64},{160,96},{192,0},{224,... | collective-permute-start | bytes 24584 | tf_op jit(solution)/shard_map/ppermute | solution.py:351
  68.4 2.9 %collective-permute-start.12 = (f32[1,16,128]{2,1,0:T(8,128)S(1)}, f32[1,16,128]{2,1,0:T(8,128)S(1)}, u32[]{:S(2)}, u32[]{:S(2)}) collective-permute-start(f32[1,16,128]{2,1,0:T(8,128)S(1)} %add.35), channel_id=1, source_target_pairs={{0,8},{1,9},{2,10},{3,11},{4,12},{5,13},{6,14},{7,15},{8,0},{9,1},... | collective-permute-start | bytes 24584 | tf_op jit(solution)/shard_map/ppermute | solution.py:351
  71.3 4.5 %collective-permute-start.13 = (f32[2,16,128]{2,1,0:T(8,128)S(1)}, f32[2,16,128]{2,1,0:T(8,128)S(1)}, u32[]{:S(2)}, u32[]{:S(2)}) collective-permute-start(f32[2,16,128]{2,1,0:T(8,128)S(1)} %pad_maximum_fusion.1), channel_id=1, source_target_pairs={{0,24},{1,25},{2,26},{3,27},{4,28},{5,29},{6,30},{7,31},{8,16},{9,... | collective-permute-start | bytes 49160 | tf_op jit(solution)/shard_map/ppermute | solution.py:351
  75.9 6.8 %collective-permute-start.14 = (f32[4,16,128]{2,1,0:T(8,128)S(1)}, f32[4,16,128]{2,1,0:T(8,128)S(1)}, u32[]{:S(2)}, u32[]{:S(2)}) collective-permute-start(f32[4,16,128]{2,1,0:T(8,128)S(1)} %pad_maximum_fusion.mine), channel_id=1, source_target_pairs={{0,32},{32,0},{64,96},{96,64},{128,160},{160,128},{192,224},{224,1... | collective-permute-start | bytes 98312 | tf_op jit(solution)/shard_map/ppermute | solution.py:351
  83.1 13.2 %collective-permute-start.15 = (f32[40,8,128]{2,1,0:T(8,128)S(1)}, f32[40,8,128]{2,1,0:T(8,128)S(1)}, u32[]{:S(2)}, u32[]{:S(2)}) collective-permute-start(f32[40,8,128]{2,1,0:T(8,128)S(1)} %shard_map.125.sent), channel_id=1, source_target_pairs={{0,3},{1,6},{2,5},{3,0},{4,7},{5,2},{6,1},{7,4},{8,11},{9,14},{10,... | collective-permute-start | bytes 491528 | tf_op jit(solution)/shard_map/ppermute | solution.py:351
  96.3 12.2 %collective-permute-start.16 = (f32[48,8,128]{2,1,0:T(8,128)S(1)}, f32[48,8,128]{2,1,0:T(8,128)S(1)}, u32[]{:S(2)}, u32[]{:S(2)}) collective-permute-start(f32[48,8,128]{2,1,0:T(8,128)S(1)} %shard_map.126.sent), channel_id=1, source_target_pairs={{0,7},{1,2},{2,1},{3,4},{4,3},{5,6},{6,5},{7,0},{8,15},{9,10},{10,... | collective-permute-start | bytes 589832 | tf_op jit(solution)/shard_map/ppermute | solution.py:351
  108.6 13.6 %collective-permute-start.17 = (f32[64,8,128]{2,1,0:T(8,128)S(1)}, f32[64,8,128]{2,1,0:T(8,128)S(1)}, u32[]{:S(2)}, u32[]{:S(2)}) collective-permute-start(f32[64,8,128]{2,1,0:T(8,128)S(1)} %shard_map.127.sent), channel_id=1, source_target_pairs={{0,1},{1,0},{2,3},{3,2},{4,5},{5,4},{6,7},{7,6},{8,9},{9,8},{10,11... | collective-permute-start | bytes 786440 | tf_op jit(solution)/shard_map/ppermute | solution.py:351
  122.2 3.2 %collective-permute-start.18 = (f32[64,8,128]{2,1,0:T(8,128)S(1)}, f32[64,8,128]{2,1,0:T(8,128)S(1)}, u32[]{:S(2)}, u32[]{:S(2)}) collective-permute-start(f32[64,8,128]{2,1,0:T(8,128)S(1)} %get-tuple-element.40.mine), channel_id=1, source_target_pairs={{0,32},{32,0},{64,96},{96,64},{128,160},{160,128},{192,224},{224,1... | collective-permute-start | bytes 786440 | tf_op jit(solution)/shard_map/ppermute | solution.py:351
  134.9 4.3 %collective-permute-start.19 = (f32[32,448]{1,0:T(8,128)S(1)}, f32[32,448]{1,0:T(8,128)S(1)}, u32[]{:S(2)}, u32[]{:S(2)}) collective-permute-start(f32[32,448]{1,0:T(8,128)S(1)} %get-tuple-element.43), channel_id=1, source_target_pairs={{0,64},{32,96},{64,0},{96,32},{128,192},{160,224},{192,128},{224,1... | collective-permute-start | bytes 172040 | tf_op jit(solution)/shard_map/ppermute | solution.py:351
  139.3 7.3 %collective-permute-start.20 = (f32[32,448]{1,0:T(8,128)S(1)}, f32[32,448]{1,0:T(8,128)S(1)}, u32[]{:S(2)}, u32[]{:S(2)}) collective-permute-start(f32[32,448]{1,0:T(8,128)S(1)} %add.36), channel_id=1, source_target_pairs={{0,192},{32,224},{64,128},{96,160},{128,64},{160,96},{192,0},{224,... | collective-permute-start | bytes 172040 | tf_op jit(solution)/shard_map/ppermute | solution.py:351
  146.5 1.7 %collective-permute-start.21 = (f32[32,448]{1,0:T(8,128)S(1)}, f32[32,448]{1,0:T(8,128)S(1)}, u32[]{:S(2)}, u32[]{:S(2)}) collective-permute-start(f32[32,448]{1,0:T(8,128)S(1)} %add.37), channel_id=1, source_target_pairs={{0,32},{32,0},{64,96},{96,64},{128,160},{160,128},{192,224},{224,1... | collective-permute-start | bytes 172040 | tf_op jit(solution)/shard_map/ppermute | solution.py:351
  (8 other events, 268.8 us)
Sparse Core Ops, SparseCore 0:
  10.6 115.4 all-gather.2

commit v6 on v5

--- a/solution.py
+++ b/solution.py
@@ -19,6 +19,7 @@
 NX, NZ, NDP = 4, 8, 8
 NMP = NX * NZ
 FACTOR = 32
+QUARTER = FACTOR // NX
 LANES = 128
 F32, BF16 = jnp.float32, jnp.bfloat16
 MIB = 1 << 20
@@ -149,7 +150,7 @@
     store_blocks(both[count // 2 :], message, FACTOR)
 
 
-def piece_kernel(core_ref, sent, kept, came, *refs):
+def piece_kernel(member_ref, core_ref, place_ref, sent, kept, came, *refs):
     acts_refs, keep, send = refs[:NX], refs[NX], refs[NX + 1]
     blocks = acts_refs[0].shape[0] // LANES
     half = keep.shape[1]
@@ -160,39 +161,48 @@
         factors.append(split3(rows_of(sent, block, blocks, FACTOR) + rows_of(came, block, blocks, FACTOR)))
     factor = jnp.concatenate(factors, axis=1)
     for place in range(NX):
+        x = lax.div(place_ref[member_ref[0], place], NZ)
         piece = fold3(dot_nn(factor, acts_refs[place][...]))
-        keep[place] = jnp.where(lower, piece[:half], piece[half:]) + errors[place]
-        send[place] = jnp.where(lower, piece[half:], piece[:half])
-
-
-def start_kernel(core_ref, mine, theirs, *refs):
+        keep[x] = jnp.where(lower, piece[:half], piece[half:]) + errors[place]
+        send[x] = jnp.where(lower, piece[half:], piece[:half])
+
+
+def start_kernel(member_ref, core_ref, place_ref, mine, theirs, *refs):
     acts_refs, message = refs[:NX], refs[NX]
     lower = core_ref[0] == 0
+    rows = acts_refs[0].shape[0] // NX
+    home = lax.div(member_ref[0], NZ)
+    quarter = pl.ds(pl.multiple_of(home * rows, rows), rows)
     total = None
     for place in range(NX):
-        first, second = mine[place] * (1.0 / NDP), theirs[place] * (1.0 / NDP)
+        x = lax.div(place_ref[member_ref[0], place], NZ)
+        first, second = mine[x] * (1.0 / NDP), theirs[x] * (1.0 / NDP)
         panel = jnp.concatenate([jnp.where(lower, first, second), jnp.where(lower, second, first)], axis=0)
-        part = dot_nt(split3(panel), acts_refs[place][...])
+        part = dot_nt(split3(panel), acts_refs[place][quarter, :])
         total = part if total is None else total + part
     tiles_of(fold3(total), message)
-    store_blocks(mine[...] * (1.0 / NDP), message, FACTOR)
+    store_blocks(mine[home][None] * (1.0 / NDP), message, QUARTER)
 
 
 def double_kernel(sent, came, message):
-    count = sent.shape[0] - FACTOR
-    message[:FACTOR] = sent[:FACTOR] + came[:FACTOR]
-    message[FACTOR : FACTOR + count] = sent[FACTOR:]
-    message[FACTOR + count :] = came[FACTOR:]
-
-
-def last_kernel(sent, came, factor, rows):
-    count = sent.shape[0] - FACTOR
-    factor[...] = sent[:FACTOR] + came[:FACTOR]
-    rows[:count] = sent[FACTOR:]
-    rows[count:] = came[FACTOR:]
-
-
-def ortho_kernel(member_ref, core_ref, place_ref, mine, theirs, tokens, gt_ref, et_hbm, split, right, panel, et_ref, sems):
+    count = sent.shape[0] - QUARTER
+    message[:QUARTER] = sent[:QUARTER] + came[:QUARTER]
+    message[QUARTER : QUARTER + count] = sent[QUARTER:]
+    message[QUARTER + count :] = came[QUARTER:]
+
+
+def part_kernel(sent, came, factor, rows):
+    each = sent.shape[0] // 2
+    count = each - QUARTER
+    for place in range(NX):
+        ref = sent if place < 2 else came
+        start = place % 2 * each
+        factor[place * QUARTER : (place + 1) * QUARTER] = ref[start : start + QUARTER]
+        rows[place * count : (place + 1) * count] = ref[start + QUARTER : start + each]
+
+
+def ortho_kernel(member_ref, core_ref, place_ref, mine, theirs, tokens, gt_ref, et_hbm, split, right, panel, et_ref, factors,
+                 sems):
     chunks, width = et_ref.shape[0], et_ref.shape[2]
     copies = [
         pltpu.make_async_copy(et_hbm.at[:, chunk * width : (chunk + 1) * width], et_ref.at[chunk], sems.at[chunk])
@@ -246,8 +256,13 @@
             panel[block, index : index + 1, :] = row * scale
     for block in range(blocks):
         split[block] = split3(panel[block])
-    columns = gt_ref.shape[1] // LANES
-    factor = jnp.concatenate([rows_of(tokens, column, columns, FACTOR) for column in range(columns)], axis=1)
+    columns = factors.shape[2] // LANES
+    for place in range(NX):
+        tiles = tokens.at[pl.ds(place * QUARTER, QUARTER)]
+        factors[lax.div(place_ref[member, place * NZ], NZ)] = jnp.concatenate(
+            [rows_of(tiles, column, columns, FACTOR) for column in range(columns)], axis=1
+        )
+    factor = jnp.concatenate([factors[x] for x in range(NX)], axis=1)
     grads = fold3(dot_nt(split3(factor), gt_ref[...]))
     total = None
     for chunk in range(chunks):
@@ -342,7 +357,7 @@
         in_specs=specs or [VMEM] * len(args),
         out_specs=out_specs or jax.tree.map(lambda _: VMEM, outs),
         scratch_shapes=scratch,
-        compiler_params=pltpu.CompilerParams(vmem_limit_bytes=limit * MIB),
+        compiler_params=pltpu.CompilerParams(vmem_limit_bytes=int(limit * MIB)),
         cost_estimate=pl.CostEstimate(flops=flops, bytes_accessed=moved, transcendentals=0),
     )(*args)
 
@@ -378,13 +393,13 @@
             pltpu.VMEM((rank, ff), F32), pltpu.VMEM((chunks, ff, width), BF16), pltpu.VMEM((NMP, rank, LANES), F32),
             pltpu.SemaphoreType.DMA((chunks + 1,)),
         ],
-        limit=60, flops=6 * rank * ff * model, moved=2 * ff * model,
+        limit=56, flops=6 * rank * ff * model, moved=2 * ff * model,
     )
     theirs = swap(send, "dp", ALONG_DP[0])
     factor = call(
         token_kernel, array((FACTOR, 8, LANES), F32), (q_prev, gt), specs=[HBM] * 2,
         scratch=[pltpu.VMEM((rank, ff), F32), pltpu.VMEM((ff, tokens), BF16), pltpu.SemaphoreType.DMA((2,))],
-        limit=58, flops=6 * rank * ff * tokens, moved=2 * ff * tokens,
+        limit=16, flops=6 * rank * ff * tokens, moved=2 * ff * tokens,
     )
     count = NMP // 2
     message = lambda tiles: array((FACTOR + tiles, 8, LANES), F32)
@@ -392,45 +407,47 @@
     sent, keep = call(open_kernel, [message(2 * count), kept(count)], (factor, mine, theirs), moved=MIB)
     ring = [acts] + [swap(acts, "mp", level) for level in ALONG_X]
     ring.append(swap(acts, "mp", [(x + 2) % NX * NZ + z for x in range(NX) for z in range(NZ)]))
-    for level in ALONG_Z[:0:-1]:
+    for place, level in enumerate(ALONG_Z[:0:-1]):
         came = swap(sent, "mp", level)
         count //= 2
         sent, keep = call(halve_kernel, [message(2 * count), kept(count)], (sent, keep, came), moved=MIB)
+        if place == 0:
+            sent, ring[1:3] = lax.optimization_barrier((sent, ring[1:3]))
     came = swap(sent, "mp", ALONG_Z[0])
 
     keep, send = call(
-        piece_kernel, [kept(NX), kept(NX)], (core, sent, keep, came, *ring), specs=[SMEM] + [VMEM] * 7, moved=MIB
+        piece_kernel, [kept(NX), kept(NX)], (member, core, table, sent, keep, came, *ring),
+        specs=[SMEM] * 3 + [VMEM] * 7, moved=MIB,
     )
     keep = keep + swap(send, "dp", ALONG_DP[0])
-    keep = keep[:2] + swap(keep[2:], "mp", ALONG_X[1])
-    keep = keep[:1] + swap(keep[1:], "mp", ALONG_X[0])
-    keep = total(keep, "dp", ALONG_DP[1:])
-    for level in ALONG_X:
-        keep = jnp.concatenate([keep, swap(keep, "mp", level)])
+    keep = total(total(keep, "mp", ALONG_X), "dp", ALONG_DP[1:])
     sent = call(
-        start_kernel, message(2 * NX), (core, keep, swap(keep, "dp", ALONG_DP[0]), *ring),
-        specs=[SMEM] + [VMEM] * 6, moved=MIB,
-    )
-    for place, level in enumerate(ALONG_Z[:-1]):
-        sent = call(double_kernel, message(4 * NX << place), (sent, swap(sent, "mp", level)), moved=MIB)
+        start_kernel, array((QUARTER + 2, 8, LANES), F32), (member, core, table, keep, swap(keep, "dp", ALONG_DP[0]), *ring),
+        specs=[SMEM] * 3 + [VMEM] * 6, moved=MIB,
+    )
+    for place, level in enumerate(ALONG_Z):
+        came = swap(sent, "mp", level)
+        sent = call(double_kernel, array((QUARTER + (4 << place), 8, LANES), F32), (sent, came), moved=MIB)
+    sent = jnp.concatenate([sent, swap(sent, "mp", ALONG_X[0])])
     factor, mine = call(
-        last_kernel, [array((FACTOR, 8, LANES), F32), array((2 * NMP, 8, LANES), F32)],
-        (sent, swap(sent, "mp", ALONG_Z[-1])), moved=MIB,
+        part_kernel, [array((FACTOR, 8, LANES), F32), array((2 * NMP, 8, LANES), F32)],
+        (sent, swap(sent, "mp", ALONG_X[1])), moved=MIB,
     )
     basis, right = call(
         ortho_kernel, [array((NMP, 3 * rank, LANES), BF16), array((rank, ff), F32)],
-        (member, core, table, mine, swap(mine, "dp", ALONG_DP[0]), factor, gt, et),
+        (member, core, jnp.asarray(met(ALONG_Z + ALONG_X, NMP)), mine, swap(mine, "dp", ALONG_DP[0]), factor, gt, et),
         specs=[SMEM] * 3 + [VMEM] * 4 + [HBM],
         scratch=[
             pltpu.VMEM((NMP + 1, rank, LANES), F32),
             pltpu.VMEM((chunks, ff, width), BF16),
+            pltpu.VMEM((NX, rank, tokens // NX), F32),
             pltpu.SemaphoreType.DMA((chunks,)),
         ],
         limit=24, flops=8 * rank * ff * model, moved=2 * ff * model,
     )
-    right, gathered = lax.optimization_barrier((right, gathered))
+    right, gathered = lax.optimization_barrier((total(right, "dp", ALONG_DP[1:2]), gathered))
     halves = []
-    for part, level in enumerate(ALONG_DP[1:]):
+    for part, level in enumerate((ALONG_DP[2], ALONG_DP[0])):
         half = call(
             functools.partial(field_kernel, part * NMP // 2), array((NMP // 2, ff, LANES), F32), (gathered, et, gt),
             specs=[HBM] * 3,
@@ -446,7 +463,6 @@
         )
         right, half = lax.optimization_barrier((total(right, "dp", [level]), half))
         halves.append(half)
-    right = total(right, "dp", ALONG_DP[:1])
 
     block = array((ff, width), F32)
     outs = call(

time: 160 us -> 148 us (0.925)
  waiting for transfers between devices: 69.2 us -> 50 us
  starting transfers between devices: 43.9 us -> 52.4 us
    ppermute x22, waiting for transfers between devices: 68.5 us -> 49.3 us  [swap(): return lax.ppermute(value, axis, list(enumerate(level)))]
    ppermute x22, starting transfers between devices: 43.8 us -> 52.4 us  [swap(): return lax.ppermute(value, axis, list(enumerate(level)))]
    pallas_call x14 -> x15, Pallas kernels: 30.3 us -> 30 us  [call(): pl.pallas_call(kernel, out_shape=outs, in_specs=specs or [VMEM] * len(arg...]
  transfers between devices with their start and end apart: 23 -> 23, of which waited for: 18 -> 20; matrix products, arithmetic and copies ran while one was open for 0% -> 0% of each run, Pallas kernels for 16% -> 17%
where the time goes in v6:
time: 148 us
  starting transfers between devices  52.4 us (35%)
  waiting for transfers between devices  50 us (34%)
  Pallas kernels  30 us (20%)
  between operations  14.3 us (10%)
    ppermute x22, starting transfers between devices, swap(): return lax.ppermute(value, axis, list(enumerate(level)))  52.4 us
    ppermute x22, waiting for transfers between devices, swap(): return lax.ppermute(value, axis, list(enumerate(level)))  49.3 us
    pallas_call x15, Pallas kernels, call(): pl.pallas_call(kernel, out_shape=outs, in_specs=specs or [VMEM] * len(arg...  30 us
  transfers between devices with their start and end apart: 23, of which 20 were waited for; matrix products, arithmetic and copies ran while one was open for 0% of the time, Pallas kernels for 17%

profile of v6, /device:TPU:1, one launch (start us, length us, event | category | flops | bytes accessed | tf_op | source)
XLA Modules:
  0.0 147.8 jit_solution(1885353618329663850)
XLA Ops:
  8.0 4.7 %shard_map.129 = (f32[32,16,128]{2,1,0:T(8,128)}, f32[32,16,128]{2,1,0:T(8,128)}) custom-call(s32[1]{0:T(128)} %bitcast.1.member_ref, s32[1]{0:T(128)S(6)} %select_n.7.core_ref, s32[32,32]{1,0:T(8,128)} %constant.32.clone.place_ref, f32[32,448]{1,0:T(8,128)} %q_hbm.3, bf16[448,4096]{1,0:T(8,128)(2,1)} %bitcast.12), custom_call_target="tpu_custom_call" | custom-call | flops 352321536 | bytes 3670016 | tf_op jit(solution)/shard_map/pallas_call | solution.py:354
  12.7 3.3 %collective-permute-start = (f32[32,16,128]{2,1,0:T(8,128)}, f32[32,16,128]{2,1,0:T(8,128)S(1)}, u32[]{:S(2)}, u32[]{:S(2)}) collective-permute-start(f32[32,16,128]{2,1,0:T(8,128)} %get-tuple-element.34), channel_id=1, source_target_pairs={{0,32},{32,0},{64,96},{96,64},{128,160},{160,128},{192,224},{224,1... | collective-permute-start | bytes 786440 | tf_op jit(solution)/shard_map/ppermute | solution.py:366
  18.5 2.4 %collective-permute-start.3 = (bf16[1024,128]{1,0:T(8,128)(2,1)S(1)}, bf16[1024,128]{1,0:T(8,128)(2,1)S(1)}, u32[]{:S(2)}, u32[]{:S(2)}) collective-permute-start(bf16[1024,128]{1,0:T(8,128)(2,1)S(1)} %copy-done.2), channel_id=1, source_target_pairs={{0,24},{1,25},{2,26},{3,27},{4,28},{5,29},{6,30},{7,31},{8,16},{9,... | collective-permute-start | bytes 786440 | tf_op jit(solution)/shard_map/ppermute | solution.py:366
  20.9 5.1 %collective-permute-done.1.came = f32[64,8,128]{2,1,0:T(8,128)S(1)} collective-permute-done((f32[64,8,128]{2,1,0:T(8,128)S(1)}, f32[64,8,128]{2,1,0:T(8,128)S(1)}, u32[]{:S(2)}, u32[]{:S(2)}) %collective-permute-start.1) | collective-permute-done | bytes 262176 | tf_op jit(solution)/shard_map/ppermute | solution.py:366
  27.8 4.8 %collective-permute-start.4 = (f32[48,8,128]{2,1,0:T(8,128)S(1)}, f32[48,8,128]{2,1,0:T(8,128)S(1)}, u32[]{:S(2)}, u32[]{:S(2)}) collective-permute-start(f32[48,8,128]{2,1,0:T(8,128)S(1)} %get-tuple-element.38.sent), channel_id=1, source_target_pairs={{0,7},{1,2},{2,1},{3,4},{4,3},{5,6},{6,5},{7,0},{8,15},{9,10},{10,... | collective-permute-start | bytes 589832 | tf_op jit(solution)/shard_map/ppermute | solution.py:366
  33.0 3.4 %collective-permute-done.4.came = f32[48,8,128]{2,1,0:T(8,128)S(1)} collective-permute-done((f32[48,8,128]{2,1,0:T(8,128)S(1)}, f32[48,8,128]{2,1,0:T(8,128)S(1)}, u32[]{:S(2)}, u32[]{:S(2)}) %collective-permute-start.4) | collective-permute-done | bytes 196640 | tf_op jit(solution)/shard_map/ppermute | solution.py:366
  36.5 2.9 %collective-permute-start.5 = (f32[40,8,128]{2,1,0:T(8,128)S(1)}, f32[40,8,128]{2,1,0:T(8,128)S(1)}, u32[]{:S(2)}, u32[]{:S(2)}) collective-permute-start(f32[40,8,128]{2,1,0:T(8,128)S(1)} %get-tuple-element.40.sent), channel_id=1, source_target_pairs={{0,3},{1,6},{2,5},{3,0},{4,7},{5,2},{6,1},{7,4},{8,11},{9,14},{10,... | collective-permute-start | bytes 491528 | tf_op jit(solution)/shard_map/ppermute | solution.py:366
  40.1 8.4 %collective-permute-done.5.came = f32[40,8,128]{2,1,0:T(8,128)S(1)} collective-permute-done((f32[40,8,128]{2,1,0:T(8,128)S(1)}, f32[40,8,128]{2,1,0:T(8,128)S(1)}, u32[]{:S(2)}, u32[]{:S(2)}) %collective-permute-start.5) | collective-permute-done | bytes 163872 | tf_op jit(solution)/shard_map/ppermute | solution.py:366
  49.7 4.4 %collective-permute-start.7 = (f32[4,16,128]{2,1,0:T(8,128)S(1)}, f32[4,16,128]{2,1,0:T(8,128)S(1)}, u32[]{:S(2)}, u32[]{:S(2)}) collective-permute-start(f32[4,16,128]{2,1,0:T(8,128)S(1)} %get-tuple-element.45), channel_id=1, source_target_pairs={{0,32},{32,0},{64,96},{96,64},{128,160},{160,128},{192,224},{224,1... | collective-permute-start | bytes 98312 | tf_op jit(solution)/shard_map/ppermute | solution.py:366
  58.4 2.6 %collective-permute-start.9 = (f32[4,16,128]{2,1,0:T(8,128)S(1)}, f32[4,16,128]{2,1,0:T(8,128)S(1)}, u32[]{:S(2)}, u32[]{:S(2)}) collective-permute-start(f32[4,16,128]{2,1,0:T(8,128)S(1)} %add.32), channel_id=1, source_target_pairs={{0,24},{1,25},{2,26},{3,27},{4,28},{5,29},{6,30},{7,31},{8,16},{9,... | collective-permute-start | bytes 98312 | tf_op jit(solution)/shard_map/ppermute | solution.py:366
  65.3 2.9 %collective-permute-start.11 = (f32[4,16,128]{2,1,0:T(8,128)S(1)}, f32[4,16,128]{2,1,0:T(8,128)S(1)}, u32[]{:S(2)}, u32[]{:S(2)}) collective-permute-start(f32[4,16,128]{2,1,0:T(8,128)S(1)} %add.34), channel_id=1, source_target_pairs={{0,192},{32,224},{64,128},{96,160},{128,64},{160,96},{192,0},{224,... | collective-permute-start | bytes 98312 | tf_op jit(solution)/shard_map/ppermute | solution.py:366
  69.5 4.2 %collective-permute-start.12 = (f32[4,16,128]{2,1,0:T(8,128)S(1)}, f32[4,16,128]{2,1,0:T(8,128)S(1)}, u32[]{:S(2)}, u32[]{:S(2)}) collective-permute-start(f32[4,16,128]{2,1,0:T(8,128)S(1)} %add.35.mine), channel_id=1, source_target_pairs={{0,32},{32,0},{64,96},{96,64},{128,160},{160,128},{192,224},{224,1... | collective-permute-start | bytes 98312 | tf_op jit(solution)/shard_map/ppermute | solution.py:366
  75.6 3.3 %collective-permute-start.13 = (f32[10,8,128]{2,1,0:T(8,128)S(1)}, f32[10,8,128]{2,1,0:T(8,128)S(1)}, u32[]{:S(2)}, u32[]{:S(2)}) collective-permute-start(f32[10,8,128]{2,1,0:T(8,128)S(1)} %shard_map.134.sent), channel_id=1, source_target_pairs={{0,3},{1,6},{2,5},{3,0},{4,7},{5,2},{6,1},{7,4},{8,11},{9,14},{10,... | collective-permute-start | bytes 122888 | tf_op jit(solution)/shard_map/ppermute | solution.py:366
  80.5 2.7 %collective-permute-start.14 = (f32[12,8,128]{2,1,0:T(8,128)S(1)}, f32[12,8,128]{2,1,0:T(8,128)S(1)}, u32[]{:S(2)}, u32[]{:S(2)}) collective-permute-start(f32[12,8,128]{2,1,0:T(8,128)S(1)} %shard_map.135.sent), channel_id=1, source_target_pairs={{0,7},{1,2},{2,1},{3,4},{4,3},{5,6},{6,5},{7,0},{8,15},{9,10},{10,... | collective-permute-start | bytes 147464 | tf_op jit(solution)/shard_map/ppermute | solution.py:366
  85.6 4.9 %collective-permute-done.15.came = f32[16,8,128]{2,1,0:T(8,128)S(1)} collective-permute-done((f32[16,8,128]{2,1,0:T(8,128)S(1)}, f32[16,8,128]{2,1,0:T(8,128)S(1)}, u32[]{:S(2)}, u32[]{:S(2)}) %collective-permute-start.15) | collective-permute-done | bytes 65568 | tf_op jit(solution)/shard_map/ppermute | solution.py:366
  91.4 5.1 %collective-permute-done.16 = f32[24,8,128]{2,1,0:T(8,128)S(1)} collective-permute-done((f32[24,8,128]{2,1,0:T(8,128)S(1)}, f32[24,8,128]{2,1,0:T(8,128)S(1)}, u32[]{:S(2)}, u32[]{:S(2)}) %collective-permute-start.16) | collective-permute-done | bytes 98336 | tf_op jit(solution)/shard_map/ppermute | solution.py:366
  96.5 5.3 %collective-permute-start.17 = (f32[48,8,128]{2,1,0:T(8,128)S(1)}, f32[48,8,128]{2,1,0:T(8,128)S(1)}, u32[]{:S(2)}, u32[]{:S(2)}) collective-permute-start(f32[48,8,128]{2,1,0:T(8,128)S(1)} %pad_maximum_fusion.sent), channel_id=1, source_target_pairs={{0,24},{1,25},{2,26},{3,27},{4,28},{5,29},{6,30},{7,31},{8,16},{9,... | collective-permute-start | bytes 589832 | tf_op jit(solution)/shard_map/ppermute | solution.py:366
  101.8 4.9 %collective-permute-done.17.came = f32[48,8,128]{2,1,0:T(8,128)S(1)} collective-permute-done((f32[48,8,128]{2,1,0:T(8,128)S(1)}, f32[48,8,128]{2,1,0:T(8,128)S(1)}, u32[]{:S(2)}, u32[]{:S(2)}) %collective-permute-start.17) | collective-permute-done | bytes 196640 | tf_op jit(solution)/shard_map/ppermute | solution.py:366
  106.7 2.7 %collective-permute-start.18 = (f32[64,8,128]{2,1,0:T(8,128)S(1)}, f32[64,8,128]{2,1,0:T(8,128)S(1)}, u32[]{:S(2)}, u32[]{:S(2)}) collective-permute-start(f32[64,8,128]{2,1,0:T(8,128)S(1)} %get-tuple-element.46.mine), channel_id=1, source_target_pairs={{0,32},{32,0},{64,96},{96,64},{128,160},{160,128},{192,224},{224,1... | collective-permute-start | bytes 786440 | tf_op jit(solution)/shard_map/ppermute | solution.py:366
  110.6 9.4 %shard_map.139 = (bf16[32,96,128]{2,1,0:T(8,128)(2,1)S(1)}, f32[32,448]{1,0:T(8,128)S(1)}) custom-call(s32[1]{0:T(128)} %bitcast.1.member_ref, s32[1]{0:T(128)S(6)} %select_n.7.core_ref, s32[32,32]{1,0:T(8,128)S(1)} %copy-done.9, f32[64,8,128]{2,1,0:T(8,128)S(1)} %get-tuple-element.46.mine, f32[64,8,128]{2,1,0:T(8,128)S(1)} %collective-permute-done.18.theirs, ...), custom_call_target="tpu_custom_call" | custom-call | flops 469762048 | bytes 3670016 | tf_op jit(solution)/shard_map/pallas_call | solution.py:354
  123.2 2.8 %collective-permute-start.20 = (f32[32,448]{1,0:T(8,128)S(1)}, f32[32,448]{1,0:T(8,128)S(1)}, u32[]{:S(2)}, u32[]{:S(2)}) collective-permute-start(f32[32,448]{1,0:T(8,128)S(1)} %add.36), channel_id=1, source_target_pairs={{0,192},{32,224},{64,128},{96,160},{128,64},{160,96},{192,0},{224,... | collective-permute-start | bytes 172040 | tf_op jit(solution)/shard_map/ppermute | solution.py:366
  126.0 4.2 %shard_map.140.lower = f32[16,448,128]{2,1,0:T(8,128)S(1)} custom-call(bf16[32,1024,128]{2,1,0:T(8,128)(2,1)} %bitcast.23, bf16[448,4096]{1,0:T(8,128)(2,1)} %bitcast.13, bf16[448,1024]{1,0:T(8,128)(2,1)S(1)} %bitcast.18), custom_call_target="tpu_custom_call" | custom-call | flops 1879048192 | bytes 10485760 | tf_op jit(solution)/shard_map/pallas_call | solution.py:354
  132.2 4.2 %shard_map.141.upper = f32[16,448,128]{2,1,0:T(8,128)S(1)} custom-call(bf16[32,1024,128]{2,1,0:T(8,128)(2,1)} %bitcast.24, bf16[448,4096]{1,0:T(8,128)(2,1)} %bitcast.14, bf16[448,1024]{1,0:T(8,128)(2,1)S(1)} %bitcast.19), custom_call_target="tpu_custom_call" | custom-call | flops 1879048192 | bytes 10485760 | tf_op jit(solution)/shard_map/pallas_call | solution.py:354
  136.4 4.5 %shard_map.142 = (f32[448,512]{1,0:T(8,128)}, f32[448,512]{1,0:T(8,128)}, f32[448,512]{1,0:T(8,128)}, bf16[448,4096]{1,0:T(8,128)(2,1)}, f32[32,448]{1,0:T(8,128)}) custom-call(s32[1]{0:T(128)} %bitcast.dp_ref, f32[32,448]{1,0:T(8,128)S(1)} %add.38.sum_ref, bf16[32,96,128]{2,1,0:T(8,128)(2,1)S(1)} %get-tuple-element.53.basis_ref, ...), custom_call_target="tpu_custom_call" | custom-call | flops 704643072 | bytes 20971520 | tf_op jit(solution)/shard_map/pallas_call | solution.py:354
  (67 shorter events, 30.5 us)
Async XLA Ops:
  7.2 116.0 %all-gather.3.cloned.1.call-start = ((), (), s32[]{:S(2)}) async-start(), calls=%async_computation | async-start | bytes 8650752 | tf_op jit(solution)/shard_map/all_gather | solution.py:385
  8.0 102.6 %copy-start.9 = (s32[32,32]{1,0:T(8,128)S(1)}, s32[32,32]{1,0:T(8,128)}, u32[]{:S(2)}) copy-start(s32[32,32]{1,0:T(8,128)} %constant.33.clone.place_ref) | copy-start | bytes 12292
  12.7 4.7 %collective-permute-start = (f32[32,16,128]{2,1,0:T(8,128)}, f32[32,16,128]{2,1,0:T(8,128)S(1)}, u32[]{:S(2)}, u32[]{:S(2)}) collective-permute-start(f32[32,16,128]{2,1,0:T(8,128)} %get-tuple-element.34), channel_id=1, source_target_pairs={{0,32},{32,0},{64,96},{96,64},{128,160},{160,128},{192,224},{224,1... | collective-permute-start | bytes 786440 | tf_op jit(solution)/shard_map/ppermute | solution.py:366
  18.4 7.6 %collective-permute-start.1 = (f32[64,8,128]{2,1,0:T(8,128)S(1)}, f32[64,8,128]{2,1,0:T(8,128)S(1)}, u32[]{:S(2)}, u32[]{:S(2)}) collective-permute-start(f32[64,8,128]{2,1,0:T(8,128)S(1)} %get-tuple-element.35.sent), channel_id=1, source_target_pairs={{0,1},{1,0},{2,3},{3,2},{4,5},{5,4},{6,7},{7,6},{8,9},{9,8},{10,11... | collective-permute-start | bytes 786440 | tf_op jit(solution)/shard_map/ppermute | solution.py:366
  18.5 8.7 %collective-permute-start.3 = (bf16[1024,128]{1,0:T(8,128)(2,1)S(1)}, bf16[1024,128]{1,0:T(8,128)(2,1)S(1)}, u32[]{:S(2)}, u32[]{:S(2)}) collective-permute-start(bf16[1024,128]{1,0:T(8,128)(2,1)S(1)} %copy-done.2), channel_id=1, source_target_pairs={{0,24},{1,25},{2,26},{3,27},{4,28},{5,29},{6,30},{7,31},{8,16},{9,... | collective-permute-start | bytes 786440 | tf_op jit(solution)/shard_map/ppermute | solution.py:366
  20.9 6.9 %collective-permute-start.2 = (bf16[1024,128]{1,0:T(8,128)(2,1)S(1)}, bf16[1024,128]{1,0:T(8,128)(2,1)S(1)}, u32[]{:S(2)}, u32[]{:S(2)}) collective-permute-start(bf16[1024,128]{1,0:T(8,128)(2,1)S(1)} %copy-done.2), channel_id=1, source_target_pairs={{0,8},{1,9},{2,10},{3,11},{4,12},{5,13},{6,14},{7,15},{8,0},{9,1},... | collective-permute-start | bytes 786440 | tf_op jit(solution)/shard_map/ppermute | solution.py:366
  27.8 8.7 %collective-permute-start.4 = (f32[48,8,128]{2,1,0:T(8,128)S(1)}, f32[48,8,128]{2,1,0:T(8,128)S(1)}, u32[]{:S(2)}, u32[]{:S(2)}) collective-permute-start(f32[48,8,128]{2,1,0:T(8,128)S(1)} %get-tuple-element.38.sent), channel_id=1, source_target_pairs={{0,7},{1,2},{2,1},{3,4},{4,3},{5,6},{6,5},{7,0},{8,15},{9,10},{10,... | collective-permute-start | bytes 589832 | tf_op jit(solution)/shard_map/ppermute | solution.py:366
  32.5 7.6 %collective-permute-start.6 = (bf16[1024,128]{1,0:T(8,128)(2,1)S(1)}, bf16[1024,128]{1,0:T(8,128)(2,1)S(1)}, u32[]{:S(2)}, u32[]{:S(2)}) collective-permute-start(bf16[1024,128]{1,0:T(8,128)(2,1)S(1)} %copy-done.2), channel_id=1, source_target_pairs={{0,16},{1,17},{2,18},{3,19},{4,20},{5,21},{6,22},{7,23},{8,24},{9,... | collective-permute-start | bytes 786440 | tf_op jit(solution)/shard_map/ppermute | solution.py:366
  36.5 12.1 %collective-permute-start.5 = (f32[40,8,128]{2,1,0:T(8,128)S(1)}, f32[40,8,128]{2,1,0:T(8,128)S(1)}, u32[]{:S(2)}, u32[]{:S(2)}) collective-permute-start(f32[40,8,128]{2,1,0:T(8,128)S(1)} %get-tuple-element.40.sent), channel_id=1, source_target_pairs={{0,3},{1,6},{2,5},{3,0},{4,7},{5,2},{6,1},{7,4},{8,11},{9,14},{10,... | collective-permute-start | bytes 491528 | tf_op jit(solution)/shard_map/ppermute | solution.py:366
  49.7 5.3 %collective-permute-start.7 = (f32[4,16,128]{2,1,0:T(8,128)S(1)}, f32[4,16,128]{2,1,0:T(8,128)S(1)}, u32[]{:S(2)}, u32[]{:S(2)}) collective-permute-start(f32[4,16,128]{2,1,0:T(8,128)S(1)} %get-tuple-element.45), channel_id=1, source_target_pairs={{0,32},{32,0},{64,96},{96,64},{128,160},{160,128},{192,224},{224,1... | collective-permute-start | bytes 98312 | tf_op jit(solution)/shard_map/ppermute | solution.py:366
  55.0 3.3 %collective-permute-start.8 = (f32[4,16,128]{2,1,0:T(8,128)S(1)}, f32[4,16,128]{2,1,0:T(8,128)S(1)}, u32[]{:S(2)}, u32[]{:S(2)}) collective-permute-start(f32[4,16,128]{2,1,0:T(8,128)S(1)} %add.31), channel_id=1, source_target_pairs={{0,8},{1,9},{2,10},{3,11},{4,12},{5,13},{6,14},{7,15},{8,0},{9,1},... | collective-permute-start | bytes 98312 | tf_op jit(solution)/shard_map/ppermute | solution.py:366
  58.4 4.0 %collective-permute-start.9 = (f32[4,16,128]{2,1,0:T(8,128)S(1)}, f32[4,16,128]{2,1,0:T(8,128)S(1)}, u32[]{:S(2)}, u32[]{:S(2)}) collective-permute-start(f32[4,16,128]{2,1,0:T(8,128)S(1)} %add.32), channel_id=1, source_target_pairs={{0,24},{1,25},{2,26},{3,27},{4,28},{5,29},{6,30},{7,31},{8,16},{9,... | collective-permute-start | bytes 98312 | tf_op jit(solution)/shard_map/ppermute | solution.py:366
  62.3 3.0 %collective-permute-start.10 = (f32[4,16,128]{2,1,0:T(8,128)S(1)}, f32[4,16,128]{2,1,0:T(8,128)S(1)}, u32[]{:S(2)}, u32[]{:S(2)}) collective-permute-start(f32[4,16,128]{2,1,0:T(8,128)S(1)} %add.33), channel_id=1, source_target_pairs={{0,64},{32,96},{64,0},{96,32},{128,192},{160,224},{192,128},{224,1... | collective-permute-start | bytes 98312 | tf_op jit(solution)/shard_map/ppermute | solution.py:366
  65.3 4.2 %collective-permute-start.11 = (f32[4,16,128]{2,1,0:T(8,128)S(1)}, f32[4,16,128]{2,1,0:T(8,128)S(1)}, u32[]{:S(2)}, u32[]{:S(2)}) collective-permute-start(f32[4,16,128]{2,1,0:T(8,128)S(1)} %add.34), channel_id=1, source_target_pairs={{0,192},{32,224},{64,128},{96,160},{128,64},{160,96},{192,0},{224,... | collective-permute-start | bytes 98312 | tf_op jit(solution)/shard_map/ppermute | solution.py:366
  69.5 5.0 %collective-permute-start.12 = (f32[4,16,128]{2,1,0:T(8,128)S(1)}, f32[4,16,128]{2,1,0:T(8,128)S(1)}, u32[]{:S(2)}, u32[]{:S(2)}) collective-permute-start(f32[4,16,128]{2,1,0:T(8,128)S(1)} %add.35.mine), channel_id=1, source_target_pairs={{0,32},{32,0},{64,96},{96,64},{128,160},{160,128},{192,224},{224,1... | collective-permute-start | bytes 98312 | tf_op jit(solution)/shard_map/ppermute | solution.py:366
  75.6 4.9 %collective-permute-start.13 = (f32[10,8,128]{2,1,0:T(8,128)S(1)}, f32[10,8,128]{2,1,0:T(8,128)S(1)}, u32[]{:S(2)}, u32[]{:S(2)}) collective-permute-start(f32[10,8,128]{2,1,0:T(8,128)S(1)} %shard_map.134.sent), channel_id=1, source_target_pairs={{0,3},{1,6},{2,5},{3,0},{4,7},{5,2},{6,1},{7,4},{8,11},{9,14},{10,... | collective-permute-start | bytes 122888 | tf_op jit(solution)/shard_map/ppermute | solution.py:366
  80.5 5.0 %collective-permute-start.14 = (f32[12,8,128]{2,1,0:T(8,128)S(1)}, f32[12,8,128]{2,1,0:T(8,128)S(1)}, u32[]{:S(2)}, u32[]{:S(2)}) collective-permute-start(f32[12,8,128]{2,1,0:T(8,128)S(1)} %shard_map.135.sent), channel_id=1, source_target_pairs={{0,7},{1,2},{2,1},{3,4},{4,3},{5,6},{6,5},{7,0},{8,15},{9,10},{10,... | collective-permute-start | bytes 147464 | tf_op jit(solution)/shard_map/ppermute | solution.py:366
  85.5 5.0 %collective-permute-start.15 = (f32[16,8,128]{2,1,0:T(8,128)S(1)}, f32[16,8,128]{2,1,0:T(8,128)S(1)}, u32[]{:S(2)}, u32[]{:S(2)}) collective-permute-start(f32[16,8,128]{2,1,0:T(8,128)S(1)} %shard_map.136.sent), channel_id=1, source_target_pairs={{0,1},{1,0},{2,3},{3,2},{4,5},{5,4},{6,7},{7,6},{8,9},{9,8},{10,11... | collective-permute-start | bytes 196616 | tf_op jit(solution)/shard_map/ppermute | solution.py:366
  90.5 6.0 %collective-permute-start.16 = (f32[24,8,128]{2,1,0:T(8,128)S(1)}, f32[24,8,128]{2,1,0:T(8,128)S(1)}, u32[]{:S(2)}, u32[]{:S(2)}) collective-permute-start(f32[24,8,128]{2,1,0:T(8,128)S(1)} %shard_map.137), channel_id=1, source_target_pairs={{0,8},{1,9},{2,10},{3,11},{4,12},{5,13},{6,14},{7,15},{8,0},{9,1},... | collective-permute-start | bytes 294920 | tf_op jit(solution)/shard_map/ppermute | solution.py:366
  96.5 10.1 %collective-permute-start.17 = (f32[48,8,128]{2,1,0:T(8,128)S(1)}, f32[48,8,128]{2,1,0:T(8,128)S(1)}, u32[]{:S(2)}, u32[]{:S(2)}) collective-permute-start(f32[48,8,128]{2,1,0:T(8,128)S(1)} %pad_maximum_fusion.sent), channel_id=1, source_target_pairs={{0,24},{1,25},{2,26},{3,27},{4,28},{5,29},{6,30},{7,31},{8,16},{9,... | collective-permute-start | bytes 589832 | tf_op jit(solution)/shard_map/ppermute | solution.py:366
  106.7 3.9 %collective-permute-start.18 = (f32[64,8,128]{2,1,0:T(8,128)S(1)}, f32[64,8,128]{2,1,0:T(8,128)S(1)}, u32[]{:S(2)}, u32[]{:S(2)}) collective-permute-start(f32[64,8,128]{2,1,0:T(8,128)S(1)} %get-tuple-element.46.mine), channel_id=1, source_target_pairs={{0,32},{32,0},{64,96},{96,64},{128,160},{160,128},{192,224},{224,1... | collective-permute-start | bytes 786440 | tf_op jit(solution)/shard_map/ppermute | solution.py:366
  120.0 3.2 %collective-permute-start.19 = (f32[32,448]{1,0:T(8,128)S(1)}, f32[32,448]{1,0:T(8,128)S(1)}, u32[]{:S(2)}, u32[]{:S(2)}) collective-permute-start(f32[32,448]{1,0:T(8,128)S(1)} %get-tuple-element.48), channel_id=1, source_target_pairs={{0,64},{32,96},{64,0},{96,32},{128,192},{160,224},{192,128},{224,1... | collective-permute-start | bytes 172040 | tf_op jit(solution)/shard_map/ppermute | solution.py:366
  123.2 7.0 %collective-permute-start.20 = (f32[32,448]{1,0:T(8,128)S(1)}, f32[32,448]{1,0:T(8,128)S(1)}, u32[]{:S(2)}, u32[]{:S(2)}) collective-permute-start(f32[32,448]{1,0:T(8,128)S(1)} %add.36), channel_id=1, source_target_pairs={{0,192},{32,224},{64,128},{96,160},{128,64},{160,96},{192,0},{224,... | collective-permute-start | bytes 172040 | tf_op jit(solution)/shard_map/ppermute | solution.py:366
  130.3 6.1 %collective-permute-start.21 = (f32[32,448]{1,0:T(8,128)S(1)}, f32[32,448]{1,0:T(8,128)S(1)}, u32[]{:S(2)}, u32[]{:S(2)}) collective-permute-start(f32[32,448]{1,0:T(8,128)S(1)} %add.37), channel_id=1, source_target_pairs={{0,32},{32,0},{64,96},{96,64},{128,160},{160,128},{192,224},{224,1... | collective-permute-start | bytes 172040 | tf_op jit(solution)/shard_map/ppermute | solution.py:366
  (9 other events, 187.8 us)
Sparse Core Ops, SparseCore 0:
  10.6 104.6 all-gather.2

commit v7 on v6

--- a/solution.py
+++ b/solution.py
@@ -222,6 +222,21 @@
     square = panel.shape[1:]
     same = lax.broadcasted_iota(jnp.int32, square, 0) == lax.broadcasted_iota(jnp.int32, square, 1)
     panel[NMP] = jnp.where(same, 1.0, 0.0)
+    columns = factors.shape[2] // LANES
+    for place in range(NX):
+        tiles = tokens.at[pl.ds(place * QUARTER, QUARTER)]
+        factors[lax.div(place_ref[member, place * NZ], NZ)] = jnp.concatenate(
+            [rows_of(tiles, column, columns, FACTOR) for column in range(columns)], axis=1
+        )
+    factor = jnp.concatenate([factors[x] for x in range(NX)], axis=1)
+    grads = fold3(dot_nt(split3(factor), gt_ref[...]))
+    for copy in copies:
+        copy.wait()
+    total = None
+    for chunk in range(chunks):
+        part = dot_nt(et_ref[chunk], split3(wide(panel, chunk, width)))
+        total = part if total is None else total + part
+    grads = grads + fold3(total.T)
     blocks, count = NMP, panel.shape[1]
     groups = count // 8
 
@@ -256,24 +271,11 @@
             panel[block, index : index + 1, :] = row * scale
     for block in range(blocks):
         split[block] = split3(panel[block])
-    columns = factors.shape[2] // LANES
-    for place in range(NX):
-        tiles = tokens.at[pl.ds(place * QUARTER, QUARTER)]
-        factors[lax.div(place_ref[member, place * NZ], NZ)] = jnp.concatenate(
-            [rows_of(tiles, column, columns, FACTOR) for column in range(columns)], axis=1
-        )
-    factor = jnp.concatenate([factors[x] for x in range(NX)], axis=1)
-    grads = fold3(dot_nt(split3(factor), gt_ref[...]))
-    total = None
-    for chunk in range(chunks):
-        copies[chunk].wait()
-        part = dot_nt(et_ref[chunk], wide(split, chunk, width))
-        total = part if total is None else total + part
     turned = lax.dot_general(
         panel[NMP][:, :count], grads, (((1,), (0,)), ((), ())), precision=lax.Precision.HIGHEST,
         preferred_element_type=F32,
     )
-    right[...] = turned + fold3(total.T)
+    right[...] = turned
 
 
 def wide(ref, chunk, width):
@@ -384,6 +386,9 @@
 
     gathered = lax.all_gather(acts, "mp", axis=0)
 
+    ring = [acts] + [swap(acts, "mp", level) for level in ALONG_X]
+    ring.append(swap(acts, "mp", [(x + 2) % NX * NZ + z for x in range(NX) for z in range(NZ)]))
+
     half = rank // 2
     table = jnp.asarray(met(ALONG_X + ALONG_Z, NMP))
     blocks = array((NMP, half, LANES), F32)
@@ -401,18 +406,17 @@
         scratch=[pltpu.VMEM((rank, ff), F32), pltpu.VMEM((ff, tokens), BF16), pltpu.SemaphoreType.DMA((2,))],
         limit=16, flops=6 * rank * ff * tokens, moved=2 * ff * tokens,
     )
+    theirs, factor, ring[1:3] = lax.optimization_barrier((theirs, factor, ring[1:3]))
     count = NMP // 2
     message = lambda tiles: array((FACTOR + tiles, 8, LANES), F32)
     kept = lambda count: array((count, half, LANES), F32)
     sent, keep = call(open_kernel, [message(2 * count), kept(count)], (factor, mine, theirs), moved=MIB)
-    ring = [acts] + [swap(acts, "mp", level) for level in ALONG_X]
-    ring.append(swap(acts, "mp", [(x + 2) % NX * NZ + z for x in range(NX) for z in range(NZ)]))
     for place, level in enumerate(ALONG_Z[:0:-1]):
         came = swap(sent, "mp", level)
         count //= 2
         sent, keep = call(halve_kernel, [message(2 * count), kept(count)], (sent, keep, came), moved=MIB)
         if place == 0:
-            sent, ring[1:3] = lax.optimization_barrier((sent, ring[1:3]))
+            sent, ring[3] = lax.optimization_barrier((sent, ring[3]))
     came = swap(sent, "mp", ALONG_Z[0])
 
     keep, send = call(

time: 148 us -> 149 us (level)
  waiting for transfers between devices: 50 us -> 52.4 us
    ppermute x22, waiting for transfers between devices: 49.3 us -> 51.7 us  [swap(): return lax.ppermute(value, axis, list(enumerate(level)))]
  transfers between devices with their start and end apart: 23 -> 23, of which waited for: 20 -> 19; matrix products, arithmetic and copies ran while one was open for 0% -> 0% of each run, Pallas kernels for 17% -> 16%
where the time goes in v7:
time: 149 us
  starting transfers between devices  52.8 us (35%)
  waiting for transfers between devices  52.4 us (35%)
  Pallas kernels  28.6 us (19%)
  between operations  14.3 us (10%)
    ppermute x22, starting transfers between devices, swap(): return lax.ppermute(value, axis, list(enumerate(level)))  52.8 us
    ppermute x22, waiting for transfers between devices, swap(): return lax.ppermute(value, axis, list(enumerate(level)))  51.7 us
    pallas_call x15, Pallas kernels, call(): pl.pallas_call(kernel, out_shape=outs, in_specs=specs or [VMEM] * len(arg...  28.6 us
  transfers between devices with their start and end apart: 23, of which 19 were waited for; matrix products, arithmetic and copies ran while one was open for 0% of the time, Pallas kernels for 16%

profile of v7, /device:TPU:1, one launch (start us, length us, event | category | flops | bytes accessed | tf_op | source)
XLA Modules:
  0.0 149.2 jit_solution(10110028720980858638)
XLA Ops:
  7.9 3.4 %collective-permute-start.2 = (bf16[1024,128]{1,0:T(8,128)(2,1)}, bf16[1024,128]{1,0:T(8,128)(2,1)S(1)}, u32[]{:S(2)}, u32[]{:S(2)}) collective-permute-start(bf16[1024,128]{1,0:T(8,128)(2,1)} %refs_0_.3), channel_id=1, source_target_pairs={{0,24},{1,25},{2,26},{3,27},{4,28},{5,29},{6,30},{7,31},{8,16},{9,... | collective-permute-start | bytes 786440 | tf_op jit(solution)/shard_map/ppermute | solution.py:368
  11.3 4.7 %shard_map.128 = (f32[32,16,128]{2,1,0:T(8,128)}, f32[32,16,128]{2,1,0:T(8,128)}) custom-call(s32[1]{0:T(128)} %bitcast.1.member_ref, s32[1]{0:T(128)S(6)} %select_n.7.core_ref, s32[32,32]{1,0:T(8,128)} %constant.32.clone.place_ref, f32[32,448]{1,0:T(8,128)} %q_hbm.3, bf16[448,4096]{1,0:T(8,128)(2,1)} %bitcast.12), custom_call_target="tpu_custom_call" | custom-call | flops 352321536 | bytes 3670016 | tf_op jit(solution)/shard_map/pallas_call | solution.py:356
  23.1 3.3 %collective-permute-done.3.came = f32[64,8,128]{2,1,0:T(8,128)S(1)} collective-permute-done((f32[64,8,128]{2,1,0:T(8,128)S(1)}, f32[64,8,128]{2,1,0:T(8,128)S(1)}, u32[]{:S(2)}, u32[]{:S(2)}) %collective-permute-start.3) | collective-permute-done | bytes 262176 | tf_op jit(solution)/shard_map/ppermute | solution.py:368
  26.4 2.5 %collective-permute-done.4.refs_3_ = bf16[1024,128]{1,0:T(8,128)(2,1)S(1)} collective-permute-done((bf16[1024,128]{1,0:T(8,128)(2,1)S(1)}, bf16[1024,128]{1,0:T(8,128)(2,1)S(1)}, u32[]{:S(2)}, u32[]{:S(2)}) %collective-permute-start.4) | collective-permute-done | bytes 262176 | tf_op jit(solution)/shard_map/ppermute | solution.py:368
  28.9 4.7 %collective-permute-start.5 = (f32[48,8,128]{2,1,0:T(8,128)S(1)}, f32[48,8,128]{2,1,0:T(8,128)S(1)}, u32[]{:S(2)}, u32[]{:S(2)}) collective-permute-start(f32[48,8,128]{2,1,0:T(8,128)S(1)} %get-tuple-element.43.sent), channel_id=1, source_target_pairs={{0,7},{1,2},{2,1},{3,4},{4,3},{5,6},{6,5},{7,0},{8,15},{9,10},{10,... | collective-permute-start | bytes 589832 | tf_op jit(solution)/shard_map/ppermute | solution.py:368
  33.6 3.3 %collective-permute-done.5.came = f32[48,8,128]{2,1,0:T(8,128)S(1)} collective-permute-done((f32[48,8,128]{2,1,0:T(8,128)S(1)}, f32[48,8,128]{2,1,0:T(8,128)S(1)}, u32[]{:S(2)}, u32[]{:S(2)}) %collective-permute-start.5) | collective-permute-done | bytes 196640 | tf_op jit(solution)/shard_map/ppermute | solution.py:368
  39.4 7.4 %collective-permute-done.6.came = f32[40,8,128]{2,1,0:T(8,128)S(1)} collective-permute-done((f32[40,8,128]{2,1,0:T(8,128)S(1)}, f32[40,8,128]{2,1,0:T(8,128)S(1)}, u32[]{:S(2)}, u32[]{:S(2)}) %collective-permute-start.6) | collective-permute-done | bytes 163872 | tf_op jit(solution)/shard_map/ppermute | solution.py:368
  47.9 8.8 %collective-permute-start.7 = (f32[4,16,128]{2,1,0:T(8,128)S(1)}, f32[4,16,128]{2,1,0:T(8,128)S(1)}, u32[]{:S(2)}, u32[]{:S(2)}) collective-permute-start(f32[4,16,128]{2,1,0:T(8,128)S(1)} %get-tuple-element.51), channel_id=1, source_target_pairs={{0,32},{32,0},{64,96},{96,64},{128,160},{160,128},{192,224},{224,1... | collective-permute-start | bytes 98312 | tf_op jit(solution)/shard_map/ppermute | solution.py:368
  57.6 3.4 %collective-permute-start.8 = (f32[4,16,128]{2,1,0:T(8,128)S(1)}, f32[4,16,128]{2,1,0:T(8,128)S(1)}, u32[]{:S(2)}, u32[]{:S(2)}) collective-permute-start(f32[4,16,128]{2,1,0:T(8,128)S(1)} %add.31), channel_id=1, source_target_pairs={{0,8},{1,9},{2,10},{3,11},{4,12},{5,13},{6,14},{7,15},{8,0},{9,1},... | collective-permute-start | bytes 98312 | tf_op jit(solution)/shard_map/ppermute | solution.py:368
  62.9 3.4 %collective-permute-done.9 = f32[4,16,128]{2,1,0:T(8,128)S(1)} collective-permute-done((f32[4,16,128]{2,1,0:T(8,128)S(1)}, f32[4,16,128]{2,1,0:T(8,128)S(1)}, u32[]{:S(2)}, u32[]{:S(2)}) %collective-permute-start.9) | collective-permute-done | bytes 32800 | tf_op jit(solution)/shard_map/ppermute | solution.py:368
  69.0 3.1 %collective-permute-start.11 = (f32[4,16,128]{2,1,0:T(8,128)S(1)}, f32[4,16,128]{2,1,0:T(8,128)S(1)}, u32[]{:S(2)}, u32[]{:S(2)}) collective-permute-start(f32[4,16,128]{2,1,0:T(8,128)S(1)} %add.34), channel_id=1, source_target_pairs={{0,192},{32,224},{64,128},{96,160},{128,64},{160,96},{192,0},{224,... | collective-permute-start | bytes 98312 | tf_op jit(solution)/shard_map/ppermute | solution.py:368
  73.8 3.8 %collective-permute-start.12 = (f32[4,16,128]{2,1,0:T(8,128)S(1)}, f32[4,16,128]{2,1,0:T(8,128)S(1)}, u32[]{:S(2)}, u32[]{:S(2)}) collective-permute-start(f32[4,16,128]{2,1,0:T(8,128)S(1)} %add.35.mine), channel_id=1, source_target_pairs={{0,32},{32,0},{64,96},{96,64},{128,160},{160,128},{192,224},{224,1... | collective-permute-start | bytes 98312 | tf_op jit(solution)/shard_map/ppermute | solution.py:368
  81.8 2.9 %collective-permute-done.13.came = f32[10,8,128]{2,1,0:T(8,128)S(1)} collective-permute-done((f32[10,8,128]{2,1,0:T(8,128)S(1)}, f32[10,8,128]{2,1,0:T(8,128)S(1)}, u32[]{:S(2)}, u32[]{:S(2)}) %collective-permute-start.13) | collective-permute-done | bytes 40992 | tf_op jit(solution)/shard_map/ppermute | solution.py:368
  84.7 3.5 %collective-permute-start.14 = (f32[12,8,128]{2,1,0:T(8,128)S(1)}, f32[12,8,128]{2,1,0:T(8,128)S(1)}, u32[]{:S(2)}, u32[]{:S(2)}) collective-permute-start(f32[12,8,128]{2,1,0:T(8,128)S(1)} %shard_map.135.sent), channel_id=1, source_target_pairs={{0,7},{1,2},{2,1},{3,4},{4,3},{5,6},{6,5},{7,0},{8,15},{9,10},{10,... | collective-permute-start | bytes 147464 | tf_op jit(solution)/shard_map/ppermute | solution.py:368
  88.2 2.9 %collective-permute-done.14.came = f32[12,8,128]{2,1,0:T(8,128)S(1)} collective-permute-done((f32[12,8,128]{2,1,0:T(8,128)S(1)}, f32[12,8,128]{2,1,0:T(8,128)S(1)}, u32[]{:S(2)}, u32[]{:S(2)}) %collective-permute-start.14) | collective-permute-done | bytes 49184 | tf_op jit(solution)/shard_map/ppermute | solution.py:368
  91.2 4.8 %collective-permute-done.15.came = f32[16,8,128]{2,1,0:T(8,128)S(1)} collective-permute-done((f32[16,8,128]{2,1,0:T(8,128)S(1)}, f32[16,8,128]{2,1,0:T(8,128)S(1)}, u32[]{:S(2)}, u32[]{:S(2)}) %collective-permute-start.15) | collective-permute-done | bytes 65568 | tf_op jit(solution)/shard_map/ppermute | solution.py:368
  96.2 6.0 %collective-permute-done.16 = f32[24,8,128]{2,1,0:T(8,128)S(1)} collective-permute-done((f32[24,8,128]{2,1,0:T(8,128)S(1)}, f32[24,8,128]{2,1,0:T(8,128)S(1)}, u32[]{:S(2)}, u32[]{:S(2)}) %collective-permute-start.16) | collective-permute-done | bytes 98336 | tf_op jit(solution)/shard_map/ppermute | solution.py:368
  103.6 4.8 %collective-permute-done.17.came = f32[48,8,128]{2,1,0:T(8,128)S(1)} collective-permute-done((f32[48,8,128]{2,1,0:T(8,128)S(1)}, f32[48,8,128]{2,1,0:T(8,128)S(1)}, u32[]{:S(2)}, u32[]{:S(2)}) %collective-permute-start.17) | collective-permute-done | bytes 196640 | tf_op jit(solution)/shard_map/ppermute | solution.py:368
  108.4 4.1 %collective-permute-start.18 = (f32[64,8,128]{2,1,0:T(8,128)S(1)}, f32[64,8,128]{2,1,0:T(8,128)S(1)}, u32[]{:S(2)}, u32[]{:S(2)}) collective-permute-start(f32[64,8,128]{2,1,0:T(8,128)S(1)} %get-tuple-element.52.mine), channel_id=1, source_target_pairs={{0,32},{32,0},{64,96},{96,64},{128,160},{160,128},{192,224},{224,1... | collective-permute-start | bytes 786440 | tf_op jit(solution)/shard_map/ppermute | solution.py:368
  113.6 8.0 %shard_map.139 = (bf16[32,96,128]{2,1,0:T(8,128)(2,1)S(1)}, f32[32,448]{1,0:T(8,128)S(1)}) custom-call(s32[1]{0:T(128)} %bitcast.1.member_ref, s32[1]{0:T(128)S(6)} %select_n.7.core_ref, s32[32,32]{1,0:T(8,128)S(1)} %copy-done.9, f32[64,8,128]{2,1,0:T(8,128)S(1)} %get-tuple-element.52.mine, f32[64,8,128]{2,1,0:T(8,128)S(1)} %collective-permute-done.18.theirs, ...), custom_call_target="tpu_custom_call" | custom-call | flops 469762048 | bytes 3670016 | tf_op jit(solution)/shard_map/pallas_call | solution.py:356
  122.3 2.5 %collective-permute-done.19 = f32[32,448]{1,0:T(8,128)S(1)} collective-permute-done((f32[32,448]{1,0:T(8,128)S(1)}, f32[32,448]{1,0:T(8,128)S(1)}, u32[]{:S(2)}, u32[]{:S(2)}) %collective-permute-start.19) | collective-permute-done | bytes 57376 | tf_op jit(solution)/shard_map/ppermute | solution.py:368
  127.3 4.2 %shard_map.140.lower = f32[16,448,128]{2,1,0:T(8,128)S(1)} custom-call(bf16[32,1024,128]{2,1,0:T(8,128)(2,1)} %bitcast.23, bf16[448,4096]{1,0:T(8,128)(2,1)} %bitcast.13, bf16[448,1024]{1,0:T(8,128)(2,1)S(1)} %bitcast.18), custom_call_target="tpu_custom_call" | custom-call | flops 1879048192 | bytes 10485760 | tf_op jit(solution)/shard_map/pallas_call | solution.py:356
  133.5 4.2 %shard_map.141.upper = f32[16,448,128]{2,1,0:T(8,128)S(1)} custom-call(bf16[32,1024,128]{2,1,0:T(8,128)(2,1)} %bitcast.24, bf16[448,4096]{1,0:T(8,128)(2,1)} %bitcast.14, bf16[448,1024]{1,0:T(8,128)(2,1)S(1)} %bitcast.19), custom_call_target="tpu_custom_call" | custom-call | flops 1879048192 | bytes 10485760 | tf_op jit(solution)/shard_map/pallas_call | solution.py:356
  137.8 4.5 %shard_map.142 = (f32[448,512]{1,0:T(8,128)}, f32[448,512]{1,0:T(8,128)}, f32[448,512]{1,0:T(8,128)}, bf16[448,4096]{1,0:T(8,128)(2,1)}, f32[32,448]{1,0:T(8,128)}) custom-call(s32[1]{0:T(128)} %bitcast.dp_ref, f32[32,448]{1,0:T(8,128)S(1)} %add.38.sum_ref, bf16[32,96,128]{2,1,0:T(8,128)(2,1)S(1)} %get-tuple-element.59.basis_ref, ...), custom_call_target="tpu_custom_call" | custom-call | flops 704643072 | bytes 20971520 | tf_op jit(solution)/shard_map/pallas_call | solution.py:356
  (67 shorter events, 30.8 us)
Async XLA Ops:
  7.2 117.7 %all-gather.3.cloned.1.call-start = ((), (), s32[]{:S(2)}) async-start(), calls=%async_computation | async-start | bytes 8650752 | tf_op jit(solution)/shard_map/all_gather | solution.py:387
  7.9 10.0 %collective-permute-start.2 = (bf16[1024,128]{1,0:T(8,128)(2,1)}, bf16[1024,128]{1,0:T(8,128)(2,1)S(1)}, u32[]{:S(2)}, u32[]{:S(2)}) collective-permute-start(bf16[1024,128]{1,0:T(8,128)(2,1)} %refs_0_.3), channel_id=1, source_target_pairs={{0,24},{1,25},{2,26},{3,27},{4,28},{5,29},{6,30},{7,31},{8,16},{9,... | collective-permute-start | bytes 786440 | tf_op jit(solution)/shard_map/ppermute | solution.py:368
  11.3 7.1 %collective-permute-start.1 = (bf16[1024,128]{1,0:T(8,128)(2,1)}, bf16[1024,128]{1,0:T(8,128)(2,1)S(1)}, u32[]{:S(2)}, u32[]{:S(2)}) collective-permute-start(bf16[1024,128]{1,0:T(8,128)(2,1)} %refs_0_.3), channel_id=1, source_target_pairs={{0,8},{1,9},{2,10},{3,11},{4,12},{5,13},{6,14},{7,15},{8,0},{9,1},... | collective-permute-start | bytes 786440 | tf_op jit(solution)/shard_map/ppermute | solution.py:368
  11.3 102.3 %copy-start.9 = (s32[32,32]{1,0:T(8,128)S(1)}, s32[32,32]{1,0:T(8,128)}, u32[]{:S(2)}) copy-start(s32[32,32]{1,0:T(8,128)} %constant.33.clone.place_ref) | copy-start | bytes 12292
  16.1 2.6 %collective-permute-start = (f32[32,16,128]{2,1,0:T(8,128)}, f32[32,16,128]{2,1,0:T(8,128)S(1)}, u32[]{:S(2)}, u32[]{:S(2)}) collective-permute-start(f32[32,16,128]{2,1,0:T(8,128)} %get-tuple-element.36), channel_id=1, source_target_pairs={{0,32},{32,0},{64,96},{96,64},{128,160},{160,128},{192,224},{224,1... | collective-permute-start | bytes 786440 | tf_op jit(solution)/shard_map/ppermute | solution.py:368
  19.7 6.7 %collective-permute-start.3 = (f32[64,8,128]{2,1,0:T(8,128)S(1)}, f32[64,8,128]{2,1,0:T(8,128)S(1)}, u32[]{:S(2)}, u32[]{:S(2)}) collective-permute-start(f32[64,8,128]{2,1,0:T(8,128)S(1)} %get-tuple-element.40.sent), channel_id=1, source_target_pairs={{0,1},{1,0},{2,3},{3,2},{4,5},{5,4},{6,7},{7,6},{8,9},{9,8},{10,11... | collective-permute-start | bytes 786440 | tf_op jit(solution)/shard_map/ppermute | solution.py:368
  21.4 7.5 %collective-permute-start.4 = (bf16[1024,128]{1,0:T(8,128)(2,1)S(1)}, bf16[1024,128]{1,0:T(8,128)(2,1)S(1)}, u32[]{:S(2)}, u32[]{:S(2)}) collective-permute-start(bf16[1024,128]{1,0:T(8,128)(2,1)S(1)} %copy-done.2), channel_id=1, source_target_pairs={{0,16},{1,17},{2,18},{3,19},{4,20},{5,21},{6,22},{7,23},{8,24},{9,... | collective-permute-start | bytes 786440 | tf_op jit(solution)/shard_map/ppermute | solution.py:368
  28.9 8.0 %collective-permute-start.5 = (f32[48,8,128]{2,1,0:T(8,128)S(1)}, f32[48,8,128]{2,1,0:T(8,128)S(1)}, u32[]{:S(2)}, u32[]{:S(2)}) collective-permute-start(f32[48,8,128]{2,1,0:T(8,128)S(1)} %get-tuple-element.43.sent), channel_id=1, source_target_pairs={{0,7},{1,2},{2,1},{3,4},{4,3},{5,6},{6,5},{7,0},{8,15},{9,10},{10,... | collective-permute-start | bytes 589832 | tf_op jit(solution)/shard_map/ppermute | solution.py:368
  37.0 9.8 %collective-permute-start.6 = (f32[40,8,128]{2,1,0:T(8,128)S(1)}, f32[40,8,128]{2,1,0:T(8,128)S(1)}, u32[]{:S(2)}, u32[]{:S(2)}) collective-permute-start(f32[40,8,128]{2,1,0:T(8,128)S(1)} %get-tuple-element.45.sent), channel_id=1, source_target_pairs={{0,3},{1,6},{2,5},{3,0},{4,7},{5,2},{6,1},{7,4},{8,11},{9,14},{10,... | collective-permute-start | bytes 491528 | tf_op jit(solution)/shard_map/ppermute | solution.py:368
  47.9 9.6 %collective-permute-start.7 = (f32[4,16,128]{2,1,0:T(8,128)S(1)}, f32[4,16,128]{2,1,0:T(8,128)S(1)}, u32[]{:S(2)}, u32[]{:S(2)}) collective-permute-start(f32[4,16,128]{2,1,0:T(8,128)S(1)} %get-tuple-element.51), channel_id=1, source_target_pairs={{0,32},{32,0},{64,96},{96,64},{128,160},{160,128},{192,224},{224,1... | collective-permute-start | bytes 98312 | tf_op jit(solution)/shard_map/ppermute | solution.py:368
  57.6 4.7 %collective-permute-start.8 = (f32[4,16,128]{2,1,0:T(8,128)S(1)}, f32[4,16,128]{2,1,0:T(8,128)S(1)}, u32[]{:S(2)}, u32[]{:S(2)}) collective-permute-start(f32[4,16,128]{2,1,0:T(8,128)S(1)} %add.31), channel_id=1, source_target_pairs={{0,8},{1,9},{2,10},{3,11},{4,12},{5,13},{6,14},{7,15},{8,0},{9,1},... | collective-permute-start | bytes 98312 | tf_op jit(solution)/shard_map/ppermute | solution.py:368
  62.2 4.0 %collective-permute-start.9 = (f32[4,16,128]{2,1,0:T(8,128)S(1)}, f32[4,16,128]{2,1,0:T(8,128)S(1)}, u32[]{:S(2)}, u32[]{:S(2)}) collective-permute-start(f32[4,16,128]{2,1,0:T(8,128)S(1)} %add.32), channel_id=1, source_target_pairs={{0,24},{1,25},{2,26},{3,27},{4,28},{5,29},{6,30},{7,31},{8,16},{9,... | collective-permute-start | bytes 98312 | tf_op jit(solution)/shard_map/ppermute | solution.py:368
  66.2 2.8 %collective-permute-start.10 = (f32[4,16,128]{2,1,0:T(8,128)S(1)}, f32[4,16,128]{2,1,0:T(8,128)S(1)}, u32[]{:S(2)}, u32[]{:S(2)}) collective-permute-start(f32[4,16,128]{2,1,0:T(8,128)S(1)} %add.33), channel_id=1, source_target_pairs={{0,64},{32,96},{64,0},{96,32},{128,192},{160,224},{192,128},{224,1... | collective-permute-start | bytes 98312 | tf_op jit(solution)/shard_map/ppermute | solution.py:368
  69.0 4.8 %collective-permute-start.11 = (f32[4,16,128]{2,1,0:T(8,128)S(1)}, f32[4,16,128]{2,1,0:T(8,128)S(1)}, u32[]{:S(2)}, u32[]{:S(2)}) collective-permute-start(f32[4,16,128]{2,1,0:T(8,128)S(1)} %add.34), channel_id=1, source_target_pairs={{0,192},{32,224},{64,128},{96,160},{128,64},{160,96},{192,0},{224,... | collective-permute-start | bytes 98312 | tf_op jit(solution)/shard_map/ppermute | solution.py:368
  73.8 4.7 %collective-permute-start.12 = (f32[4,16,128]{2,1,0:T(8,128)S(1)}, f32[4,16,128]{2,1,0:T(8,128)S(1)}, u32[]{:S(2)}, u32[]{:S(2)}) collective-permute-start(f32[4,16,128]{2,1,0:T(8,128)S(1)} %add.35.mine), channel_id=1, source_target_pairs={{0,32},{32,0},{64,96},{96,64},{128,160},{160,128},{192,224},{224,1... | collective-permute-start | bytes 98312 | tf_op jit(solution)/shard_map/ppermute | solution.py:368
  79.5 5.2 %collective-permute-start.13 = (f32[10,8,128]{2,1,0:T(8,128)S(1)}, f32[10,8,128]{2,1,0:T(8,128)S(1)}, u32[]{:S(2)}, u32[]{:S(2)}) collective-permute-start(f32[10,8,128]{2,1,0:T(8,128)S(1)} %shard_map.134.sent), channel_id=1, source_target_pairs={{0,3},{1,6},{2,5},{3,0},{4,7},{5,2},{6,1},{7,4},{8,11},{9,14},{10,... | collective-permute-start | bytes 122888 | tf_op jit(solution)/shard_map/ppermute | solution.py:368
  84.7 6.4 %collective-permute-start.14 = (f32[12,8,128]{2,1,0:T(8,128)S(1)}, f32[12,8,128]{2,1,0:T(8,128)S(1)}, u32[]{:S(2)}, u32[]{:S(2)}) collective-permute-start(f32[12,8,128]{2,1,0:T(8,128)S(1)} %shard_map.135.sent), channel_id=1, source_target_pairs={{0,7},{1,2},{2,1},{3,4},{4,3},{5,6},{6,5},{7,0},{8,15},{9,10},{10,... | collective-permute-start | bytes 147464 | tf_op jit(solution)/shard_map/ppermute | solution.py:368
  91.1 5.0 %collective-permute-start.15 = (f32[16,8,128]{2,1,0:T(8,128)S(1)}, f32[16,8,128]{2,1,0:T(8,128)S(1)}, u32[]{:S(2)}, u32[]{:S(2)}) collective-permute-start(f32[16,8,128]{2,1,0:T(8,128)S(1)} %shard_map.136.sent), channel_id=1, source_target_pairs={{0,1},{1,0},{2,3},{3,2},{4,5},{5,4},{6,7},{7,6},{8,9},{9,8},{10,11... | collective-permute-start | bytes 196616 | tf_op jit(solution)/shard_map/ppermute | solution.py:368
  96.1 6.1 %collective-permute-start.16 = (f32[24,8,128]{2,1,0:T(8,128)S(1)}, f32[24,8,128]{2,1,0:T(8,128)S(1)}, u32[]{:S(2)}, u32[]{:S(2)}) collective-permute-start(f32[24,8,128]{2,1,0:T(8,128)S(1)} %shard_map.137), channel_id=1, source_target_pairs={{0,8},{1,9},{2,10},{3,11},{4,12},{5,13},{6,14},{7,15},{8,0},{9,1},... | collective-permute-start | bytes 294920 | tf_op jit(solution)/shard_map/ppermute | solution.py:368
  102.2 6.2 %collective-permute-start.17 = (f32[48,8,128]{2,1,0:T(8,128)S(1)}, f32[48,8,128]{2,1,0:T(8,128)S(1)}, u32[]{:S(2)}, u32[]{:S(2)}) collective-permute-start(f32[48,8,128]{2,1,0:T(8,128)S(1)} %pad_maximum_fusion.sent), channel_id=1, source_target_pairs={{0,24},{1,25},{2,26},{3,27},{4,28},{5,29},{6,30},{7,31},{8,16},{9,... | collective-permute-start | bytes 589832 | tf_op jit(solution)/shard_map/ppermute | solution.py:368
  108.4 5.2 %collective-permute-start.18 = (f32[64,8,128]{2,1,0:T(8,128)S(1)}, f32[64,8,128]{2,1,0:T(8,128)S(1)}, u32[]{:S(2)}, u32[]{:S(2)}) collective-permute-start(f32[64,8,128]{2,1,0:T(8,128)S(1)} %get-tuple-element.52.mine), channel_id=1, source_target_pairs={{0,32},{32,0},{64,96},{96,64},{128,160},{160,128},{192,224},{224,1... | collective-permute-start | bytes 786440 | tf_op jit(solution)/shard_map/ppermute | solution.py:368
  121.6 3.2 %collective-permute-start.19 = (f32[32,448]{1,0:T(8,128)S(1)}, f32[32,448]{1,0:T(8,128)S(1)}, u32[]{:S(2)}, u32[]{:S(2)}) collective-permute-start(f32[32,448]{1,0:T(8,128)S(1)} %get-tuple-element.54), channel_id=1, source_target_pairs={{0,64},{32,96},{64,0},{96,32},{128,192},{160,224},{192,128},{224,1... | collective-permute-start | bytes 172040 | tf_op jit(solution)/shard_map/ppermute | solution.py:368
  124.9 6.7 %collective-permute-start.20 = (f32[32,448]{1,0:T(8,128)S(1)}, f32[32,448]{1,0:T(8,128)S(1)}, u32[]{:S(2)}, u32[]{:S(2)}) collective-permute-start(f32[32,448]{1,0:T(8,128)S(1)} %add.36), channel_id=1, source_target_pairs={{0,192},{32,224},{64,128},{96,160},{128,64},{160,96},{192,0},{224,... | collective-permute-start | bytes 172040 | tf_op jit(solution)/shard_map/ppermute | solution.py:368
  131.6 6.1 %collective-permute-start.21 = (f32[32,448]{1,0:T(8,128)S(1)}, f32[32,448]{1,0:T(8,128)S(1)}, u32[]{:S(2)}, u32[]{:S(2)}) collective-permute-start(f32[32,448]{1,0:T(8,128)S(1)} %add.37), channel_id=1, source_target_pairs={{0,32},{32,0},{64,96},{96,64},{128,160},{160,128},{192,224},{224,1... | collective-permute-start | bytes 172040 | tf_op jit(solution)/shard_map/ppermute | solution.py:368
  (9 other events, 191.2 us)
Sparse Core Ops, SparseCore 0:
  10.6 105.0 all-gather.2

commit v8 on v7

--- a/solution.py
+++ b/solution.py
@@ -119,7 +119,10 @@
         copy.start()
     for copy in copies:
         copy.wait()
-    tiles_of(fold3(dot_nn(split3(q_ref[...]), gt_ref[...])), out)
+    total = fold3(dot_nn(split3(q_ref[...]), gt_ref[...]))
+    width = total.shape[1] // NX
+    for x in range(NX):
+        tiles_of(total[:, x * width : (x + 1) * width], out.at[x])
 
 
 def store_blocks(value, out, start):
@@ -134,54 +137,74 @@
     )
 
 
-def open_kernel(tokens, mine, theirs, message, keep):
-    message[:FACTOR] = tokens[...]
+def deal_kernel(member_ref, place_ref, acts_ref, *outs):
+    rows = outs[0].shape[0]
+    for place in range(NX):
+        x = lax.div(place_ref[member_ref[0], place * NZ], NZ)
+        outs[place][...] = acts_ref[pl.ds(pl.multiple_of(x * rows, rows), rows), :]
+
+
+def open_kernel(member_ref, place_ref, tokens, mine, theirs, message, keep_tokens, keep):
+    half = NX // 2
+    for place in range(half):
+        for out, other in ((keep_tokens, place), (message, place + half)):
+            x = lax.div(place_ref[member_ref[0], other * NZ], NZ)
+            out[place * QUARTER : (place + 1) * QUARTER] = tokens[x]
     both = mine[...] + theirs[...]
-    half = both.shape[0] // 2
-    keep[...] = both[:half]
-    store_blocks(both[half:], message, FACTOR)
-
-
-def halve_kernel(sent, kept, came, message, keep):
-    message[:FACTOR] = sent[:FACTOR] + came[:FACTOR]
-    count = kept.shape[0]
-    both = kept[...] + load_blocks(came, FACTOR, count)
-    keep[...] = both[: count // 2]
-    store_blocks(both[count // 2 :], message, FACTOR)
+    count = both.shape[0] // 2
+    keep[...] = both[:count]
+    store_blocks(both[count:], message, half * QUARTER)
+
+
+def narrow_kernel(tokens, kept, came, message, keep_tokens, keep):
+    count, blocks = tokens.shape[0], kept.shape[0]
+    factor = tokens[...] + came[:count]
+    both = kept[...] + load_blocks(came, count, blocks)
+    keep_tokens[...] = factor[: count // 2]
+    keep[...] = both[: blocks // 2]
+    message[: count // 2] = factor[count // 2 :]
+    store_blocks(both[blocks // 2 :], message, count // 2)
+
+
+def halve_kernel(tokens, kept, came, message, keep):
+    blocks = kept.shape[0]
+    message[:QUARTER] = tokens[:QUARTER] + came[:QUARTER]
+    both = kept[...] + load_blocks(came, QUARTER, blocks)
+    keep[...] = both[: blocks // 2]
+    store_blocks(both[blocks // 2 :], message, QUARTER)
 
 
 def piece_kernel(member_ref, core_ref, place_ref, sent, kept, came, *refs):
     acts_refs, keep, send = refs[:NX], refs[NX], refs[NX + 1]
-    blocks = acts_refs[0].shape[0] // LANES
+    columns = acts_refs[0].shape[0] // LANES
     half = keep.shape[1]
     lower = core_ref[0] == 0
-    errors = kept[...] + load_blocks(came, FACTOR, NX)
-    factors = []
-    for block in range(blocks):
-        factors.append(split3(rows_of(sent, block, blocks, FACTOR) + rows_of(came, block, blocks, FACTOR)))
-    factor = jnp.concatenate(factors, axis=1)
+    errors = (kept[...] + load_blocks(came, QUARTER, 1))[0]
+    factor = jnp.concatenate(
+        [rows_of(sent, column, columns, FACTOR) + rows_of(came, column, columns, FACTOR) for column in range(columns)],
+        axis=1,
+    )
+    factor = split3(factor)
     for place in range(NX):
-        x = lax.div(place_ref[member_ref[0], place], NZ)
+        x = lax.div(place_ref[member_ref[0], place * NZ], NZ)
         piece = fold3(dot_nn(factor, acts_refs[place][...]))
-        keep[x] = jnp.where(lower, piece[:half], piece[half:]) + errors[place]
+        stays = jnp.where(lower, piece[:half], piece[half:])
+        keep[x] = stays + errors if place == 0 else stays
         send[x] = jnp.where(lower, piece[half:], piece[:half])
 
 
 def start_kernel(member_ref, core_ref, place_ref, mine, theirs, *refs):
     acts_refs, message = refs[:NX], refs[NX]
     lower = core_ref[0] == 0
-    rows = acts_refs[0].shape[0] // NX
-    home = lax.div(member_ref[0], NZ)
-    quarter = pl.ds(pl.multiple_of(home * rows, rows), rows)
     total = None
     for place in range(NX):
-        x = lax.div(place_ref[member_ref[0], place], NZ)
+        x = lax.div(place_ref[member_ref[0], place * NZ], NZ)
         first, second = mine[x] * (1.0 / NDP), theirs[x] * (1.0 / NDP)
         panel = jnp.concatenate([jnp.where(lower, first, second), jnp.where(lower, second, first)], axis=0)
-        part = dot_nt(split3(panel), acts_refs[place][quarter, :])
+        part = dot_nt(split3(panel), acts_refs[place][...])
         total = part if total is None else total + part
     tiles_of(fold3(total), message)
-    store_blocks(mine[home][None] * (1.0 / NDP), message, QUARTER)
+    store_blocks(mine[lax.div(member_ref[0], NZ)][None] * (1.0 / NDP), message, QUARTER)
 
 
 def double_kernel(sent, came, message):
@@ -386,14 +409,18 @@
 
     gathered = lax.all_gather(acts, "mp", axis=0)
 
-    ring = [acts] + [swap(acts, "mp", level) for level in ALONG_X]
-    ring.append(swap(acts, "mp", [(x + 2) % NX * NZ + z for x in range(NX) for z in range(NZ)]))
+    table = jnp.asarray(met(ALONG_Z + ALONG_X, NMP))
+    quarters = call(
+        deal_kernel, [array((tokens // NX, LANES), BF16)] * NX, (member, table, acts), specs=[SMEM, SMEM, VMEM], moved=MIB
+    )
+    late, quarters = lax.optimization_barrier((q_prev, quarters))
+    across = [(x + 2) % NX * NZ + z for x in range(NX) for z in range(NZ)]
+    ring = [quarters[0]] + [swap(rows, "mp", level) for rows, level in zip(quarters[1:], (*ALONG_X, across))]
 
     half = rank // 2
-    table = jnp.asarray(met(ALONG_X + ALONG_Z, NMP))
     blocks = array((NMP, half, LANES), F32)
     mine, send = call(
-        error_kernel, [blocks, blocks], (member, core, table, q_prev, et), specs=[SMEM] * 3 + [HBM] * 2,
+        error_kernel, [blocks, blocks], (member, core, table, late, et), specs=[SMEM] * 3 + [HBM] * 2,
         scratch=[
             pltpu.VMEM((rank, ff), F32), pltpu.VMEM((chunks, ff, width), BF16), pltpu.VMEM((NMP, rank, LANES), F32),
             pltpu.SemaphoreType.DMA((chunks + 1,)),
@@ -402,22 +429,23 @@
     )
     theirs = swap(send, "dp", ALONG_DP[0])
     factor = call(
-        token_kernel, array((FACTOR, 8, LANES), F32), (q_prev, gt), specs=[HBM] * 2,
+        token_kernel, array((NX, QUARTER, 8, LANES), F32), (q_prev, gt), specs=[HBM] * 2,
         scratch=[pltpu.VMEM((rank, ff), F32), pltpu.VMEM((ff, tokens), BF16), pltpu.SemaphoreType.DMA((2,))],
         limit=16, flops=6 * rank * ff * tokens, moved=2 * ff * tokens,
     )
-    theirs, factor, ring[1:3] = lax.optimization_barrier((theirs, factor, ring[1:3]))
-    count = NMP // 2
-    message = lambda tiles: array((FACTOR + tiles, 8, LANES), F32)
+    theirs, factor, ring = lax.optimization_barrier((theirs, factor, ring))
+    tiles = lambda count: array((count, 8, LANES), F32)
     kept = lambda count: array((count, half, LANES), F32)
-    sent, keep = call(open_kernel, [message(2 * count), kept(count)], (factor, mine, theirs), moved=MIB)
-    for place, level in enumerate(ALONG_Z[:0:-1]):
-        came = swap(sent, "mp", level)
-        count //= 2
-        sent, keep = call(halve_kernel, [message(2 * count), kept(count)], (sent, keep, came), moved=MIB)
-        if place == 0:
-            sent, ring[3] = lax.optimization_barrier((sent, ring[3]))
-    came = swap(sent, "mp", ALONG_Z[0])
+    sent, part, keep = call(
+        open_kernel, [tiles(48), tiles(2 * QUARTER), kept(16)], (member, table, factor, mine, theirs),
+        specs=[SMEM, SMEM] + [VMEM] * 3, moved=MIB,
+    )
+    came = swap(sent, "mp", ALONG_X[1])
+    sent, part, keep = call(narrow_kernel, [tiles(24), tiles(QUARTER), kept(8)], (part, keep, came), moved=MIB)
+    came = swap(sent, "mp", ALONG_X[0])
+    for count, level in zip((4, 2, 1), ALONG_Z[::-1]):
+        sent, keep = call(halve_kernel, [tiles(QUARTER + 2 * count), kept(count)], (part, keep, came), moved=MIB)
+        part, came = sent, swap(sent, "mp", level)
 
     keep, send = call(
         piece_kernel, [kept(NX), kept(NX)], (member, core, table, sent, keep, came, *ring),
@@ -439,7 +467,7 @@
     )
     basis, right = call(
         ortho_kernel, [array((NMP, 3 * rank, LANES), BF16), array((rank, ff), F32)],
-        (member, core, jnp.asarray(met(ALONG_Z + ALONG_X, NMP)), mine, swap(mine, "dp", ALONG_DP[0]), factor, gt, et),
+        (member, core, table, mine, swap(mine, "dp", ALONG_DP[0]), factor, gt, et),
         specs=[SMEM] * 3 + [VMEM] * 4 + [HBM],
         scratch=[
             pltpu.VMEM((NMP + 1, rank, LANES), F32),
@@ -449,9 +477,9 @@
         ],
         limit=24, flops=8 * rank * ff * model, moved=2 * ff * model,
     )
-    right, gathered = lax.optimization_barrier((total(right, "dp", ALONG_DP[1:2]), gathered))
+    right, gathered = lax.optimization_barrier((right, gathered))
     halves = []
-    for part, level in enumerate((ALONG_DP[2], ALONG_DP[0])):
+    for part, level in enumerate(ALONG_DP[1:]):
         half = call(
             functools.partial(field_kernel, part * NMP // 2), array((NMP // 2, ff, LANES), F32), (gathered, et, gt),
             specs=[HBM] * 3,
@@ -467,6 +495,7 @@
         )
         right, half = lax.optimization_barrier((total(right, "dp", [level]), half))
         halves.append(half)
+    right = total(right, "dp", ALONG_DP[:1])
 
     block = array((ff, width), F32)
     outs = call(

time: 149 us -> 148 us (level)
  starting transfers between devices: 52.8 us -> 49.8 us
  local copies, waits for them, and re-layouts: 1 us -> 2.65 us
  Pallas kernels: 28.6 us -> 30.1 us
    ppermute x22 -> x24, starting transfers between devices: 52.8 us -> 49.8 us  [swap(): return lax.ppermute(value, axis, list(enumerate(level)))]
    unnamed x20, local copies, waits for them, and re-layouts: 1 us -> 2.65 us
    pallas_call x15 -> x18, Pallas kernels: 28.6 us -> 30.1 us  [call(): pl.pallas_call(kernel, out_shape=outs, in_specs=specs or [VMEM] * len(arg...]
    ppermute x22 -> x24, waiting for transfers between devices: 51.7 us -> 50.5 us  [swap(): return lax.ppermute(value, axis, list(enumerate(level)))]
  transfers between devices with their start and end apart: 23 -> 25, of which waited for: 19 -> 20; matrix products, arithmetic and copies ran while one was open for 0% -> 0% of each run, Pallas kernels for 16% -> 17%
where the time goes in v8:
time: 148 us
  waiting for transfers between devices  51.2 us (35%)
  starting transfers between devices  49.8 us (34%)
  Pallas kernels  30.1 us (20%)
  between operations  14.3 us (10%)
  local copies, waits for them, and re-layouts  2.65 us (2%)
    ppermute x24, waiting for transfers between devices, swap(): return lax.ppermute(value, axis, list(enumerate(level)))  50.5 us
    ppermute x24, starting transfers between devices, swap(): return lax.ppermute(value, axis, list(enumerate(level)))  49.8 us
    pallas_call x18, Pallas kernels, call(): pl.pallas_call(kernel, out_shape=outs, in_specs=specs or [VMEM] * len(arg...  30.1 us
  transfers between devices with their start and end apart: 25, of which 20 were waited for; matrix products, arithmetic and copies ran while one was open for 0% of the time, Pallas kernels for 17%

profile of v8, /device:TPU:1, one launch (start us, length us, event | category | flops | bytes accessed | tf_op | source)
XLA Modules:
  0.0 148.2 jit_solution(11102386781548252979)
XLA Ops:
  10.4 4.8 %shard_map.120 = (f32[32,16,128]{2,1,0:T(8,128)}, f32[32,16,128]{2,1,0:T(8,128)}) custom-call(s32[1]{0:T(128)} %bitcast.1.member_ref, s32[1]{0:T(128)S(6)} %select_n.7.core_ref, s32[32,32]{1,0:T(8,128)} %constant.30.clone.place_ref, f32[32,448]{1,0:T(8,128)} %q_hbm.2, bf16[448,4096]{1,0:T(8,128)(2,1)} %bitcast.12), custom_call_target="tpu_custom_call" | custom-call | flops 352321536 | bytes 3670016 | tf_op jit(solution)/shard_map/pallas_call | solution.py:379
  15.2 3.3 %collective-permute-start = (f32[32,16,128]{2,1,0:T(8,128)}, f32[32,16,128]{2,1,0:T(8,128)S(1)}, u32[]{:S(2)}, u32[]{:S(2)}) collective-permute-start(f32[32,16,128]{2,1,0:T(8,128)} %get-tuple-element.56), channel_id=1, source_target_pairs={{0,32},{32,0},{64,96},{96,64},{128,160},{160,128},{192,224},{224,1... | collective-permute-start | bytes 786440 | tf_op jit(solution)/shard_map/ppermute | solution.py:391
  27.7 7.5 %collective-permute-done.4.came = f32[48,8,128]{2,1,0:T(8,128)S(1)} collective-permute-done((f32[48,8,128]{2,1,0:T(8,128)S(1)}, f32[48,8,128]{2,1,0:T(8,128)S(1)}, u32[]{:S(2)}, u32[]{:S(2)}) %collective-permute-start.4) | collective-permute-done | bytes 196640 | tf_op jit(solution)/shard_map/ppermute | solution.py:391
  35.4 3.9 %collective-permute-done.5.came = f32[24,8,128]{2,1,0:T(8,128)S(1)} collective-permute-done((f32[24,8,128]{2,1,0:T(8,128)S(1)}, f32[24,8,128]{2,1,0:T(8,128)S(1)}, u32[]{:S(2)}, u32[]{:S(2)}) %collective-permute-start.5) | collective-permute-done | bytes 98336 | tf_op jit(solution)/shard_map/ppermute | solution.py:391
  39.2 3.1 %collective-permute-start.6 = (f32[16,8,128]{2,1,0:T(8,128)S(1)}, f32[16,8,128]{2,1,0:T(8,128)S(1)}, u32[]{:S(2)}, u32[]{:S(2)}) collective-permute-start(f32[16,8,128]{2,1,0:T(8,128)S(1)} %get-tuple-element.70.tokens), channel_id=1, source_target_pairs={{0,1},{1,0},{2,3},{3,2},{4,5},{5,4},{6,7},{7,6},{8,9},{9,8},{10,11... | collective-permute-start | bytes 196616 | tf_op jit(solution)/shard_map/ppermute | solution.py:391
  42.3 2.9 %collective-permute-done.6.came = f32[16,8,128]{2,1,0:T(8,128)S(1)} collective-permute-done((f32[16,8,128]{2,1,0:T(8,128)S(1)}, f32[16,8,128]{2,1,0:T(8,128)S(1)}, u32[]{:S(2)}, u32[]{:S(2)}) %collective-permute-start.6) | collective-permute-done | bytes 65568 | tf_op jit(solution)/shard_map/ppermute | solution.py:391
  49.5 4.1 %collective-permute-start.8 = (f32[10,8,128]{2,1,0:T(8,128)S(1)}, f32[10,8,128]{2,1,0:T(8,128)S(1)}, u32[]{:S(2)}, u32[]{:S(2)}) collective-permute-start(f32[10,8,128]{2,1,0:T(8,128)S(1)} %get-tuple-element.74.sent), channel_id=1, source_target_pairs={{0,3},{1,6},{2,5},{3,0},{4,7},{5,2},{6,1},{7,4},{8,11},{9,14},{10,... | collective-permute-start | bytes 122888 | tf_op jit(solution)/shard_map/ppermute | solution.py:391
  56.3 4.5 %collective-permute-start.9 = (f32[4,16,128]{2,1,0:T(8,128)S(1)}, f32[4,16,128]{2,1,0:T(8,128)S(1)}, u32[]{:S(2)}, u32[]{:S(2)}) collective-permute-start(f32[4,16,128]{2,1,0:T(8,128)S(1)} %get-tuple-element.81), channel_id=1, source_target_pairs={{0,32},{32,0},{64,96},{96,64},{128,160},{160,128},{192,224},{224,1... | collective-permute-start | bytes 98312 | tf_op jit(solution)/shard_map/ppermute | solution.py:391
  61.8 2.8 %collective-permute-done.10 = f32[4,16,128]{2,1,0:T(8,128)S(1)} collective-permute-done((f32[4,16,128]{2,1,0:T(8,128)S(1)}, f32[4,16,128]{2,1,0:T(8,128)S(1)}, u32[]{:S(2)}, u32[]{:S(2)}) %collective-permute-start.10) | collective-permute-done | bytes 32800 | tf_op jit(solution)/shard_map/ppermute | solution.py:391
  71.7 3.8 %collective-permute-start.13 = (f32[4,16,128]{2,1,0:T(8,128)S(1)}, f32[4,16,128]{2,1,0:T(8,128)S(1)}, u32[]{:S(2)}, u32[]{:S(2)}) collective-permute-start(f32[4,16,128]{2,1,0:T(8,128)S(1)} %add.34), channel_id=1, source_target_pairs={{0,192},{32,224},{64,128},{96,160},{128,64},{160,96},{192,0},{224,... | collective-permute-start | bytes 98312 | tf_op jit(solution)/shard_map/ppermute | solution.py:391
  77.1 3.6 %collective-permute-start.14 = (f32[4,16,128]{2,1,0:T(8,128)S(1)}, f32[4,16,128]{2,1,0:T(8,128)S(1)}, u32[]{:S(2)}, u32[]{:S(2)}) collective-permute-start(f32[4,16,128]{2,1,0:T(8,128)S(1)} %add.35.mine), channel_id=1, source_target_pairs={{0,32},{32,0},{64,96},{96,64},{128,160},{160,128},{192,224},{224,1... | collective-permute-start | bytes 98312 | tf_op jit(solution)/shard_map/ppermute | solution.py:391
  82.6 3.9 %collective-permute-start.15 = (f32[10,8,128]{2,1,0:T(8,128)S(1)}, f32[10,8,128]{2,1,0:T(8,128)S(1)}, u32[]{:S(2)}, u32[]{:S(2)}) collective-permute-start(f32[10,8,128]{2,1,0:T(8,128)S(1)} %shard_map.128.sent), channel_id=1, source_target_pairs={{0,3},{1,6},{2,5},{3,0},{4,7},{5,2},{6,1},{7,4},{8,11},{9,14},{10,... | collective-permute-start | bytes 122888 | tf_op jit(solution)/shard_map/ppermute | solution.py:391
  86.5 2.7 %collective-permute-done.15.came = f32[10,8,128]{2,1,0:T(8,128)S(1)} collective-permute-done((f32[10,8,128]{2,1,0:T(8,128)S(1)}, f32[10,8,128]{2,1,0:T(8,128)S(1)}, u32[]{:S(2)}, u32[]{:S(2)}) %collective-permute-start.15) | collective-permute-done | bytes 40992 | tf_op jit(solution)/shard_map/ppermute | solution.py:391
  89.2 2.5 %collective-permute-start.16 = (f32[12,8,128]{2,1,0:T(8,128)S(1)}, f32[12,8,128]{2,1,0:T(8,128)S(1)}, u32[]{:S(2)}, u32[]{:S(2)}) collective-permute-start(f32[12,8,128]{2,1,0:T(8,128)S(1)} %shard_map.129.sent), channel_id=1, source_target_pairs={{0,7},{1,2},{2,1},{3,4},{4,3},{5,6},{6,5},{7,0},{8,15},{9,10},{10,... | collective-permute-start | bytes 147464 | tf_op jit(solution)/shard_map/ppermute | solution.py:391
  91.7 3.1 %collective-permute-done.16.came = f32[12,8,128]{2,1,0:T(8,128)S(1)} collective-permute-done((f32[12,8,128]{2,1,0:T(8,128)S(1)}, f32[12,8,128]{2,1,0:T(8,128)S(1)}, u32[]{:S(2)}, u32[]{:S(2)}) %collective-permute-start.16) | collective-permute-done | bytes 49184 | tf_op jit(solution)/shard_map/ppermute | solution.py:391
  96.0 3.8 %collective-permute-done.17.came = f32[16,8,128]{2,1,0:T(8,128)S(1)} collective-permute-done((f32[16,8,128]{2,1,0:T(8,128)S(1)}, f32[16,8,128]{2,1,0:T(8,128)S(1)}, u32[]{:S(2)}, u32[]{:S(2)}) %collective-permute-start.17) | collective-permute-done | bytes 65568 | tf_op jit(solution)/shard_map/ppermute | solution.py:391
  100.0 3.9 %collective-permute-done.18 = f32[24,8,128]{2,1,0:T(8,128)S(1)} collective-permute-done((f32[24,8,128]{2,1,0:T(8,128)S(1)}, f32[24,8,128]{2,1,0:T(8,128)S(1)}, u32[]{:S(2)}, u32[]{:S(2)}) %collective-permute-start.18) | collective-permute-done | bytes 98336 | tf_op jit(solution)/shard_map/ppermute | solution.py:391
  105.8 4.5 %collective-permute-done.19.came = f32[48,8,128]{2,1,0:T(8,128)S(1)} collective-permute-done((f32[48,8,128]{2,1,0:T(8,128)S(1)}, f32[48,8,128]{2,1,0:T(8,128)S(1)}, u32[]{:S(2)}, u32[]{:S(2)}) %collective-permute-start.19) | collective-permute-done | bytes 196640 | tf_op jit(solution)/shard_map/ppermute | solution.py:391
  110.3 4.1 %collective-permute-start.20 = (f32[64,8,128]{2,1,0:T(8,128)S(1)}, f32[64,8,128]{2,1,0:T(8,128)S(1)}, u32[]{:S(2)}, u32[]{:S(2)}) collective-permute-start(f32[64,8,128]{2,1,0:T(8,128)S(1)} %get-tuple-element.82.mine), channel_id=1, source_target_pairs={{0,32},{32,0},{64,96},{96,64},{128,160},{160,128},{192,224},{224,1... | collective-permute-start | bytes 786440 | tf_op jit(solution)/shard_map/ppermute | solution.py:391
  115.5 8.0 %shard_map.133 = (bf16[32,96,128]{2,1,0:T(8,128)(2,1)S(1)}, f32[32,448]{1,0:T(8,128)S(1)}) custom-call(s32[1]{0:T(128)} %bitcast.1.member_ref, s32[1]{0:T(128)S(6)} %select_n.7.core_ref, s32[32,32]{1,0:T(8,128)S(1)} %copy-done.7, f32[64,8,128]{2,1,0:T(8,128)S(1)} %get-tuple-element.82.mine, f32[64,8,128]{2,1,0:T(8,128)S(1)} %collective-permute-done.20.theirs, ...), custom_call_target="tpu_custom_call" | custom-call | flops 469762048 | bytes 3670016 | tf_op jit(solution)/shard_map/pallas_call | solution.py:379
  124.2 4.2 %shard_map.134.lower = f32[16,448,128]{2,1,0:T(8,128)S(1)} custom-call(bf16[32,1024,128]{2,1,0:T(8,128)(2,1)} %bitcast.23, bf16[448,4096]{1,0:T(8,128)(2,1)} %bitcast.13, bf16[448,1024]{1,0:T(8,128)(2,1)S(1)} %bitcast.18), custom_call_target="tpu_custom_call" | custom-call | flops 1879048192 | bytes 10485760 | tf_op jit(solution)/shard_map/pallas_call | solution.py:379
  128.5 2.4 %collective-permute-start.22 = (f32[32,448]{1,0:T(8,128)S(1)}, f32[32,448]{1,0:T(8,128)S(1)}, u32[]{:S(2)}, u32[]{:S(2)}) collective-permute-start(f32[32,448]{1,0:T(8,128)S(1)} %add.36), channel_id=1, source_target_pairs={{0,192},{32,224},{64,128},{96,160},{128,64},{160,96},{192,0},{224,... | collective-permute-start | bytes 172040 | tf_op jit(solution)/shard_map/ppermute | solution.py:391
  130.9 4.2 %shard_map.135.upper = f32[16,448,128]{2,1,0:T(8,128)S(1)} custom-call(bf16[32,1024,128]{2,1,0:T(8,128)(2,1)} %bitcast.24, bf16[448,4096]{1,0:T(8,128)(2,1)} %bitcast.14, bf16[448,1024]{1,0:T(8,128)(2,1)S(1)} %bitcast.19), custom_call_target="tpu_custom_call" | custom-call | flops 1879048192 | bytes 10485760 | tf_op jit(solution)/shard_map/pallas_call | solution.py:379
  136.8 4.5 %shard_map.136 = (f32[448,512]{1,0:T(8,128)}, f32[448,512]{1,0:T(8,128)}, f32[448,512]{1,0:T(8,128)}, bf16[448,4096]{1,0:T(8,128)(2,1)}, f32[32,448]{1,0:T(8,128)}) custom-call(s32[1]{0:T(128)} %bitcast.dp_ref, f32[32,448]{1,0:T(8,128)S(1)} %add.38.sum_ref, bf16[32,96,128]{2,1,0:T(8,128)(2,1)S(1)} %get-tuple-element.89.basis_ref, ...), custom_call_target="tpu_custom_call" | custom-call | flops 704643072 | bytes 20971520 | tf_op jit(solution)/shard_map/pallas_call | solution.py:379
  (74 shorter events, 37.8 us)
Async XLA Ops:
  7.2 116.4 %all-gather.3.cloned.1.call-start = ((), (), s32[]{:S(2)}) async-start(), calls=%async_computation | async-start | bytes 8650752 | tf_op jit(solution)/shard_map/all_gather | solution.py:410
  15.2 9.3 %collective-permute-start = (f32[32,16,128]{2,1,0:T(8,128)}, f32[32,16,128]{2,1,0:T(8,128)S(1)}, u32[]{:S(2)}, u32[]{:S(2)}) collective-permute-start(f32[32,16,128]{2,1,0:T(8,128)} %get-tuple-element.56), channel_id=1, source_target_pairs={{0,32},{32,0},{64,96},{96,64},{128,160},{160,128},{192,224},{224,1... | collective-permute-start | bytes 786440 | tf_op jit(solution)/shard_map/ppermute | solution.py:391
  18.6 3.9 %collective-permute-start.1 = (bf16[256,128]{1,0:T(8,128)(2,1)S(1)}, bf16[256,128]{1,0:T(8,128)(2,1)S(1)}, u32[]{:S(2)}, u32[]{:S(2)}) collective-permute-start(bf16[256,128]{1,0:T(8,128)(2,1)S(1)} %get-tuple-element.58), channel_id=1, source_target_pairs={{0,8},{1,9},{2,10},{3,11},{4,12},{5,13},{6,14},{7,15},{8,0},{9,1},... | collective-permute-start | bytes 196616 | tf_op jit(solution)/shard_map/ppermute | solution.py:391
  18.6 4.7 %collective-permute-start.2 = (bf16[256,128]{1,0:T(8,128)(2,1)S(1)}, bf16[256,128]{1,0:T(8,128)(2,1)S(1)}, u32[]{:S(2)}, u32[]{:S(2)}) collective-permute-start(bf16[256,128]{1,0:T(8,128)(2,1)S(1)} %get-tuple-element.59), channel_id=1, source_target_pairs={{0,24},{1,25},{2,26},{3,27},{4,28},{5,29},{6,30},{7,31},{8,16},{9,... | collective-permute-start | bytes 196616 | tf_op jit(solution)/shard_map/ppermute | solution.py:391
  19.9 4.6 %collective-permute-start.3 = (bf16[256,128]{1,0:T(8,128)(2,1)S(1)}, bf16[256,128]{1,0:T(8,128)(2,1)S(1)}, u32[]{:S(2)}, u32[]{:S(2)}) collective-permute-start(bf16[256,128]{1,0:T(8,128)(2,1)S(1)} %get-tuple-element.60), channel_id=1, source_target_pairs={{0,16},{1,17},{2,18},{3,19},{4,20},{5,21},{6,22},{7,23},{8,24},{9,... | collective-permute-start | bytes 196616 | tf_op jit(solution)/shard_map/ppermute | solution.py:391
  26.3 8.9 %collective-permute-start.4 = (f32[48,8,128]{2,1,0:T(8,128)S(1)}, f32[48,8,128]{2,1,0:T(8,128)S(1)}, u32[]{:S(2)}, u32[]{:S(2)}) collective-permute-start(f32[48,8,128]{2,1,0:T(8,128)S(1)} %get-tuple-element.66), channel_id=1, source_target_pairs={{0,24},{1,25},{2,26},{3,27},{4,28},{5,29},{6,30},{7,31},{8,16},{9,... | collective-permute-start | bytes 589832 | tf_op jit(solution)/shard_map/ppermute | solution.py:391
  35.3 4.0 %collective-permute-start.5 = (f32[24,8,128]{2,1,0:T(8,128)S(1)}, f32[24,8,128]{2,1,0:T(8,128)S(1)}, u32[]{:S(2)}, u32[]{:S(2)}) collective-permute-start(f32[24,8,128]{2,1,0:T(8,128)S(1)} %get-tuple-element.69), channel_id=1, source_target_pairs={{0,8},{1,9},{2,10},{3,11},{4,12},{5,13},{6,14},{7,15},{8,0},{9,1},... | collective-permute-start | bytes 294920 | tf_op jit(solution)/shard_map/ppermute | solution.py:391
  39.2 6.0 %collective-permute-start.6 = (f32[16,8,128]{2,1,0:T(8,128)S(1)}, f32[16,8,128]{2,1,0:T(8,128)S(1)}, u32[]{:S(2)}, u32[]{:S(2)}) collective-permute-start(f32[16,8,128]{2,1,0:T(8,128)S(1)} %get-tuple-element.70.tokens), channel_id=1, source_target_pairs={{0,1},{1,0},{2,3},{3,2},{4,5},{5,4},{6,7},{7,6},{8,9},{9,8},{10,11... | collective-permute-start | bytes 196616 | tf_op jit(solution)/shard_map/ppermute | solution.py:391
  45.3 4.2 %collective-permute-start.7 = (f32[12,8,128]{2,1,0:T(8,128)S(1)}, f32[12,8,128]{2,1,0:T(8,128)S(1)}, u32[]{:S(2)}, u32[]{:S(2)}) collective-permute-start(f32[12,8,128]{2,1,0:T(8,128)S(1)} %get-tuple-element.72.tokens), channel_id=1, source_target_pairs={{0,7},{1,2},{2,1},{3,4},{4,3},{5,6},{6,5},{7,0},{8,15},{9,10},{10,... | collective-permute-start | bytes 147464 | tf_op jit(solution)/shard_map/ppermute | solution.py:391
  49.5 5.8 %collective-permute-start.8 = (f32[10,8,128]{2,1,0:T(8,128)S(1)}, f32[10,8,128]{2,1,0:T(8,128)S(1)}, u32[]{:S(2)}, u32[]{:S(2)}) collective-permute-start(f32[10,8,128]{2,1,0:T(8,128)S(1)} %get-tuple-element.74.sent), channel_id=1, source_target_pairs={{0,3},{1,6},{2,5},{3,0},{4,7},{5,2},{6,1},{7,4},{8,11},{9,14},{10,... | collective-permute-start | bytes 122888 | tf_op jit(solution)/shard_map/ppermute | solution.py:391
  56.3 5.4 %collective-permute-start.9 = (f32[4,16,128]{2,1,0:T(8,128)S(1)}, f32[4,16,128]{2,1,0:T(8,128)S(1)}, u32[]{:S(2)}, u32[]{:S(2)}) collective-permute-start(f32[4,16,128]{2,1,0:T(8,128)S(1)} %get-tuple-element.81), channel_id=1, source_target_pairs={{0,32},{32,0},{64,96},{96,64},{128,160},{160,128},{192,224},{224,1... | collective-permute-start | bytes 98312 | tf_op jit(solution)/shard_map/ppermute | solution.py:391
  61.7 2.8 %collective-permute-start.10 = (f32[4,16,128]{2,1,0:T(8,128)S(1)}, f32[4,16,128]{2,1,0:T(8,128)S(1)}, u32[]{:S(2)}, u32[]{:S(2)}) collective-permute-start(f32[4,16,128]{2,1,0:T(8,128)S(1)} %add.31), channel_id=1, source_target_pairs={{0,8},{1,9},{2,10},{3,11},{4,12},{5,13},{6,14},{7,15},{8,0},{9,1},... | collective-permute-start | bytes 98312 | tf_op jit(solution)/shard_map/ppermute | solution.py:391
  64.5 4.0 %collective-permute-start.11 = (f32[4,16,128]{2,1,0:T(8,128)S(1)}, f32[4,16,128]{2,1,0:T(8,128)S(1)}, u32[]{:S(2)}, u32[]{:S(2)}) collective-permute-start(f32[4,16,128]{2,1,0:T(8,128)S(1)} %add.32), channel_id=1, source_target_pairs={{0,24},{1,25},{2,26},{3,27},{4,28},{5,29},{6,30},{7,31},{8,16},{9,... | collective-permute-start | bytes 98312 | tf_op jit(solution)/shard_map/ppermute | solution.py:391
  68.5 3.2 %collective-permute-start.12 = (f32[4,16,128]{2,1,0:T(8,128)S(1)}, f32[4,16,128]{2,1,0:T(8,128)S(1)}, u32[]{:S(2)}, u32[]{:S(2)}) collective-permute-start(f32[4,16,128]{2,1,0:T(8,128)S(1)} %add.33), channel_id=1, source_target_pairs={{0,64},{32,96},{64,0},{96,32},{128,192},{160,224},{192,128},{224,1... | collective-permute-start | bytes 98312 | tf_op jit(solution)/shard_map/ppermute | solution.py:391
  71.7 5.5 %collective-permute-start.13 = (f32[4,16,128]{2,1,0:T(8,128)S(1)}, f32[4,16,128]{2,1,0:T(8,128)S(1)}, u32[]{:S(2)}, u32[]{:S(2)}) collective-permute-start(f32[4,16,128]{2,1,0:T(8,128)S(1)} %add.34), channel_id=1, source_target_pairs={{0,192},{32,224},{64,128},{96,160},{128,64},{160,96},{192,0},{224,... | collective-permute-start | bytes 98312 | tf_op jit(solution)/shard_map/ppermute | solution.py:391
  77.1 4.4 %collective-permute-start.14 = (f32[4,16,128]{2,1,0:T(8,128)S(1)}, f32[4,16,128]{2,1,0:T(8,128)S(1)}, u32[]{:S(2)}, u32[]{:S(2)}) collective-permute-start(f32[4,16,128]{2,1,0:T(8,128)S(1)} %add.35.mine), channel_id=1, source_target_pairs={{0,32},{32,0},{64,96},{96,64},{128,160},{160,128},{192,224},{224,1... | collective-permute-start | bytes 98312 | tf_op jit(solution)/shard_map/ppermute | solution.py:391
  82.6 6.6 %collective-permute-start.15 = (f32[10,8,128]{2,1,0:T(8,128)S(1)}, f32[10,8,128]{2,1,0:T(8,128)S(1)}, u32[]{:S(2)}, u32[]{:S(2)}) collective-permute-start(f32[10,8,128]{2,1,0:T(8,128)S(1)} %shard_map.128.sent), channel_id=1, source_target_pairs={{0,3},{1,6},{2,5},{3,0},{4,7},{5,2},{6,1},{7,4},{8,11},{9,14},{10,... | collective-permute-start | bytes 122888 | tf_op jit(solution)/shard_map/ppermute | solution.py:391
  89.2 5.6 %collective-permute-start.16 = (f32[12,8,128]{2,1,0:T(8,128)S(1)}, f32[12,8,128]{2,1,0:T(8,128)S(1)}, u32[]{:S(2)}, u32[]{:S(2)}) collective-permute-start(f32[12,8,128]{2,1,0:T(8,128)S(1)} %shard_map.129.sent), channel_id=1, source_target_pairs={{0,7},{1,2},{2,1},{3,4},{4,3},{5,6},{6,5},{7,0},{8,15},{9,10},{10,... | collective-permute-start | bytes 147464 | tf_op jit(solution)/shard_map/ppermute | solution.py:391
  94.9 5.0 %collective-permute-start.17 = (f32[16,8,128]{2,1,0:T(8,128)S(1)}, f32[16,8,128]{2,1,0:T(8,128)S(1)}, u32[]{:S(2)}, u32[]{:S(2)}) collective-permute-start(f32[16,8,128]{2,1,0:T(8,128)S(1)} %shard_map.130.sent), channel_id=1, source_target_pairs={{0,1},{1,0},{2,3},{3,2},{4,5},{5,4},{6,7},{7,6},{8,9},{9,8},{10,11... | collective-permute-start | bytes 196616 | tf_op jit(solution)/shard_map/ppermute | solution.py:391
  99.9 4.0 %collective-permute-start.18 = (f32[24,8,128]{2,1,0:T(8,128)S(1)}, f32[24,8,128]{2,1,0:T(8,128)S(1)}, u32[]{:S(2)}, u32[]{:S(2)}) collective-permute-start(f32[24,8,128]{2,1,0:T(8,128)S(1)} %shard_map.131), channel_id=1, source_target_pairs={{0,8},{1,9},{2,10},{3,11},{4,12},{5,13},{6,14},{7,15},{8,0},{9,1},... | collective-permute-start | bytes 294920 | tf_op jit(solution)/shard_map/ppermute | solution.py:391
  103.8 6.4 %collective-permute-start.19 = (f32[48,8,128]{2,1,0:T(8,128)S(1)}, f32[48,8,128]{2,1,0:T(8,128)S(1)}, u32[]{:S(2)}, u32[]{:S(2)}) collective-permute-start(f32[48,8,128]{2,1,0:T(8,128)S(1)} %pad_maximum_fusion.sent), channel_id=1, source_target_pairs={{0,24},{1,25},{2,26},{3,27},{4,28},{5,29},{6,30},{7,31},{8,16},{9,... | collective-permute-start | bytes 589832 | tf_op jit(solution)/shard_map/ppermute | solution.py:391
  110.3 5.3 %collective-permute-start.20 = (f32[64,8,128]{2,1,0:T(8,128)S(1)}, f32[64,8,128]{2,1,0:T(8,128)S(1)}, u32[]{:S(2)}, u32[]{:S(2)}) collective-permute-start(f32[64,8,128]{2,1,0:T(8,128)S(1)} %get-tuple-element.82.mine), channel_id=1, source_target_pairs={{0,32},{32,0},{64,96},{96,64},{128,160},{160,128},{192,224},{224,1... | collective-permute-start | bytes 786440 | tf_op jit(solution)/shard_map/ppermute | solution.py:391
  123.6 4.8 %collective-permute-start.21 = (f32[32,448]{1,0:T(8,128)S(1)}, f32[32,448]{1,0:T(8,128)S(1)}, u32[]{:S(2)}, u32[]{:S(2)}) collective-permute-start(f32[32,448]{1,0:T(8,128)S(1)} %get-tuple-element.85), channel_id=1, source_target_pairs={{0,64},{32,96},{64,0},{96,32},{128,192},{160,224},{192,128},{224,1... | collective-permute-start | bytes 172040 | tf_op jit(solution)/shard_map/ppermute | solution.py:391
  128.5 6.6 %collective-permute-start.22 = (f32[32,448]{1,0:T(8,128)S(1)}, f32[32,448]{1,0:T(8,128)S(1)}, u32[]{:S(2)}, u32[]{:S(2)}) collective-permute-start(f32[32,448]{1,0:T(8,128)S(1)} %add.36), channel_id=1, source_target_pairs={{0,192},{32,224},{64,128},{96,160},{128,64},{160,96},{192,0},{224,... | collective-permute-start | bytes 172040 | tf_op jit(solution)/shard_map/ppermute | solution.py:391
  (11 other events, 176.2 us)
Sparse Core Ops, SparseCore 0:
  10.6 104.1 all-gather.2

commit v9 on v8

--- a/solution.py
+++ b/solution.py
@@ -410,17 +410,11 @@
     gathered = lax.all_gather(acts, "mp", axis=0)
 
     table = jnp.asarray(met(ALONG_Z + ALONG_X, NMP))
-    quarters = call(
-        deal_kernel, [array((tokens // NX, LANES), BF16)] * NX, (member, table, acts), specs=[SMEM, SMEM, VMEM], moved=MIB
-    )
-    late, quarters = lax.optimization_barrier((q_prev, quarters))
-    across = [(x + 2) % NX * NZ + z for x in range(NX) for z in range(NZ)]
-    ring = [quarters[0]] + [swap(rows, "mp", level) for rows, level in zip(quarters[1:], (*ALONG_X, across))]
 
     half = rank // 2
     blocks = array((NMP, half, LANES), F32)
     mine, send = call(
-        error_kernel, [blocks, blocks], (member, core, table, late, et), specs=[SMEM] * 3 + [HBM] * 2,
+        error_kernel, [blocks, blocks], (member, core, table, q_prev, et), specs=[SMEM] * 3 + [HBM] * 2,
         scratch=[
             pltpu.VMEM((rank, ff), F32), pltpu.VMEM((chunks, ff, width), BF16), pltpu.VMEM((NMP, rank, LANES), F32),
             pltpu.SemaphoreType.DMA((chunks + 1,)),
@@ -433,18 +427,25 @@
         scratch=[pltpu.VMEM((rank, ff), F32), pltpu.VMEM((ff, tokens), BF16), pltpu.SemaphoreType.DMA((2,))],
         limit=16, flops=6 * rank * ff * tokens, moved=2 * ff * tokens,
     )
-    theirs, factor, ring = lax.optimization_barrier((theirs, factor, ring))
     tiles = lambda count: array((count, 8, LANES), F32)
     kept = lambda count: array((count, half, LANES), F32)
     sent, part, keep = call(
         open_kernel, [tiles(48), tiles(2 * QUARTER), kept(16)], (member, table, factor, mine, theirs),
         specs=[SMEM, SMEM] + [VMEM] * 3, moved=MIB,
     )
+    sent, late = lax.optimization_barrier((sent, acts))
+    quarters = call(
+        deal_kernel, [array((tokens // NX, LANES), BF16)] * NX, (member, table, late), specs=[SMEM, SMEM, VMEM], moved=MIB
+    )
+    across = [(x + 2) % NX * NZ + z for x in range(NX) for z in range(NZ)]
+    ring = [quarters[0]] + [swap(rows, "mp", level) for rows, level in zip(quarters[1:], (*ALONG_X, across))]
     came = swap(sent, "mp", ALONG_X[1])
     sent, part, keep = call(narrow_kernel, [tiles(24), tiles(QUARTER), kept(8)], (part, keep, came), moved=MIB)
     came = swap(sent, "mp", ALONG_X[0])
     for count, level in zip((4, 2, 1), ALONG_Z[::-1]):
         sent, keep = call(halve_kernel, [tiles(QUARTER + 2 * count), kept(count)], (part, keep, came), moved=MIB)
+        if count == 1:
+            sent, ring = lax.optimization_barrier((sent, ring))
         part, came = sent, swap(sent, "mp", level)
 
     keep, send = call(

time: 148 us -> 142 us (0.959)
  starting transfers between devices: 49.8 us -> 47.2 us
  waiting for transfers between devices: 51.2 us -> 49.1 us
  local copies, waits for them, and re-layouts: 2.65 us -> 0.99 us
    ppermute x24, starting transfers between devices: 49.8 us -> 47.2 us  [swap(): return lax.ppermute(value, axis, list(enumerate(level)))]
    ppermute x24, waiting for transfers between devices: 50.5 us -> 48.4 us  [swap(): return lax.ppermute(value, axis, list(enumerate(level)))]
    unnamed x20 -> x18, local copies, waits for them, and re-layouts: 2.65 us -> 0.99 us
  transfers between devices with their start and end apart: 25 -> 25, of which waited for: 20 -> 18; matrix products, arithmetic and copies ran while one was open for 0% -> 0% of each run, Pallas kernels for 17% -> 18%
where the time goes in v9:
time: 142 us
  waiting for transfers between devices  49.1 us (35%)
  starting transfers between devices  47.2 us (33%)
  Pallas kernels  29.9 us (21%)
  between operations  14.4 us (10%)
    ppermute x24, waiting for transfers between devices, swap(): return lax.ppermute(value, axis, list(enumerate(level)))  48.4 us
    ppermute x24, starting transfers between devices, swap(): return lax.ppermute(value, axis, list(enumerate(level)))  47.2 us
    pallas_call x18, Pallas kernels, call(): pl.pallas_call(kernel, out_shape=outs, in_specs=specs or [VMEM] * len(arg...  29.9 us
  transfers between devices with their start and end apart: 25, of which 18 were waited for; matrix products, arithmetic and copies ran while one was open for 0% of the time, Pallas kernels for 18%

profile of v9, /device:TPU:1, one launch (start us, length us, event | category | flops | bytes accessed | tf_op | source)
XLA Modules:
  0.0 141.7 jit_solution(3580492496079768747)
XLA Ops:
  8.0 4.6 %shard_map.120 = (f32[32,16,128]{2,1,0:T(8,128)}, f32[32,16,128]{2,1,0:T(8,128)}) custom-call(s32[1]{0:T(128)} %bitcast.1.member_ref, s32[1]{0:T(128)S(6)} %select_n.7.core_ref, s32[32,32]{1,0:T(8,128)} %constant.30.clone.place_ref, f32[32,448]{1,0:T(8,128)} %q_hbm.3, bf16[448,4096]{1,0:T(8,128)(2,1)} %bitcast.12), custom_call_target="tpu_custom_call" | custom-call | flops 352321536 | bytes 3670016 | tf_op jit(solution)/shard_map/pallas_call | solution.py:379
  12.6 3.3 %collective-permute-start = (f32[32,16,128]{2,1,0:T(8,128)}, f32[32,16,128]{2,1,0:T(8,128)S(1)}, u32[]{:S(2)}, u32[]{:S(2)}) collective-permute-start(f32[32,16,128]{2,1,0:T(8,128)} %get-tuple-element.48), channel_id=1, source_target_pairs={{0,32},{32,0},{64,96},{96,64},{128,160},{160,128},{192,224},{224,1... | collective-permute-start | bytes 786440 | tf_op jit(solution)/shard_map/ppermute | solution.py:391
  19.9 6.6 %collective-permute-done.1.came = f32[48,8,128]{2,1,0:T(8,128)S(1)} collective-permute-done((f32[48,8,128]{2,1,0:T(8,128)S(1)}, f32[48,8,128]{2,1,0:T(8,128)S(1)}, u32[]{:S(2)}, u32[]{:S(2)}) %collective-permute-start.1) | collective-permute-done | bytes 196640 | tf_op jit(solution)/shard_map/ppermute | solution.py:391
  26.6 5.1 %collective-permute-done.2.came = f32[24,8,128]{2,1,0:T(8,128)S(1)} collective-permute-done((f32[24,8,128]{2,1,0:T(8,128)S(1)}, f32[24,8,128]{2,1,0:T(8,128)S(1)}, u32[]{:S(2)}, u32[]{:S(2)}) %collective-permute-start.2) | collective-permute-done | bytes 98336 | tf_op jit(solution)/shard_map/ppermute | solution.py:391
  36.1 5.4 %collective-permute-start.4 = (f32[12,8,128]{2,1,0:T(8,128)S(1)}, f32[12,8,128]{2,1,0:T(8,128)S(1)}, u32[]{:S(2)}, u32[]{:S(2)}) collective-permute-start(f32[12,8,128]{2,1,0:T(8,128)S(1)} %get-tuple-element.58.tokens), channel_id=1, source_target_pairs={{0,7},{1,2},{2,1},{3,4},{4,3},{5,6},{6,5},{7,0},{8,15},{9,10},{10,... | collective-permute-start | bytes 147464 | tf_op jit(solution)/shard_map/ppermute | solution.py:391
  43.4 2.1 %collective-permute-start.8 = (f32[10,8,128]{2,1,0:T(8,128)S(1)}, f32[10,8,128]{2,1,0:T(8,128)S(1)}, u32[]{:S(2)}, u32[]{:S(2)}) collective-permute-start(f32[10,8,128]{2,1,0:T(8,128)S(1)} %get-tuple-element.66.sent), channel_id=1, source_target_pairs={{0,3},{1,6},{2,5},{3,0},{4,7},{5,2},{6,1},{7,4},{8,11},{9,14},{10,... | collective-permute-start | bytes 122888 | tf_op jit(solution)/shard_map/ppermute | solution.py:391
  45.5 3.1 %collective-permute-done.8.came = f32[10,8,128]{2,1,0:T(8,128)S(1)} collective-permute-done((f32[10,8,128]{2,1,0:T(8,128)S(1)}, f32[10,8,128]{2,1,0:T(8,128)S(1)}, u32[]{:S(2)}, u32[]{:S(2)}) %collective-permute-start.8) | collective-permute-done | bytes 40992 | tf_op jit(solution)/shard_map/ppermute | solution.py:391
  49.6 4.1 %collective-permute-start.9 = (f32[4,16,128]{2,1,0:T(8,128)S(1)}, f32[4,16,128]{2,1,0:T(8,128)S(1)}, u32[]{:S(2)}, u32[]{:S(2)}) collective-permute-start(f32[4,16,128]{2,1,0:T(8,128)S(1)} %get-tuple-element.73), channel_id=1, source_target_pairs={{0,32},{32,0},{64,96},{96,64},{128,160},{160,128},{192,224},{224,1... | collective-permute-start | bytes 98312 | tf_op jit(solution)/shard_map/ppermute | solution.py:391
  54.5 2.8 %collective-permute-done.10 = f32[4,16,128]{2,1,0:T(8,128)S(1)} collective-permute-done((f32[4,16,128]{2,1,0:T(8,128)S(1)}, f32[4,16,128]{2,1,0:T(8,128)S(1)}, u32[]{:S(2)}, u32[]{:S(2)}) %collective-permute-start.10) | collective-permute-done | bytes 32800 | tf_op jit(solution)/shard_map/ppermute | solution.py:391
  57.3 2.5 %collective-permute-start.11 = (f32[4,16,128]{2,1,0:T(8,128)S(1)}, f32[4,16,128]{2,1,0:T(8,128)S(1)}, u32[]{:S(2)}, u32[]{:S(2)}) collective-permute-start(f32[4,16,128]{2,1,0:T(8,128)S(1)} %add.32), channel_id=1, source_target_pairs={{0,24},{1,25},{2,26},{3,27},{4,28},{5,29},{6,30},{7,31},{8,16},{9,... | collective-permute-start | bytes 98312 | tf_op jit(solution)/shard_map/ppermute | solution.py:391
  64.0 2.5 %collective-permute-start.13 = (f32[4,16,128]{2,1,0:T(8,128)S(1)}, f32[4,16,128]{2,1,0:T(8,128)S(1)}, u32[]{:S(2)}, u32[]{:S(2)}) collective-permute-start(f32[4,16,128]{2,1,0:T(8,128)S(1)} %add.34), channel_id=1, source_target_pairs={{0,192},{32,224},{64,128},{96,160},{128,64},{160,96},{192,0},{224,... | collective-permute-start | bytes 98312 | tf_op jit(solution)/shard_map/ppermute | solution.py:391
  68.0 4.9 %collective-permute-start.14 = (f32[4,16,128]{2,1,0:T(8,128)S(1)}, f32[4,16,128]{2,1,0:T(8,128)S(1)}, u32[]{:S(2)}, u32[]{:S(2)}) collective-permute-start(f32[4,16,128]{2,1,0:T(8,128)S(1)} %add.35.mine), channel_id=1, source_target_pairs={{0,32},{32,0},{64,96},{96,64},{128,160},{160,128},{192,224},{224,1... | collective-permute-start | bytes 98312 | tf_op jit(solution)/shard_map/ppermute | solution.py:391
  74.8 2.9 %collective-permute-start.15 = (f32[10,8,128]{2,1,0:T(8,128)S(1)}, f32[10,8,128]{2,1,0:T(8,128)S(1)}, u32[]{:S(2)}, u32[]{:S(2)}) collective-permute-start(f32[10,8,128]{2,1,0:T(8,128)S(1)} %shard_map.128.sent), channel_id=1, source_target_pairs={{0,3},{1,6},{2,5},{3,0},{4,7},{5,2},{6,1},{7,4},{8,11},{9,14},{10,... | collective-permute-start | bytes 122888 | tf_op jit(solution)/shard_map/ppermute | solution.py:391
  77.7 2.4 %collective-permute-done.15.came = f32[10,8,128]{2,1,0:T(8,128)S(1)} collective-permute-done((f32[10,8,128]{2,1,0:T(8,128)S(1)}, f32[10,8,128]{2,1,0:T(8,128)S(1)}, u32[]{:S(2)}, u32[]{:S(2)}) %collective-permute-start.15) | collective-permute-done | bytes 40992 | tf_op jit(solution)/shard_map/ppermute | solution.py:391
  80.1 2.5 %collective-permute-start.16 = (f32[12,8,128]{2,1,0:T(8,128)S(1)}, f32[12,8,128]{2,1,0:T(8,128)S(1)}, u32[]{:S(2)}, u32[]{:S(2)}) collective-permute-start(f32[12,8,128]{2,1,0:T(8,128)S(1)} %shard_map.129.sent), channel_id=1, source_target_pairs={{0,7},{1,2},{2,1},{3,4},{4,3},{5,6},{6,5},{7,0},{8,15},{9,10},{10,... | collective-permute-start | bytes 147464 | tf_op jit(solution)/shard_map/ppermute | solution.py:391
  84.7 3.4 %collective-permute-start.17 = (f32[16,8,128]{2,1,0:T(8,128)S(1)}, f32[16,8,128]{2,1,0:T(8,128)S(1)}, u32[]{:S(2)}, u32[]{:S(2)}) collective-permute-start(f32[16,8,128]{2,1,0:T(8,128)S(1)} %shard_map.130.sent), channel_id=1, source_target_pairs={{0,1},{1,0},{2,3},{3,2},{4,5},{5,4},{6,7},{7,6},{8,9},{9,8},{10,11... | collective-permute-start | bytes 196616 | tf_op jit(solution)/shard_map/ppermute | solution.py:391
  88.1 3.5 %collective-permute-done.17.came = f32[16,8,128]{2,1,0:T(8,128)S(1)} collective-permute-done((f32[16,8,128]{2,1,0:T(8,128)S(1)}, f32[16,8,128]{2,1,0:T(8,128)S(1)}, u32[]{:S(2)}, u32[]{:S(2)}) %collective-permute-start.17) | collective-permute-done | bytes 65568 | tf_op jit(solution)/shard_map/ppermute | solution.py:391
  91.8 6.1 %collective-permute-done.18 = f32[24,8,128]{2,1,0:T(8,128)S(1)} collective-permute-done((f32[24,8,128]{2,1,0:T(8,128)S(1)}, f32[24,8,128]{2,1,0:T(8,128)S(1)}, u32[]{:S(2)}, u32[]{:S(2)}) %collective-permute-start.18) | collective-permute-done | bytes 98336 | tf_op jit(solution)/shard_map/ppermute | solution.py:391
  99.2 5.8 %collective-permute-done.19.came = f32[48,8,128]{2,1,0:T(8,128)S(1)} collective-permute-done((f32[48,8,128]{2,1,0:T(8,128)S(1)}, f32[48,8,128]{2,1,0:T(8,128)S(1)}, u32[]{:S(2)}, u32[]{:S(2)}) %collective-permute-start.19) | collective-permute-done | bytes 196640 | tf_op jit(solution)/shard_map/ppermute | solution.py:391
  105.0 3.1 %collective-permute-start.20 = (f32[64,8,128]{2,1,0:T(8,128)S(1)}, f32[64,8,128]{2,1,0:T(8,128)S(1)}, u32[]{:S(2)}, u32[]{:S(2)}) collective-permute-start(f32[64,8,128]{2,1,0:T(8,128)S(1)} %get-tuple-element.74.mine), channel_id=1, source_target_pairs={{0,32},{32,0},{64,96},{96,64},{128,160},{160,128},{192,224},{224,1... | collective-permute-start | bytes 786440 | tf_op jit(solution)/shard_map/ppermute | solution.py:391
  109.2 8.0 %shard_map.133 = (bf16[32,96,128]{2,1,0:T(8,128)(2,1)S(1)}, f32[32,448]{1,0:T(8,128)S(1)}) custom-call(s32[1]{0:T(128)} %bitcast.1.member_ref, s32[1]{0:T(128)S(6)} %select_n.7.core_ref, s32[32,32]{1,0:T(8,128)S(1)} %copy-done.6, f32[64,8,128]{2,1,0:T(8,128)S(1)} %get-tuple-element.74.mine, f32[64,8,128]{2,1,0:T(8,128)S(1)} %collective-permute-done.20.theirs, ...), custom_call_target="tpu_custom_call" | custom-call | flops 469762048 | bytes 3670016 | tf_op jit(solution)/shard_map/pallas_call | solution.py:379
  117.9 4.2 %shard_map.134.lower = f32[16,448,128]{2,1,0:T(8,128)S(1)} custom-call(bf16[32,1024,128]{2,1,0:T(8,128)(2,1)} %bitcast.23, bf16[448,4096]{1,0:T(8,128)(2,1)} %bitcast.13, bf16[448,1024]{1,0:T(8,128)(2,1)S(1)} %bitcast.18), custom_call_target="tpu_custom_call" | custom-call | flops 1879048192 | bytes 10485760 | tf_op jit(solution)/shard_map/pallas_call | solution.py:379
  124.1 4.2 %shard_map.135.upper = f32[16,448,128]{2,1,0:T(8,128)S(1)} custom-call(bf16[32,1024,128]{2,1,0:T(8,128)(2,1)} %bitcast.24, bf16[448,4096]{1,0:T(8,128)(2,1)} %bitcast.14, bf16[448,1024]{1,0:T(8,128)(2,1)S(1)} %bitcast.19), custom_call_target="tpu_custom_call" | custom-call | flops 1879048192 | bytes 10485760 | tf_op jit(solution)/shard_map/pallas_call | solution.py:379
  130.3 4.5 %shard_map.136 = (f32[448,512]{1,0:T(8,128)}, f32[448,512]{1,0:T(8,128)}, f32[448,512]{1,0:T(8,128)}, bf16[448,4096]{1,0:T(8,128)(2,1)}, f32[32,448]{1,0:T(8,128)}) custom-call(s32[1]{0:T(128)} %bitcast.dp_ref, f32[32,448]{1,0:T(8,128)S(1)} %add.38.sum_ref, bf16[32,96,128]{2,1,0:T(8,128)(2,1)S(1)} %get-tuple-element.81.basis_ref, ...), custom_call_target="tpu_custom_call" | custom-call | flops 704643072 | bytes 20971520 | tf_op jit(solution)/shard_map/pallas_call | solution.py:379
  (72 shorter events, 29.7 us)
Async XLA Ops:
  7.2 110.0 %all-gather.3.cloned.1.call-start = ((), (), s32[]{:S(2)}) async-start(), calls=%async_computation | async-start | bytes 8650752 | tf_op jit(solution)/shard_map/all_gather | solution.py:410
  12.6 4.7 %collective-permute-start = (f32[32,16,128]{2,1,0:T(8,128)}, f32[32,16,128]{2,1,0:T(8,128)S(1)}, u32[]{:S(2)}, u32[]{:S(2)}) collective-permute-start(f32[32,16,128]{2,1,0:T(8,128)} %get-tuple-element.48), channel_id=1, source_target_pairs={{0,32},{32,0},{64,96},{96,64},{128,160},{160,128},{192,224},{224,1... | collective-permute-start | bytes 786440 | tf_op jit(solution)/shard_map/ppermute | solution.py:391
  19.1 7.4 %collective-permute-start.1 = (f32[48,8,128]{2,1,0:T(8,128)S(1)}, f32[48,8,128]{2,1,0:T(8,128)S(1)}, u32[]{:S(2)}, u32[]{:S(2)}) collective-permute-start(f32[48,8,128]{2,1,0:T(8,128)S(1)} %get-tuple-element.52), channel_id=1, source_target_pairs={{0,24},{1,25},{2,26},{3,27},{4,28},{5,29},{6,30},{7,31},{8,16},{9,... | collective-permute-start | bytes 589832 | tf_op jit(solution)/shard_map/ppermute | solution.py:391
  26.5 5.2 %collective-permute-start.2 = (f32[24,8,128]{2,1,0:T(8,128)S(1)}, f32[24,8,128]{2,1,0:T(8,128)S(1)}, u32[]{:S(2)}, u32[]{:S(2)}) collective-permute-start(f32[24,8,128]{2,1,0:T(8,128)S(1)} %get-tuple-element.55), channel_id=1, source_target_pairs={{0,8},{1,9},{2,10},{3,11},{4,12},{5,13},{6,14},{7,15},{8,0},{9,1},... | collective-permute-start | bytes 294920 | tf_op jit(solution)/shard_map/ppermute | solution.py:391
  31.8 4.3 %collective-permute-start.3 = (f32[16,8,128]{2,1,0:T(8,128)S(1)}, f32[16,8,128]{2,1,0:T(8,128)S(1)}, u32[]{:S(2)}, u32[]{:S(2)}) collective-permute-start(f32[16,8,128]{2,1,0:T(8,128)S(1)} %get-tuple-element.56.tokens), channel_id=1, source_target_pairs={{0,1},{1,0},{2,3},{3,2},{4,5},{5,4},{6,7},{7,6},{8,9},{9,8},{10,11... | collective-permute-start | bytes 196616 | tf_op jit(solution)/shard_map/ppermute | solution.py:391
  32.7 10.6 %collective-permute-start.5 = (bf16[256,128]{1,0:T(8,128)(2,1)S(1)}, bf16[256,128]{1,0:T(8,128)(2,1)S(1)}, u32[]{:S(2)}, u32[]{:S(2)}) collective-permute-start(bf16[256,128]{1,0:T(8,128)(2,1)S(1)} %get-tuple-element.63), channel_id=1, source_target_pairs={{0,8},{1,9},{2,10},{3,11},{4,12},{5,13},{6,14},{7,15},{8,0},{9,1},... | collective-permute-start | bytes 196616 | tf_op jit(solution)/shard_map/ppermute | solution.py:391
  32.8 10.5 %collective-permute-start.6 = (bf16[256,128]{1,0:T(8,128)(2,1)S(1)}, bf16[256,128]{1,0:T(8,128)(2,1)S(1)}, u32[]{:S(2)}, u32[]{:S(2)}) collective-permute-start(bf16[256,128]{1,0:T(8,128)(2,1)S(1)} %get-tuple-element.64), channel_id=1, source_target_pairs={{0,24},{1,25},{2,26},{3,27},{4,28},{5,29},{6,30},{7,31},{8,16},{9,... | collective-permute-start | bytes 196616 | tf_op jit(solution)/shard_map/ppermute | solution.py:391
  34.0 9.4 %collective-permute-start.7 = (bf16[256,128]{1,0:T(8,128)(2,1)S(1)}, bf16[256,128]{1,0:T(8,128)(2,1)S(1)}, u32[]{:S(2)}, u32[]{:S(2)}) collective-permute-start(bf16[256,128]{1,0:T(8,128)(2,1)S(1)} %get-tuple-element.65), channel_id=1, source_target_pairs={{0,16},{1,17},{2,18},{3,19},{4,20},{5,21},{6,22},{7,23},{8,24},{9,... | collective-permute-start | bytes 196616 | tf_op jit(solution)/shard_map/ppermute | solution.py:391
  36.1 7.2 %collective-permute-start.4 = (f32[12,8,128]{2,1,0:T(8,128)S(1)}, f32[12,8,128]{2,1,0:T(8,128)S(1)}, u32[]{:S(2)}, u32[]{:S(2)}) collective-permute-start(f32[12,8,128]{2,1,0:T(8,128)S(1)} %get-tuple-element.58.tokens), channel_id=1, source_target_pairs={{0,7},{1,2},{2,1},{3,4},{4,3},{5,6},{6,5},{7,0},{8,15},{9,10},{10,... | collective-permute-start | bytes 147464 | tf_op jit(solution)/shard_map/ppermute | solution.py:391
  43.4 5.2 %collective-permute-start.8 = (f32[10,8,128]{2,1,0:T(8,128)S(1)}, f32[10,8,128]{2,1,0:T(8,128)S(1)}, u32[]{:S(2)}, u32[]{:S(2)}) collective-permute-start(f32[10,8,128]{2,1,0:T(8,128)S(1)} %get-tuple-element.66.sent), channel_id=1, source_target_pairs={{0,3},{1,6},{2,5},{3,0},{4,7},{5,2},{6,1},{7,4},{8,11},{9,14},{10,... | collective-permute-start | bytes 122888 | tf_op jit(solution)/shard_map/ppermute | solution.py:391
  49.6 4.9 %collective-permute-start.9 = (f32[4,16,128]{2,1,0:T(8,128)S(1)}, f32[4,16,128]{2,1,0:T(8,128)S(1)}, u32[]{:S(2)}, u32[]{:S(2)}) collective-permute-start(f32[4,16,128]{2,1,0:T(8,128)S(1)} %get-tuple-element.73), channel_id=1, source_target_pairs={{0,32},{32,0},{64,96},{96,64},{128,160},{160,128},{192,224},{224,1... | collective-permute-start | bytes 98312 | tf_op jit(solution)/shard_map/ppermute | solution.py:391
  54.5 2.8 %collective-permute-start.10 = (f32[4,16,128]{2,1,0:T(8,128)S(1)}, f32[4,16,128]{2,1,0:T(8,128)S(1)}, u32[]{:S(2)}, u32[]{:S(2)}) collective-permute-start(f32[4,16,128]{2,1,0:T(8,128)S(1)} %add.31), channel_id=1, source_target_pairs={{0,8},{1,9},{2,10},{3,11},{4,12},{5,13},{6,14},{7,15},{8,0},{9,1},... | collective-permute-start | bytes 98312 | tf_op jit(solution)/shard_map/ppermute | solution.py:391
  57.3 4.0 %collective-permute-start.11 = (f32[4,16,128]{2,1,0:T(8,128)S(1)}, f32[4,16,128]{2,1,0:T(8,128)S(1)}, u32[]{:S(2)}, u32[]{:S(2)}) collective-permute-start(f32[4,16,128]{2,1,0:T(8,128)S(1)} %add.32), channel_id=1, source_target_pairs={{0,24},{1,25},{2,26},{3,27},{4,28},{5,29},{6,30},{7,31},{8,16},{9,... | collective-permute-start | bytes 98312 | tf_op jit(solution)/shard_map/ppermute | solution.py:391
  61.3 2.8 %collective-permute-start.12 = (f32[4,16,128]{2,1,0:T(8,128)S(1)}, f32[4,16,128]{2,1,0:T(8,128)S(1)}, u32[]{:S(2)}, u32[]{:S(2)}) collective-permute-start(f32[4,16,128]{2,1,0:T(8,128)S(1)} %add.33), channel_id=1, source_target_pairs={{0,64},{32,96},{64,0},{96,32},{128,192},{160,224},{192,128},{224,1... | collective-permute-start | bytes 98312 | tf_op jit(solution)/shard_map/ppermute | solution.py:391
  64.0 4.0 %collective-permute-start.13 = (f32[4,16,128]{2,1,0:T(8,128)S(1)}, f32[4,16,128]{2,1,0:T(8,128)S(1)}, u32[]{:S(2)}, u32[]{:S(2)}) collective-permute-start(f32[4,16,128]{2,1,0:T(8,128)S(1)} %add.34), channel_id=1, source_target_pairs={{0,192},{32,224},{64,128},{96,160},{128,64},{160,96},{192,0},{224,... | collective-permute-start | bytes 98312 | tf_op jit(solution)/shard_map/ppermute | solution.py:391
  68.0 5.8 %collective-permute-start.14 = (f32[4,16,128]{2,1,0:T(8,128)S(1)}, f32[4,16,128]{2,1,0:T(8,128)S(1)}, u32[]{:S(2)}, u32[]{:S(2)}) collective-permute-start(f32[4,16,128]{2,1,0:T(8,128)S(1)} %add.35.mine), channel_id=1, source_target_pairs={{0,32},{32,0},{64,96},{96,64},{128,160},{160,128},{192,224},{224,1... | collective-permute-start | bytes 98312 | tf_op jit(solution)/shard_map/ppermute | solution.py:391
  74.8 5.3 %collective-permute-start.15 = (f32[10,8,128]{2,1,0:T(8,128)S(1)}, f32[10,8,128]{2,1,0:T(8,128)S(1)}, u32[]{:S(2)}, u32[]{:S(2)}) collective-permute-start(f32[10,8,128]{2,1,0:T(8,128)S(1)} %shard_map.128.sent), channel_id=1, source_target_pairs={{0,3},{1,6},{2,5},{3,0},{4,7},{5,2},{6,1},{7,4},{8,11},{9,14},{10,... | collective-permute-start | bytes 122888 | tf_op jit(solution)/shard_map/ppermute | solution.py:391
  80.1 4.6 %collective-permute-start.16 = (f32[12,8,128]{2,1,0:T(8,128)S(1)}, f32[12,8,128]{2,1,0:T(8,128)S(1)}, u32[]{:S(2)}, u32[]{:S(2)}) collective-permute-start(f32[12,8,128]{2,1,0:T(8,128)S(1)} %shard_map.129.sent), channel_id=1, source_target_pairs={{0,7},{1,2},{2,1},{3,4},{4,3},{5,6},{6,5},{7,0},{8,15},{9,10},{10,... | collective-permute-start | bytes 147464 | tf_op jit(solution)/shard_map/ppermute | solution.py:391
  84.7 7.0 %collective-permute-start.17 = (f32[16,8,128]{2,1,0:T(8,128)S(1)}, f32[16,8,128]{2,1,0:T(8,128)S(1)}, u32[]{:S(2)}, u32[]{:S(2)}) collective-permute-start(f32[16,8,128]{2,1,0:T(8,128)S(1)} %shard_map.130.sent), channel_id=1, source_target_pairs={{0,1},{1,0},{2,3},{3,2},{4,5},{5,4},{6,7},{7,6},{8,9},{9,8},{10,11... | collective-permute-start | bytes 196616 | tf_op jit(solution)/shard_map/ppermute | solution.py:391
  91.7 6.2 %collective-permute-start.18 = (f32[24,8,128]{2,1,0:T(8,128)S(1)}, f32[24,8,128]{2,1,0:T(8,128)S(1)}, u32[]{:S(2)}, u32[]{:S(2)}) collective-permute-start(f32[24,8,128]{2,1,0:T(8,128)S(1)} %shard_map.131), channel_id=1, source_target_pairs={{0,8},{1,9},{2,10},{3,11},{4,12},{5,13},{6,14},{7,15},{8,0},{9,1},... | collective-permute-start | bytes 294920 | tf_op jit(solution)/shard_map/ppermute | solution.py:391
  97.9 7.0 %collective-permute-start.19 = (f32[48,8,128]{2,1,0:T(8,128)S(1)}, f32[48,8,128]{2,1,0:T(8,128)S(1)}, u32[]{:S(2)}, u32[]{:S(2)}) collective-permute-start(f32[48,8,128]{2,1,0:T(8,128)S(1)} %pad_maximum_fusion.sent), channel_id=1, source_target_pairs={{0,24},{1,25},{2,26},{3,27},{4,28},{5,29},{6,30},{7,31},{8,16},{9,... | collective-permute-start | bytes 589832 | tf_op jit(solution)/shard_map/ppermute | solution.py:391
  105.0 4.2 %collective-permute-start.20 = (f32[64,8,128]{2,1,0:T(8,128)S(1)}, f32[64,8,128]{2,1,0:T(8,128)S(1)}, u32[]{:S(2)}, u32[]{:S(2)}) collective-permute-start(f32[64,8,128]{2,1,0:T(8,128)S(1)} %get-tuple-element.74.mine), channel_id=1, source_target_pairs={{0,32},{32,0},{64,96},{96,64},{128,160},{160,128},{192,224},{224,1... | collective-permute-start | bytes 786440 | tf_op jit(solution)/shard_map/ppermute | solution.py:391
  117.2 4.9 %collective-permute-start.21 = (f32[32,448]{1,0:T(8,128)S(1)}, f32[32,448]{1,0:T(8,128)S(1)}, u32[]{:S(2)}, u32[]{:S(2)}) collective-permute-start(f32[32,448]{1,0:T(8,128)S(1)} %get-tuple-element.77), channel_id=1, source_target_pairs={{0,64},{32,96},{64,0},{96,32},{128,192},{160,224},{192,128},{224,1... | collective-permute-start | bytes 172040 | tf_op jit(solution)/shard_map/ppermute | solution.py:391
  122.2 6.1 %collective-permute-start.22 = (f32[32,448]{1,0:T(8,128)S(1)}, f32[32,448]{1,0:T(8,128)S(1)}, u32[]{:S(2)}, u32[]{:S(2)}) collective-permute-start(f32[32,448]{1,0:T(8,128)S(1)} %add.36), channel_id=1, source_target_pairs={{0,192},{32,224},{64,128},{96,160},{128,64},{160,96},{192,0},{224,... | collective-permute-start | bytes 172040 | tf_op jit(solution)/shard_map/ppermute | solution.py:391
  (10 other events, 176.1 us)
Sparse Core Ops, SparseCore 0:
  10.6 103.1 all-gather.2

commit v10 on v9

--- a/solution.py
+++ b/solution.py
@@ -41,6 +41,27 @@
     return np.array(held, np.int32)
 
 
+def x_at(place):
+    x = lax.div(lax.axis_index("mp"), NZ)
+    if place & 2:
+        x = NX - 1 - x
+    if place & 1:
+        x = x + 1 - 2 * lax.rem(x, 2)
+    return x
+
+
+def member_at(place):
+    z = lax.rem(lax.axis_index("mp"), NZ)
+    for bit, far in ((4, 1), (2, -1), (1, 3)):
+        if place & bit:
+            z = lax.rem(z + NZ + far * (1 - 2 * lax.rem(z, 2)), NZ)
+    return x_at(place // NZ) * NZ + z
+
+
+def lower_core():
+    return lax.rem(lax.axis_index("dp"), 2) == 0
+
+
 def split3(value):
     hi = value.astype(BF16)
     rest = value - hi.astype(F32)
@@ -87,7 +108,7 @@
     return jnp.concatenate([tiles[row * columns + column] for row in range(rows // 8)], axis=0)
 
 
-def error_kernel(member_ref, core_ref, place_ref, q_hbm, et_hbm, keep, send, q_ref, et_ref, parts, sems):
+def error_kernel(q_hbm, et_hbm, keep, send, q_ref, et_ref, parts, sems):
     count, width = et_ref.shape[0], et_ref.shape[2]
     copies = [
         pltpu.make_async_copy(et_hbm.at[:, chunk * width : (chunk + 1) * width], et_ref.at[chunk], sems.at[chunk])
@@ -106,9 +127,9 @@
         part = fold3(dot_nn(split, et_ref[chunk]))
         for block in range(blocks):
             parts[chunk * blocks + block] = lanes(part, block)
-    lower = core_ref[0] == 0
+    lower = lower_core()
     for place in range(NMP):
-        block = parts[place_ref[member_ref[0], place]]
+        block = parts[member_at(place)]
         keep[place] = jnp.where(lower, block[:half], block[half:])
         send[place] = jnp.where(lower, block[half:], block[:half])
 
@@ -137,18 +158,18 @@
     )
 
 
-def deal_kernel(member_ref, place_ref, acts_ref, *outs):
+def deal_kernel(acts_ref, *outs):
     rows = outs[0].shape[0]
     for place in range(NX):
-        x = lax.div(place_ref[member_ref[0], place * NZ], NZ)
+        x = x_at(place)
         outs[place][...] = acts_ref[pl.ds(pl.multiple_of(x * rows, rows), rows), :]
 
 
-def open_kernel(member_ref, place_ref, tokens, mine, theirs, message, keep_tokens, keep):
+def open_kernel(tokens, mine, theirs, message, keep_tokens, keep):
     half = NX // 2
     for place in range(half):
         for out, other in ((keep_tokens, place), (message, place + half)):
-            x = lax.div(place_ref[member_ref[0], other * NZ], NZ)
+            x = x_at(other)
             out[place * QUARTER : (place + 1) * QUARTER] = tokens[x]
     both = mine[...] + theirs[...]
     count = both.shape[0] // 2
@@ -174,11 +195,11 @@
     store_blocks(both[blocks // 2 :], message, QUARTER)
 
 
-def piece_kernel(member_ref, core_ref, place_ref, sent, kept, came, *refs):
+def piece_kernel(sent, kept, came, *refs):
     acts_refs, keep, send = refs[:NX], refs[NX], refs[NX + 1]
     columns = acts_refs[0].shape[0] // LANES
     half = keep.shape[1]
-    lower = core_ref[0] == 0
+    lower = lower_core()
     errors = (kept[...] + load_blocks(came, QUARTER, 1))[0]
     factor = jnp.concatenate(
         [rows_of(sent, column, columns, FACTOR) + rows_of(came, column, columns, FACTOR) for column in range(columns)],
@@ -186,25 +207,25 @@
     )
     factor = split3(factor)
     for place in range(NX):
-        x = lax.div(place_ref[member_ref[0], place * NZ], NZ)
+        x = x_at(place)
         piece = fold3(dot_nn(factor, acts_refs[place][...]))
         stays = jnp.where(lower, piece[:half], piece[half:])
         keep[x] = stays + errors if place == 0 else stays
         send[x] = jnp.where(lower, piece[half:], piece[:half])
 
 
-def start_kernel(member_ref, core_ref, place_ref, mine, theirs, *refs):
+def start_kernel(mine, theirs, *refs):
     acts_refs, message = refs[:NX], refs[NX]
-    lower = core_ref[0] == 0
+    lower = lower_core()
     total = None
     for place in range(NX):
-        x = lax.div(place_ref[member_ref[0], place * NZ], NZ)
+        x = x_at(place)
         first, second = mine[x] * (1.0 / NDP), theirs[x] * (1.0 / NDP)
         panel = jnp.concatenate([jnp.where(lower, first, second), jnp.where(lower, second, first)], axis=0)
         part = dot_nt(split3(panel), acts_refs[place][...])
         total = part if total is None else total + part
     tiles_of(fold3(total), message)
-    store_blocks(mine[lax.div(member_ref[0], NZ)][None] * (1.0 / NDP), message, QUARTER)
+    store_blocks(mine[x_at(0)][None] * (1.0 / NDP), message, QUARTER)
 
 
 def double_kernel(sent, came, message):
@@ -224,7 +245,7 @@
         rows[place * count : (place + 1) * count] = ref[start + QUARTER : start + each]
 
 
-def ortho_kernel(member_ref, core_ref, place_ref, mine, theirs, tokens, gt_ref, et_hbm, split, right, panel, et_ref, factors,
+def ortho_kernel(mine, theirs, tokens, gt_ref, et_hbm, split, right, panel, et_ref, factors,
                  sems):
     chunks, width = et_ref.shape[0], et_ref.shape[2]
     copies = [
@@ -233,13 +254,12 @@
     ]
     for copy in copies:
         copy.start()
-    member = member_ref[0]
-    lower = core_ref[0] == 0
+    lower = lower_core()
     half = panel.shape[1] // 2
     for place in range(NMP):
         first = jnp.concatenate([mine[2 * place], mine[2 * place + 1]], axis=0)
         second = jnp.concatenate([theirs[2 * place], theirs[2 * place + 1]], axis=0)
-        block = place_ref[member, place]
+        block = member_at(place)
         panel[block, :half] = jnp.where(lower, first, second)
         panel[block, half:] = jnp.where(lower, second, first)
     square = panel.shape[1:]
@@ -248,7 +268,7 @@
     columns = factors.shape[2] // LANES
     for place in range(NX):
         tiles = tokens.at[pl.ds(place * QUARTER, QUARTER)]
-        factors[lax.div(place_ref[member, place * NZ], NZ)] = jnp.concatenate(
+        factors[x_at(place)] = jnp.concatenate(
             [rows_of(tiles, column, columns, FACTOR) for column in range(columns)], axis=1
         )
     factor = jnp.concatenate([factors[x] for x in range(NX)], axis=1)
@@ -331,7 +351,7 @@
     lax.fori_loop(0, chunks, body, 0)
 
 
-def final_kernel(dp_ref, sum_ref, basis_ref, lower, upper, weight, moment1, moment2, new_weight, new_moment1,
+def final_kernel(sum_ref, basis_ref, lower, upper, weight, moment1, moment2, new_weight, new_moment1,
                  new_moment2, new_error, q_new, updated, rounded, sems):
     mean = sum_ref[...] * (1.0 / NDP)
     q_new[...] = mean
@@ -354,7 +374,7 @@
         copy.start()
         copies.append(copy)
 
-    update = approx_of(dp_ref[0])
+    update = approx_of(lax.axis_index("dp"))
     first = beta_one * moment1[...] + (1.0 - beta_one) * update
     second = beta_two * moment2[...] + (1.0 - beta_two) * update * update
     updated[0] = first
@@ -398,9 +418,6 @@
 
 
 def shards(acts, grad_out, error_buffer, q_prev, weight, moment1, moment2):
-    member = lax.axis_index("mp").astype(jnp.int32).reshape(1)
-    dp = lax.axis_index("dp").astype(jnp.int32).reshape(1)
-    core = dp % 2
     gt, et = grad_out.T, error_buffer.T
     rank, ff = q_prev.shape
     tokens, model = acts.shape[0], et.shape[1]
@@ -409,12 +426,11 @@
 
     gathered = lax.all_gather(acts, "mp", axis=0)
 
-    table = jnp.asarray(met(ALONG_Z + ALONG_X, NMP))
 
     half = rank // 2
     blocks = array((NMP, half, LANES), F32)
     mine, send = call(
-        error_kernel, [blocks, blocks], (member, core, table, q_prev, et), specs=[SMEM] * 3 + [HBM] * 2,
+        error_kernel, [blocks, blocks], (q_prev, et), specs=[HBM] * 2,
         scratch=[
             pltpu.VMEM((rank, ff), F32), pltpu.VMEM((chunks, ff, width), BF16), pltpu.VMEM((NMP, rank, LANES), F32),
             pltpu.SemaphoreType.DMA((chunks + 1,)),
@@ -430,12 +446,11 @@
     tiles = lambda count: array((count, 8, LANES), F32)
     kept = lambda count: array((count, half, LANES), F32)
     sent, part, keep = call(
-        open_kernel, [tiles(48), tiles(2 * QUARTER), kept(16)], (member, table, factor, mine, theirs),
-        specs=[SMEM, SMEM] + [VMEM] * 3, moved=MIB,
+        open_kernel, [tiles(48), tiles(2 * QUARTER), kept(16)], (factor, mine, theirs), moved=MIB,
     )
     sent, late = lax.optimization_barrier((sent, acts))
     quarters = call(
-        deal_kernel, [array((tokens // NX, LANES), BF16)] * NX, (member, table, late), specs=[SMEM, SMEM, VMEM], moved=MIB
+        deal_kernel, [array((tokens // NX, LANES), BF16)] * NX, (late,), moved=MIB
     )
     across = [(x + 2) % NX * NZ + z for x in range(NX) for z in range(NZ)]
     ring = [quarters[0]] + [swap(rows, "mp", level) for rows, level in zip(quarters[1:], (*ALONG_X, across))]
@@ -449,14 +464,13 @@
         part, came = sent, swap(sent, "mp", level)
 
     keep, send = call(
-        piece_kernel, [kept(NX), kept(NX)], (member, core, table, sent, keep, came, *ring),
-        specs=[SMEM] * 3 + [VMEM] * 7, moved=MIB,
+        piece_kernel, [kept(NX), kept(NX)], (sent, keep, came, *ring), moved=MIB,
     )
     keep = keep + swap(send, "dp", ALONG_DP[0])
     keep = total(total(keep, "mp", ALONG_X), "dp", ALONG_DP[1:])
     sent = call(
-        start_kernel, array((QUARTER + 2, 8, LANES), F32), (member, core, table, keep, swap(keep, "dp", ALONG_DP[0]), *ring),
-        specs=[SMEM] * 3 + [VMEM] * 6, moved=MIB,
+        start_kernel, array((QUARTER + 2, 8, LANES), F32), (keep, swap(keep, "dp", ALONG_DP[0]), *ring),
+        moved=MIB,
     )
     for place, level in enumerate(ALONG_Z):
         came = swap(sent, "mp", level)
@@ -468,8 +482,8 @@
     )
     basis, right = call(
         ortho_kernel, [array((NMP, 3 * rank, LANES), BF16), array((rank, ff), F32)],
-        (member, core, table, mine, swap(mine, "dp", ALONG_DP[0]), factor, gt, et),
-        specs=[SMEM] * 3 + [VMEM] * 4 + [HBM],
+        (mine, swap(mine, "dp", ALONG_DP[0]), factor, gt, et),
+        specs=[VMEM] * 4 + [HBM],
         scratch=[
             pltpu.VMEM((NMP + 1, rank, LANES), F32),
             pltpu.VMEM((chunks, ff, width), BF16),
@@ -502,8 +516,8 @@
     outs = call(
         final_kernel,
         [block] * 3 + [array((ff, model), BF16), array((rank, ff), F32)],
-        (dp, right, basis, *halves, weight.T, moment1.T, moment2.T),
-        specs=[SMEM] + [VMEM] * 7,
+        (right, basis, *halves, weight.T, moment1.T, moment2.T),
+        specs=[VMEM] * 7,
         out_specs=[HBM] * 4 + [VMEM],
         scratch=[
             pltpu.VMEM((3, ff, width), F32),

time: 142 us -> 142 us (level)
  waiting for transfers between devices: 49.1 us -> 55.2 us
  Pallas kernels: 29.9 us -> 25.1 us
  starting transfers between devices: 47.2 us -> 45.7 us
    ppermute x24, waiting for transfers between devices: 48.4 us -> 54.5 us  [swap(): return lax.ppermute(value, axis, list(enumerate(level)))]
    pallas_call x18, Pallas kernels: 29.9 us -> 25.1 us  [call(): pl.pallas_call(kernel, out_shape=outs, in_specs=specs or [VMEM] * len(arg...]
    ppermute x24, starting transfers between devices: 47.2 us -> 45.6 us  [swap(): return lax.ppermute(value, axis, list(enumerate(level)))]
  transfers between devices with their start and end apart: 25 -> 25, of which waited for: 18 -> 19; matrix products, arithmetic and copies ran while one was open for 0% -> 0% of each run, Pallas kernels for 18% -> 15%
where the time goes in v10:
time: 142 us; the launch traced here: 141 us
  waiting for transfers between devices  55.2 us (39%)
  starting transfers between devices  45.7 us (32%)
  Pallas kernels  25.1 us (18%)
  between operations  14.3 us (10%)
    ppermute x24, waiting for transfers between devices, swap(): return lax.ppermute(value, axis, list(enumerate(level)))  54.5 us
    ppermute x24, starting transfers between devices, swap(): return lax.ppermute(value, axis, list(enumerate(level)))  45.6 us
    pallas_call x18, Pallas kernels, call(): pl.pallas_call(kernel, out_shape=outs, in_specs=specs or [VMEM] * len(arg...  25.1 us
  transfers between devices with their start and end apart: 25, of which 19 were waited for; matrix products, arithmetic and copies ran while one was open for 0% of the time, Pallas kernels for 15%

profile of v10, /device:TPU:1, one launch (start us, length us, event | category | flops | bytes accessed | tf_op | source)
XLA Modules:
  0.0 141.4 jit_solution(6022473302678753174)
XLA Ops:
  7.9 3.8 %shard_map.111 = (f32[32,16,128]{2,1,0:T(8,128)}, f32[32,16,128]{2,1,0:T(8,128)}) custom-call(f32[32,448]{1,0:T(8,128)} %q_hbm.3, bf16[448,4096]{1,0:T(8,128)(2,1)} %bitcast.10), custom_call_target="tpu_custom_call" | custom-call | flops 352321536 | bytes 3670016 | tf_op jit(solution)/shard_map/pallas_call | solution.py:399
  11.8 3.3 %collective-permute-start = (f32[32,16,128]{2,1,0:T(8,128)}, f32[32,16,128]{2,1,0:T(8,128)S(1)}, u32[]{:S(2)}, u32[]{:S(2)}) collective-permute-start(f32[32,16,128]{2,1,0:T(8,128)} %get-tuple-element.48), channel_id=1, source_target_pairs={{0,32},{32,0},{64,96},{96,64},{128,160},{160,128},{192,224},{224,1... | collective-permute-start | bytes 786440 | tf_op jit(solution)/shard_map/ppermute | solution.py:411
  18.3 6.6 %collective-permute-done.1.came = f32[48,8,128]{2,1,0:T(8,128)S(1)} collective-permute-done((f32[48,8,128]{2,1,0:T(8,128)S(1)}, f32[48,8,128]{2,1,0:T(8,128)S(1)}, u32[]{:S(2)}, u32[]{:S(2)}) %collective-permute-start.1) | collective-permute-done | bytes 196640 | tf_op jit(solution)/shard_map/ppermute | solution.py:411
  25.0 3.5 %collective-permute-done.2.came = f32[24,8,128]{2,1,0:T(8,128)S(1)} collective-permute-done((f32[24,8,128]{2,1,0:T(8,128)S(1)}, f32[24,8,128]{2,1,0:T(8,128)S(1)}, u32[]{:S(2)}, u32[]{:S(2)}) %collective-permute-start.2) | collective-permute-done | bytes 98336 | tf_op jit(solution)/shard_map/ppermute | solution.py:411
  28.7 2.4 %collective-permute-start.6 = (bf16[256,128]{1,0:T(8,128)(2,1)S(1)}, bf16[256,128]{1,0:T(8,128)(2,1)S(1)}, u32[]{:S(2)}, u32[]{:S(2)}) collective-permute-start(bf16[256,128]{1,0:T(8,128)(2,1)S(1)} %get-tuple-element.64), channel_id=1, source_target_pairs={{0,24},{1,25},{2,26},{3,27},{4,28},{5,29},{6,30},{7,31},{8,16},{9,... | collective-permute-start | bytes 196616 | tf_op jit(solution)/shard_map/ppermute | solution.py:411
  32.4 5.5 %collective-permute-start.4 = (f32[12,8,128]{2,1,0:T(8,128)S(1)}, f32[12,8,128]{2,1,0:T(8,128)S(1)}, u32[]{:S(2)}, u32[]{:S(2)}) collective-permute-start(f32[12,8,128]{2,1,0:T(8,128)S(1)} %get-tuple-element.58.tokens), channel_id=1, source_target_pairs={{0,7},{1,2},{2,1},{3,4},{4,3},{5,6},{6,5},{7,0},{8,15},{9,10},{10,... | collective-permute-start | bytes 147464 | tf_op jit(solution)/shard_map/ppermute | solution.py:411
  39.7 2.0 %collective-permute-start.8 = (f32[10,8,128]{2,1,0:T(8,128)S(1)}, f32[10,8,128]{2,1,0:T(8,128)S(1)}, u32[]{:S(2)}, u32[]{:S(2)}) collective-permute-start(f32[10,8,128]{2,1,0:T(8,128)S(1)} %get-tuple-element.66.sent), channel_id=1, source_target_pairs={{0,3},{1,6},{2,5},{3,0},{4,7},{5,2},{6,1},{7,4},{8,11},{9,14},{10,... | collective-permute-start | bytes 122888 | tf_op jit(solution)/shard_map/ppermute | solution.py:411
  41.7 3.7 %collective-permute-done.8.came = f32[10,8,128]{2,1,0:T(8,128)S(1)} collective-permute-done((f32[10,8,128]{2,1,0:T(8,128)S(1)}, f32[10,8,128]{2,1,0:T(8,128)S(1)}, u32[]{:S(2)}, u32[]{:S(2)}) %collective-permute-start.8) | collective-permute-done | bytes 40992 | tf_op jit(solution)/shard_map/ppermute | solution.py:411
  45.5 5.4 %collective-permute-start.9 = (f32[4,16,128]{2,1,0:T(8,128)S(1)}, f32[4,16,128]{2,1,0:T(8,128)S(1)}, u32[]{:S(2)}, u32[]{:S(2)}) collective-permute-start(f32[4,16,128]{2,1,0:T(8,128)S(1)} %get-tuple-element.73), channel_id=1, source_target_pairs={{0,32},{32,0},{64,96},{96,64},{128,160},{160,128},{192,224},{224,1... | collective-permute-start | bytes 98312 | tf_op jit(solution)/shard_map/ppermute | solution.py:411
  51.8 3.2 %collective-permute-done.10 = f32[4,16,128]{2,1,0:T(8,128)S(1)} collective-permute-done((f32[4,16,128]{2,1,0:T(8,128)S(1)}, f32[4,16,128]{2,1,0:T(8,128)S(1)}, u32[]{:S(2)}, u32[]{:S(2)}) %collective-permute-start.10) | collective-permute-done | bytes 32800 | tf_op jit(solution)/shard_map/ppermute | solution.py:411
  61.7 2.4 %collective-permute-start.13 = (f32[4,16,128]{2,1,0:T(8,128)S(1)}, f32[4,16,128]{2,1,0:T(8,128)S(1)}, u32[]{:S(2)}, u32[]{:S(2)}) collective-permute-start(f32[4,16,128]{2,1,0:T(8,128)S(1)} %add.27), channel_id=1, source_target_pairs={{0,192},{32,224},{64,128},{96,160},{128,64},{160,96},{192,0},{224,... | collective-permute-start | bytes 98312 | tf_op jit(solution)/shard_map/ppermute | solution.py:411
  65.7 4.5 %collective-permute-start.14 = (f32[4,16,128]{2,1,0:T(8,128)S(1)}, f32[4,16,128]{2,1,0:T(8,128)S(1)}, u32[]{:S(2)}, u32[]{:S(2)}) collective-permute-start(f32[4,16,128]{2,1,0:T(8,128)S(1)} %add.28.mine), channel_id=1, source_target_pairs={{0,32},{32,0},{64,96},{96,64},{128,160},{160,128},{192,224},{224,1... | collective-permute-start | bytes 98312 | tf_op jit(solution)/shard_map/ppermute | solution.py:411
  71.3 2.5 %collective-permute-start.15 = (f32[10,8,128]{2,1,0:T(8,128)S(1)}, f32[10,8,128]{2,1,0:T(8,128)S(1)}, u32[]{:S(2)}, u32[]{:S(2)}) collective-permute-start(f32[10,8,128]{2,1,0:T(8,128)S(1)} %shard_map.119.sent), channel_id=1, source_target_pairs={{0,3},{1,6},{2,5},{3,0},{4,7},{5,2},{6,1},{7,4},{8,11},{9,14},{10,... | collective-permute-start | bytes 122888 | tf_op jit(solution)/shard_map/ppermute | solution.py:411
  73.7 3.4 %collective-permute-done.15.came = f32[10,8,128]{2,1,0:T(8,128)S(1)} collective-permute-done((f32[10,8,128]{2,1,0:T(8,128)S(1)}, f32[10,8,128]{2,1,0:T(8,128)S(1)}, u32[]{:S(2)}, u32[]{:S(2)}) %collective-permute-start.15) | collective-permute-done | bytes 40992 | tf_op jit(solution)/shard_map/ppermute | solution.py:411
  77.2 3.0 %collective-permute-start.16 = (f32[12,8,128]{2,1,0:T(8,128)S(1)}, f32[12,8,128]{2,1,0:T(8,128)S(1)}, u32[]{:S(2)}, u32[]{:S(2)}) collective-permute-start(f32[12,8,128]{2,1,0:T(8,128)S(1)} %shard_map.120.sent), channel_id=1, source_target_pairs={{0,7},{1,2},{2,1},{3,4},{4,3},{5,6},{6,5},{7,0},{8,15},{9,10},{10,... | collective-permute-start | bytes 147464 | tf_op jit(solution)/shard_map/ppermute | solution.py:411
  80.3 2.3 %collective-permute-done.16.came = f32[12,8,128]{2,1,0:T(8,128)S(1)} collective-permute-done((f32[12,8,128]{2,1,0:T(8,128)S(1)}, f32[12,8,128]{2,1,0:T(8,128)S(1)}, u32[]{:S(2)}, u32[]{:S(2)}) %collective-permute-start.16) | collective-permute-done | bytes 49184 | tf_op jit(solution)/shard_map/ppermute | solution.py:411
  83.1 4.6 %collective-permute-done.17.came = f32[16,8,128]{2,1,0:T(8,128)S(1)} collective-permute-done((f32[16,8,128]{2,1,0:T(8,128)S(1)}, f32[16,8,128]{2,1,0:T(8,128)S(1)}, u32[]{:S(2)}, u32[]{:S(2)}) %collective-permute-start.17) | collective-permute-done | bytes 65568 | tf_op jit(solution)/shard_map/ppermute | solution.py:411
  87.8 6.1 %collective-permute-done.18 = f32[24,8,128]{2,1,0:T(8,128)S(1)} collective-permute-done((f32[24,8,128]{2,1,0:T(8,128)S(1)}, f32[24,8,128]{2,1,0:T(8,128)S(1)}, u32[]{:S(2)}, u32[]{:S(2)}) %collective-permute-start.18) | collective-permute-done | bytes 98336 | tf_op jit(solution)/shard_map/ppermute | solution.py:411
  95.6 9.7 %collective-permute-done.19.came = f32[48,8,128]{2,1,0:T(8,128)S(1)} collective-permute-done((f32[48,8,128]{2,1,0:T(8,128)S(1)}, f32[48,8,128]{2,1,0:T(8,128)S(1)}, u32[]{:S(2)}, u32[]{:S(2)}) %collective-permute-start.19) | collective-permute-done | bytes 196640 | tf_op jit(solution)/shard_map/ppermute | solution.py:411
  108.0 7.2 %shard_map.124 = (bf16[32,96,128]{2,1,0:T(8,128)(2,1)S(1)}, f32[32,448]{1,0:T(8,128)S(1)}) custom-call(f32[64,8,128]{2,1,0:T(8,128)S(1)} %get-tuple-element.74.mine, f32[64,8,128]{2,1,0:T(8,128)S(1)} %collective-permute-done.20.theirs, f32[32,8,128]{2,1,0:T(8,128)S(1)} %get-tuple-element.75.tokens, bf16[448,1024]{1,0:T(8,128)(2,1)S(1)} %bitcast.15, ...), custom_call_target="tpu_custom_call" | custom-call | flops 469762048 | bytes 3670016 | tf_op jit(solution)/shard_map/pallas_call | solution.py:399
  116.7 4.2 %shard_map.125.lower = f32[16,448,128]{2,1,0:T(8,128)S(1)} custom-call(bf16[32,1024,128]{2,1,0:T(8,128)(2,1)} %bitcast.21, bf16[448,4096]{1,0:T(8,128)(2,1)} %bitcast.11, bf16[448,1024]{1,0:T(8,128)(2,1)S(1)} %bitcast.16), custom_call_target="tpu_custom_call" | custom-call | flops 1879048192 | bytes 10485760 | tf_op jit(solution)/shard_map/pallas_call | solution.py:399
  122.8 4.2 %shard_map.126.upper = f32[16,448,128]{2,1,0:T(8,128)S(1)} custom-call(bf16[32,1024,128]{2,1,0:T(8,128)(2,1)} %bitcast.22, bf16[448,4096]{1,0:T(8,128)(2,1)} %bitcast.12, bf16[448,1024]{1,0:T(8,128)(2,1)S(1)} %bitcast.17), custom_call_target="tpu_custom_call" | custom-call | flops 1879048192 | bytes 10485760 | tf_op jit(solution)/shard_map/pallas_call | solution.py:399
  127.1 2.0 %collective-permute-start.23 = (f32[32,448]{1,0:T(8,128)S(1)}, f32[32,448]{1,0:T(8,128)S(1)}, u32[]{:S(2)}, u32[]{:S(2)}) collective-permute-start(f32[32,448]{1,0:T(8,128)S(1)} %add.30), channel_id=1, source_target_pairs={{0,32},{32,0},{64,96},{96,64},{128,160},{160,128},{192,224},{224,1... | collective-permute-start | bytes 172040 | tf_op jit(solution)/shard_map/ppermute | solution.py:411
  130.0 4.5 %shard_map.127 = (f32[448,512]{1,0:T(8,128)}, f32[448,512]{1,0:T(8,128)}, f32[448,512]{1,0:T(8,128)}, bf16[448,4096]{1,0:T(8,128)(2,1)}, f32[32,448]{1,0:T(8,128)}) custom-call(f32[32,448]{1,0:T(8,128)S(1)} %add.31.sum_ref, bf16[32,96,128]{2,1,0:T(8,128)(2,1)S(1)} %get-tuple-element.81.basis_ref, f32[16,448,128]{2,1,0:T(8,128)S(1)} %shard_map.125.lower, ...), custom_call_target="tpu_custom_call" | custom-call | flops 704643072 | bytes 20971520 | tf_op jit(solution)/shard_map/pallas_call | solution.py:399
  (70 shorter events, 26.9 us)
Async XLA Ops:
  7.2 108.0 %all-gather.3.cloned.1.call-start = ((), (), s32[]{:S(2)}) async-start(), calls=%async_computation | async-start | bytes 8650752 | tf_op jit(solution)/shard_map/all_gather | solution.py:427
  11.8 4.7 %collective-permute-start = (f32[32,16,128]{2,1,0:T(8,128)}, f32[32,16,128]{2,1,0:T(8,128)S(1)}, u32[]{:S(2)}, u32[]{:S(2)}) collective-permute-start(f32[32,16,128]{2,1,0:T(8,128)} %get-tuple-element.48), channel_id=1, source_target_pairs={{0,32},{32,0},{64,96},{96,64},{128,160},{160,128},{192,224},{224,1... | collective-permute-start | bytes 786440 | tf_op jit(solution)/shard_map/ppermute | solution.py:411
  17.5 7.4 %collective-permute-start.1 = (f32[48,8,128]{2,1,0:T(8,128)S(1)}, f32[48,8,128]{2,1,0:T(8,128)S(1)}, u32[]{:S(2)}, u32[]{:S(2)}) collective-permute-start(f32[48,8,128]{2,1,0:T(8,128)S(1)} %get-tuple-element.52), channel_id=1, source_target_pairs={{0,24},{1,25},{2,26},{3,27},{4,28},{5,29},{6,30},{7,31},{8,16},{9,... | collective-permute-start | bytes 589832 | tf_op jit(solution)/shard_map/ppermute | solution.py:411
  24.9 3.6 %collective-permute-start.2 = (f32[24,8,128]{2,1,0:T(8,128)S(1)}, f32[24,8,128]{2,1,0:T(8,128)S(1)}, u32[]{:S(2)}, u32[]{:S(2)}) collective-permute-start(f32[24,8,128]{2,1,0:T(8,128)S(1)} %get-tuple-element.55), channel_id=1, source_target_pairs={{0,8},{1,9},{2,10},{3,11},{4,12},{5,13},{6,14},{7,15},{8,0},{9,1},... | collective-permute-start | bytes 294920 | tf_op jit(solution)/shard_map/ppermute | solution.py:411
  28.5 3.9 %collective-permute-start.3 = (f32[16,8,128]{2,1,0:T(8,128)S(1)}, f32[16,8,128]{2,1,0:T(8,128)S(1)}, u32[]{:S(2)}, u32[]{:S(2)}) collective-permute-start(f32[16,8,128]{2,1,0:T(8,128)S(1)} %get-tuple-element.56.tokens), channel_id=1, source_target_pairs={{0,1},{1,0},{2,3},{3,2},{4,5},{5,4},{6,7},{7,6},{8,9},{9,8},{10,11... | collective-permute-start | bytes 196616 | tf_op jit(solution)/shard_map/ppermute | solution.py:411
  28.6 11.0 %collective-permute-start.5 = (bf16[256,128]{1,0:T(8,128)(2,1)S(1)}, bf16[256,128]{1,0:T(8,128)(2,1)S(1)}, u32[]{:S(2)}, u32[]{:S(2)}) collective-permute-start(bf16[256,128]{1,0:T(8,128)(2,1)S(1)} %get-tuple-element.63), channel_id=1, source_target_pairs={{0,8},{1,9},{2,10},{3,11},{4,12},{5,13},{6,14},{7,15},{8,0},{9,1},... | collective-permute-start | bytes 196616 | tf_op jit(solution)/shard_map/ppermute | solution.py:411
  28.7 10.9 %collective-permute-start.6 = (bf16[256,128]{1,0:T(8,128)(2,1)S(1)}, bf16[256,128]{1,0:T(8,128)(2,1)S(1)}, u32[]{:S(2)}, u32[]{:S(2)}) collective-permute-start(bf16[256,128]{1,0:T(8,128)(2,1)S(1)} %get-tuple-element.64), channel_id=1, source_target_pairs={{0,24},{1,25},{2,26},{3,27},{4,28},{5,29},{6,30},{7,31},{8,16},{9,... | collective-permute-start | bytes 196616 | tf_op jit(solution)/shard_map/ppermute | solution.py:411
  31.2 8.5 %collective-permute-start.7 = (bf16[256,128]{1,0:T(8,128)(2,1)S(1)}, bf16[256,128]{1,0:T(8,128)(2,1)S(1)}, u32[]{:S(2)}, u32[]{:S(2)}) collective-permute-start(bf16[256,128]{1,0:T(8,128)(2,1)S(1)} %get-tuple-element.65), channel_id=1, source_target_pairs={{0,16},{1,17},{2,18},{3,19},{4,20},{5,21},{6,22},{7,23},{8,24},{9,... | collective-permute-start | bytes 196616 | tf_op jit(solution)/shard_map/ppermute | solution.py:411
  32.4 7.2 %collective-permute-start.4 = (f32[12,8,128]{2,1,0:T(8,128)S(1)}, f32[12,8,128]{2,1,0:T(8,128)S(1)}, u32[]{:S(2)}, u32[]{:S(2)}) collective-permute-start(f32[12,8,128]{2,1,0:T(8,128)S(1)} %get-tuple-element.58.tokens), channel_id=1, source_target_pairs={{0,7},{1,2},{2,1},{3,4},{4,3},{5,6},{6,5},{7,0},{8,15},{9,10},{10,... | collective-permute-start | bytes 147464 | tf_op jit(solution)/shard_map/ppermute | solution.py:411
  39.7 5.7 %collective-permute-start.8 = (f32[10,8,128]{2,1,0:T(8,128)S(1)}, f32[10,8,128]{2,1,0:T(8,128)S(1)}, u32[]{:S(2)}, u32[]{:S(2)}) collective-permute-start(f32[10,8,128]{2,1,0:T(8,128)S(1)} %get-tuple-element.66.sent), channel_id=1, source_target_pairs={{0,3},{1,6},{2,5},{3,0},{4,7},{5,2},{6,1},{7,4},{8,11},{9,14},{10,... | collective-permute-start | bytes 122888 | tf_op jit(solution)/shard_map/ppermute | solution.py:411
  45.5 6.2 %collective-permute-start.9 = (f32[4,16,128]{2,1,0:T(8,128)S(1)}, f32[4,16,128]{2,1,0:T(8,128)S(1)}, u32[]{:S(2)}, u32[]{:S(2)}) collective-permute-start(f32[4,16,128]{2,1,0:T(8,128)S(1)} %get-tuple-element.73), channel_id=1, source_target_pairs={{0,32},{32,0},{64,96},{96,64},{128,160},{160,128},{192,224},{224,1... | collective-permute-start | bytes 98312 | tf_op jit(solution)/shard_map/ppermute | solution.py:411
  51.8 3.2 %collective-permute-start.10 = (f32[4,16,128]{2,1,0:T(8,128)S(1)}, f32[4,16,128]{2,1,0:T(8,128)S(1)}, u32[]{:S(2)}, u32[]{:S(2)}) collective-permute-start(f32[4,16,128]{2,1,0:T(8,128)S(1)} %add.24), channel_id=1, source_target_pairs={{0,8},{1,9},{2,10},{3,11},{4,12},{5,13},{6,14},{7,15},{8,0},{9,1},... | collective-permute-start | bytes 98312 | tf_op jit(solution)/shard_map/ppermute | solution.py:411
  54.9 4.0 %collective-permute-start.11 = (f32[4,16,128]{2,1,0:T(8,128)S(1)}, f32[4,16,128]{2,1,0:T(8,128)S(1)}, u32[]{:S(2)}, u32[]{:S(2)}) collective-permute-start(f32[4,16,128]{2,1,0:T(8,128)S(1)} %add.25), channel_id=1, source_target_pairs={{0,24},{1,25},{2,26},{3,27},{4,28},{5,29},{6,30},{7,31},{8,16},{9,... | collective-permute-start | bytes 98312 | tf_op jit(solution)/shard_map/ppermute | solution.py:411
  58.9 2.8 %collective-permute-start.12 = (f32[4,16,128]{2,1,0:T(8,128)S(1)}, f32[4,16,128]{2,1,0:T(8,128)S(1)}, u32[]{:S(2)}, u32[]{:S(2)}) collective-permute-start(f32[4,16,128]{2,1,0:T(8,128)S(1)} %add.26), channel_id=1, source_target_pairs={{0,64},{32,96},{64,0},{96,32},{128,192},{160,224},{192,128},{224,1... | collective-permute-start | bytes 98312 | tf_op jit(solution)/shard_map/ppermute | solution.py:411
  61.7 4.0 %collective-permute-start.13 = (f32[4,16,128]{2,1,0:T(8,128)S(1)}, f32[4,16,128]{2,1,0:T(8,128)S(1)}, u32[]{:S(2)}, u32[]{:S(2)}) collective-permute-start(f32[4,16,128]{2,1,0:T(8,128)S(1)} %add.27), channel_id=1, source_target_pairs={{0,192},{32,224},{64,128},{96,160},{128,64},{160,96},{192,0},{224,... | collective-permute-start | bytes 98312 | tf_op jit(solution)/shard_map/ppermute | solution.py:411
  65.7 5.4 %collective-permute-start.14 = (f32[4,16,128]{2,1,0:T(8,128)S(1)}, f32[4,16,128]{2,1,0:T(8,128)S(1)}, u32[]{:S(2)}, u32[]{:S(2)}) collective-permute-start(f32[4,16,128]{2,1,0:T(8,128)S(1)} %add.28.mine), channel_id=1, source_target_pairs={{0,32},{32,0},{64,96},{96,64},{128,160},{160,128},{192,224},{224,1... | collective-permute-start | bytes 98312 | tf_op jit(solution)/shard_map/ppermute | solution.py:411
  71.3 5.9 %collective-permute-start.15 = (f32[10,8,128]{2,1,0:T(8,128)S(1)}, f32[10,8,128]{2,1,0:T(8,128)S(1)}, u32[]{:S(2)}, u32[]{:S(2)}) collective-permute-start(f32[10,8,128]{2,1,0:T(8,128)S(1)} %shard_map.119.sent), channel_id=1, source_target_pairs={{0,3},{1,6},{2,5},{3,0},{4,7},{5,2},{6,1},{7,4},{8,11},{9,14},{10,... | collective-permute-start | bytes 122888 | tf_op jit(solution)/shard_map/ppermute | solution.py:411
  77.2 5.4 %collective-permute-start.16 = (f32[12,8,128]{2,1,0:T(8,128)S(1)}, f32[12,8,128]{2,1,0:T(8,128)S(1)}, u32[]{:S(2)}, u32[]{:S(2)}) collective-permute-start(f32[12,8,128]{2,1,0:T(8,128)S(1)} %shard_map.120.sent), channel_id=1, source_target_pairs={{0,7},{1,2},{2,1},{3,4},{4,3},{5,6},{6,5},{7,0},{8,15},{9,10},{10,... | collective-permute-start | bytes 147464 | tf_op jit(solution)/shard_map/ppermute | solution.py:411
  82.6 5.1 %collective-permute-start.17 = (f32[16,8,128]{2,1,0:T(8,128)S(1)}, f32[16,8,128]{2,1,0:T(8,128)S(1)}, u32[]{:S(2)}, u32[]{:S(2)}) collective-permute-start(f32[16,8,128]{2,1,0:T(8,128)S(1)} %shard_map.121.sent), channel_id=1, source_target_pairs={{0,1},{1,0},{2,3},{3,2},{4,5},{5,4},{6,7},{7,6},{8,9},{9,8},{10,11... | collective-permute-start | bytes 196616 | tf_op jit(solution)/shard_map/ppermute | solution.py:411
  87.7 6.2 %collective-permute-start.18 = (f32[24,8,128]{2,1,0:T(8,128)S(1)}, f32[24,8,128]{2,1,0:T(8,128)S(1)}, u32[]{:S(2)}, u32[]{:S(2)}) collective-permute-start(f32[24,8,128]{2,1,0:T(8,128)S(1)} %shard_map.122), channel_id=1, source_target_pairs={{0,8},{1,9},{2,10},{3,11},{4,12},{5,13},{6,14},{7,15},{8,0},{9,1},... | collective-permute-start | bytes 294920 | tf_op jit(solution)/shard_map/ppermute | solution.py:411
  93.9 11.4 %collective-permute-start.19 = (f32[48,8,128]{2,1,0:T(8,128)S(1)}, f32[48,8,128]{2,1,0:T(8,128)S(1)}, u32[]{:S(2)}, u32[]{:S(2)}) collective-permute-start(f32[48,8,128]{2,1,0:T(8,128)S(1)} %pad_maximum_fusion.sent), channel_id=1, source_target_pairs={{0,24},{1,25},{2,26},{3,27},{4,28},{5,29},{6,30},{7,31},{8,16},{9,... | collective-permute-start | bytes 589832 | tf_op jit(solution)/shard_map/ppermute | solution.py:411
  115.2 5.7 %collective-permute-start.21 = (f32[32,448]{1,0:T(8,128)S(1)}, f32[32,448]{1,0:T(8,128)S(1)}, u32[]{:S(2)}, u32[]{:S(2)}) collective-permute-start(f32[32,448]{1,0:T(8,128)S(1)} %get-tuple-element.77), channel_id=1, source_target_pairs={{0,64},{32,96},{64,0},{96,32},{128,192},{160,224},{192,128},{224,1... | collective-permute-start | bytes 172040 | tf_op jit(solution)/shard_map/ppermute | solution.py:411
  121.0 6.0 %collective-permute-start.22 = (f32[32,448]{1,0:T(8,128)S(1)}, f32[32,448]{1,0:T(8,128)S(1)}, u32[]{:S(2)}, u32[]{:S(2)}) collective-permute-start(f32[32,448]{1,0:T(8,128)S(1)} %add.29), channel_id=1, source_target_pairs={{0,192},{32,224},{64,128},{96,160},{128,64},{160,96},{192,0},{224,... | collective-permute-start | bytes 172040 | tf_op jit(solution)/shard_map/ppermute | solution.py:411
  127.1 2.9 %collective-permute-start.23 = (f32[32,448]{1,0:T(8,128)S(1)}, f32[32,448]{1,0:T(8,128)S(1)}, u32[]{:S(2)}, u32[]{:S(2)}) collective-permute-start(f32[32,448]{1,0:T(8,128)S(1)} %add.30), channel_id=1, source_target_pairs={{0,32},{32,0},{64,96},{96,64},{128,160},{160,128},{192,224},{224,1... | collective-permute-start | bytes 172040 | tf_op jit(solution)/shard_map/ppermute | solution.py:411
  (9 other events, 168.1 us)
Sparse Core Ops, SparseCore 0:
  10.6 104.4 all-gather.2
